TPU v7x, 32 devices: a whole 2x2x4 slice. The times are simulated.
32 devices in a mesh: group: 4 (over y, core), member: 8 (over z, x).
Axes of the slice: x: 2, y: 2, z: 4, core: 2. Of those that a mesh axis runs over, the one named last changes fastest.
Arguments:
- heads: bfloat16 [65536, 768], P(('group', 'member')), may hold values from -16 to 16
- new_heads: bfloat16 [64, 768], P('group'), may hold values from -16 to 16
- vectors: bfloat16 [32, 128, 768], P(('group', 'member')), may hold values from -16 to 16
- near_ids: int32 [32, 64], P(('group', 'member')), may hold values from 0 to 16383, as said below
Outputs:
- density: float32 [64], P('group')
- spread: float32 [64], P('group')
- reassign: float32 [32, 64, 128], P(('group', 'member'))
Inputs may be any that keep to these rules, and one draw needn't show every extreme that they name: `near_ids`: each row holds 64 different numbers; of one row at most 16 lie in one range j * 2048 to (j + 1) * 2048 - 1, and exactly 16 in some such range.
All inputs are finite; a program needn't handle non-finite values.
Results may differ from a plain program's by a relative error of at most 0.0003.
Values may be sent and summed in bfloat16 or wider, within the bound.
No kernel may reach another device: no remote copies, remote signals or barrier semaphores. Data moves between devices by JAX's collectives and lax.ppermute only.
A program may use at most 64 MiB of HBM per device.

v0:
```python
import jax
import jax.numpy as jnp
from jax import lax
from jax.sharding import PartitionSpec as P


def passed_along(value, axis, steps):
    count = lax.axis_size(axis)
    pairs = [(source, (source + steps) % count) for source in range(count)]
    return lax.ppermute(value, axis, pairs)


def crowding(block, heads, head_sq, width):
    query_sq = jnp.sum(jnp.square(block.astype(jnp.float32)), axis=1)
    dots = lax.dot_general(
        block, heads, (((1,), (1,)), ((), ())), preferred_element_type=jnp.float32
    )
    excess = (query_sq[:, None] + head_sq[None, :] - 2.0 * dots) / width
    weight = 1.0 / jnp.square(1.0 + excess)
    return jnp.stack([jnp.sum(weight, axis=1), jnp.sum(weight * excess, axis=1)])


def distances(vec, rows, width):
    vec_sq = jnp.sum(jnp.square(vec.astype(jnp.float32)), axis=2)
    row_sq = jnp.sum(jnp.square(rows.astype(jnp.float32)), axis=2)
    dots = jnp.einsum("pbd,pkd->pkb", vec, rows, preferred_element_type=jnp.float32)
    return (row_sq[:, :, None] + vec_sq[:, None, :] - 2.0 * dots) / width


def per_device(heads, new_heads, vectors, near_ids):
    head_dev = heads.shape[0]
    width = heads.shape[1]
    groups = lax.axis_size("group")
    members = lax.axis_size("member")
    here = lax.axis_index("group")
    me = lax.axis_index("member")
    head_sq = jnp.sum(jnp.square(heads.astype(jnp.float32)), axis=1)
    new_count = new_heads.shape[0]
    table = jnp.zeros((groups, 2, new_count), jnp.float32)
    table = lax.dynamic_update_slice(
        table, crowding(new_heads, heads, head_sq, width)[None], (here, 0, 0)
    )

    def advance(step, carry):
        block, sums = carry
        block = passed_along(block, "group", 1)
        anchor = (here - step) % groups
        sums = lax.dynamic_update_slice(
            sums, crowding(block, heads, head_sq, width)[None], (anchor, 0, 0)
        )
        return (block, sums)

    unused, table = lax.fori_loop(1, groups, advance, (new_heads, table))
    mine = lax.psum_scatter(table, "group", scatter_dimension=0, tiled=True)
    mine = lax.psum(mine, "member")
    total_heads = float(head_dev * groups * members)
    density = jnp.log(mine[0, 0] / total_heads)
    spread = mine[0, 1] / mine[0, 0]
    lists = lax.all_gather(near_ids, "member", axis=0, tiled=True)
    blocks = lax.all_gather(vectors, "member", axis=0, tiled=True)
    owner = lists // head_dev
    local = lists % head_dev
    rows = jnp.take(heads, local, axis=0)
    rows, owned = (rows, owner == me)
    reassign = lax.psum_scatter(
        jnp.where(owned[:, :, None], distances(blocks, rows, width), 0.0),
        "member",
        scatter_dimension=0,
        tiled=True,
    )
    return (density, spread, reassign)


def solution(mesh):
    placed = (
        P(("group", "member"), None),
        P("group", None),
        P(("group", "member"), None, None),
        P(("group", "member"), None),
    )
    return jax.shard_map(
        per_device,
        mesh=mesh,
        in_specs=placed,
        out_specs=(P("group"), P("group"), P(("group", "member"), None, None)),
        check_vma=False,
    )
```

profile of v0, /device:TPU:0, one launch (start us, length us, event | category | flops | bytes accessed | tf_op | source)
XLA Modules:
  0.0 129.0 jit_solution(6749447470785828070)
XLA Ops:
  7.2 0.0 all-gather.3.cloned.1.call-start
  7.2 0.7 copy.19
  8.0 0.0 reduce-scatter.2.cloned.1.call-start
  8.0 22.3 %all-gather = s32[8,1,64]{2,1,0:T(1,128)S(1)} all-gather(s32[1,1,64]{2,1,0:T(1,128)} %bitcast.42), channel_id=1, replica_groups=mesh['group'=4,'member'=8] {'member'}, dimensions={0}, use_global_device_ids=true | all-gather | bytes 2304 | tf_op jit(solution)/shard_map/all_gather | solution.py:59
  30.4 0.1 reshape.24
  30.5 1.2 dynamic-slice
  31.7 5.5 %gather_fusion = bf16[512,768]{1,0:T(8,128)(2,1)} fusion(bf16[2048,768]{1,0:T(8,128)(2,1)} %param.6, s32[1024]{0:T(1024)S(1)} %pad_clamp_fusion), kind=kCustom, calls=%fused_computation | custom fusion | bytes 1574912 | tf_op jit(solution)/shard_map/jit(_take)/gather | solution.py:63
  37.3 0.1 multiply_reduce_fusion.6
  37.4 0.7 multiply_reduce_fusion.2
  38.1 1.1 fusion.8
  39.2 0.4 multiply_reduce_fusion.4
  39.6 17.5 %all-gather.3.cloned.1.call-done = bf16[8,128,768]{2,1,0:T(8,128)(2,1)} async-done(((bf16[1,128,768]{2,1,0:T(8,128)(2,1)}), bf16[8,128,768]{2,1,0:T(8,128)(2,1)}) %all-gather.3.cloned.1.call-update) | async-done | bytes 1572880 | tf_op jit(solution)/shard_map/all_gather | solution.py:60
  57.1 1.8 %multiply_reduce_fusion.3 = f32[8,128]{1,0:T(8,128)S(1)} fusion(bf16[8,128,768]{2,1,0:T(8,128)(2,1)} %all-gather.3.cloned.1.call-done), kind=kLoop, calls=%fused_computation.10 | loop fusion | flops 2358272 | bytes 1576960 | tf_op jit(solution)/shard_map/reduce_sum | solution.py:24
  58.9 3.1 %fusion.6 = f32[8,64,128]{2,1,0:T(8,128)} fusion(bf16[8,128,768]{2,1,0:T(8,128)(2,1)} %all-gather.3.cloned.1.call-done, bf16[8,64,768]{2,1,0:T(8,128)(2,1)} %bitcast.35, pred[8,64]{1,0:T(8,128)(4,1)S(1)} %get-tuple-element.175, f32[8,128]{1,0:T(8,128)S(1)} %multiply_reduce_fusion.3, f32[8,64]{1,0:T(8,128)S(1)} %multiply_reduce_fusion.4, ...), kind=kOutput, calls=%fused_computation.18 | convolution fusion | flops 101384192 | bytes 2628608 | tf_op jit(solution)/shard_map/pbd,pkd->pkb/dot_general | solution.py:26
  62.0 13.6 %while.17 = (s32[]{:T(128)}, bf16[16,768]{1,0:T(8,128)(2,1)S(1)}, f32[4,2,16]{2,1,0:T(2,128)S(1)}, f32[2048]{0:T(1024)S(1)}, bf16[2048,768]{1,0:T(8,128)(2,1)S(1...) while((s32[]{:T(128)}, bf16[16,768]{1,0:T(8,128)(2,1)S(1)}, f32[4,2,16]{2,1,0:T(2,128)S(1)}, ...), condition=%wide.region_8.9_spmd, body=%wide.region_4.8_spmd.sunk | while | flops 50696192 | bytes 3353132 | solution.py:53
  62.0 0.1 collective-permute-start
  62.1 3.2 %collective-permute-done = bf16[16,768]{1,0:T(8,128)(2,1)S(1)} collective-permute-done((bf16[16,768]{1,0:T(8,128)(2,1)S(1)}, bf16[16,768]{1,0:T(8,128)(2,1)S(1)}, u32[]{:S(2)}, u32[]{:S(2)}) %collective-permute-start) | collective-permute-done | bytes 24608 | tf_op jit(solution)/shard_map/while/body/eval_jaxpr/ppermute | solution.py:10
  65.3 0.1 multiply_reduce_fusion.8
  65.4 1.1 fusion.26
  66.5 0.1 collective-permute-start
  66.6 3.2 %collective-permute-done = bf16[16,768]{1,0:T(8,128)(2,1)S(1)} collective-permute-done((bf16[16,768]{1,0:T(8,128)(2,1)S(1)}, bf16[16,768]{1,0:T(8,128)(2,1)S(1)}, u32[]{:S(2)}, u32[]{:S(2)}) %collective-permute-start) | collective-permute-done | bytes 24608 | tf_op jit(solution)/shard_map/while/body/eval_jaxpr/ppermute | solution.py:10
  69.8 0.1 multiply_reduce_fusion.8
  69.9 1.1 fusion.26
  71.0 0.1 collective-permute-start
  71.1 3.2 %collective-permute-done = bf16[16,768]{1,0:T(8,128)(2,1)S(1)} collective-permute-done((bf16[16,768]{1,0:T(8,128)(2,1)S(1)}, bf16[16,768]{1,0:T(8,128)(2,1)S(1)}, u32[]{:S(2)}, u32[]{:S(2)}) %collective-permute-start) | collective-permute-done | bytes 24608 | tf_op jit(solution)/shard_map/while/body/eval_jaxpr/ppermute | solution.py:10
  74.3 0.1 multiply_reduce_fusion.8
  74.5 1.1 fusion.26
  75.6 6.1 %all-reduce = f32[4,2,16]{2,1,0:T(2,128)S(1)} all-reduce(f32[4,2,16]{2,1,0:T(2,128)S(1)} %get-tuple-element.158), channel_id=2, replica_groups=mesh['group'=4,'member'=8] {'group'}, use_global_device_ids=true, to_apply=%region_9.10.clone | all-reduce | flops 128 | bytes 1024
  81.6 0.6 constant_dynamic-slice_fusion
  82.3 19.3 %psum.7 = f32[1,2,16]{2,1,0:T(2,128)S(1)} all-reduce(f32[1,2,16]{2,1,0:T(2,128)S(1)} %constant_dynamic-slice_fusion), channel_id=1, replica_groups=mesh['group'=4,'member'=8] {'member'}, use_global_device_ids=true, to_apply=%region_10.11 | all-reduce | flops 32 | bytes 256 | tf_op jit(solution)/shard_map/psum | solution.py:55
  101.5 0.5 fusion.13
  102.0 20.1 %reduce-scatter.2.cloned.1.call-done = f32[1,64,128]{2,1,0:T(8,128)} async-done(((f32[8,64,128]{2,1,0:T(8,128)}), f32[1,64,128]{2,1,0:T(8,128)}) %reduce-scatter.2.cloned.1.call-update) | async-done | bytes 32784 | tf_op jit(solution)/shard_map/reduce_scatter | solution.py:65
  (16 shorter events, 0.2 us)
Async XLA Ops:
  7.2 49.9 %all-gather.3.cloned.1.call-start = ((), (), s32[]{:S(2)}) async-start(), calls=%async_computation.1 | async-start | bytes 1769472 | tf_op jit(solution)/shard_map/all_gather | solution.py:60
  8.0 114.2 %reduce-scatter.2.cloned.1.call-start = ((), (), s32[]{:S(2)}) async-start(), calls=%async_computation.2 | async-start | bytes 294912 | tf_op jit(solution)/shard_map/reduce_scatter | solution.py:65
  31.7 5.7 %copy-start = (bf16[2048,768]{1,0:T(8,128)(2,1)S(1)}, bf16[2048,768]{1,0:T(8,128)(2,1)}, u32[]{:S(2)}) copy-start(bf16[2048,768]{1,0:T(8,128)(2,1)} %param.6) | copy-start | bytes 9437188
  37.4 1.8 %copy-start.1 = (bf16[512,768]{1,0:T(8,128)(2,1)S(1)}, bf16[512,768]{1,0:T(8,128)(2,1)}, u32[]{:S(2)}) copy-start(bf16[512,768]{1,0:T(8,128)(2,1)} %gather_fusion) | copy-start | bytes 2359300
  62.0 3.3 %collective-permute-start = (bf16[16,768]{1,0:T(8,128)(2,1)S(1)}, bf16[16,768]{1,0:T(8,128)(2,1)S(1)}, u32[]{:S(2)}, u32[]{:S(2)}) collective-permute-start(bf16[16,768]{1,0:T(8,128)(2,1)S(1)} %get-tuple-element.232), channel_id=1, source_target_pairs={{0,8},{8,16},{16,24},{24,0},{1,9},{9,17},{17,25},{25,1},{2,10},{10... | collective-permute-start | bytes 73736 | tf_op jit(solution)/shard_map/while/body/eval_jaxpr/ppermute | solution.py:10
  66.5 3.3 %collective-permute-start = (bf16[16,768]{1,0:T(8,128)(2,1)S(1)}, bf16[16,768]{1,0:T(8,128)(2,1)S(1)}, u32[]{:S(2)}, u32[]{:S(2)}) collective-permute-start(bf16[16,768]{1,0:T(8,128)(2,1)S(1)} %get-tuple-element.232), channel_id=1, source_target_pairs={{0,8},{8,16},{16,24},{24,0},{1,9},{9,17},{17,25},{25,1},{2,10},{10... | collective-permute-start | bytes 73736 | tf_op jit(solution)/shard_map/while/body/eval_jaxpr/ppermute | solution.py:10
  71.0 3.3 %collective-permute-start = (bf16[16,768]{1,0:T(8,128)(2,1)S(1)}, bf16[16,768]{1,0:T(8,128)(2,1)S(1)}, u32[]{:S(2)}, u32[]{:S(2)}) collective-permute-start(bf16[16,768]{1,0:T(8,128)(2,1)S(1)} %get-tuple-element.232), channel_id=1, source_target_pairs={{0,8},{8,16},{16,24},{24,0},{1,9},{9,17},{17,25},{25,1},{2,10},{10... | collective-permute-start | bytes 73736 | tf_op jit(solution)/shard_map/while/body/eval_jaxpr/ppermute | solution.py:10
Sparse Core Ops, SparseCore 0:
  10.2 46.8 all-gather.2
  62.1 60.0 reduce-scatter.1
where the time goes:
time: 129 us
  blocking collectives  47.7 us (37%)
  waiting for transfers between devices  47.3 us (37%)
  between operations  14.1 us (11%)
  local copies, waits for them, and re-layouts  8.25 us (6%)
  matrix products  7.29 us (6%)
  other arithmetic  3.94 us (3%)
    all_gather x1, blocking collectives, per_device(): lists = lax.all_gather(near_ids, 'member', axis=0, tiled=True)  22.3 us
    reduce_scatter x1, waiting for transfers between devices, per_device(): lax.psum_scatter(jnp.where(owned[:, :, None], distances(blocks, rows, wid...  20.1 us
    psum x1, blocking collectives, per_device(): mine = lax.psum(mine, 'member')  19.3 us
    all_gather x1, waiting for transfers between devices, per_device(): blocks = lax.all_gather(vectors, 'member', axis=0, tiled=True)  17.5 us
    ppermute x3, waiting for transfers between devices, passed_along(): return lax.ppermute(value, axis, pairs)  9.64 us
    unnamed x1, blocking collectives  6.07 us
    gather x1, local copies, waits for them, and re-layouts, per_device(): rows = jnp.take(heads, local, axis=0)  5.55 us
    dot_general x4, matrix products, crowding(): lax.dot_general(block, heads, (((1,), (1,)), ((), ())), preferred_element...  4.22 us
  transfers between devices with their start and end apart: 5, of which 5 were waited for; matrix products, arithmetic and copies ran while one was open for 11% of the time, Pallas kernels for 0%

commit v1 on v0

v1 whole, which is shorter than its diff:
```python
import jax
import jax.numpy as jnp
from jax import lax
from jax.sharding import PartitionSpec as P


def from_partner(value, axis, mask):
    count = lax.axis_size(axis)
    return lax.ppermute(value, axis, [(source, source ^ mask) for source in range(count)])


def tree_sum(parts):
    while len(parts) > 1:
        parts = [parts[i] + parts[i + 1] for i in range(0, len(parts), 2)]
    return parts[0]


def per_device(heads, new_heads, vectors, near_ids):
    head_dev, width = heads.shape
    new_count = new_heads.shape[0]
    near = near_ids.shape[1]
    groups = lax.axis_size("group")
    members = lax.axis_size("member")
    most = 2 * near // members
    me = lax.axis_index("member")

    lists = [near_ids] + [from_partner(near_ids, "member", mask) for mask in range(1, members)]
    blocks = [new_heads] + [from_partner(new_heads, "group", mask) for mask in range(1, groups)]

    head_sq = jnp.sum(jnp.square(heads.astype(jnp.float32)), axis=1)

    ids = jnp.concatenate(lists, axis=0)
    local = ids - me * head_dev
    owned = (local >= 0) & (local < head_dev)
    rank = jnp.cumsum(owned.astype(jnp.int32), axis=1) - 1
    slots = jnp.arange(most, dtype=jnp.int32)
    pick = owned[:, None, :] & (rank[:, None, :] == slots[None, :, None])
    wanted = jnp.sum(jnp.where(pick, local[:, None, :] + 1, 0), axis=2).reshape(-1) - 1
    onehot = (wanted[:, None] == jnp.arange(head_dev, dtype=jnp.int32)[None, :]).astype(jnp.bfloat16)
    rows = jnp.dot(onehot, heads, preferred_element_type=jnp.float32).astype(jnp.bfloat16)
    rows = rows.reshape(members, most, width)
    listed = [rows[0]] + [from_partner(rows[mask], "member", mask) for mask in range(1, members)]

    queries = jnp.concatenate(blocks, axis=0)
    query_sq = jnp.sum(jnp.square(queries.astype(jnp.float32)), axis=1)
    dots = lax.dot_general(
        queries, heads, (((1,), (1,)), ((), ())), preferred_element_type=jnp.float32
    )
    excess = (query_sq[:, None] + head_sq[None, :] - 2.0 * dots) / width
    weight = 1.0 / jnp.square(1.0 + excess)
    sums = jnp.stack([jnp.sum(weight, axis=1), jnp.sum(weight * excess, axis=1)])
    sums = sums.reshape(2, groups, new_count)
    mine = tree_sum(
        [sums[:, 0]] + [from_partner(sums[:, mask], "group", mask) for mask in range(1, groups)]
    )
    mine = tree_sum([mine] + [from_partner(mine, "member", mask) for mask in range(1, members)])
    total_heads = float(head_dev * groups * members)
    density = jnp.log(mine[0] / total_heads)
    spread = mine[1] / mine[0]

    owner = near_ids[0] // head_dev
    earlier = jnp.tril(jnp.ones((near, near), jnp.bool_), -1)
    place = jnp.sum((earlier & (owner[:, None] == owner[None, :])).astype(jnp.int32), axis=1)
    source = (owner ^ me) * most + place
    back = (source[:, None] == jnp.arange(members * most, dtype=jnp.int32)[None, :]).astype(jnp.bfloat16)
    near_rows = jnp.dot(
        back, jnp.concatenate(listed, axis=0), preferred_element_type=jnp.float32
    ).astype(jnp.bfloat16)
    vec = vectors[0]
    vec_sq = jnp.sum(jnp.square(vec.astype(jnp.float32)), axis=1)
    row_sq = jnp.sum(jnp.square(near_rows.astype(jnp.float32)), axis=1)
    dots = lax.dot_general(
        near_rows, vec, (((1,), (1,)), ((), ())), preferred_element_type=jnp.float32
    )
    reassign = (row_sq[:, None] + vec_sq[None, :] - 2.0 * dots) / width
    return (density, spread, reassign[None])


def solution(mesh):
    placed = (
        P(("group", "member"), None),
        P("group", None),
        P(("group", "member"), None, None),
        P(("group", "member"), None),
    )
    return jax.shard_map(
        per_device,
        mesh=mesh,
        in_specs=placed,
        out_specs=(P("group"), P("group"), P(("group", "member"), None, None)),
        check_vma=False,
    )
```

time: 129 us -> 71.5 us (0.55)
  blocking collectives: 47.7 us -> 0 us
  starting transfers between devices: 0.25 us -> 34.5 us
  waiting for transfers between devices: 47.3 us -> 18.5 us
  between operations: 14.1 us -> 0.82 us
  matrix products: 7.29 us -> 3.5 us
  other arithmetic: 3.94 us -> 6.29 us
    ppermute x3 -> x27, starting transfers between devices: 0.17 us -> 34.5 us  [from_partner(): lax.ppermute(value, axis, [(source, source ^ mask) for source in range(co...]
    all_gather x1 -> x0, blocking collectives: 22.3 us -> none  [per_device(): lists = lax.all_gather(near_ids, 'member', axis=0, tiled=True)]
    reduce_scatter x1 -> x0, waiting for transfers between devices: 20.1 us -> none  [per_device(): lax.psum_scatter(jnp.where(owned[:, :, None], distances(blocks, rows, wid...]
    psum x1 -> x0, blocking collectives: 19.3 us -> none  [per_device(): mine = lax.psum(mine, 'member')]
    all_gather x1 -> x0, waiting for transfers between devices: 17.5 us -> none  [per_device(): blocks = lax.all_gather(vectors, 'member', axis=0, tiled=True)]
    ppermute x3 -> x27, waiting for transfers between devices: 9.64 us -> 18.5 us  [from_partner(): lax.ppermute(value, axis, [(source, source ^ mask) for source in range(co...]
    unnamed x1 -> x0, blocking collectives: 6.07 us -> none
    gather x1 -> x0, local copies, waits for them, and re-layouts: 5.55 us -> none  [per_device(): rows = jnp.take(heads, local, axis=0)]
  transfers between devices with their start and end apart: 5 -> 27, of which waited for: 5 -> 11; matrix products, arithmetic and copies ran while one was open for 11% -> 23% of each run, Pallas kernels for 0% -> 0%
where the time goes in v1:
time: 71.5 us; the launch traced here: 70.9 us
  starting transfers between devices  34.5 us (48%)
  waiting for transfers between devices  18.5 us (26%)
  local copies, waits for them, and re-layouts  7.34 us (10%)
  other arithmetic  6.29 us (9%)
  matrix products  3.5 us (5%)
  between operations  0.82 us (1%)
    ppermute x27, starting transfers between devices, from_partner(): lax.ppermute(value, axis, [(source, source ^ mask) for source in range(co...  34.5 us
    ppermute x27, waiting for transfers between devices, from_partner(): lax.ppermute(value, axis, [(source, source ^ mask) for source in range(co...  18.5 us
    unnamed x18, local copies, waits for them, and re-layouts  4.34 us
    reduce_sum x1, other arithmetic, per_device(): head_sq = jnp.sum(jnp.square(heads.astype(jnp.float32)), axis=1)  2.57 us
    dot_general x1, matrix products, per_device(): lax.dot_general(queries, heads, (((1,), (1,)), ((), ())), preferred_eleme...  1.72 us
    another operation x3, local copies, waits for them, and re-layouts, per_device(): jnp.stack([jnp.sum(weight, axis=1), jnp.sum(weight * excess, axis=1)])  1.48 us
  transfers between devices with their start and end apart: 27, of which 11 were waited for; matrix products, arithmetic and copies ran while one was open for 23% of the time, Pallas kernels for 0%

profile of v1, /device:TPU:0, one launch (start us, length us, event | category | flops | bytes accessed | tf_op | source)
XLA Modules:
  0.0 70.9 jit_solution(805622188274392218)
XLA Ops:
  0.7 3.0 %collective-permute-start.13 = (s32[1,64]{1,0:T(1,128)}, s32[1,64]{1,0:T(1,128)S(1)}, u32[]{:S(2)}, u32[]{:S(2)}) collective-permute-start(s32[1,64]{1,0:T(1,128)} %param.7), channel_id=1, source_target_pairs={{0,1},{1,0},{2,3},{3,2},{4,5},{5,4},{6,7},{7,6},{8,9},{9,8},{10,11... | collective-permute-start | bytes 776 | tf_op jit(solution)/shard_map/ppermute | solution.py:9
  3.7 1.6 %collective-permute-start.14 = (s32[1,64]{1,0:T(1,128)}, s32[1,64]{1,0:T(1,128)S(1)}, u32[]{:S(2)}, u32[]{:S(2)}) collective-permute-start(s32[1,64]{1,0:T(1,128)} %param.7), channel_id=1, source_target_pairs={{0,2},{1,3},{2,0},{3,1},{4,6},{5,7},{6,4},{7,5},{8,10},{9,11},{10,... | collective-permute-start | bytes 776 | tf_op jit(solution)/shard_map/ppermute | solution.py:9
  5.2 3.0 %collective-permute-start.16 = (s32[1,64]{1,0:T(1,128)}, s32[1,64]{1,0:T(1,128)S(1)}, u32[]{:S(2)}, u32[]{:S(2)}) collective-permute-start(s32[1,64]{1,0:T(1,128)} %param.7), channel_id=1, source_target_pairs={{0,4},{1,5},{2,6},{3,7},{4,0},{5,1},{6,2},{7,3},{8,12},{9,13},{10,... | collective-permute-start | bytes 776 | tf_op jit(solution)/shard_map/ppermute | solution.py:9
  8.2 1.3 %collective-permute-start.17 = (s32[1,64]{1,0:T(1,128)}, s32[1,64]{1,0:T(1,128)S(1)}, u32[]{:S(2)}, u32[]{:S(2)}) collective-permute-start(s32[1,64]{1,0:T(1,128)} %param.7), channel_id=1, source_target_pairs={{0,5},{1,4},{2,7},{3,6},{4,1},{5,0},{6,3},{7,2},{8,13},{9,12},{10,... | collective-permute-start | bytes 776 | tf_op jit(solution)/shard_map/ppermute | solution.py:9
  10.9 1.0 %multiply_reduce_fusion.2 = f32[128]{0:T(128)S(1)} fusion(bf16[1,128,768]{2,1,0:T(8,128)(2,1)} %param.6), kind=kLoop, calls=%fused_computation.15 | loop fusion | flops 294784 | bytes 197120 | tf_op jit(solution)/shard_map/reduce_sum | solution.py:70
  11.9 2.6 %multiply_reduce_fusion = f32[2048]{0:T(1024)S(1)} fusion(bf16[2048,768]{1,0:T(8,128)(2,1)} %param.4), kind=kLoop, calls=%fused_computation | loop fusion | flops 4716544 | bytes 3153920 | tf_op jit(solution)/shard_map/reduce_sum | solution.py:30
  14.7 1.3 %constant_dynamic-update-slice_fusion.3 = bf16[64,768]{1,0:T(8,128)(2,1)} fusion(bf16[16,768]{1,0:T(8,128)(2,1)} %param.5), kind=kLoop, calls=%fused_computation.29 | loop fusion | bytes 49152
  16.1 3.6 %collective-permute-start.18 = (s32[1,64]{1,0:T(1,128)S(1)}, s32[1,64]{1,0:T(1,128)S(1)}, u32[]{:S(2)}, u32[]{:S(2)}) collective-permute-start(s32[1,64]{1,0:T(1,128)S(1)} %copy-done.3), channel_id=1, source_target_pairs={{0,6},{1,7},{2,4},{3,5},{4,2},{5,3},{6,0},{7,1},{8,14},{9,15},{10,... | collective-permute-start | bytes 776 | tf_op jit(solution)/shard_map/ppermute | solution.py:9
  19.8 1.7 %collective-permute-start.1 = (bf16[16,768]{1,0:T(8,128)(2,1)}, bf16[16,768]{1,0:T(8,128)(2,1)}, u32[]{:S(2)}, u32[]{:S(2)}) collective-permute-start(bf16[16,768]{1,0:T(8,128)(2,1)} %param.5), channel_id=1, source_target_pairs={{0,16},{8,24},{16,0},{24,8},{1,17},{9,25},{17,1},{25,9},{2,18},{10... | collective-permute-start | bytes 73736 | tf_op jit(solution)/shard_map/ppermute | solution.py:9
  21.6 4.3 %collective-permute-done.19 = s32[1,64]{1,0:T(1,128)S(1)} collective-permute-done((s32[1,64]{1,0:T(1,128)S(1)}, s32[1,64]{1,0:T(1,128)S(1)}, u32[]{:S(2)}, u32[]{:S(2)}) %collective-permute-start.19) | collective-permute-done | bytes 288 | tf_op jit(solution)/shard_map/ppermute | solution.py:9
  28.3 0.7 %constant_dynamic-update-slice_fusion.2 = bf16[64,768]{1,0:T(8,128)(2,1)S(1)} fusion(bf16[64,768]{1,0:T(8,128)(2,1)S(1)} %copy-done.2, bf16[16,768]{1,0:T(8,128)(2,1)} %collective-permute-done), kind=kLoop, calls=%fused_computation.28 | loop fusion | bytes 49152
  29.1 0.7 %constant_dynamic-update-slice_fusion.1 = bf16[64,768]{1,0:T(8,128)(2,1)S(1)} fusion(bf16[64,768]{1,0:T(8,128)(2,1)S(1)} %constant_dynamic-update-slice_fusion.2, bf16[16,768]{1,0:T(8,128)(2,1)} %collective-permute-done.1), kind=kLoop, calls=%fused_computation.27 | loop fusion | bytes 49152
  29.8 0.7 %constant_dynamic-update-slice_fusion = bf16[64,768]{1,0:T(8,128)(2,1)S(1)} fusion(bf16[64,768]{1,0:T(8,128)(2,1)S(1)} %constant_dynamic-update-slice_fusion.1, bf16[16,768]{1,0:T(8,128)(2,1)} %collective-permute-done.2), kind=kLoop, calls=%fused_computation.26 | loop fusion | bytes 49152 | tf_op jit(solution)/shard_map/concatenate | solution.py:44
  30.7 1.7 %multiply_reduce_fusion.1 = (f32[64]{0:T(128)}, f32[64]{0:T(128)}) fusion(bf16[64,768]{1,0:T(8,128)(2,1)S(1)} %constant_dynamic-update-slice_fusion, bf16[2048,768]{1,0:T(8,128)(2,1)S(1)} %copy-done, f32[2048]{0:T(1024)S(1)} %multiply_reduce_fusion, f32[64]{0:T(128)S(1)} %multiply_reduce_fusion.4), kind=kOutput, calls=%fused_computation.12 | convolution fusion | flops 202637184 | bytes 3252992 | tf_op jit(solution)/shard_map/dot_general | solution.py:46
  34.0 1.6 %collective-permute-start.4 = (f32[2,16]{1,0:T(2,128)S(1)}, f32[2,16]{1,0:T(2,128)S(1)}, u32[]{:S(2)}, u32[]{:S(2)}) collective-permute-start(f32[2,16]{1,0:T(2,128)S(1)} %bitcast.33), channel_id=1, source_target_pairs={{0,16},{8,24},{16,0},{24,8},{1,17},{9,25},{17,1},{25,9},{2,18},{10... | collective-permute-start | bytes 392 | tf_op jit(solution)/shard_map/ppermute | solution.py:9
  35.8 1.8 %collective-permute-done.4 = f32[2,16]{1,0:T(2,128)S(1)} collective-permute-done((f32[2,16]{1,0:T(2,128)S(1)}, f32[2,16]{1,0:T(2,128)S(1)}, u32[]{:S(2)}, u32[]{:S(2)}) %collective-permute-start.4) | collective-permute-done | bytes 160 | tf_op jit(solution)/shard_map/ppermute | solution.py:9
  37.6 0.9 %collective-permute-done.5 = f32[2,16]{1,0:T(2,128)S(1)} collective-permute-done((f32[2,16]{1,0:T(2,128)S(1)}, f32[2,16]{1,0:T(2,128)S(1)}, u32[]{:S(2)}, u32[]{:S(2)}) %collective-permute-start.5) | collective-permute-done | bytes 160 | tf_op jit(solution)/shard_map/ppermute | solution.py:9
  38.6 1.7 %collective-permute-start.10 = (f32[2,16]{1,0:T(2,128)S(1)}, f32[2,16]{1,0:T(2,128)S(1)}, u32[]{:S(2)}, u32[]{:S(2)}) collective-permute-start(f32[2,16]{1,0:T(2,128)S(1)} %add_add_fusion.1), channel_id=1, source_target_pairs={{0,5},{1,4},{2,7},{3,6},{4,1},{5,0},{6,3},{7,2},{8,13},{9,12},{10,... | collective-permute-start | bytes 392 | tf_op jit(solution)/shard_map/ppermute | solution.py:9
  40.3 1.3 %collective-permute-start.22 = (bf16[16,768]{1,0:T(8,128)(2,1)}, bf16[16,768]{1,0:T(8,128)(2,1)S(1)}, u32[]{:S(2)}, u32[]{:S(2)}) collective-permute-start(bf16[16,768]{1,0:T(8,128)(2,1)} %get-tuple-element.11), channel_id=1, source_target_pairs={{0,3},{1,2},{2,1},{3,0},{4,7},{5,6},{6,5},{7,4},{8,11},{9,10},{10,... | collective-permute-start | bytes 73736 | tf_op jit(solution)/shard_map/ppermute | solution.py:9
  41.6 2.3 %collective-permute-start.11 = (f32[2,16]{1,0:T(2,128)S(1)}, f32[2,16]{1,0:T(2,128)S(1)}, u32[]{:S(2)}, u32[]{:S(2)}) collective-permute-start(f32[2,16]{1,0:T(2,128)S(1)} %add_add_fusion.1), channel_id=1, source_target_pairs={{0,6},{1,7},{2,4},{3,5},{4,2},{5,3},{6,0},{7,1},{8,14},{9,15},{10,... | collective-permute-start | bytes 392 | tf_op jit(solution)/shard_map/ppermute | solution.py:9
  43.9 1.5 %collective-permute-start.12 = (f32[2,16]{1,0:T(2,128)S(1)}, f32[2,16]{1,0:T(2,128)S(1)}, u32[]{:S(2)}, u32[]{:S(2)}) collective-permute-start(f32[2,16]{1,0:T(2,128)S(1)} %add_add_fusion.1), channel_id=1, source_target_pairs={{0,7},{1,6},{2,5},{3,4},{4,3},{5,2},{6,1},{7,0},{8,15},{9,14},{10,... | collective-permute-start | bytes 392 | tf_op jit(solution)/shard_map/ppermute | solution.py:9
  45.4 1.6 %collective-permute-done.11 = f32[2,16]{1,0:T(2,128)S(1)} collective-permute-done((f32[2,16]{1,0:T(2,128)S(1)}, f32[2,16]{1,0:T(2,128)S(1)}, u32[]{:S(2)}, u32[]{:S(2)}) %collective-permute-start.11) | collective-permute-done | bytes 160 | tf_op jit(solution)/shard_map/ppermute | solution.py:9
  47.5 2.7 %collective-permute-done.12 = f32[2,16]{1,0:T(2,128)S(1)} collective-permute-done((f32[2,16]{1,0:T(2,128)S(1)}, f32[2,16]{1,0:T(2,128)S(1)}, u32[]{:S(2)}, u32[]{:S(2)}) %collective-permute-start.12) | collective-permute-done | bytes 160 | tf_op jit(solution)/shard_map/ppermute | solution.py:9
  50.5 2.6 %collective-permute-start.8 = (f32[2,16]{1,0:T(2,128)S(1)}, f32[2,16]{1,0:T(2,128)S(1)}, u32[]{:S(2)}, u32[]{:S(2)}) collective-permute-start(f32[2,16]{1,0:T(2,128)S(1)} %add_add_fusion.1), channel_id=1, source_target_pairs={{0,3},{1,2},{2,1},{3,0},{4,7},{5,6},{6,5},{7,4},{8,11},{9,10},{10,... | collective-permute-start | bytes 392 | tf_op jit(solution)/shard_map/ppermute | solution.py:9
  55.0 1.7 %collective-permute-start.23 = (bf16[16,768]{1,0:T(8,128)(2,1)}, bf16[16,768]{1,0:T(8,128)(2,1)S(1)}, u32[]{:S(2)}, u32[]{:S(2)}) collective-permute-start(bf16[16,768]{1,0:T(8,128)(2,1)} %get-tuple-element.10), channel_id=1, source_target_pairs={{0,4},{1,5},{2,6},{3,7},{4,0},{5,1},{6,2},{7,3},{8,12},{9,13},{10,... | collective-permute-start | bytes 73736 | tf_op jit(solution)/shard_map/ppermute | solution.py:9
  56.7 1.5 %collective-permute-done.9 = f32[2,16]{1,0:T(2,128)S(1)} collective-permute-done((f32[2,16]{1,0:T(2,128)S(1)}, f32[2,16]{1,0:T(2,128)S(1)}, u32[]{:S(2)}, u32[]{:S(2)}) %collective-permute-start.9) | collective-permute-done | bytes 160 | tf_op jit(solution)/shard_map/ppermute | solution.py:9
  58.2 0.9 %collective-permute-start.24 = (bf16[16,768]{1,0:T(8,128)(2,1)}, bf16[16,768]{1,0:T(8,128)(2,1)S(1)}, u32[]{:S(2)}, u32[]{:S(2)}) collective-permute-start(bf16[16,768]{1,0:T(8,128)(2,1)} %get-tuple-element.9), channel_id=1, source_target_pairs={{0,5},{1,4},{2,7},{3,6},{4,1},{5,0},{6,3},{7,2},{8,13},{9,12},{10,... | collective-permute-start | bytes 73736 | tf_op jit(solution)/shard_map/ppermute | solution.py:9
  59.7 2.6 %collective-permute-start.25 = (bf16[16,768]{1,0:T(8,128)(2,1)}, bf16[16,768]{1,0:T(8,128)(2,1)S(1)}, u32[]{:S(2)}, u32[]{:S(2)}) collective-permute-start(bf16[16,768]{1,0:T(8,128)(2,1)} %get-tuple-element.8), channel_id=1, source_target_pairs={{0,6},{1,7},{2,4},{3,5},{4,2},{5,3},{6,0},{7,1},{8,14},{9,15},{10,... | collective-permute-start | bytes 73736 | tf_op jit(solution)/shard_map/ppermute | solution.py:9
  62.3 0.7 %constant_dynamic-update-slice_fusion.12 = bf16[128,768]{1,0:T(8,128)(2,1)S(1)} fusion(bf16[128,768]{1,0:T(8,128)(2,1)S(1)} %get-tuple-element.14, bf16[16,768]{1,0:T(8,128)(2,1)} %collective-permute-done.20), kind=kLoop, calls=%fused_computation.38 | loop fusion | bytes 49152
  63.0 1.7 %collective-permute-start.26 = (bf16[16,768]{1,0:T(8,128)(2,1)}, bf16[16,768]{1,0:T(8,128)(2,1)S(1)}, u32[]{:S(2)}, u32[]{:S(2)}) collective-permute-start(bf16[16,768]{1,0:T(8,128)(2,1)} %get-tuple-element.7), channel_id=1, source_target_pairs={{0,7},{1,6},{2,5},{3,4},{4,3},{5,2},{6,1},{7,0},{8,15},{9,14},{10,... | collective-permute-start | bytes 73736 | tf_op jit(solution)/shard_map/ppermute | solution.py:9
  65.6 4.2 %collective-permute-done.26 = bf16[16,768]{1,0:T(8,128)(2,1)S(1)} collective-permute-done((bf16[16,768]{1,0:T(8,128)(2,1)}, bf16[16,768]{1,0:T(8,128)(2,1)S(1)}, u32[]{:S(2)}, u32[]{:S(2)}) %collective-permute-start.26) | collective-permute-done | bytes 24608 | tf_op jit(solution)/shard_map/ppermute | solution.py:9
  70.1 0.8 %fusion.4 = f32[1,64,128]{2,1,0:T(8,128)} fusion(bf16[64,768]{1,0:T(8,128)(2,1)S(1)} %get-tuple-element.22, bf16[1,128,768]{2,1,0:T(8,128)(2,1)S(1)} %copy-done.1, f32[128]{0:T(128)S(1)} %multiply_reduce_fusion.2, f32[64]{0:T(128)S(1)} %get-tuple-element.21), kind=kOutput, calls=%fused_computation.9 | convolution fusion | flops 12615680 | bytes 328448 | tf_op jit(solution)/shard_map/dot_general | solution.py:72
  (69 shorter events, 10.6 us)
Async XLA Ops:
  0.6 14.1 %copy-start.3 = (s32[1,64]{1,0:T(1,128)S(1)}, s32[1,64]{1,0:T(1,128)}, u32[]{:S(2)}) copy-start(s32[1,64]{1,0:T(1,128)} %param.7) | copy-start | bytes 772
  0.6 25.8 %copy-start = (bf16[2048,768]{1,0:T(8,128)(2,1)S(1)}, bf16[2048,768]{1,0:T(8,128)(2,1)}, u32[]{:S(2)}) copy-start(bf16[2048,768]{1,0:T(8,128)(2,1)} %param.4) | copy-start | bytes 9437188
  0.7 15.4 %collective-permute-start.13 = (s32[1,64]{1,0:T(1,128)}, s32[1,64]{1,0:T(1,128)S(1)}, u32[]{:S(2)}, u32[]{:S(2)}) collective-permute-start(s32[1,64]{1,0:T(1,128)} %param.7), channel_id=1, source_target_pairs={{0,1},{1,0},{2,3},{3,2},{4,5},{5,4},{6,7},{7,6},{8,9},{9,8},{10,11... | collective-permute-start | bytes 776 | tf_op jit(solution)/shard_map/ppermute | solution.py:9
  3.7 16.0 %collective-permute-start.14 = (s32[1,64]{1,0:T(1,128)}, s32[1,64]{1,0:T(1,128)S(1)}, u32[]{:S(2)}, u32[]{:S(2)}) collective-permute-start(s32[1,64]{1,0:T(1,128)} %param.7), channel_id=1, source_target_pairs={{0,2},{1,3},{2,0},{3,1},{4,6},{5,7},{6,4},{7,5},{8,10},{9,11},{10,... | collective-permute-start | bytes 776 | tf_op jit(solution)/shard_map/ppermute | solution.py:9
  5.2 14.5 %collective-permute-start.15 = (s32[1,64]{1,0:T(1,128)}, s32[1,64]{1,0:T(1,128)S(1)}, u32[]{:S(2)}, u32[]{:S(2)}) collective-permute-start(s32[1,64]{1,0:T(1,128)} %param.7), channel_id=1, source_target_pairs={{0,3},{1,2},{2,1},{3,0},{4,7},{5,6},{6,5},{7,4},{8,11},{9,10},{10,... | collective-permute-start | bytes 776 | tf_op jit(solution)/shard_map/ppermute | solution.py:9
  5.2 14.5 %collective-permute-start.16 = (s32[1,64]{1,0:T(1,128)}, s32[1,64]{1,0:T(1,128)S(1)}, u32[]{:S(2)}, u32[]{:S(2)}) collective-permute-start(s32[1,64]{1,0:T(1,128)} %param.7), channel_id=1, source_target_pairs={{0,4},{1,5},{2,6},{3,7},{4,0},{5,1},{6,2},{7,3},{8,12},{9,13},{10,... | collective-permute-start | bytes 776 | tf_op jit(solution)/shard_map/ppermute | solution.py:9
  8.2 13.2 %collective-permute-start.17 = (s32[1,64]{1,0:T(1,128)}, s32[1,64]{1,0:T(1,128)S(1)}, u32[]{:S(2)}, u32[]{:S(2)}) collective-permute-start(s32[1,64]{1,0:T(1,128)} %param.7), channel_id=1, source_target_pairs={{0,5},{1,4},{2,7},{3,6},{4,1},{5,0},{6,3},{7,2},{8,13},{9,12},{10,... | collective-permute-start | bytes 776 | tf_op jit(solution)/shard_map/ppermute | solution.py:9
  16.1 5.6 %collective-permute-start.18 = (s32[1,64]{1,0:T(1,128)S(1)}, s32[1,64]{1,0:T(1,128)S(1)}, u32[]{:S(2)}, u32[]{:S(2)}) collective-permute-start(s32[1,64]{1,0:T(1,128)S(1)} %copy-done.3), channel_id=1, source_target_pairs={{0,6},{1,7},{2,4},{3,5},{4,2},{5,3},{6,0},{7,1},{8,14},{9,15},{10,... | collective-permute-start | bytes 776 | tf_op jit(solution)/shard_map/ppermute | solution.py:9
  19.7 6.2 %collective-permute-start.19 = (s32[1,64]{1,0:T(1,128)S(1)}, s32[1,64]{1,0:T(1,128)S(1)}, u32[]{:S(2)}, u32[]{:S(2)}) collective-permute-start(s32[1,64]{1,0:T(1,128)S(1)} %copy-done.3), channel_id=1, source_target_pairs={{0,7},{1,6},{2,5},{3,4},{4,3},{5,2},{6,1},{7,0},{8,15},{9,14},{10,... | collective-permute-start | bytes 776 | tf_op jit(solution)/shard_map/ppermute | solution.py:9
  19.7 8.6 %collective-permute-start = (bf16[16,768]{1,0:T(8,128)(2,1)}, bf16[16,768]{1,0:T(8,128)(2,1)}, u32[]{:S(2)}, u32[]{:S(2)}) collective-permute-start(bf16[16,768]{1,0:T(8,128)(2,1)} %param.5), channel_id=1, source_target_pairs={{0,8},{8,0},{16,24},{24,16},{1,9},{9,1},{17,25},{25,17},{2,10},{10... | collective-permute-start | bytes 73736 | tf_op jit(solution)/shard_map/ppermute | solution.py:9
  19.8 9.3 %collective-permute-start.1 = (bf16[16,768]{1,0:T(8,128)(2,1)}, bf16[16,768]{1,0:T(8,128)(2,1)}, u32[]{:S(2)}, u32[]{:S(2)}) collective-permute-start(bf16[16,768]{1,0:T(8,128)(2,1)} %param.5), channel_id=1, source_target_pairs={{0,16},{8,24},{16,0},{24,8},{1,17},{9,25},{17,1},{25,9},{2,18},{10... | collective-permute-start | bytes 73736 | tf_op jit(solution)/shard_map/ppermute | solution.py:9
  21.5 8.4 %collective-permute-start.2 = (bf16[16,768]{1,0:T(8,128)(2,1)}, bf16[16,768]{1,0:T(8,128)(2,1)}, u32[]{:S(2)}, u32[]{:S(2)}) collective-permute-start(bf16[16,768]{1,0:T(8,128)(2,1)} %param.5), channel_id=1, source_target_pairs={{0,24},{8,16},{16,8},{24,0},{1,25},{9,17},{17,9},{25,1},{2,26},{10... | collective-permute-start | bytes 73736 | tf_op jit(solution)/shard_map/ppermute | solution.py:9
  26.5 1.9 %copy-start.2 = (bf16[64,768]{1,0:T(8,128)(2,1)S(1)}, bf16[64,768]{1,0:T(8,128)(2,1)}, u32[]{:S(2)}) copy-start(bf16[64,768]{1,0:T(8,128)(2,1)} %constant_dynamic-update-slice_fusion.3) | copy-start | bytes 294916
  27.1 43.0 %copy-start.1 = (bf16[1,128,768]{2,1,0:T(8,128)(2,1)S(1)}, bf16[1,128,768]{2,1,0:T(8,128)(2,1)}, u32[]{:S(2)}) copy-start(bf16[1,128,768]{2,1,0:T(8,128)(2,1)} %param.6) | copy-start | bytes 589828
  27.8 31.9 %collective-permute-start.20 = (bf16[16,768]{1,0:T(8,128)(2,1)}, bf16[16,768]{1,0:T(8,128)(2,1)}, u32[]{:S(2)}, u32[]{:S(2)}) collective-permute-start(bf16[16,768]{1,0:T(8,128)(2,1)} %get-tuple-element.13), channel_id=1, source_target_pairs={{0,1},{1,0},{2,3},{3,2},{4,5},{5,4},{6,7},{7,6},{8,9},{9,8},{10,11... | collective-permute-start | bytes 73736 | tf_op jit(solution)/shard_map/ppermute | solution.py:9
  28.3 34.7 %collective-permute-start.21 = (bf16[16,768]{1,0:T(8,128)(2,1)}, bf16[16,768]{1,0:T(8,128)(2,1)}, u32[]{:S(2)}, u32[]{:S(2)}) collective-permute-start(bf16[16,768]{1,0:T(8,128)(2,1)} %get-tuple-element.12), channel_id=1, source_target_pairs={{0,2},{1,3},{2,0},{3,1},{4,6},{5,7},{6,4},{7,5},{8,10},{9,11},{10,... | collective-permute-start | bytes 73736 | tf_op jit(solution)/shard_map/ppermute | solution.py:9
  33.9 1.9 %collective-permute-start.3 = (f32[2,16]{1,0:T(2,128)S(1)}, f32[2,16]{1,0:T(2,128)S(1)}, u32[]{:S(2)}, u32[]{:S(2)}) collective-permute-start(f32[2,16]{1,0:T(2,128)S(1)} %bitcast.34), channel_id=1, source_target_pairs={{0,8},{8,0},{16,24},{24,16},{1,9},{9,1},{17,25},{25,17},{2,10},{10... | collective-permute-start | bytes 392 | tf_op jit(solution)/shard_map/ppermute | solution.py:9
  34.0 3.6 %collective-permute-start.4 = (f32[2,16]{1,0:T(2,128)S(1)}, f32[2,16]{1,0:T(2,128)S(1)}, u32[]{:S(2)}, u32[]{:S(2)}) collective-permute-start(f32[2,16]{1,0:T(2,128)S(1)} %bitcast.33), channel_id=1, source_target_pairs={{0,16},{8,24},{16,0},{24,8},{1,17},{9,25},{17,1},{25,9},{2,18},{10... | collective-permute-start | bytes 392 | tf_op jit(solution)/shard_map/ppermute | solution.py:9
  35.6 3.0 %collective-permute-start.5 = (f32[2,16]{1,0:T(2,128)S(1)}, f32[2,16]{1,0:T(2,128)S(1)}, u32[]{:S(2)}, u32[]{:S(2)}) collective-permute-start(f32[2,16]{1,0:T(2,128)S(1)} %bitcast.32), channel_id=1, source_target_pairs={{0,24},{8,16},{16,8},{24,0},{1,25},{9,17},{17,9},{25,1},{2,26},{10... | collective-permute-start | bytes 392 | tf_op jit(solution)/shard_map/ppermute | solution.py:9
  38.6 5.4 %collective-permute-start.10 = (f32[2,16]{1,0:T(2,128)S(1)}, f32[2,16]{1,0:T(2,128)S(1)}, u32[]{:S(2)}, u32[]{:S(2)}) collective-permute-start(f32[2,16]{1,0:T(2,128)S(1)} %add_add_fusion.1), channel_id=1, source_target_pairs={{0,5},{1,4},{2,7},{3,6},{4,1},{5,0},{6,3},{7,2},{8,13},{9,12},{10,... | collective-permute-start | bytes 392 | tf_op jit(solution)/shard_map/ppermute | solution.py:9
  40.3 25.2 %collective-permute-start.22 = (bf16[16,768]{1,0:T(8,128)(2,1)}, bf16[16,768]{1,0:T(8,128)(2,1)S(1)}, u32[]{:S(2)}, u32[]{:S(2)}) collective-permute-start(bf16[16,768]{1,0:T(8,128)(2,1)} %get-tuple-element.11), channel_id=1, source_target_pairs={{0,3},{1,2},{2,1},{3,0},{4,7},{5,6},{6,5},{7,4},{8,11},{9,10},{10,... | collective-permute-start | bytes 73736 | tf_op jit(solution)/shard_map/ppermute | solution.py:9
  41.6 5.4 %collective-permute-start.11 = (f32[2,16]{1,0:T(2,128)S(1)}, f32[2,16]{1,0:T(2,128)S(1)}, u32[]{:S(2)}, u32[]{:S(2)}) collective-permute-start(f32[2,16]{1,0:T(2,128)S(1)} %add_add_fusion.1), channel_id=1, source_target_pairs={{0,6},{1,7},{2,4},{3,5},{4,2},{5,3},{6,0},{7,1},{8,14},{9,15},{10,... | collective-permute-start | bytes 392 | tf_op jit(solution)/shard_map/ppermute | solution.py:9
  43.9 6.3 %collective-permute-start.12 = (f32[2,16]{1,0:T(2,128)S(1)}, f32[2,16]{1,0:T(2,128)S(1)}, u32[]{:S(2)}, u32[]{:S(2)}) collective-permute-start(f32[2,16]{1,0:T(2,128)S(1)} %add_add_fusion.1), channel_id=1, source_target_pairs={{0,7},{1,6},{2,5},{3,4},{4,3},{5,2},{6,1},{7,0},{8,15},{9,14},{10,... | collective-permute-start | bytes 392 | tf_op jit(solution)/shard_map/ppermute | solution.py:9
  47.0 3.6 %collective-permute-start.6 = (f32[2,16]{1,0:T(2,128)S(1)}, f32[2,16]{1,0:T(2,128)S(1)}, u32[]{:S(2)}, u32[]{:S(2)}) collective-permute-start(f32[2,16]{1,0:T(2,128)S(1)} %add_add_fusion.1), channel_id=1, source_target_pairs={{0,1},{1,0},{2,3},{3,2},{4,5},{5,4},{6,7},{7,6},{8,9},{9,8},{10,11... | collective-permute-start | bytes 392 | tf_op jit(solution)/shard_map/ppermute | solution.py:9
  50.2 3.6 %collective-permute-start.7 = (f32[2,16]{1,0:T(2,128)S(1)}, f32[2,16]{1,0:T(2,128)S(1)}, u32[]{:S(2)}, u32[]{:S(2)}) collective-permute-start(f32[2,16]{1,0:T(2,128)S(1)} %add_add_fusion.1), channel_id=1, source_target_pairs={{0,2},{1,3},{2,0},{3,1},{4,6},{5,7},{6,4},{7,5},{8,10},{9,11},{10,... | collective-permute-start | bytes 392 | tf_op jit(solution)/shard_map/ppermute | solution.py:9
  50.5 4.5 %collective-permute-start.8 = (f32[2,16]{1,0:T(2,128)S(1)}, f32[2,16]{1,0:T(2,128)S(1)}, u32[]{:S(2)}, u32[]{:S(2)}) collective-permute-start(f32[2,16]{1,0:T(2,128)S(1)} %add_add_fusion.1), channel_id=1, source_target_pairs={{0,3},{1,2},{2,1},{3,0},{4,7},{5,6},{6,5},{7,4},{8,11},{9,10},{10,... | collective-permute-start | bytes 392 | tf_op jit(solution)/shard_map/ppermute | solution.py:9
  53.8 4.5 %collective-permute-start.9 = (f32[2,16]{1,0:T(2,128)S(1)}, f32[2,16]{1,0:T(2,128)S(1)}, u32[]{:S(2)}, u32[]{:S(2)}) collective-permute-start(f32[2,16]{1,0:T(2,128)S(1)} %add_add_fusion.1), channel_id=1, source_target_pairs={{0,4},{1,5},{2,6},{3,7},{4,0},{5,1},{6,2},{7,3},{8,12},{9,13},{10,... | collective-permute-start | bytes 392 | tf_op jit(solution)/shard_map/ppermute | solution.py:9
  55.0 10.5 %collective-permute-start.23 = (bf16[16,768]{1,0:T(8,128)(2,1)}, bf16[16,768]{1,0:T(8,128)(2,1)S(1)}, u32[]{:S(2)}, u32[]{:S(2)}) collective-permute-start(bf16[16,768]{1,0:T(8,128)(2,1)} %get-tuple-element.10), channel_id=1, source_target_pairs={{0,4},{1,5},{2,6},{3,7},{4,0},{5,1},{6,2},{7,3},{8,12},{9,13},{10,... | collective-permute-start | bytes 73736 | tf_op jit(solution)/shard_map/ppermute | solution.py:9
  58.2 7.3 %collective-permute-start.24 = (bf16[16,768]{1,0:T(8,128)(2,1)}, bf16[16,768]{1,0:T(8,128)(2,1)S(1)}, u32[]{:S(2)}, u32[]{:S(2)}) collective-permute-start(bf16[16,768]{1,0:T(8,128)(2,1)} %get-tuple-element.9), channel_id=1, source_target_pairs={{0,5},{1,4},{2,7},{3,6},{4,1},{5,0},{6,3},{7,2},{8,13},{9,12},{10,... | collective-permute-start | bytes 73736 | tf_op jit(solution)/shard_map/ppermute | solution.py:9
  59.7 5.8 %collective-permute-start.25 = (bf16[16,768]{1,0:T(8,128)(2,1)}, bf16[16,768]{1,0:T(8,128)(2,1)S(1)}, u32[]{:S(2)}, u32[]{:S(2)}) collective-permute-start(bf16[16,768]{1,0:T(8,128)(2,1)} %get-tuple-element.8), channel_id=1, source_target_pairs={{0,6},{1,7},{2,4},{3,5},{4,2},{5,3},{6,0},{7,1},{8,14},{9,15},{10,... | collective-permute-start | bytes 73736 | tf_op jit(solution)/shard_map/ppermute | solution.py:9
  63.0 6.7 %collective-permute-start.26 = (bf16[16,768]{1,0:T(8,128)(2,1)}, bf16[16,768]{1,0:T(8,128)(2,1)S(1)}, u32[]{:S(2)}, u32[]{:S(2)}) collective-permute-start(bf16[16,768]{1,0:T(8,128)(2,1)} %get-tuple-element.7), channel_id=1, source_target_pairs={{0,7},{1,6},{2,5},{3,4},{4,3},{5,2},{6,1},{7,0},{8,15},{9,14},{10,... | collective-permute-start | bytes 73736 | tf_op jit(solution)/shard_map/ppermute | solution.py:9

commit v2 on v1

v2 whole, which is shorter than its diff:
```python
import jax
import jax.numpy as jnp
from jax import lax
from jax.sharding import PartitionSpec as P


def to_each(value, axis):
    return lax.all_to_all(value, axis, 0, 0, tiled=True)


def per_device(heads, new_heads, vectors, near_ids):
    head_dev, width = heads.shape
    new_count = new_heads.shape[0]
    near = near_ids.shape[1]
    groups = lax.axis_size("group")
    members = lax.axis_size("member")
    most = 2 * near // members
    me = lax.axis_index("member")

    ids = to_each(jnp.broadcast_to(near_ids, (members, near)), "member")
    queries = to_each(jnp.tile(new_heads, (groups, 1)), "group")

    head_sq = jnp.sum(jnp.square(heads.astype(jnp.float32)), axis=1)

    local = ids - me * head_dev
    owned = (local >= 0) & (local < head_dev)
    rank = jnp.cumsum(owned.astype(jnp.int32), axis=1) - 1
    slots = jnp.arange(most, dtype=jnp.int32)
    pick = owned[:, None, :] & (rank[:, None, :] == slots[None, :, None])
    wanted = jnp.sum(jnp.where(pick, local[:, None, :] + 1, 0), axis=2).reshape(-1) - 1
    onehot = (wanted[:, None] == jnp.arange(head_dev, dtype=jnp.int32)[None, :]).astype(jnp.bfloat16)
    rows = jnp.dot(onehot, heads, preferred_element_type=jnp.float32).astype(jnp.bfloat16)
    listed = to_each(rows, "member")

    query_sq = jnp.sum(jnp.square(queries.astype(jnp.float32)), axis=1)
    dots = lax.dot_general(
        queries, heads, (((1,), (1,)), ((), ())), preferred_element_type=jnp.float32
    )
    excess = (query_sq[:, None] + head_sq[None, :] - 2.0 * dots) / width
    weight = 1.0 / jnp.square(1.0 + excess)
    sums = jnp.stack([jnp.sum(weight, axis=1), jnp.sum(weight * excess, axis=1)])
    sums = jnp.transpose(sums.reshape(2, groups, new_count), (1, 0, 2))
    sums = jnp.broadcast_to(sums[:, None], (groups, members, 2, new_count))
    sums = to_each(sums.reshape(groups * members, 2, new_count), ("group", "member"))
    mine = jnp.sum(sums, axis=0)
    total_heads = float(head_dev * groups * members)
    density = jnp.log(mine[0] / total_heads)
    spread = mine[1] / mine[0]

    owner = near_ids[0] // head_dev
    earlier = jnp.tril(jnp.ones((near, near), jnp.bool_), -1)
    place = jnp.sum((earlier & (owner[:, None] == owner[None, :])).astype(jnp.int32), axis=1)
    source = owner * most + place
    back = (source[:, None] == jnp.arange(members * most, dtype=jnp.int32)[None, :]).astype(jnp.bfloat16)
    near_rows = jnp.dot(
        back, listed, preferred_element_type=jnp.float32
    ).astype(jnp.bfloat16)
    vec = vectors[0]
    vec_sq = jnp.sum(jnp.square(vec.astype(jnp.float32)), axis=1)
    row_sq = jnp.sum(jnp.square(near_rows.astype(jnp.float32)), axis=1)
    dots = lax.dot_general(
        near_rows, vec, (((1,), (1,)), ((), ())), preferred_element_type=jnp.float32
    )
    reassign = (row_sq[:, None] + vec_sq[None, :] - 2.0 * dots) / width
    return (density, spread, reassign[None])


def solution(mesh):
    placed = (
        P(("group", "member"), None),
        P("group", None),
        P(("group", "member"), None, None),
        P(("group", "member"), None),
    )
    return jax.shard_map(
        per_device,
        mesh=mesh,
        in_specs=placed,
        out_specs=(P("group"), P("group"), P(("group", "member"), None, None)),
        check_vma=False,
    )
```

time: 71.5 us -> 49.6 us (0.69)
  starting transfers between devices: 34.5 us -> 16.8 us
  local copies, waits for them, and re-layouts: 7.34 us -> 3.04 us
  waiting for transfers between devices: 18.5 us -> 19.6 us
  other arithmetic: 6.29 us -> 5.36 us
    ppermute x27 -> x0, starting transfers between devices: 34.5 us -> none  [from_partner(): lax.ppermute(value, axis, [(source, source ^ mask) for source in range(co...]
    all_to_all x0 -> x4, waiting for transfers between devices: none -> 19.6 us  [to_each(): return lax.all_to_all(value, axis, 0, 0, tiled=True)]
    ppermute x27 -> x0, waiting for transfers between devices: 18.5 us -> none  [from_partner(): lax.ppermute(value, axis, [(source, source ^ mask) for source in range(co...]
    all_to_all x0 -> x4, starting transfers between devices: none -> 16.8 us  [to_each(): return lax.all_to_all(value, axis, 0, 0, tiled=True)]
    unnamed x18 -> x8, local copies, waits for them, and re-layouts: 4.34 us -> 0.02 us
    broadcast_in_dim x0 -> x1, local copies, waits for them, and re-layouts: none -> 1.41 us  [per_device(): ids = to_each(jnp.broadcast_to(near_ids, (members, near)), 'member')]
    another operation x3 -> x2, local copies, waits for them, and re-layouts: 1.48 us -> 0.16 us  [per_device(): jnp.stack([jnp.sum(weight, axis=1), jnp.sum(weight * excess, axis=1)])]
    reduce_sum x1, other arithmetic: 1.05 us -> 0.12 us  [per_device(): vec_sq = jnp.sum(jnp.square(vec.astype(jnp.float32)), axis=1)]
  transfers between devices with their start and end apart: 27 -> 4, of which waited for: 11 -> 4; matrix products, arithmetic and copies ran while one was open for 23% -> 13% of each run, Pallas kernels for 0% -> 0%
where the time goes in v2:
time: 49.6 us; the launch traced here: 49.2 us
  waiting for transfers between devices  19.6 us (40%)
  starting transfers between devices  16.8 us (34%)
  other arithmetic  5.36 us (11%)
  matrix products  3.65 us (7%)
  local copies, waits for them, and re-layouts  3.04 us (6%)
  between operations  0.76 us (2%)
    all_to_all x4, waiting for transfers between devices, to_each(): return lax.all_to_all(value, axis, 0, 0, tiled=True)  19.6 us
    all_to_all x4, starting transfers between devices, to_each(): return lax.all_to_all(value, axis, 0, 0, tiled=True)  16.8 us
    reduce_sum x1, other arithmetic, per_device(): head_sq = jnp.sum(jnp.square(heads.astype(jnp.float32)), axis=1)  2.57 us
    broadcast_in_dim x1, local copies, waits for them, and re-layouts, per_device(): ids = to_each(jnp.broadcast_to(near_ids, (members, near)), 'member')  1.41 us
    dot_general x1, matrix products, per_device(): jnp.dot(onehot, heads, preferred_element_type=jnp.float32)  1.31 us
    dot_general x1, matrix products, per_device(): lax.dot_general(queries, heads, (((1,), (1,)), ((), ())), preferred_eleme...  1.2 us
  transfers between devices with their start and end apart: 4, of which 4 were waited for; matrix products, arithmetic and copies ran while one was open for 13% of the time, Pallas kernels for 0%

profile of v2, /device:TPU:0, one launch (start us, length us, event | category | flops | bytes accessed | tf_op | source)
XLA Modules:
  0.0 49.2 jit_solution(9520787566174096364)
XLA Ops:
  0.6 0.0 copy-start.3
  0.6 0.0 copy-start
  0.7 1.4 %broadcast_in_dim.22 = s32[8,1,64]{2,1,0:T(1,128)} broadcast(s32[64]{0:T(128)} %bitcast.38), dimensions={2} | broadcast | bytes 2304 | tf_op jit(solution)/shard_map/broadcast_in_dim | solution.py:20
  2.1 7.3 %all-to-all-start.2 = ((s32[8,1,64]{2,1,0:T(1,128)}), s32[8,1,64]{2,1,0:T(1,128)S(1)}, u32[]{:S(2)}, u32[]{:S(2)}) async-start(s32[8,1,64]{2,1,0:T(1,128)} %broadcast_in_dim.22), calls=%async_computation.2 | async-start | bytes 8192 | tf_op jit(solution)/shard_map/all_to_all | solution.py:8
  9.3 0.7 %and_select_fusion.1 = s32[64]{0:T(128)S(1)} fusion(s32[1,64]{1,0:T(1,128)} %param.7), kind=kLoop, calls=%fused_computation.34 | loop fusion | flops 960 | bytes 512 | tf_op jit(solution)/shard_map/jit(floor_divide)/jit(_where)/select_n | solution.py:50
  10.0 0.7 %fusion.11 = s32[64]{0:T(128)S(1)} fusion(s32[1,64]{1,0:T(1,128)} %param.7), kind=kLoop, calls=%fused_computation.41 | loop fusion | flops 960 | bytes 512 | tf_op jit(solution)/shard_map/eq | solution.py:52
  10.7 2.6 %multiply_reduce_fusion = f32[2048]{0:T(1024)S(1)} fusion(bf16[2048,768]{1,0:T(8,128)(2,1)} %param.4), kind=kLoop, calls=%fused_computation | loop fusion | flops 4716544 | bytes 3153920 | tf_op jit(solution)/shard_map/reduce_sum | solution.py:23
  13.2 0.2 convert_reduce_fusion
  13.4 2.3 %all-to-all-done.2 = s32[8,1,64]{2,1,0:T(1,128)S(1)} async-done(((s32[8,1,64]{2,1,0:T(1,128)}), s32[8,1,64]{2,1,0:T(1,128)S(1)}, u32[]{:S(2)}, u32[]{:S(2)}) %all-to-all-start.2) | async-done | bytes 2080 | tf_op jit(solution)/shard_map/all_to_all | solution.py:8
  15.7 0.6 %tile.2 = bf16[4,16,768]{2,1,0:T(8,128)(2,1)} broadcast(bf16[16,768]{1,0:T(8,128)(2,1)S(1)} %copy-done.2), dimensions={1,2} | broadcast | bytes 122880 | tf_op jit(solution)/shard_map/tile | solution.py:21
  16.3 3.3 %all-to-all-start = ((bf16[4,16,768]{2,1,0:T(8,128)(2,1)}), bf16[4,16,768]{2,1,0:T(8,128)(2,1)S(1)}, u32[]{:S(2)}, u32[]{:S(2)}) async-start(bf16[4,16,768]{2,1,0:T(8,128)(2,1)} %tile.2), calls=%async_computation | async-start | bytes 196608 | tf_op jit(solution)/shard_map/all_to_all | solution.py:8
  19.7 0.2 reduce_window_sum.14
  19.9 0.2 select_reduce_fusion
  20.1 0.1 sub.40
  20.2 3.7 %all-to-all-done = bf16[4,16,768]{2,1,0:T(8,128)(2,1)S(1)} async-done(((bf16[4,16,768]{2,1,0:T(8,128)(2,1)}), bf16[4,16,768]{2,1,0:T(8,128)(2,1)S(1)}, u32[]{:S(2)}, u32[]{:S(2)}) %all-to-all-start) | async-done | bytes 98336 | tf_op jit(solution)/shard_map/all_to_all | solution.py:8
  23.9 0.1 multiply_reduce_fusion.4
  24.0 0.1 add.73
  24.1 0.0 copy-done
  24.1 1.2 %fusion.6 = (f32[64]{0:T(128)S(1)}, f32[64]{0:T(128)S(1)}) fusion(bf16[64,768]{1,0:T(8,128)(2,1)S(1)} %bitcast.35, bf16[2048,768]{1,0:T(8,128)(2,1)S(1)} %copy-done, f32[2048]{0:T(1024)S(1)} %multiply_reduce_fusion, f32[64]{0:T(128)S(1)} %add.73), kind=kOutput, calls=%fused_computation.14 | convolution fusion | flops 202637184 | bytes 3252992 | tf_op jit(solution)/shard_map/dot_general | solution.py:36
  25.3 0.0 copy-start.1
  25.3 0.1 stack.10
  25.4 0.1 stack.9
  25.5 0.6 %copy.15 = f32[32,2,16]{2,1,0:T(2,128)} copy(f32[32,2,16]{2,0,1:T(8,128)S(1)} %broadcast_bitcast_fusion) | data formatting | bytes 8192 | tf_op jit(solution)/shard_map/reshape | solution.py:44
  26.1 2.8 %all-to-all-start.1 = ((f32[32,2,16]{2,1,0:T(2,128)}), f32[32,2,16]{2,1,0:T(2,128)S(1)}, u32[]{:S(2)}, u32[]{:S(2)}) async-start(f32[32,2,16]{2,1,0:T(2,128)} %copy.15), calls=%async_computation.1 | async-start | bytes 65536 | tf_op jit(solution)/shard_map/all_to_all | solution.py:8
  29.0 1.3 %convolution_convert_fusion = bf16[128,768]{1,0:T(8,128)(2,1)} fusion(bf16[2048,768]{1,0:T(8,128)(2,1)S(1)} %copy-done, s32[128]{0:T(128)S(1)} %sub.40), kind=kOutput, calls=%fused_computation.4 | convolution fusion | flops 403013632 | bytes 3342848 | tf_op jit(solution)/shard_map/dot_general | solution.py:32
  30.3 5.9 %all-to-all-done.1 = f32[32,2,16]{2,1,0:T(2,128)S(1)} async-done(((f32[32,2,16]{2,1,0:T(2,128)}), f32[32,2,16]{2,1,0:T(2,128)S(1)}, u32[]{:S(2)}, u32[]{:S(2)}) %all-to-all-start.1) | async-done | bytes 4128 | tf_op jit(solution)/shard_map/all_to_all | solution.py:8
  36.2 3.4 %all-to-all-start.3 = ((bf16[8,16,768]{2,1,0:T(8,128)(2,1)}), bf16[8,16,768]{2,1,0:T(8,128)(2,1)S(1)}, u32[]{:S(2)}, u32[]{:S(2)}) async-start(bf16[8,16,768]{2,1,0:T(8,128)(2,1)} %bitcast.10), calls=%async_computation.3 | async-start | bytes 393216 | tf_op jit(solution)/shard_map/all_to_all | solution.py:8
  39.6 0.1 multiply_reduce_fusion.2
  39.7 0.5 %fusion.12 = (f32[16]{0:T(128)}, f32[16]{0:T(128)}) fusion(f32[2,16]{1,0:T(2,128)S(1)} %reduce_sum.85), kind=kLoop, calls=%fused_computation.46 | loop fusion | flops 32 | bytes 256 | tf_op jit(solution)/shard_map/div | solution.py:48
  40.3 7.7 %all-to-all-done.3 = bf16[8,16,768]{2,1,0:T(8,128)(2,1)S(1)} async-done(((bf16[8,16,768]{2,1,0:T(8,128)(2,1)}), bf16[8,16,768]{2,1,0:T(8,128)(2,1)S(1)}, u32[]{:S(2)}, u32[]{:S(2)}) %all-to-all-start.3) | async-done | bytes 196640 | tf_op jit(solution)/shard_map/all_to_all | solution.py:8
  48.0 0.3 multiply_reduce_fusion.3
  48.3 0.8 %fusion.4 = f32[1,64,128]{2,1,0:T(8,128)} fusion(bf16[64,768]{1,0:T(8,128)(2,1)S(1)} %get-tuple-element.10, bf16[1,128,768]{2,1,0:T(8,128)(2,1)S(1)} %copy-done.1, f32[128]{0:T(128)S(1)} %multiply_reduce_fusion.2, f32[64]{0:T(128)S(1)} %get-tuple-element.9), kind=kOutput, calls=%fused_computation.9 | convolution fusion | flops 12615680 | bytes 328448 | tf_op jit(solution)/shard_map/dot_general | solution.py:61
  (13 shorter events, 0.1 us)
Async XLA Ops:
  0.6 12.8 %copy-start.3 = (s32[1,64]{1,0:T(1,128)S(1)}, s32[1,64]{1,0:T(1,128)}, u32[]{:S(2)}) copy-start(s32[1,64]{1,0:T(1,128)} %param.7) | copy-start | bytes 772
  0.6 23.5 %copy-start = (bf16[2048,768]{1,0:T(8,128)(2,1)S(1)}, bf16[2048,768]{1,0:T(8,128)(2,1)}, u32[]{:S(2)}) copy-start(bf16[2048,768]{1,0:T(8,128)(2,1)} %param.4) | copy-start | bytes 9437188
  0.7 15.1 %copy-start.2 = (bf16[16,768]{1,0:T(8,128)(2,1)S(1)}, bf16[16,768]{1,0:T(8,128)(2,1)}, u32[]{:S(2)}) copy-start(bf16[16,768]{1,0:T(8,128)(2,1)} %param.5) | copy-start | bytes 73732
  2.1 13.6 %all-to-all-start.2 = ((s32[8,1,64]{2,1,0:T(1,128)}), s32[8,1,64]{2,1,0:T(1,128)S(1)}, u32[]{:S(2)}, u32[]{:S(2)}) async-start(s32[8,1,64]{2,1,0:T(1,128)} %broadcast_in_dim.22), calls=%async_computation.2 | async-start | bytes 8192 | tf_op jit(solution)/shard_map/all_to_all | solution.py:8
  16.3 7.6 %all-to-all-start = ((bf16[4,16,768]{2,1,0:T(8,128)(2,1)}), bf16[4,16,768]{2,1,0:T(8,128)(2,1)S(1)}, u32[]{:S(2)}, u32[]{:S(2)}) async-start(bf16[4,16,768]{2,1,0:T(8,128)(2,1)} %tile.2), calls=%async_computation | async-start | bytes 196608 | tf_op jit(solution)/shard_map/all_to_all | solution.py:8
  25.3 14.3 %copy-start.1 = (bf16[1,128,768]{2,1,0:T(8,128)(2,1)S(1)}, bf16[1,128,768]{2,1,0:T(8,128)(2,1)}, u32[]{:S(2)}) copy-start(bf16[1,128,768]{2,1,0:T(8,128)(2,1)} %param.6) | copy-start | bytes 589828
  26.1 10.0 %all-to-all-start.1 = ((f32[32,2,16]{2,1,0:T(2,128)}), f32[32,2,16]{2,1,0:T(2,128)S(1)}, u32[]{:S(2)}, u32[]{:S(2)}) async-start(f32[32,2,16]{2,1,0:T(2,128)} %copy.15), calls=%async_computation.1 | async-start | bytes 65536 | tf_op jit(solution)/shard_map/all_to_all | solution.py:8
  36.2 11.8 %all-to-all-start.3 = ((bf16[8,16,768]{2,1,0:T(8,128)(2,1)}), bf16[8,16,768]{2,1,0:T(8,128)(2,1)S(1)}, u32[]{:S(2)}, u32[]{:S(2)}) async-start(bf16[8,16,768]{2,1,0:T(8,128)(2,1)} %bitcast.10), calls=%async_computation.3 | async-start | bytes 393216 | tf_op jit(solution)/shard_map/all_to_all | solution.py:8

commit v3 on v2

v3 whole, which is shorter than its diff:
```python
import functools

import jax
import jax.numpy as jnp
from jax import lax
from jax.experimental import pallas as pl
from jax.experimental.pallas import tpu as pltpu
from jax.sharding import PartitionSpec as P

VMEM = pltpu.MemorySpace.VMEM
LANES = 128
LIMIT = 24 * 2**20


def from_partner(value, axis, mask):
    count = lax.axis_size(axis)
    return lax.ppermute(value, axis, [(source, source ^ mask) for source in range(count)])


def to_each(value, axis):
    return lax.all_to_all(value, axis, 0, 0, tiled=True)


def call(body, shapes, operands, flops, moved):
    return pl.pallas_call(
        body,
        out_shape=shapes,
        in_specs=[pl.BlockSpec(memory_space=VMEM)] * len(operands),
        out_specs=jax.tree.map(lambda unused: pl.BlockSpec(memory_space=VMEM), shapes),
        compiler_params=pltpu.CompilerParams(vmem_limit_bytes=LIMIT),
        cost_estimate=pl.CostEstimate(flops=flops, bytes_accessed=moved, transcendentals=0),
    )(*operands)


def iota(shape, dim):
    return lax.broadcasted_iota(jnp.int32, shape, dim)


def gather_kernel(members, most, ids_ref, heads_ref, rows_ref):
    head_dev = heads_ref.shape[0]
    near = ids_ref.shape[1]
    me = lax.axis_index("member")
    ids = jnp.concatenate([ids_ref[pl.ds(me ^ member, 1), :] for member in range(members)], axis=0)
    local = ids - me * head_dev
    owned = (local >= 0) & (local < head_dev)
    earlier = (iota((near, near), 0) < iota((near, near), 1)).astype(jnp.bfloat16)
    rank = jnp.dot(owned.astype(jnp.bfloat16), earlier, preferred_element_type=jnp.float32)
    rank = jnp.where(owned, rank.astype(jnp.int32), -1)
    shape = (members, most, near)
    pick = jnp.broadcast_to(rank[:, None, :], shape) == iota(shape, 1)
    wanted = jnp.sum(
        jnp.where(pick, jnp.broadcast_to(local[:, None, :] + 1, shape), 0), axis=2, keepdims=True
    ).reshape(members * most, 1)
    onehot = (wanted == iota((members * most, head_dev), 1) + 1).astype(jnp.bfloat16)
    rows_ref[...] = jnp.dot(
        onehot, heads_ref[...], preferred_element_type=jnp.float32
    ).astype(jnp.bfloat16)


def crowd_kernel(groups, members, heads_ref, *refs):
    query_refs, sums_ref = refs[:groups], refs[groups]
    head_dev, width = heads_ref.shape
    new_count = query_refs[0].shape[0]
    here = lax.axis_index("group")
    queries = jnp.concatenate([ref[...] for ref in query_refs], axis=0)
    squares = jnp.square(queries.astype(jnp.float32))
    query_sq = jnp.sum(squares, axis=1, keepdims=True)
    total_w = jnp.zeros((groups * new_count, 1), jnp.float32)
    total_we = jnp.zeros((groups * new_count, 1), jnp.float32)
    tile = 512
    for start in range(0, head_dev, tile):
        block = heads_ref[start:start + tile, :]
        dots = lax.dot_general(
            queries, block, (((1,), (1,)), ((), ())), preferred_element_type=jnp.float32
        )
        parts = jnp.square(block.astype(jnp.float32))
        folded = parts[:, :LANES]
        for column in range(LANES, width, LANES):
            folded = folded + parts[:, column:column + LANES]
        head_sq = jnp.sum(folded.T, axis=0, keepdims=True)
        excess = (query_sq + head_sq - 2.0 * dots) * (1.0 / width)
        inverse = 1.0 / (1.0 + excess)
        weight = inverse * inverse
        total_w = total_w + jnp.sum(weight, axis=1, keepdims=True)
        total_we = total_we + jnp.sum(weight * excess, axis=1, keepdims=True)
    shape = (new_count, LANES)
    lane = iota(shape, 1)
    row = iota(shape, 0)
    for mask in range(groups):
        part = slice(mask * new_count, (mask + 1) * new_count)
        spread_out = jnp.where(lane == row, total_w[part], 0.0) + jnp.where(
            lane == row + new_count, total_we[part], 0.0
        )
        message = jnp.sum(spread_out, axis=0, keepdims=True)
        first = pl.multiple_of((here ^ mask) * members, members)
        sums_ref[pl.ds(first, members), :] = jnp.broadcast_to(message, (members, LANES))


def near_kernel(most, head_dev, ids_ref, listed_ref, vectors_ref, out_ref):
    near = ids_ref.shape[1]
    width = vectors_ref.shape[2]
    block = vectors_ref.shape[1]
    square = (near, near)
    owner_row = jnp.broadcast_to(lax.div(ids_ref[...], head_dev), square)
    eye = iota(square, 0) == iota(square, 1)
    owner = jnp.sum(jnp.where(eye, owner_row, 0), axis=1, keepdims=True)
    before = (owner_row == owner) & (iota(square, 1) < iota(square, 0))
    place = jnp.sum(before.astype(jnp.int32), axis=1, keepdims=True)
    source = owner * most + place
    back = (source == iota((near, listed_ref.shape[0]), 1)).astype(jnp.bfloat16)
    rows32 = jnp.dot(back, listed_ref[...], preferred_element_type=jnp.float32)
    row_sq = jnp.sum(jnp.square(rows32), axis=1, keepdims=True)
    vec = vectors_ref[0]
    vec_sq = jnp.sum(jnp.square(vec.astype(jnp.float32)), axis=1, keepdims=True)
    turned = iota((block, block), 0) == iota((block, block), 1)
    vec_sq = jnp.sum(jnp.where(turned, vec_sq, 0.0), axis=0, keepdims=True)
    dots = lax.dot_general(
        rows32.astype(jnp.bfloat16), vec, (((1,), (1,)), ((), ())),
        preferred_element_type=jnp.float32,
    )
    out_ref[0] = (row_sq + vec_sq - 2.0 * dots) * (1.0 / width)


def final_kernel(new_count, total_heads, sums_ref, density_ref, spread_ref):
    total = jnp.sum(sums_ref[...], axis=0, keepdims=True)
    total_w = total[:, :new_count]
    total_we = total[:, new_count:2 * new_count]
    density_ref[...] = jnp.log(total_w * (1.0 / total_heads))
    spread_ref[...] = total_we / total_w


def per_device(heads, new_heads, vectors, near_ids):
    head_dev, width = heads.shape
    new_count = new_heads.shape[0]
    near = near_ids.shape[1]
    groups = lax.axis_size("group")
    members = lax.axis_size("member")
    most = 2 * near // members

    ids = near_ids
    blocks = [new_heads]
    mask = 1
    while mask < members:
        ids = jnp.concatenate([ids, from_partner(ids, "member", mask)], axis=0)
        mask *= 2
    for mask in range(1, groups):
        blocks.append(from_partner(new_heads, "group", mask))

    rows = call(
        functools.partial(gather_kernel, members, most),
        jax.ShapeDtypeStruct((members * most, width), jnp.bfloat16),
        (ids, heads),
        2 * members * most * head_dev * width,
        heads.size * 2,
    )
    listed = to_each(rows, "member")

    sums = call(
        functools.partial(crowd_kernel, groups, members),
        jax.ShapeDtypeStruct((groups * members, LANES), jnp.float32),
        (heads, *blocks),
        2 * groups * new_count * head_dev * width,
        heads.size * 2,
    )
    sums = to_each(sums, ("group", "member"))
    density, spread = call(
        functools.partial(final_kernel, new_count, float(head_dev * groups * members)),
        (jax.ShapeDtypeStruct((1, new_count), jnp.float32),) * 2,
        (sums,),
        groups * members * LANES,
        groups * members * LANES * 4,
    )
    reassign = call(
        functools.partial(near_kernel, most, head_dev),
        jax.ShapeDtypeStruct((1, near, vectors.shape[1]), jnp.float32),
        (near_ids, listed, vectors),
        4 * near * vectors.shape[1] * width,
        vectors.size * 4,
    )
    return (density[0], spread[0], reassign)


def solution(mesh):
    placed = (
        P(("group", "member"), None),
        P("group", None),
        P(("group", "member"), None, None),
        P(("group", "member"), None),
    )
    return jax.shard_map(
        per_device,
        mesh=mesh,
        in_specs=placed,
        out_specs=(P("group"), P("group"), P(("group", "member"), None, None)),
        check_vma=False,
    )
```

time: 49.6 us -> 46.7 us (0.942)
  Pallas kernels: 0 us -> 5.36 us
  matrix products: 3.65 us -> 0 us
  other arithmetic: 5.36 us -> 2.07 us
  waiting for transfers between devices: 19.6 us -> 18.7 us
    ppermute x0 -> x6, starting transfers between devices: none -> 10 us  [from_partner(): lax.ppermute(value, axis, [(source, source ^ mask) for source in range(co...]
    all_to_all x4 -> x2, starting transfers between devices: 16.8 us -> 6.92 us  [to_each(): return lax.all_to_all(value, axis, 0, 0, tiled=True)]
    all_to_all x4 -> x2, waiting for transfers between devices: 19.6 us -> 13.1 us  [to_each(): return lax.all_to_all(value, axis, 0, 0, tiled=True)]
    ppermute x0 -> x6, waiting for transfers between devices: none -> 5.58 us  [from_partner(): lax.ppermute(value, axis, [(source, source ^ mask) for source in range(co...]
    pallas_call x0 -> x4, Pallas kernels: none -> 5.36 us  [call(): pl.pallas_call(body, out_shape=shapes, in_specs=[pl.BlockSpec(memory_spac...]
    dot_general x4 -> x0, matrix products: 3.65 us -> none  [the longest x1 1.31 us: per_device(): jnp.dot(onehot, heads, preferred_element_type=jnp.float32)]
    reduce_sum x6 -> x0, other arithmetic: 3.23 us -> none  [the longest x1 2.57 us: per_device(): head_sq = jnp.sum(jnp.square(heads.astype(jnp.float32)), axis=1)]
    unnamed x8 -> x10, local copies, waits for them, and re-layouts: 0.02 us -> 2.64 us
  transfers between devices with their start and end apart: 4 -> 8, of which waited for: 4 -> 6; matrix products, arithmetic and copies ran while one was open for 13% -> 2% of each run, Pallas kernels for 0% -> 5%
where the time goes in v3:
time: 46.7 us; the launch traced here: 46.3 us
  waiting for transfers between devices  18.7 us (40%)
  starting transfers between devices  16.9 us (36%)
  Pallas kernels  5.36 us (11%)
  local copies, waits for them, and re-layouts  2.64 us (6%)
  other arithmetic  2.07 us (4%)
  between operations  0.67 us (1%)
    all_to_all x2, waiting for transfers between devices, to_each(): return lax.all_to_all(value, axis, 0, 0, tiled=True)  13.1 us
    ppermute x6, starting transfers between devices, from_partner(): lax.ppermute(value, axis, [(source, source ^ mask) for source in range(co...  10 us
    all_to_all x2, starting transfers between devices, to_each(): return lax.all_to_all(value, axis, 0, 0, tiled=True)  6.92 us
    ppermute x6, waiting for transfers between devices, from_partner(): lax.ppermute(value, axis, [(source, source ^ mask) for source in range(co...  5.58 us
    pallas_call x4, Pallas kernels, call(): pl.pallas_call(body, out_shape=shapes, in_specs=[pl.BlockSpec(memory_spac...  5.36 us
    unnamed x10, local copies, waits for them, and re-layouts  2.64 us
    concatenate x3, other arithmetic, per_device(): ids = jnp.concatenate([ids, from_partner(ids, 'member', mask)], axis=0)  2.07 us
  transfers between devices with their start and end apart: 8, of which 6 were waited for; matrix products, arithmetic and copies ran while one was open for 2% of the time, Pallas kernels for 5%

profile of v3, /device:TPU:0, one launch (start us, length us, event | category | flops | bytes accessed | tf_op | source)
XLA Modules:
  0.0 46.3 jit_solution(111336857163882520)
XLA Ops:
  0.6 3.0 %collective-permute-start.3 = (s32[1,64]{1,0:T(1,128)}, s32[1,64]{1,0:T(1,128)S(1)}, u32[]{:S(2)}, u32[]{:S(2)}) collective-permute-start(s32[1,64]{1,0:T(1,128)} %ids_ref.1), channel_id=1, source_target_pairs={{0,1},{1,0},{2,3},{3,2},{4,5},{5,4},{6,7},{7,6},{8,9},{9,8},{10,11... | collective-permute-start | bytes 776 | tf_op jit(solution)/shard_map/ppermute | solution.py:17
  3.6 1.7 %collective-permute-done.3 = s32[1,64]{1,0:T(1,128)S(1)} collective-permute-done((s32[1,64]{1,0:T(1,128)}, s32[1,64]{1,0:T(1,128)S(1)}, u32[]{:S(2)}, u32[]{:S(2)}) %collective-permute-start.3) | collective-permute-done | bytes 288 | tf_op jit(solution)/shard_map/ppermute | solution.py:17
  5.3 0.7 %pad_add_fusion.2 = s32[2,64]{1,0:T(2,128)S(1)} fusion(s32[1,64]{1,0:T(1,128)S(1)} %collective-permute-done.3, s32[1,64]{1,0:T(1,128)} %ids_ref.1), kind=kLoop, calls=%fused_computation.2 | loop fusion | flops 128 | bytes 1024 | tf_op jit(solution)/shard_map/concatenate | solution.py:144
  6.0 2.1 %collective-permute-start.4 = (s32[2,64]{1,0:T(2,128)S(1)}, s32[2,64]{1,0:T(2,128)S(1)}, u32[]{:S(2)}, u32[]{:S(2)}) collective-permute-start(s32[2,64]{1,0:T(2,128)S(1)} %pad_add_fusion.2), channel_id=1, source_target_pairs={{0,2},{1,3},{2,0},{3,1},{4,6},{5,7},{6,4},{7,5},{8,10},{9,11},{10,... | collective-permute-start | bytes 1544 | tf_op jit(solution)/shard_map/ppermute | solution.py:17
  8.1 1.5 %collective-permute-done.4 = s32[2,64]{1,0:T(2,128)S(1)} collective-permute-done((s32[2,64]{1,0:T(2,128)S(1)}, s32[2,64]{1,0:T(2,128)S(1)}, u32[]{:S(2)}, u32[]{:S(2)}) %collective-permute-start.4) | collective-permute-done | bytes 544 | tf_op jit(solution)/shard_map/ppermute | solution.py:17
  9.6 0.7 %pad_add_fusion.1 = s32[4,64]{1,0:T(4,128)S(1)} fusion(s32[2,64]{1,0:T(2,128)S(1)} %collective-permute-done.4, s32[1,64]{1,0:T(1,128)S(1)} %collective-permute-done.3, s32[1,64]{1,0:T(1,128)} %ids_ref.1), kind=kLoop, calls=%fused_computation.1 | loop fusion | flops 512 | bytes 2048 | tf_op jit(solution)/shard_map/concatenate | solution.py:144
  10.3 3.0 %collective-permute-start.5 = (s32[4,64]{1,0:T(4,128)S(1)}, s32[4,64]{1,0:T(4,128)S(1)}, u32[]{:S(2)}, u32[]{:S(2)}) collective-permute-start(s32[4,64]{1,0:T(4,128)S(1)} %pad_add_fusion.1), channel_id=1, source_target_pairs={{0,4},{1,5},{2,6},{3,7},{4,0},{5,1},{6,2},{7,3},{8,12},{9,13},{10,... | collective-permute-start | bytes 3080 | tf_op jit(solution)/shard_map/ppermute | solution.py:17
  13.3 0.0 collective-permute-start
  13.3 1.5 %collective-permute-start.1 = (bf16[16,768]{1,0:T(8,128)(2,1)}, bf16[16,768]{1,0:T(8,128)(2,1)S(1)}, u32[]{:S(2)}, u32[]{:S(2)}) collective-permute-start(bf16[16,768]{1,0:T(8,128)(2,1)} %refs_0_.1), channel_id=1, source_target_pairs={{0,16},{8,24},{16,0},{24,8},{1,17},{9,25},{17,1},{25,9},{2,18},{10... | collective-permute-start | bytes 73736 | tf_op jit(solution)/shard_map/ppermute | solution.py:17
  14.8 0.3 collective-permute-start.2
  15.2 0.0 collective-permute-done.5
  15.2 0.0 copy-start.4
  15.2 0.7 %pad_add_fusion.ids_ref = s32[8,64]{1,0:T(8,128)S(1)} fusion(s32[4,64]{1,0:T(4,128)S(1)} %collective-permute-done.5, s32[2,64]{1,0:T(2,128)S(1)} %collective-permute-done.4, s32[1,64]{1,0:T(1,128)S(1)} %collective-permute-done.3, s32[1,64]{1,0:T(1,128)} %ids_ref.1), kind=kLoop, calls=%fused_computation | loop fusion | flops 1536 | bytes 4096 | tf_op jit(solution)/shard_map/concatenate | solution.py:144
  15.9 0.0 collective-permute-done.refs_1_
  15.9 1.4 %collective-permute-done.1.refs_2_ = bf16[16,768]{1,0:T(8,128)(2,1)S(1)} collective-permute-done((bf16[16,768]{1,0:T(8,128)(2,1)}, bf16[16,768]{1,0:T(8,128)(2,1)S(1)}, u32[]{:S(2)}, u32[]{:S(2)}) %collective-permute-start.1) | collective-permute-done | bytes 24608 | tf_op jit(solution)/shard_map/ppermute | solution.py:17
  17.3 0.9 %collective-permute-done.2.refs_3_ = bf16[16,768]{1,0:T(8,128)(2,1)S(1)} collective-permute-done((bf16[16,768]{1,0:T(8,128)(2,1)}, bf16[16,768]{1,0:T(8,128)(2,1)S(1)}, u32[]{:S(2)}, u32[]{:S(2)}) %collective-permute-start.2) | collective-permute-done | bytes 24608 | tf_op jit(solution)/shard_map/ppermute | solution.py:17
  18.3 1.9 %copy-done = bf16[2048,768]{1,0:T(8,128)(2,1)S(1)} copy-done((bf16[2048,768]{1,0:T(8,128)(2,1)S(1)}, bf16[2048,768]{1,0:T(8,128)(2,1)}, u32[]{:S(2)}) %copy-start) | copy-done | bytes 3145752
  20.2 0.0 copy-start.3
  20.2 0.7 %copy-done.3 = bf16[16,768]{1,0:T(8,128)(2,1)S(1)} copy-done((bf16[16,768]{1,0:T(8,128)(2,1)S(1)}, bf16[16,768]{1,0:T(8,128)(2,1)}, u32[]{:S(2)}) %copy-start.3) | copy-done | bytes 24600
  20.9 0.0 copy-start.1
  20.9 0.0 copy-start.2
  20.9 2.2 %shard_map.67 = f32[32,128]{1,0:T(8,128)} custom-call(bf16[2048,768]{1,0:T(8,128)(2,1)S(1)} %copy-done, bf16[16,768]{1,0:T(8,128)(2,1)S(1)} %copy-done.3, bf16[16,768]{1,0:T(8,128)(2,1)S(1)} %collective-permute-done.refs_1_, bf16[16,768]{1,0:T(8,128)(2,1)S(1)} %collective-permute-done.1.refs_2_, bf16[16,768]{1,0:T(8,128)(2,1)S(1)} %collective-permute-done.2.refs_3_), custom_call_target="tpu_custom_call" | custom-call | flops 201326592 | bytes 3145728 | tf_op jit(solution)/shard_map/pallas_call | solution.py:25
  23.1 3.5 %all-to-all-start = ((f32[32,1,128]{2,1,0:T(1,128)}), f32[32,1,128]{2,1,0:T(1,128)S(1)}, u32[]{:S(2)}, u32[]{:S(2)}) async-start(f32[32,1,128]{2,1,0:T(1,128)} %bitcast.1), calls=%async_computation | async-start | bytes 32768 | tf_op jit(solution)/shard_map/all_to_all | solution.py:21
  26.6 0.0 copy-done.1
  26.6 1.5 %shard_map.69 = bf16[128,768]{1,0:T(8,128)(2,1)} custom-call(s32[8,64]{1,0:T(8,128)S(1)} %pad_add_fusion.ids_ref, bf16[2048,768]{1,0:T(8,128)(2,1)S(1)} %copy-done.1), custom_call_target="tpu_custom_call" | custom-call | flops 402653184 | bytes 3145728 | tf_op jit(solution)/shard_map/pallas_call | solution.py:25
  28.1 5.6 %all-to-all-done = f32[32,1,128]{2,1,0:T(1,128)S(1)} async-done(((f32[32,1,128]{2,1,0:T(1,128)}), f32[32,1,128]{2,1,0:T(1,128)S(1)}, u32[]{:S(2)}, u32[]{:S(2)}) %all-to-all-start) | async-done | bytes 16416 | tf_op jit(solution)/shard_map/all_to_all | solution.py:21
  33.7 3.4 %all-to-all-start.1 = ((bf16[8,16,768]{2,1,0:T(8,128)(2,1)}), bf16[8,16,768]{2,1,0:T(8,128)(2,1)S(1)}, u32[]{:S(2)}, u32[]{:S(2)}) async-start(bf16[8,16,768]{2,1,0:T(8,128)(2,1)} %bitcast.5), calls=%async_computation.1 | async-start | bytes 393216 | tf_op jit(solution)/shard_map/all_to_all | solution.py:21
  37.1 0.7 %shard_map.68 = (f32[1,16]{1,0:T(1,128)}, f32[1,16]{1,0:T(1,128)}) custom-call(f32[32,128]{1,0:T(8,128)S(1)} %bitcast.9), custom_call_target="tpu_custom_call" | custom-call | flops 4096 | bytes 16384 | tf_op jit(solution)/shard_map/pallas_call | solution.py:25
  37.7 7.5 %all-to-all-done.1 = bf16[8,16,768]{2,1,0:T(8,128)(2,1)S(1)} async-done(((bf16[8,16,768]{2,1,0:T(8,128)(2,1)}), bf16[8,16,768]{2,1,0:T(8,128)(2,1)S(1)}, u32[]{:S(2)}, u32[]{:S(2)}) %all-to-all-start.1) | async-done | bytes 196640 | tf_op jit(solution)/shard_map/all_to_all | solution.py:21
  45.2 0.0 copy-done.4
  45.2 0.0 copy-done.2
  45.2 1.1 %shard_map.70 = f32[1,64,128]{2,1,0:T(8,128)} custom-call(s32[1,64]{1,0:T(1,128)S(1)} %copy-done.4, bf16[128,768]{1,0:T(8,128)(2,1)S(1)} %bitcast.8, bf16[1,128,768]{2,1,0:T(8,128)(2,1)S(1)} %copy-done.2), custom_call_target="tpu_custom_call" | custom-call | flops 25165824 | bytes 393216 | tf_op jit(solution)/shard_map/pallas_call | solution.py:25
  (1 shorter events, 0.0 us)
Async XLA Ops:
  0.6 4.7 %collective-permute-start.3 = (s32[1,64]{1,0:T(1,128)}, s32[1,64]{1,0:T(1,128)S(1)}, u32[]{:S(2)}, u32[]{:S(2)}) collective-permute-start(s32[1,64]{1,0:T(1,128)} %ids_ref.1), channel_id=1, source_target_pairs={{0,1},{1,0},{2,3},{3,2},{4,5},{5,4},{6,7},{7,6},{8,9},{9,8},{10,11... | collective-permute-start | bytes 776 | tf_op jit(solution)/shard_map/ppermute | solution.py:17
  6.0 3.6 %collective-permute-start.4 = (s32[2,64]{1,0:T(2,128)S(1)}, s32[2,64]{1,0:T(2,128)S(1)}, u32[]{:S(2)}, u32[]{:S(2)}) collective-permute-start(s32[2,64]{1,0:T(2,128)S(1)} %pad_add_fusion.2), channel_id=1, source_target_pairs={{0,2},{1,3},{2,0},{3,1},{4,6},{5,7},{6,4},{7,5},{8,10},{9,11},{10,... | collective-permute-start | bytes 1544 | tf_op jit(solution)/shard_map/ppermute | solution.py:17
  10.3 4.9 %collective-permute-start.5 = (s32[4,64]{1,0:T(4,128)S(1)}, s32[4,64]{1,0:T(4,128)S(1)}, u32[]{:S(2)}, u32[]{:S(2)}) collective-permute-start(s32[4,64]{1,0:T(4,128)S(1)} %pad_add_fusion.1), channel_id=1, source_target_pairs={{0,4},{1,5},{2,6},{3,7},{4,0},{5,1},{6,2},{7,3},{8,12},{9,13},{10,... | collective-permute-start | bytes 3080 | tf_op jit(solution)/shard_map/ppermute | solution.py:17
  13.3 2.6 %collective-permute-start = (bf16[16,768]{1,0:T(8,128)(2,1)}, bf16[16,768]{1,0:T(8,128)(2,1)S(1)}, u32[]{:S(2)}, u32[]{:S(2)}) collective-permute-start(bf16[16,768]{1,0:T(8,128)(2,1)} %refs_0_.1), channel_id=1, source_target_pairs={{0,8},{8,0},{16,24},{24,16},{1,9},{9,1},{17,25},{25,17},{2,10},{10... | collective-permute-start | bytes 73736 | tf_op jit(solution)/shard_map/ppermute | solution.py:17
  13.3 4.0 %collective-permute-start.1 = (bf16[16,768]{1,0:T(8,128)(2,1)}, bf16[16,768]{1,0:T(8,128)(2,1)S(1)}, u32[]{:S(2)}, u32[]{:S(2)}) collective-permute-start(bf16[16,768]{1,0:T(8,128)(2,1)} %refs_0_.1), channel_id=1, source_target_pairs={{0,16},{8,24},{16,0},{24,8},{1,17},{9,25},{17,1},{25,9},{2,18},{10... | collective-permute-start | bytes 73736 | tf_op jit(solution)/shard_map/ppermute | solution.py:17
  14.8 3.5 %collective-permute-start.2 = (bf16[16,768]{1,0:T(8,128)(2,1)}, bf16[16,768]{1,0:T(8,128)(2,1)S(1)}, u32[]{:S(2)}, u32[]{:S(2)}) collective-permute-start(bf16[16,768]{1,0:T(8,128)(2,1)} %refs_0_.1), channel_id=1, source_target_pairs={{0,24},{8,16},{16,8},{24,0},{1,25},{9,17},{17,9},{25,1},{2,26},{10... | collective-permute-start | bytes 73736 | tf_op jit(solution)/shard_map/ppermute | solution.py:17
  15.2 30.1 %copy-start.4 = (s32[1,64]{1,0:T(1,128)S(1)}, s32[1,64]{1,0:T(1,128)}, u32[]{:S(2)}) copy-start(s32[1,64]{1,0:T(1,128)} %ids_ref.1) | copy-start | bytes 772
  18.3 1.9 %copy-start = (bf16[2048,768]{1,0:T(8,128)(2,1)S(1)}, bf16[2048,768]{1,0:T(8,128)(2,1)}, u32[]{:S(2)}) copy-start(bf16[2048,768]{1,0:T(8,128)(2,1)} %heads_ref.3) | copy-start | bytes 9437188
  20.2 0.7 %copy-start.3 = (bf16[16,768]{1,0:T(8,128)(2,1)S(1)}, bf16[16,768]{1,0:T(8,128)(2,1)}, u32[]{:S(2)}) copy-start(bf16[16,768]{1,0:T(8,128)(2,1)} %refs_0_.1) | copy-start | bytes 73732
  20.9 5.7 %copy-start.1 = (bf16[2048,768]{1,0:T(8,128)(2,1)S(1)}, bf16[2048,768]{1,0:T(8,128)(2,1)}, u32[]{:S(2)}) copy-start(bf16[2048,768]{1,0:T(8,128)(2,1)} %heads_ref.3) | copy-start | bytes 9437188
  20.9 24.3 %copy-start.2 = (bf16[1,128,768]{2,1,0:T(8,128)(2,1)S(1)}, bf16[1,128,768]{2,1,0:T(8,128)(2,1)}, u32[]{:S(2)}) copy-start(bf16[1,128,768]{2,1,0:T(8,128)(2,1)} %vectors_ref.1) | copy-start | bytes 589828
  23.1 10.6 %all-to-all-start = ((f32[32,1,128]{2,1,0:T(1,128)}), f32[32,1,128]{2,1,0:T(1,128)S(1)}, u32[]{:S(2)}, u32[]{:S(2)}) async-start(f32[32,1,128]{2,1,0:T(1,128)} %bitcast.1), calls=%async_computation | async-start | bytes 32768 | tf_op jit(solution)/shard_map/all_to_all | solution.py:21
  33.7 11.6 %all-to-all-start.1 = ((bf16[8,16,768]{2,1,0:T(8,128)(2,1)}), bf16[8,16,768]{2,1,0:T(8,128)(2,1)S(1)}, u32[]{:S(2)}, u32[]{:S(2)}) async-start(bf16[8,16,768]{2,1,0:T(8,128)(2,1)} %bitcast.5), calls=%async_computation.1 | async-start | bytes 393216 | tf_op jit(solution)/shard_map/all_to_all | solution.py:21

commit v4 on v3

--- a/solution.py
+++ b/solution.py
@@ -21,11 +21,12 @@
     return lax.all_to_all(value, axis, 0, 0, tiled=True)
 
 
-def call(body, shapes, operands, flops, moved):
+def call(body, shapes, operands, flops, moved, unread=0):
+    spaces = [VMEM] * (len(operands) - unread) + [pl.ANY] * unread
     return pl.pallas_call(
         body,
         out_shape=shapes,
-        in_specs=[pl.BlockSpec(memory_space=VMEM)] * len(operands),
+        in_specs=[pl.BlockSpec(memory_space=space) for space in spaces],
         out_specs=jax.tree.map(lambda unused: pl.BlockSpec(memory_space=VMEM), shapes),
         compiler_params=pltpu.CompilerParams(vmem_limit_bytes=LIMIT),
         cost_estimate=pl.CostEstimate(flops=flops, bytes_accessed=moved, transcendentals=0),
@@ -36,11 +37,37 @@
     return lax.broadcasted_iota(jnp.int32, shape, dim)
 
 
-def gather_kernel(members, most, ids_ref, heads_ref, rows_ref):
+def tile_kernel(ids_ref, new_ref, out_ref, kept_ref):
+    near = ids_ref.shape[1]
+    out_ref[:, :near] = jnp.broadcast_to(ids_ref[...], (out_ref.shape[0], near))
+    kept_ref[...] = new_ref[...]
+    out_ref[:, near:] = jnp.zeros((out_ref.shape[0], out_ref.shape[1] - near), jnp.int32)
+
+
+def squares_kernel(heads_ref, kept_ref, head_sq_ref, *sems):
+    head_dev, width = heads_ref.shape
+    tile = head_dev // len(sems)
+    parts = [pl.ds(i * tile, tile) for i in range(len(sems))]
+    copies = [
+        pltpu.make_async_copy(heads_ref.at[part], kept_ref.at[part], sem)
+        for part, sem in zip(parts, sems)
+    ]
+    for copy in copies:
+        copy.start()
+    for i, copy in enumerate(copies):
+        copy.wait()
+        for first in range(i * tile, (i + 1) * tile, LANES):
+            block = jnp.square(kept_ref[first:first + LANES, :].astype(jnp.float32))
+            folded = block[:, :LANES]
+            for column in range(LANES, width, LANES):
+                folded = folded + block[:, column:column + LANES]
+            head_sq_ref[:, first:first + LANES] = jnp.sum(folded.T, axis=0, keepdims=True)
+
+
+def gather_kernel(members, most, near, ids_ref, heads_ref, rows_ref):
     head_dev = heads_ref.shape[0]
-    near = ids_ref.shape[1]
     me = lax.axis_index("member")
-    ids = jnp.concatenate([ids_ref[pl.ds(me ^ member, 1), :] for member in range(members)], axis=0)
+    ids = ids_ref[:, :near]
     local = ids - me * head_dev
     owned = (local >= 0) & (local < head_dev)
     earlier = (iota((near, near), 0) < iota((near, near), 1)).astype(jnp.bfloat16)
@@ -57,8 +84,8 @@
     ).astype(jnp.bfloat16)
 
 
-def crowd_kernel(groups, members, heads_ref, *refs):
-    query_refs, sums_ref = refs[:groups], refs[groups]
+def crowd_kernel(groups, members, heads_ref, head_sq_ref, *refs):
+    query_refs, sums_ref = refs[:groups], refs[-1]
     head_dev, width = heads_ref.shape
     new_count = query_refs[0].shape[0]
     here = lax.axis_index("group")
@@ -69,15 +96,11 @@
     total_we = jnp.zeros((groups * new_count, 1), jnp.float32)
     tile = 512
     for start in range(0, head_dev, tile):
-        block = heads_ref[start:start + tile, :]
         dots = lax.dot_general(
-            queries, block, (((1,), (1,)), ((), ())), preferred_element_type=jnp.float32
+            queries, heads_ref[start:start + tile, :], (((1,), (1,)), ((), ())),
+            preferred_element_type=jnp.float32,
         )
-        parts = jnp.square(block.astype(jnp.float32))
-        folded = parts[:, :LANES]
-        for column in range(LANES, width, LANES):
-            folded = folded + parts[:, column:column + LANES]
-        head_sq = jnp.sum(folded.T, axis=0, keepdims=True)
+        head_sq = head_sq_ref[:, start:start + tile]
         excess = (query_sq + head_sq - 2.0 * dots) * (1.0 / width)
         inverse = 1.0 / (1.0 + excess)
         weight = inverse * inverse
@@ -137,17 +160,35 @@
     members = lax.axis_size("member")
     most = 2 * near // members
 
-    ids = near_ids
-    blocks = [new_heads]
-    mask = 1
-    while mask < members:
-        ids = jnp.concatenate([ids, from_partner(ids, "member", mask)], axis=0)
-        mask *= 2
-    for mask in range(1, groups):
-        blocks.append(from_partner(new_heads, "group", mask))
+    ids, new_heads = call(
+        tile_kernel,
+        (
+            jax.ShapeDtypeStruct((members, LANES), jnp.int32),
+            jax.ShapeDtypeStruct(new_heads.shape, new_heads.dtype),
+        ),
+        (near_ids, new_heads),
+        0,
+        near * 4,
+    )
+    ids = to_each(ids, "member")
+    blocks = [new_heads] + [from_partner(new_heads, "group", mask) for mask in range(1, groups)]
+    heads, head_sq = pl.pallas_call(
+        squares_kernel,
+        out_shape=(
+            jax.ShapeDtypeStruct((head_dev, width), jnp.bfloat16),
+            jax.ShapeDtypeStruct((1, head_dev), jnp.float32),
+        ),
+        in_specs=[pl.BlockSpec(memory_space=pltpu.MemorySpace.HBM)],
+        out_specs=(pl.BlockSpec(memory_space=VMEM),) * 2,
+        scratch_shapes=[pltpu.SemaphoreType.DMA] * 4,
+        compiler_params=pltpu.CompilerParams(vmem_limit_bytes=LIMIT),
+        cost_estimate=pl.CostEstimate(
+            flops=heads.size * 2, bytes_accessed=heads.size * 2, transcendentals=0
+        ),
+    )(pltpu.with_memory_space_constraint(heads, pltpu.MemorySpace.HBM))
 
     rows = call(
-        functools.partial(gather_kernel, members, most),
+        functools.partial(gather_kernel, members, most, near),
         jax.ShapeDtypeStruct((members * most, width), jnp.bfloat16),
         (ids, heads),
         2 * members * most * head_dev * width,
@@ -158,9 +199,10 @@
     sums = call(
         functools.partial(crowd_kernel, groups, members),
         jax.ShapeDtypeStruct((groups * members, LANES), jnp.float32),
-        (heads, *blocks),
+        (heads, head_sq, *blocks, rows),
         2 * groups * new_count * head_dev * width,
         heads.size * 2,
+        unread=1,
     )
     sums = to_each(sums, ("group", "member"))
     density, spread = call(

time: 46.7 us -> 42.5 us (0.910)
  blocking collectives: 0 us -> 10.6 us
  waiting for transfers between devices: 18.7 us -> 9.93 us
  starting transfers between devices: 16.9 us -> 12.5 us
  other arithmetic: 2.07 us -> 0 us
  Pallas kernels: 5.36 us -> 7.09 us
  local copies, waits for them, and re-layouts: 2.64 us -> 1.39 us
    all_to_all x0 -> x1, blocking collectives: none -> 10.6 us  [to_each(): return lax.all_to_all(value, axis, 0, 0, tiled=True)]
    ppermute x6 -> x3, starting transfers between devices: 10 us -> 1.86 us  [from_partner(): lax.ppermute(value, axis, [(source, source ^ mask) for source in range(co...]
    ppermute x6 -> x3, waiting for transfers between devices: 5.58 us -> 0.01 us  [from_partner(): lax.ppermute(value, axis, [(source, source ^ mask) for source in range(co...]
    all_to_all x2, starting transfers between devices: 6.92 us -> 10.6 us  [to_each(): return lax.all_to_all(value, axis, 0, 0, tiled=True)]
    all_to_all x2, waiting for transfers between devices: 13.1 us -> 9.93 us  [to_each(): return lax.all_to_all(value, axis, 0, 0, tiled=True)]
    pallas_call x0 -> x1, Pallas kernels: none -> 2.1 us  [per_device(): pl.pallas_call(squares_kernel, out_shape=(jax.ShapeDtypeStruct((head_dev,...]
    concatenate x3 -> x0, other arithmetic: 2.07 us -> none  [per_device(): ids = jnp.concatenate([ids, from_partner(ids, 'member', mask)], axis=0)]
    unnamed x10 -> x8, local copies, waits for them, and re-layouts: 2.64 us -> 1.39 us
  transfers between devices with their start and end apart: 8 -> 5, of which waited for: 6 -> 2; matrix products, arithmetic and copies ran while one was open for 2% -> 0% of each run, Pallas kernels for 5% -> 10%
where the time goes in v4:
time: 42.5 us; the launch traced here: 42.2 us
  starting transfers between devices  12.5 us (29%)
  blocking collectives  10.6 us (25%)
  waiting for transfers between devices  9.93 us (23%)
  Pallas kernels  7.09 us (17%)
  local copies, waits for them, and re-layouts  1.39 us (3%)
  between operations  0.67 us (2%)
    all_to_all x2, starting transfers between devices, to_each(): return lax.all_to_all(value, axis, 0, 0, tiled=True)  10.6 us
    all_to_all x1, blocking collectives, to_each(): return lax.all_to_all(value, axis, 0, 0, tiled=True)  10.6 us
    all_to_all x2, waiting for transfers between devices, to_each(): return lax.all_to_all(value, axis, 0, 0, tiled=True)  9.93 us
    pallas_call x5, Pallas kernels, call(): pl.pallas_call(body, out_shape=shapes, in_specs=[pl.BlockSpec(memory_spac...  4.99 us
    pallas_call x1, Pallas kernels, per_device(): pl.pallas_call(squares_kernel, out_shape=(jax.ShapeDtypeStruct((head_dev,...  2.1 us
    ppermute x3, starting transfers between devices, from_partner(): lax.ppermute(value, axis, [(source, source ^ mask) for source in range(co...  1.86 us
    unnamed x8, local copies, waits for them, and re-layouts  1.39 us
  transfers between devices with their start and end apart: 5, of which 2 were waited for; matrix products, arithmetic and copies ran while one was open for 0% of the time, Pallas kernels for 10%

profile of v4, /device:TPU:0, one launch (start us, length us, event | category | flops | bytes accessed | tf_op | source)
XLA Modules:
  0.0 42.2 jit_solution(2846442200634055104)
XLA Ops:
  0.6 0.0 copy-start.1
  0.6 0.7 %copy-done.1 = bf16[16,768]{1,0:T(8,128)(2,1)S(1)} copy-done((bf16[16,768]{1,0:T(8,128)(2,1)S(1)}, bf16[16,768]{1,0:T(8,128)(2,1)}, u32[]{:S(2)}) %copy-start.1) | copy-done | bytes 24600
  1.4 0.0 copy-start.2
  1.4 0.7 %copy-done.2 = s32[1,64]{1,0:T(1,128)S(1)} copy-done((s32[1,64]{1,0:T(1,128)S(1)}, s32[1,64]{1,0:T(1,128)}, u32[]{:S(2)}) %copy-start.2) | copy-done | bytes 280
  2.0 0.6 %shard_map.68 = (s32[8,128]{1,0:T(8,128)}, bf16[16,768]{1,0:T(8,128)(2,1)S(1)}) custom-call(s32[1,64]{1,0:T(1,128)S(1)} %copy-done.2, bf16[16,768]{1,0:T(8,128)(2,1)S(1)} %copy-done.1), custom_call_target="tpu_custom_call" | custom-call | bytes 256 | tf_op jit(solution)/shard_map/pallas_call | solution.py:26
  2.6 7.3 %all-to-all-start = ((s32[8,1,128]{2,1,0:T(1,128)}), s32[8,1,128]{2,1,0:T(1,128)S(1)}, u32[]{:S(2)}, u32[]{:S(2)}) async-start(s32[8,1,128]{2,1,0:T(1,128)} %bitcast.1), calls=%async_computation | async-start | bytes 8192 | tf_op jit(solution)/shard_map/all_to_all | solution.py:21
  9.9 0.7 %collective-permute-start.2 = (bf16[16,768]{1,0:T(8,128)(2,1)S(1)}, bf16[16,768]{1,0:T(8,128)(2,1)S(1)}, u32[]{:S(2)}, u32[]{:S(2)}) collective-permute-start(bf16[16,768]{1,0:T(8,128)(2,1)S(1)} %get-tuple-element.11.refs_0_), channel_id=1, source_target_pairs={{0,24},{8,16},{16,8},{24,0},{1,25},{9,17},{17,9},{25,1},{2,26},{10... | collective-permute-start | bytes 73736 | tf_op jit(solution)/shard_map/ppermute | solution.py:17
  10.6 0.9 %collective-permute-start.1 = (bf16[16,768]{1,0:T(8,128)(2,1)S(1)}, bf16[16,768]{1,0:T(8,128)(2,1)S(1)}, u32[]{:S(2)}, u32[]{:S(2)}) collective-permute-start(bf16[16,768]{1,0:T(8,128)(2,1)S(1)} %get-tuple-element.11.refs_0_), channel_id=1, source_target_pairs={{0,16},{8,24},{16,0},{24,8},{1,17},{9,25},{17,1},{25,9},{2,18},{10... | collective-permute-start | bytes 73736 | tf_op jit(solution)/shard_map/ppermute | solution.py:17
  11.5 0.3 collective-permute-start
  11.7 2.1 %shard_map.67 = (bf16[2048,768]{1,0:T(8,128)(2,1)S(1)}, f32[1,2048]{1,0:T(1,128)S(1)}) custom-call(bf16[2048,768]{1,0:T(8,128)(2,1)} %heads_ref.1), custom_call_target="tpu_custom_call" | custom-call | flops 3145728 | bytes 3145728 | tf_op jit(solution)/shard_map/pallas_call | solution.py:175
  13.8 2.4 %all-to-all-done = s32[8,1,128]{2,1,0:T(1,128)S(1)} async-done(((s32[8,1,128]{2,1,0:T(1,128)}), s32[8,1,128]{2,1,0:T(1,128)S(1)}, u32[]{:S(2)}, u32[]{:S(2)}) %all-to-all-start) | async-done | bytes 4128 | tf_op jit(solution)/shard_map/all_to_all | solution.py:21
  16.3 0.0 copy-start
  16.3 0.0 copy-start.3
  16.3 1.4 %shard_map.69.refs_4_ = bf16[128,768]{1,0:T(8,128)(2,1)} custom-call(s32[8,128]{1,0:T(8,128)S(1)} %bitcast.15, bf16[2048,768]{1,0:T(8,128)(2,1)S(1)} %get-tuple-element.9.heads_ref), custom_call_target="tpu_custom_call" | custom-call | flops 402653184 | bytes 3145728 | tf_op jit(solution)/shard_map/pallas_call | solution.py:26
  17.7 0.0 collective-permute-done.2.refs_3_
  17.7 0.0 collective-permute-done.1.refs_2_
  17.7 0.0 collective-permute-done.refs_1_
  17.7 1.2 %shard_map.70 = f32[32,128]{1,0:T(8,128)S(1)} custom-call(bf16[2048,768]{1,0:T(8,128)(2,1)S(1)} %get-tuple-element.9.heads_ref, f32[1,2048]{1,0:T(1,128)S(1)} %get-tuple-element.10.head_sq_ref, bf16[16,768]{1,0:T(8,128)(2,1)S(1)} %get-tuple-element.11.refs_0_, bf16[16,768]{1,0:T(8,128)(2,1)S(1)} %collective-permute-done.refs_1_, ...), custom_call_target="tpu_custom_call" | custom-call | flops 201326592 | bytes 3145728 | tf_op jit(solution)/shard_map/pallas_call | solution.py:26
  18.9 10.6 %all_to_all.33 = f32[32,1,128]{2,1,0:T(1,128)S(1)} all-to-all(f32[32,1,128]{2,1,0:T(1,128)S(1)} %bitcast.13), channel_id=1, replica_groups=mesh['group'=4,'member'=8] {'group','member'}, dimensions={0} | all-to-all | bytes 32768 | tf_op jit(solution)/shard_map/all_to_all | solution.py:21
  29.5 3.4 %all-to-all-start.2 = ((bf16[8,16,768]{2,1,0:T(8,128)(2,1)}), bf16[8,16,768]{2,1,0:T(8,128)(2,1)S(1)}, u32[]{:S(2)}, u32[]{:S(2)}) async-start(bf16[8,16,768]{2,1,0:T(8,128)(2,1)} %bitcast.8), calls=%async_computation.2 | async-start | bytes 393216 | tf_op jit(solution)/shard_map/all_to_all | solution.py:21
  32.9 0.7 %shard_map.71 = (f32[1,16]{1,0:T(1,128)}, f32[1,16]{1,0:T(1,128)}) custom-call(f32[32,128]{1,0:T(8,128)S(1)} %bitcast.14), custom_call_target="tpu_custom_call" | custom-call | flops 4096 | bytes 16384 | tf_op jit(solution)/shard_map/pallas_call | solution.py:26
  33.6 7.5 %all-to-all-done.2 = bf16[8,16,768]{2,1,0:T(8,128)(2,1)S(1)} async-done(((bf16[8,16,768]{2,1,0:T(8,128)(2,1)}), bf16[8,16,768]{2,1,0:T(8,128)(2,1)S(1)}, u32[]{:S(2)}, u32[]{:S(2)}) %all-to-all-start.2) | async-done | bytes 196640 | tf_op jit(solution)/shard_map/all_to_all | solution.py:21
  41.1 0.0 copy-done
  41.1 0.0 copy-done.3
  41.1 1.1 %shard_map.72 = f32[1,64,128]{2,1,0:T(8,128)} custom-call(s32[1,64]{1,0:T(1,128)S(1)} %copy-done.3, bf16[128,768]{1,0:T(8,128)(2,1)S(1)} %bitcast.12, bf16[1,128,768]{2,1,0:T(8,128)(2,1)S(1)} %copy-done), custom_call_target="tpu_custom_call" | custom-call | flops 25165824 | bytes 393216 | tf_op jit(solution)/shard_map/pallas_call | solution.py:26
Async XLA Ops:
  0.6 0.7 %copy-start.1 = (bf16[16,768]{1,0:T(8,128)(2,1)S(1)}, bf16[16,768]{1,0:T(8,128)(2,1)}, u32[]{:S(2)}) copy-start(bf16[16,768]{1,0:T(8,128)(2,1)} %new_ref.1) | copy-start | bytes 73732
  1.4 0.7 %copy-start.2 = (s32[1,64]{1,0:T(1,128)S(1)}, s32[1,64]{1,0:T(1,128)}, u32[]{:S(2)}) copy-start(s32[1,64]{1,0:T(1,128)} %ids_ref.3) | copy-start | bytes 772
  2.6 13.6 %all-to-all-start = ((s32[8,1,128]{2,1,0:T(1,128)}), s32[8,1,128]{2,1,0:T(1,128)S(1)}, u32[]{:S(2)}, u32[]{:S(2)}) async-start(s32[8,1,128]{2,1,0:T(1,128)} %bitcast.1), calls=%async_computation | async-start | bytes 8192 | tf_op jit(solution)/shard_map/all_to_all | solution.py:21
  9.9 7.8 %collective-permute-start.2 = (bf16[16,768]{1,0:T(8,128)(2,1)S(1)}, bf16[16,768]{1,0:T(8,128)(2,1)S(1)}, u32[]{:S(2)}, u32[]{:S(2)}) collective-permute-start(bf16[16,768]{1,0:T(8,128)(2,1)S(1)} %get-tuple-element.11.refs_0_), channel_id=1, source_target_pairs={{0,24},{8,16},{16,8},{24,0},{1,25},{9,17},{17,9},{25,1},{2,26},{10... | collective-permute-start | bytes 73736 | tf_op jit(solution)/shard_map/ppermute | solution.py:17
  10.6 7.2 %collective-permute-start.1 = (bf16[16,768]{1,0:T(8,128)(2,1)S(1)}, bf16[16,768]{1,0:T(8,128)(2,1)S(1)}, u32[]{:S(2)}, u32[]{:S(2)}) collective-permute-start(bf16[16,768]{1,0:T(8,128)(2,1)S(1)} %get-tuple-element.11.refs_0_), channel_id=1, source_target_pairs={{0,16},{8,24},{16,0},{24,8},{1,17},{9,25},{17,1},{25,9},{2,18},{10... | collective-permute-start | bytes 73736 | tf_op jit(solution)/shard_map/ppermute | solution.py:17
  11.5 6.3 %collective-permute-start = (bf16[16,768]{1,0:T(8,128)(2,1)S(1)}, bf16[16,768]{1,0:T(8,128)(2,1)S(1)}, u32[]{:S(2)}, u32[]{:S(2)}) collective-permute-start(bf16[16,768]{1,0:T(8,128)(2,1)S(1)} %get-tuple-element.11.refs_0_), channel_id=1, source_target_pairs={{0,8},{8,0},{16,24},{24,16},{1,9},{9,1},{17,25},{25,17},{2,10},{10... | collective-permute-start | bytes 73736 | tf_op jit(solution)/shard_map/ppermute | solution.py:17
  16.3 24.8 %copy-start = (bf16[1,128,768]{2,1,0:T(8,128)(2,1)S(1)}, bf16[1,128,768]{2,1,0:T(8,128)(2,1)}, u32[]{:S(2)}) copy-start(bf16[1,128,768]{2,1,0:T(8,128)(2,1)} %vectors_ref.1) | copy-start | bytes 589828
  16.3 24.8 %copy-start.3 = (s32[1,64]{1,0:T(1,128)S(1)}, s32[1,64]{1,0:T(1,128)}, u32[]{:S(2)}) copy-start(s32[1,64]{1,0:T(1,128)} %ids_ref.3) | copy-start | bytes 772
  29.5 11.6 %all-to-all-start.2 = ((bf16[8,16,768]{2,1,0:T(8,128)(2,1)}), bf16[8,16,768]{2,1,0:T(8,128)(2,1)S(1)}, u32[]{:S(2)}, u32[]{:S(2)}) async-start(bf16[8,16,768]{2,1,0:T(8,128)(2,1)} %bitcast.8), calls=%async_computation.2 | async-start | bytes 393216 | tf_op jit(solution)/shard_map/all_to_all | solution.py:21

commit v5 on v4

--- a/solution.py
+++ b/solution.py
@@ -144,7 +144,7 @@
     out_ref[0] = (row_sq + vec_sq - 2.0 * dots) * (1.0 / width)
 
 
-def final_kernel(new_count, total_heads, sums_ref, density_ref, spread_ref):
+def final_kernel(new_count, total_heads, sums_ref, unused, density_ref, spread_ref):
     total = jnp.sum(sums_ref[...], axis=0, keepdims=True)
     total_w = total[:, :new_count]
     total_we = total[:, new_count:2 * new_count]
@@ -205,13 +205,6 @@
         unread=1,
     )
     sums = to_each(sums, ("group", "member"))
-    density, spread = call(
-        functools.partial(final_kernel, new_count, float(head_dev * groups * members)),
-        (jax.ShapeDtypeStruct((1, new_count), jnp.float32),) * 2,
-        (sums,),
-        groups * members * LANES,
-        groups * members * LANES * 4,
-    )
     reassign = call(
         functools.partial(near_kernel, most, head_dev),
         jax.ShapeDtypeStruct((1, near, vectors.shape[1]), jnp.float32),
@@ -219,6 +212,14 @@
         4 * near * vectors.shape[1] * width,
         vectors.size * 4,
     )
+    density, spread = call(
+        functools.partial(final_kernel, new_count, float(head_dev * groups * members)),
+        (jax.ShapeDtypeStruct((1, new_count), jnp.float32),) * 2,
+        (sums, reassign),
+        groups * members * LANES,
+        groups * members * LANES * 4,
+        unread=1,
+    )
     return (density[0], spread[0], reassign)
 
 

time: 42.5 us -> 42.8 us (level)
  blocking collectives: 10.6 us -> 0 us
  starting transfers between devices: 12.5 us -> 17.4 us
  waiting for transfers between devices: 9.93 us -> 13.6 us
  local copies, waits for them, and re-layouts: 1.39 us -> 2.89 us
  Pallas kernels: 7.09 us -> 7.7 us
    all_to_all x1 -> x0, blocking collectives: 10.6 us -> none  [to_each(): return lax.all_to_all(value, axis, 0, 0, tiled=True)]
    all_to_all x2 -> x3, starting transfers between devices: 10.6 us -> 15.5 us  [to_each(): return lax.all_to_all(value, axis, 0, 0, tiled=True)]
    ppermute x3, waiting for transfers between devices: 0.01 us -> 2.26 us  [from_partner(): lax.ppermute(value, axis, [(source, source ^ mask) for source in range(co...]
    unnamed x8 -> x14, local copies, waits for them, and re-layouts: 1.39 us -> 2.89 us
    all_to_all x2 -> x3, waiting for transfers between devices: 9.93 us -> 11.4 us  [to_each(): return lax.all_to_all(value, axis, 0, 0, tiled=True)]
    pallas_call x5, Pallas kernels: 4.99 us -> 5.6 us  [call(): pl.pallas_call(body, out_shape=shapes, in_specs=[pl.BlockSpec(memory_spac...]
  transfers between devices with their start and end apart: 5 -> 6, of which waited for: 2 -> 5; matrix products, arithmetic and copies ran while one was open for 0% -> 0% of each run, Pallas kernels for 10% -> 12%
where the time goes in v5:
time: 42.8 us; the launch traced here: 42.3 us
  starting transfers between devices  17.4 us (41%)
  waiting for transfers between devices  13.6 us (32%)
  Pallas kernels  7.7 us (18%)
  local copies, waits for them, and re-layouts  2.89 us (7%)
  between operations  0.7 us (2%)
    all_to_all x3, starting transfers between devices, to_each(): return lax.all_to_all(value, axis, 0, 0, tiled=True)  15.5 us
    all_to_all x3, waiting for transfers between devices, to_each(): return lax.all_to_all(value, axis, 0, 0, tiled=True)  11.4 us
    pallas_call x5, Pallas kernels, call(): pl.pallas_call(body, out_shape=shapes, in_specs=[pl.BlockSpec(memory_spac...  5.6 us
    unnamed x14, local copies, waits for them, and re-layouts  2.89 us
    ppermute x3, waiting for transfers between devices, from_partner(): lax.ppermute(value, axis, [(source, source ^ mask) for source in range(co...  2.26 us
    pallas_call x1, Pallas kernels, per_device(): pl.pallas_call(squares_kernel, out_shape=(jax.ShapeDtypeStruct((head_dev,...  2.1 us
    ppermute x3, starting transfers between devices, from_partner(): lax.ppermute(value, axis, [(source, source ^ mask) for source in range(co...  1.92 us
  transfers between devices with their start and end apart: 6, of which 5 were waited for; matrix products, arithmetic and copies ran while one was open for 0% of the time, Pallas kernels for 12%

profile of v5, /device:TPU:0, one launch (start us, length us, event | category | flops | bytes accessed | tf_op | source)
XLA Modules:
  0.0 42.3 jit_solution(7063355283637507974)
XLA Ops:
  0.6 0.0 copy-start.4
  0.6 0.7 %copy-done.4 = bf16[16,768]{1,0:T(8,128)(2,1)S(1)} copy-done((bf16[16,768]{1,0:T(8,128)(2,1)S(1)}, bf16[16,768]{1,0:T(8,128)(2,1)}, u32[]{:S(2)}) %copy-start.4) | copy-done | bytes 24600
  1.4 0.0 copy-start.5
  1.4 0.7 %copy-done.5 = s32[1,64]{1,0:T(1,128)S(1)} copy-done((s32[1,64]{1,0:T(1,128)S(1)}, s32[1,64]{1,0:T(1,128)}, u32[]{:S(2)}) %copy-start.5) | copy-done | bytes 280
  2.0 0.6 %shard_map.68 = (s32[8,128]{1,0:T(8,128)}, bf16[16,768]{1,0:T(8,128)(2,1)S(1)}) custom-call(s32[1,64]{1,0:T(1,128)S(1)} %copy-done.5, bf16[16,768]{1,0:T(8,128)(2,1)S(1)} %copy-done.4), custom_call_target="tpu_custom_call" | custom-call | bytes 256 | tf_op jit(solution)/shard_map/pallas_call | solution.py:26
  2.6 0.0 copy-start.2
  2.6 7.3 %all-to-all-start = ((s32[8,1,128]{2,1,0:T(1,128)}), s32[8,1,128]{2,1,0:T(1,128)S(1)}, u32[]{:S(2)}, u32[]{:S(2)}) async-start(s32[8,1,128]{2,1,0:T(1,128)} %bitcast.1), calls=%async_computation | async-start | bytes 8192 | tf_op jit(solution)/shard_map/all_to_all | solution.py:21
  9.9 2.1 %shard_map.67 = (bf16[2048,768]{1,0:T(8,128)(2,1)S(1)}, f32[1,2048]{1,0:T(1,128)S(1)}) custom-call(bf16[2048,768]{1,0:T(8,128)(2,1)} %heads_ref.1), custom_call_target="tpu_custom_call" | custom-call | flops 3145728 | bytes 3145728 | tf_op jit(solution)/shard_map/pallas_call | solution.py:175
  12.0 4.4 %all-to-all-done = s32[8,1,128]{2,1,0:T(1,128)S(1)} async-done(((s32[8,1,128]{2,1,0:T(1,128)}), s32[8,1,128]{2,1,0:T(1,128)S(1)}, u32[]{:S(2)}, u32[]{:S(2)}) %all-to-all-start) | async-done | bytes 4128 | tf_op jit(solution)/shard_map/all_to_all | solution.py:21
  16.3 0.0 copy-done.2
  16.3 0.0 copy-start
  16.3 0.0 copy-start.6
  16.3 1.5 %shard_map.69.refs_4_ = bf16[128,768]{1,0:T(8,128)(2,1)} custom-call(s32[8,128]{1,0:T(8,128)S(1)} %bitcast.14, bf16[2048,768]{1,0:T(8,128)(2,1)S(1)} %get-tuple-element.9.heads_ref), custom_call_target="tpu_custom_call" | custom-call | flops 402653184 | bytes 3145728 | tf_op jit(solution)/shard_map/pallas_call | solution.py:26
  17.8 3.4 %all-to-all-start.2 = ((bf16[8,16,768]{2,1,0:T(8,128)(2,1)}), bf16[8,16,768]{2,1,0:T(8,128)(2,1)S(1)}, u32[]{:S(2)}, u32[]{:S(2)}) async-start(bf16[8,16,768]{2,1,0:T(8,128)(2,1)} %bitcast.6), calls=%async_computation.2 | async-start | bytes 393216 | tf_op jit(solution)/shard_map/all_to_all | solution.py:21
  21.2 0.1 collective-permute-start.2
  21.3 1.6 %collective-permute-start.1 = (bf16[16,768]{1,0:T(8,128)(2,1)}, bf16[16,768]{1,0:T(8,128)(2,1)S(1)}, u32[]{:S(2)}, u32[]{:S(2)}) collective-permute-start(bf16[16,768]{1,0:T(8,128)(2,1)} %copy-done.2), channel_id=1, source_target_pairs={{0,16},{8,24},{16,0},{24,8},{1,17},{9,25},{17,1},{25,9},{2,18},{10... | collective-permute-start | bytes 73736 | tf_op jit(solution)/shard_map/ppermute | solution.py:17
  22.9 0.3 collective-permute-start
  23.1 1.8 %collective-permute-done.2.refs_3_ = bf16[16,768]{1,0:T(8,128)(2,1)S(1)} collective-permute-done((bf16[16,768]{1,0:T(8,128)(2,1)}, bf16[16,768]{1,0:T(8,128)(2,1)S(1)}, u32[]{:S(2)}, u32[]{:S(2)}) %collective-permute-start.2) | collective-permute-done | bytes 24608 | tf_op jit(solution)/shard_map/ppermute | solution.py:17
  24.9 0.5 %collective-permute-done.1.refs_2_ = bf16[16,768]{1,0:T(8,128)(2,1)S(1)} collective-permute-done((bf16[16,768]{1,0:T(8,128)(2,1)}, bf16[16,768]{1,0:T(8,128)(2,1)S(1)}, u32[]{:S(2)}, u32[]{:S(2)}) %collective-permute-start.1) | collective-permute-done | bytes 24608 | tf_op jit(solution)/shard_map/ppermute | solution.py:17
  25.4 0.0 collective-permute-done.refs_1_
  25.4 0.0 copy-start.3
  25.4 0.7 %copy-done.3 = bf16[16,768]{1,0:T(8,128)(2,1)S(1)} copy-done((bf16[16,768]{1,0:T(8,128)(2,1)S(1)}, bf16[16,768]{1,0:T(8,128)(2,1)}, u32[]{:S(2)}) %copy-start.3) | copy-done | bytes 24600
  26.1 1.8 %shard_map.70 = f32[32,128]{1,0:T(8,128)} custom-call(bf16[2048,768]{1,0:T(8,128)(2,1)S(1)} %get-tuple-element.9.heads_ref, f32[1,2048]{1,0:T(1,128)S(1)} %get-tuple-element.10.head_sq_ref, bf16[16,768]{1,0:T(8,128)(2,1)S(1)} %copy-done.3, bf16[16,768]{1,0:T(8,128)(2,1)S(1)} %collective-permute-done.refs_1_, ...), custom_call_target="tpu_custom_call" | custom-call | flops 201326592 | bytes 3145728 | tf_op jit(solution)/shard_map/pallas_call | solution.py:26
  27.9 1.0 %all-to-all-done.2 = bf16[8,16,768]{2,1,0:T(8,128)(2,1)S(1)} async-done(((bf16[8,16,768]{2,1,0:T(8,128)(2,1)}), bf16[8,16,768]{2,1,0:T(8,128)(2,1)S(1)}, u32[]{:S(2)}, u32[]{:S(2)}) %all-to-all-start.2) | async-done | bytes 196640 | tf_op jit(solution)/shard_map/all_to_all | solution.py:21
  28.9 4.9 %all-to-all-start.1 = ((f32[32,1,128]{2,1,0:T(1,128)}), f32[32,1,128]{2,1,0:T(1,128)S(1)}, u32[]{:S(2)}, u32[]{:S(2)}) async-start(f32[32,1,128]{2,1,0:T(1,128)} %bitcast.4), calls=%async_computation.1 | async-start | bytes 32768 | tf_op jit(solution)/shard_map/all_to_all | solution.py:21
  33.8 0.0 copy-done
  33.8 0.0 copy-done.6
  33.8 1.1 %shard_map.71.unused = f32[1,64,128]{2,1,0:T(8,128)} custom-call(s32[1,64]{1,0:T(1,128)S(1)} %copy-done.6, bf16[128,768]{1,0:T(8,128)(2,1)S(1)} %bitcast.12, bf16[1,128,768]{2,1,0:T(8,128)(2,1)S(1)} %copy-done), custom_call_target="tpu_custom_call" | custom-call | flops 25165824 | bytes 393216 | tf_op jit(solution)/shard_map/pallas_call | solution.py:26
  34.9 6.0 %all-to-all-done.1 = f32[32,1,128]{2,1,0:T(1,128)S(1)} async-done(((f32[32,1,128]{2,1,0:T(1,128)}), f32[32,1,128]{2,1,0:T(1,128)S(1)}, u32[]{:S(2)}, u32[]{:S(2)}) %all-to-all-start.1) | async-done | bytes 16416 | tf_op jit(solution)/shard_map/all_to_all | solution.py:21
  40.9 0.0 copy-start.1
  40.9 0.8 %copy-done.1 = f32[1,64,128]{2,1,0:T(8,128)S(1)} copy-done((f32[1,64,128]{2,1,0:T(8,128)S(1)}, f32[1,64,128]{2,1,0:T(8,128)}, u32[]{:S(2)}) %copy-start.1) | copy-done | bytes 32792
  41.7 0.7 %shard_map.72 = (f32[1,16]{1,0:T(1,128)}, f32[1,16]{1,0:T(1,128)}) custom-call(f32[32,128]{1,0:T(8,128)S(1)} %bitcast.13, f32[1,64,128]{2,1,0:T(8,128)S(1)} %copy-done.1), custom_call_target="tpu_custom_call" | custom-call | flops 4096 | bytes 16384 | tf_op jit(solution)/shard_map/pallas_call | solution.py:26
Async XLA Ops:
  0.6 0.7 %copy-start.4 = (bf16[16,768]{1,0:T(8,128)(2,1)S(1)}, bf16[16,768]{1,0:T(8,128)(2,1)}, u32[]{:S(2)}) copy-start(bf16[16,768]{1,0:T(8,128)(2,1)} %new_ref.1) | copy-start | bytes 73732
  1.4 0.7 %copy-start.5 = (s32[1,64]{1,0:T(1,128)S(1)}, s32[1,64]{1,0:T(1,128)}, u32[]{:S(2)}) copy-start(s32[1,64]{1,0:T(1,128)} %ids_ref.3) | copy-start | bytes 772
  2.6 13.7 %copy-start.2 = (bf16[16,768]{1,0:T(8,128)(2,1)}, bf16[16,768]{1,0:T(8,128)(2,1)S(1)}, u32[]{:S(2)}) copy-start(bf16[16,768]{1,0:T(8,128)(2,1)S(1)} %get-tuple-element.11.refs_0_) | copy-start | bytes 73732
  2.6 13.7 %all-to-all-start = ((s32[8,1,128]{2,1,0:T(1,128)}), s32[8,1,128]{2,1,0:T(1,128)S(1)}, u32[]{:S(2)}, u32[]{:S(2)}) async-start(s32[8,1,128]{2,1,0:T(1,128)} %bitcast.1), calls=%async_computation | async-start | bytes 8192 | tf_op jit(solution)/shard_map/all_to_all | solution.py:21
  16.3 17.5 %copy-start = (bf16[1,128,768]{2,1,0:T(8,128)(2,1)S(1)}, bf16[1,128,768]{2,1,0:T(8,128)(2,1)}, u32[]{:S(2)}) copy-start(bf16[1,128,768]{2,1,0:T(8,128)(2,1)} %vectors_ref.1) | copy-start | bytes 589828
  16.3 17.5 %copy-start.6 = (s32[1,64]{1,0:T(1,128)S(1)}, s32[1,64]{1,0:T(1,128)}, u32[]{:S(2)}) copy-start(s32[1,64]{1,0:T(1,128)} %ids_ref.3) | copy-start | bytes 772
  17.8 11.1 %all-to-all-start.2 = ((bf16[8,16,768]{2,1,0:T(8,128)(2,1)}), bf16[8,16,768]{2,1,0:T(8,128)(2,1)S(1)}, u32[]{:S(2)}, u32[]{:S(2)}) async-start(bf16[8,16,768]{2,1,0:T(8,128)(2,1)} %bitcast.6), calls=%async_computation.2 | async-start | bytes 393216 | tf_op jit(solution)/shard_map/all_to_all | solution.py:21
  21.2 3.7 %collective-permute-start.2 = (bf16[16,768]{1,0:T(8,128)(2,1)}, bf16[16,768]{1,0:T(8,128)(2,1)S(1)}, u32[]{:S(2)}, u32[]{:S(2)}) collective-permute-start(bf16[16,768]{1,0:T(8,128)(2,1)} %copy-done.2), channel_id=1, source_target_pairs={{0,24},{8,16},{16,8},{24,0},{1,25},{9,17},{17,9},{25,1},{2,26},{10... | collective-permute-start | bytes 73736 | tf_op jit(solution)/shard_map/ppermute | solution.py:17
  21.3 4.1 %collective-permute-start.1 = (bf16[16,768]{1,0:T(8,128)(2,1)}, bf16[16,768]{1,0:T(8,128)(2,1)S(1)}, u32[]{:S(2)}, u32[]{:S(2)}) collective-permute-start(bf16[16,768]{1,0:T(8,128)(2,1)} %copy-done.2), channel_id=1, source_target_pairs={{0,16},{8,24},{16,0},{24,8},{1,17},{9,25},{17,1},{25,9},{2,18},{10... | collective-permute-start | bytes 73736 | tf_op jit(solution)/shard_map/ppermute | solution.py:17
  22.9 2.5 %collective-permute-start = (bf16[16,768]{1,0:T(8,128)(2,1)}, bf16[16,768]{1,0:T(8,128)(2,1)S(1)}, u32[]{:S(2)}, u32[]{:S(2)}) collective-permute-start(bf16[16,768]{1,0:T(8,128)(2,1)} %copy-done.2), channel_id=1, source_target_pairs={{0,8},{8,0},{16,24},{24,16},{1,9},{9,1},{17,25},{25,17},{2,10},{10... | collective-permute-start | bytes 73736 | tf_op jit(solution)/shard_map/ppermute | solution.py:17
  25.4 0.7 %copy-start.3 = (bf16[16,768]{1,0:T(8,128)(2,1)S(1)}, bf16[16,768]{1,0:T(8,128)(2,1)}, u32[]{:S(2)}) copy-start(bf16[16,768]{1,0:T(8,128)(2,1)} %copy-done.2) | copy-start | bytes 73732
  28.9 12.0 %all-to-all-start.1 = ((f32[32,1,128]{2,1,0:T(1,128)}), f32[32,1,128]{2,1,0:T(1,128)S(1)}, u32[]{:S(2)}, u32[]{:S(2)}) async-start(f32[32,1,128]{2,1,0:T(1,128)} %bitcast.4), calls=%async_computation.1 | async-start | bytes 32768 | tf_op jit(solution)/shard_map/all_to_all | solution.py:21
  40.9 0.8 %copy-start.1 = (f32[1,64,128]{2,1,0:T(8,128)S(1)}, f32[1,64,128]{2,1,0:T(8,128)}, u32[]{:S(2)}) copy-start(f32[1,64,128]{2,1,0:T(8,128)} %shard_map.71.unused) | copy-start | bytes 98308

commit v6 on v5

--- a/solution.py
+++ b/solution.py
@@ -8,6 +8,7 @@
 from jax.sharding import PartitionSpec as P
 
 VMEM = pltpu.MemorySpace.VMEM
+HBM = pltpu.MemorySpace.HBM
 LANES = 128
 LIMIT = 24 * 2**20
 
@@ -19,6 +20,10 @@
 
 def to_each(value, axis):
     return lax.all_to_all(value, axis, 0, 0, tiled=True)
+
+
+def in_hbm(value):
+    return pltpu.with_memory_space_constraint(value, HBM)
 
 
 def call(body, shapes, operands, flops, moved, unread=0):
@@ -37,14 +42,7 @@
     return lax.broadcasted_iota(jnp.int32, shape, dim)
 
 
-def tile_kernel(ids_ref, new_ref, out_ref, kept_ref):
-    near = ids_ref.shape[1]
-    out_ref[:, :near] = jnp.broadcast_to(ids_ref[...], (out_ref.shape[0], near))
-    kept_ref[...] = new_ref[...]
-    out_ref[:, near:] = jnp.zeros((out_ref.shape[0], out_ref.shape[1] - near), jnp.int32)
-
-
-def squares_kernel(heads_ref, kept_ref, head_sq_ref, *sems):
+def squares_kernel(heads_ref, new_ref, kept_ref, head_sq_ref, kept_new_ref, new_sem, *sems):
     head_dev, width = heads_ref.shape
     tile = head_dev // len(sems)
     parts = [pl.ds(i * tile, tile) for i in range(len(sems))]
@@ -54,6 +52,8 @@
     ]
     for copy in copies:
         copy.start()
+    new_copy = pltpu.make_async_copy(new_ref, kept_new_ref, new_sem)
+    new_copy.start()
     for i, copy in enumerate(copies):
         copy.wait()
         for first in range(i * tile, (i + 1) * tile, LANES):
@@ -62,12 +62,15 @@
             for column in range(LANES, width, LANES):
                 folded = folded + block[:, column:column + LANES]
             head_sq_ref[:, first:first + LANES] = jnp.sum(folded.T, axis=0, keepdims=True)
-
-
-def gather_kernel(members, most, near, ids_ref, heads_ref, rows_ref):
+    new_copy.wait()
+
+
+def gather_kernel(members, most, ids_ref, heads_ref, *refs):
+    rows_ref = refs[-1]
     head_dev = heads_ref.shape[0]
+    near = ids_ref.shape[1]
     me = lax.axis_index("member")
-    ids = ids_ref[:, :near]
+    ids = jnp.concatenate([ids_ref[pl.ds(me ^ member, 1), :] for member in range(members)], axis=0)
     local = ids - me * head_dev
     owned = (local >= 0) & (local < head_dev)
     earlier = (iota((near, near), 0) < iota((near, near), 1)).astype(jnp.bfloat16)
@@ -160,46 +163,42 @@
     members = lax.axis_size("member")
     most = 2 * near // members
 
-    ids, new_heads = call(
-        tile_kernel,
-        (
-            jax.ShapeDtypeStruct((members, LANES), jnp.int32),
-            jax.ShapeDtypeStruct(new_heads.shape, new_heads.dtype),
-        ),
-        (near_ids, new_heads),
-        0,
-        near * 4,
-    )
-    ids = to_each(ids, "member")
-    blocks = [new_heads] + [from_partner(new_heads, "group", mask) for mask in range(1, groups)]
-    heads, head_sq = pl.pallas_call(
+    ids = lax.optimization_barrier(jnp.maximum(near_ids, 0))
+    mask = 1
+    while mask < members:
+        ids = jnp.concatenate([ids, from_partner(ids, "member", mask)], axis=0)
+        mask *= 2
+    others = [from_partner(new_heads, "group", mask) for mask in range(1, groups)]
+    heads, head_sq, new_heads = pl.pallas_call(
         squares_kernel,
         out_shape=(
             jax.ShapeDtypeStruct((head_dev, width), jnp.bfloat16),
             jax.ShapeDtypeStruct((1, head_dev), jnp.float32),
+            jax.ShapeDtypeStruct(new_heads.shape, new_heads.dtype),
         ),
-        in_specs=[pl.BlockSpec(memory_space=pltpu.MemorySpace.HBM)],
-        out_specs=(pl.BlockSpec(memory_space=VMEM),) * 2,
-        scratch_shapes=[pltpu.SemaphoreType.DMA] * 4,
+        in_specs=[pl.BlockSpec(memory_space=HBM)] * 2,
+        out_specs=(pl.BlockSpec(memory_space=VMEM),) * 3,
+        scratch_shapes=[pltpu.SemaphoreType.DMA] * 5,
         compiler_params=pltpu.CompilerParams(vmem_limit_bytes=LIMIT),
         cost_estimate=pl.CostEstimate(
             flops=heads.size * 2, bytes_accessed=heads.size * 2, transcendentals=0
         ),
-    )(pltpu.with_memory_space_constraint(heads, pltpu.MemorySpace.HBM))
+    )(in_hbm(heads), in_hbm(new_heads))
 
     rows = call(
-        functools.partial(gather_kernel, members, most, near),
+        functools.partial(gather_kernel, members, most),
         jax.ShapeDtypeStruct((members * most, width), jnp.bfloat16),
-        (ids, heads),
+        (ids, heads, *others),
         2 * members * most * head_dev * width,
         heads.size * 2,
+        unread=len(others),
     )
     listed = to_each(rows, "member")
 
     sums = call(
         functools.partial(crowd_kernel, groups, members),
         jax.ShapeDtypeStruct((groups * members, LANES), jnp.float32),
-        (heads, head_sq, *blocks, rows),
+        (heads, head_sq, new_heads, *others, rows),
         2 * groups * new_count * head_dev * width,
         heads.size * 2,
         unread=1,
@@ -215,7 +214,7 @@
     density, spread = call(
         functools.partial(final_kernel, new_count, float(head_dev * groups * members)),
         (jax.ShapeDtypeStruct((1, new_count), jnp.float32),) * 2,
-        (sums, reassign),
+        (sums, in_hbm(reassign)),
         groups * members * LANES,
         groups * members * LANES * 4,
         unread=1,

time: 42.8 us -> 42.7 us (level)
  starting transfers between devices: 17.4 us -> 16.7 us
  other arithmetic: 0 us -> 0.69 us
  local copies, waits for them, and re-layouts: 2.89 us -> 3.57 us
  Pallas kernels: 7.7 us -> 7.09 us
    all_to_all x3 -> x2, starting transfers between devices: 15.5 us -> 6.34 us  [to_each(): return lax.all_to_all(value, axis, 0, 0, tiled=True)]
    ppermute x3 -> x6, starting transfers between devices: 1.92 us -> 10.3 us  [from_partner(): lax.ppermute(value, axis, [(source, source ^ mask) for source in range(co...]
    all_to_all x3 -> x2, waiting for transfers between devices: 11.4 us -> 9.04 us  [to_each(): return lax.all_to_all(value, axis, 0, 0, tiled=True)]
    ppermute x3 -> x6, waiting for transfers between devices: 2.26 us -> 4.41 us  [from_partner(): lax.ppermute(value, axis, [(source, source ^ mask) for source in range(co...]
    unnamed x14 -> x20, local copies, waits for them, and re-layouts: 2.89 us -> 3.57 us
    max x0 -> x1, other arithmetic: none -> 0.66 us  [per_device(): ids = lax.optimization_barrier(jnp.maximum(near_ids, 0))]
    pallas_call x5 -> x4, Pallas kernels: 5.6 us -> 4.98 us  [call(): pl.pallas_call(body, out_shape=shapes, in_specs=[pl.BlockSpec(memory_spac...]
  transfers between devices with their start and end apart: 6 -> 8, of which waited for: 5 -> 5; matrix products, arithmetic and copies ran while one was open for 0% -> 0% of each run, Pallas kernels for 12% -> 12%
where the time goes in v6:
time: 42.7 us; the launch traced here: 42.2 us
  starting transfers between devices  16.7 us (39%)
  waiting for transfers between devices  13.4 us (31%)
  Pallas kernels  7.09 us (17%)
  local copies, waits for them, and re-layouts  3.57 us (8%)
  between operations  0.74 us (2%)
  other arithmetic  0.69 us (2%)
    ppermute x6, starting transfers between devices, from_partner(): lax.ppermute(value, axis, [(source, source ^ mask) for source in range(co...  10.3 us
    all_to_all x2, waiting for transfers between devices, to_each(): return lax.all_to_all(value, axis, 0, 0, tiled=True)  9.04 us
    all_to_all x2, starting transfers between devices, to_each(): return lax.all_to_all(value, axis, 0, 0, tiled=True)  6.34 us
    pallas_call x4, Pallas kernels, call(): pl.pallas_call(body, out_shape=shapes, in_specs=[pl.BlockSpec(memory_spac...  4.98 us
    ppermute x6, waiting for transfers between devices, from_partner(): lax.ppermute(value, axis, [(source, source ^ mask) for source in range(co...  4.41 us
    unnamed x20, local copies, waits for them, and re-layouts  3.57 us
    pallas_call x1, Pallas kernels, per_device(): pl.pallas_call(squares_kernel, out_shape=(jax.ShapeDtypeStruct((head_dev,...  2.11 us
  transfers between devices with their start and end apart: 8, of which 5 were waited for; matrix products, arithmetic and copies ran while one was open for 0% of the time, Pallas kernels for 12%

profile of v6, /device:TPU:0, one launch (start us, length us, event | category | flops | bytes accessed | tf_op | source)
XLA Modules:
  0.0 42.2 jit_solution(16076832182750515343)
XLA Ops:
  0.6 0.7 %broadcast_maximum_fusion = s32[1,64]{1,0:T(1,128)S(1)} fusion(s32[1,64]{1,0:T(1,128)} %ids_ref.1), kind=kLoop, calls=%fused_computation.3 | loop fusion | flops 64 | bytes 512 | tf_op jit(solution)/shard_map/max | solution.py:166
  1.3 2.9 %collective-permute-start.3 = (s32[1,64]{1,0:T(1,128)S(1)}, s32[1,64]{1,0:T(1,128)S(1)}, u32[]{:S(2)}, u32[]{:S(2)}) collective-permute-start(s32[1,64]{1,0:T(1,128)S(1)} %broadcast_maximum_fusion), channel_id=1, source_target_pairs={{0,1},{1,0},{2,3},{3,2},{4,5},{5,4},{6,7},{7,6},{8,9},{9,8},{10,11... | collective-permute-start | bytes 776 | tf_op jit(solution)/shard_map/ppermute | solution.py:18
  4.2 1.5 %collective-permute-done.3 = s32[1,64]{1,0:T(1,128)S(1)} collective-permute-done((s32[1,64]{1,0:T(1,128)S(1)}, s32[1,64]{1,0:T(1,128)S(1)}, u32[]{:S(2)}, u32[]{:S(2)}) %collective-permute-start.3) | collective-permute-done | bytes 288 | tf_op jit(solution)/shard_map/ppermute | solution.py:18
  5.8 2.2 %collective-permute-start.4 = (s32[2,64]{1,0:T(2,128)S(1)}, s32[2,64]{1,0:T(2,128)S(1)}, u32[]{:S(2)}, u32[]{:S(2)}) collective-permute-start(s32[2,64]{1,0:T(2,128)S(1)} %pad_add_fusion.2), channel_id=1, source_target_pairs={{0,2},{1,3},{2,0},{3,1},{4,6},{5,7},{6,4},{7,5},{8,10},{9,11},{10,... | collective-permute-start | bytes 1544 | tf_op jit(solution)/shard_map/ppermute | solution.py:18
  7.9 1.5 %collective-permute-done.4 = s32[2,64]{1,0:T(2,128)S(1)} collective-permute-done((s32[2,64]{1,0:T(2,128)S(1)}, s32[2,64]{1,0:T(2,128)S(1)}, u32[]{:S(2)}, u32[]{:S(2)}) %collective-permute-start.4) | collective-permute-done | bytes 544 | tf_op jit(solution)/shard_map/ppermute | solution.py:18
  9.5 3.1 %collective-permute-start.5 = (s32[4,64]{1,0:T(4,128)S(1)}, s32[4,64]{1,0:T(4,128)S(1)}, u32[]{:S(2)}, u32[]{:S(2)}) collective-permute-start(s32[4,64]{1,0:T(4,128)S(1)} %pad_add_fusion.1), channel_id=1, source_target_pairs={{0,4},{1,5},{2,6},{3,7},{4,0},{5,1},{6,2},{7,3},{8,12},{9,13},{10,... | collective-permute-start | bytes 3080 | tf_op jit(solution)/shard_map/ppermute | solution.py:18
  12.6 0.0 collective-permute-start
  12.6 1.6 %collective-permute-start.2 = (bf16[16,768]{1,0:T(8,128)(2,1)}, bf16[16,768]{1,0:T(8,128)(2,1)S(1)}, u32[]{:S(2)}, u32[]{:S(2)}) collective-permute-start(bf16[16,768]{1,0:T(8,128)(2,1)} %new_ref.1), channel_id=1, source_target_pairs={{0,24},{8,16},{16,8},{24,0},{1,25},{9,17},{17,9},{25,1},{2,26},{10... | collective-permute-start | bytes 73736 | tf_op jit(solution)/shard_map/ppermute | solution.py:18
  14.2 0.5 %collective-permute-start.1 = (bf16[16,768]{1,0:T(8,128)(2,1)}, bf16[16,768]{1,0:T(8,128)(2,1)S(1)}, u32[]{:S(2)}, u32[]{:S(2)}) collective-permute-start(bf16[16,768]{1,0:T(8,128)(2,1)} %new_ref.1), channel_id=1, source_target_pairs={{0,16},{8,24},{16,0},{24,8},{1,17},{9,25},{17,1},{25,9},{2,18},{10... | collective-permute-start | bytes 73736 | tf_op jit(solution)/shard_map/ppermute | solution.py:18
  14.7 2.1 %shard_map.67 = (bf16[2048,768]{1,0:T(8,128)(2,1)S(1)}, f32[1,2048]{1,0:T(1,128)S(1)}, bf16[16,768]{1,0:T(8,128)(2,1)S(1)}) custom-call(bf16[2048,768]{1,0:T(8,128)(2,1)} %heads_ref.1, bf16[16,768]{1,0:T(8,128)(2,1)} %new_ref.1), custom_call_target="tpu_custom_call" | custom-call | flops 3145728 | bytes 3145728 | tf_op jit(solution)/shard_map/pallas_call | solution.py:172
  16.8 0.0 copy-start.7
  16.9 0.0 collective-permute-done.5
  16.9 0.0 collective-permute-done.refs_0_.refs_1_
  16.9 0.0 copy-start.1
  16.9 0.0 collective-permute-done.2.refs_2_.refs_3_
  16.9 0.0 copy-start.3
  16.9 1.3 %collective-permute-done.1.refs_1_.refs_2_ = bf16[16,768]{1,0:T(8,128)(2,1)S(1)} collective-permute-done((bf16[16,768]{1,0:T(8,128)(2,1)}, bf16[16,768]{1,0:T(8,128)(2,1)S(1)}, u32[]{:S(2)}, u32[]{:S(2)}) %collective-permute-start.1) | collective-permute-done | bytes 24608 | tf_op jit(solution)/shard_map/ppermute | solution.py:18
  18.3 1.4 %shard_map.68.refs_4_ = bf16[128,768]{1,0:T(8,128)(2,1)} custom-call(s32[8,64]{1,0:T(8,128)S(1)} %pad_add_fusion.ids_ref, bf16[2048,768]{1,0:T(8,128)(2,1)S(1)} %get-tuple-element.8.heads_ref, bf16[16,768]{1,0:T(8,128)(2,1)S(1)} %collective-permute-done.refs_0_.refs_1_, bf16[16,768]{1,0:T(8,128)(2,1)S(1)} %collective-permute-done.1.refs_1_.refs_2_, ...), custom_call_target="tpu_custom_call" | custom-call | flops 402653184 | bytes 3145728 | tf_op jit(solution)/shard_map/pallas_call | solution.py:31
  19.7 0.0 copy-done.7
  19.7 0.6 %copy-done.5 = bf16[16,768]{1,0:T(8,128)(2,1)} copy-done((bf16[16,768]{1,0:T(8,128)(2,1)}, bf16[16,768]{1,0:T(8,128)(2,1)S(1)}, u32[]{:S(2)}) %copy-start.5) | copy-done | bytes 24600
  20.3 0.0 copy-done.3
  20.3 3.8 %all-to-all-start.1 = ((bf16[8,16,768]{2,1,0:T(8,128)(2,1)}), bf16[8,16,768]{2,1,0:T(8,128)(2,1)S(1)}, u32[]{:S(2)}, u32[]{:S(2)}) async-start(bf16[8,16,768]{2,1,0:T(8,128)(2,1)} %bitcast.3), calls=%async_computation.1 | async-start | bytes 393216 | tf_op jit(solution)/shard_map/all_to_all | solution.py:22
  24.1 0.7 %copy-done.2 = bf16[16,768]{1,0:T(8,128)(2,1)S(1)} copy-done((bf16[16,768]{1,0:T(8,128)(2,1)S(1)}, bf16[16,768]{1,0:T(8,128)(2,1)}, u32[]{:S(2)}) %copy-start.2) | copy-done | bytes 24600
  24.8 0.7 %copy-done.4 = bf16[16,768]{1,0:T(8,128)(2,1)S(1)} copy-done((bf16[16,768]{1,0:T(8,128)(2,1)S(1)}, bf16[16,768]{1,0:T(8,128)(2,1)}, u32[]{:S(2)}) %copy-start.4) | copy-done | bytes 24600
  25.6 0.7 %copy-done.6 = bf16[16,768]{1,0:T(8,128)(2,1)S(1)} copy-done((bf16[16,768]{1,0:T(8,128)(2,1)S(1)}, bf16[16,768]{1,0:T(8,128)(2,1)}, u32[]{:S(2)}) %copy-start.6) | copy-done | bytes 24600
  26.3 0.7 %copy-done.8 = bf16[16,768]{1,0:T(8,128)(2,1)S(1)} copy-done((bf16[16,768]{1,0:T(8,128)(2,1)S(1)}, bf16[16,768]{1,0:T(8,128)(2,1)}, u32[]{:S(2)}) %copy-start.8) | copy-done | bytes 24600
  27.0 1.8 %shard_map.69 = f32[32,128]{1,0:T(8,128)} custom-call(bf16[2048,768]{1,0:T(8,128)(2,1)S(1)} %get-tuple-element.8.heads_ref, f32[1,2048]{1,0:T(1,128)S(1)} %get-tuple-element.9.head_sq_ref, bf16[16,768]{1,0:T(8,128)(2,1)S(1)} %copy-done.8, bf16[16,768]{1,0:T(8,128)(2,1)S(1)} %copy-done.2, bf16[16,768]{1,0:T(8,128)(2,1)S(1)} %copy-done.6, ...), custom_call_target="tpu_custom_call" | custom-call | flops 201326592 | bytes 3145728 | tf_op jit(solution)/shard_map/pallas_call | solution.py:31
  28.8 3.0 %all-to-all-done.1 = bf16[8,16,768]{2,1,0:T(8,128)(2,1)S(1)} async-done(((bf16[8,16,768]{2,1,0:T(8,128)(2,1)}), bf16[8,16,768]{2,1,0:T(8,128)(2,1)S(1)}, u32[]{:S(2)}, u32[]{:S(2)}) %all-to-all-start.1) | async-done | bytes 196640 | tf_op jit(solution)/shard_map/all_to_all | solution.py:22
  31.9 2.6 %all-to-all-start = ((f32[32,1,128]{2,1,0:T(1,128)}), f32[32,1,128]{2,1,0:T(1,128)S(1)}, u32[]{:S(2)}, u32[]{:S(2)}) async-start(f32[32,1,128]{2,1,0:T(1,128)} %bitcast.1), calls=%async_computation | async-start | bytes 32768 | tf_op jit(solution)/shard_map/all_to_all | solution.py:22
  34.5 1.1 %shard_map.70.unused = f32[1,64,128]{2,1,0:T(8,128)} custom-call(s32[1,64]{1,0:T(1,128)S(1)} %copy-done.9, bf16[128,768]{1,0:T(8,128)(2,1)S(1)} %bitcast.8, bf16[1,128,768]{2,1,0:T(8,128)(2,1)S(1)} %copy-done), custom_call_target="tpu_custom_call" | custom-call | flops 25165824 | bytes 393216 | tf_op jit(solution)/shard_map/pallas_call | solution.py:31
  35.5 6.0 %all-to-all-done = f32[32,1,128]{2,1,0:T(1,128)S(1)} async-done(((f32[32,1,128]{2,1,0:T(1,128)}), f32[32,1,128]{2,1,0:T(1,128)S(1)}, u32[]{:S(2)}, u32[]{:S(2)}) %all-to-all-start) | async-done | bytes 16416 | tf_op jit(solution)/shard_map/all_to_all | solution.py:22
  41.6 0.7 %shard_map.71 = (f32[1,16]{1,0:T(1,128)}, f32[1,16]{1,0:T(1,128)}) custom-call(f32[32,128]{1,0:T(8,128)S(1)} %bitcast.9, f32[1,64,128]{2,1,0:T(8,128)} %shard_map.70.unused), custom_call_target="tpu_custom_call" | custom-call | flops 4096 | bytes 16384 | tf_op jit(solution)/shard_map/pallas_call | solution.py:31
  (13 shorter events, 0.0 us)
Async XLA Ops:
  1.3 4.5 %collective-permute-start.3 = (s32[1,64]{1,0:T(1,128)S(1)}, s32[1,64]{1,0:T(1,128)S(1)}, u32[]{:S(2)}, u32[]{:S(2)}) collective-permute-start(s32[1,64]{1,0:T(1,128)S(1)} %broadcast_maximum_fusion), channel_id=1, source_target_pairs={{0,1},{1,0},{2,3},{3,2},{4,5},{5,4},{6,7},{7,6},{8,9},{9,8},{10,11... | collective-permute-start | bytes 776 | tf_op jit(solution)/shard_map/ppermute | solution.py:18
  5.8 3.7 %collective-permute-start.4 = (s32[2,64]{1,0:T(2,128)S(1)}, s32[2,64]{1,0:T(2,128)S(1)}, u32[]{:S(2)}, u32[]{:S(2)}) collective-permute-start(s32[2,64]{1,0:T(2,128)S(1)} %pad_add_fusion.2), channel_id=1, source_target_pairs={{0,2},{1,3},{2,0},{3,1},{4,6},{5,7},{6,4},{7,5},{8,10},{9,11},{10,... | collective-permute-start | bytes 1544 | tf_op jit(solution)/shard_map/ppermute | solution.py:18
  9.5 7.4 %collective-permute-start.5 = (s32[4,64]{1,0:T(4,128)S(1)}, s32[4,64]{1,0:T(4,128)S(1)}, u32[]{:S(2)}, u32[]{:S(2)}) collective-permute-start(s32[4,64]{1,0:T(4,128)S(1)} %pad_add_fusion.1), channel_id=1, source_target_pairs={{0,4},{1,5},{2,6},{3,7},{4,0},{5,1},{6,2},{7,3},{8,12},{9,13},{10,... | collective-permute-start | bytes 3080 | tf_op jit(solution)/shard_map/ppermute | solution.py:18
  12.6 4.3 %collective-permute-start = (bf16[16,768]{1,0:T(8,128)(2,1)}, bf16[16,768]{1,0:T(8,128)(2,1)S(1)}, u32[]{:S(2)}, u32[]{:S(2)}) collective-permute-start(bf16[16,768]{1,0:T(8,128)(2,1)} %new_ref.1), channel_id=1, source_target_pairs={{0,8},{8,0},{16,24},{24,16},{1,9},{9,1},{17,25},{25,17},{2,10},{10... | collective-permute-start | bytes 73736 | tf_op jit(solution)/shard_map/ppermute | solution.py:18
  12.6 4.3 %collective-permute-start.2 = (bf16[16,768]{1,0:T(8,128)(2,1)}, bf16[16,768]{1,0:T(8,128)(2,1)S(1)}, u32[]{:S(2)}, u32[]{:S(2)}) collective-permute-start(bf16[16,768]{1,0:T(8,128)(2,1)} %new_ref.1), channel_id=1, source_target_pairs={{0,24},{8,16},{16,8},{24,0},{1,25},{9,17},{17,9},{25,1},{2,26},{10... | collective-permute-start | bytes 73736 | tf_op jit(solution)/shard_map/ppermute | solution.py:18
  14.2 4.0 %collective-permute-start.1 = (bf16[16,768]{1,0:T(8,128)(2,1)}, bf16[16,768]{1,0:T(8,128)(2,1)S(1)}, u32[]{:S(2)}, u32[]{:S(2)}) collective-permute-start(bf16[16,768]{1,0:T(8,128)(2,1)} %new_ref.1), channel_id=1, source_target_pairs={{0,16},{8,24},{16,0},{24,8},{1,17},{9,25},{17,1},{25,9},{2,18},{10... | collective-permute-start | bytes 73736 | tf_op jit(solution)/shard_map/ppermute | solution.py:18
  16.8 2.9 %copy-start.7 = (bf16[16,768]{1,0:T(8,128)(2,1)}, bf16[16,768]{1,0:T(8,128)(2,1)S(1)}, u32[]{:S(2)}) copy-start(bf16[16,768]{1,0:T(8,128)(2,1)S(1)} %get-tuple-element.10.refs_0_) | copy-start | bytes 73732
  16.9 3.4 %copy-start.1 = (bf16[16,768]{1,0:T(8,128)(2,1)}, bf16[16,768]{1,0:T(8,128)(2,1)S(1)}, u32[]{:S(2)}) copy-start(bf16[16,768]{1,0:T(8,128)(2,1)S(1)} %collective-permute-done.refs_0_.refs_1_) | copy-start | bytes 73732
  16.9 3.4 %copy-start.3 = (bf16[16,768]{1,0:T(8,128)(2,1)}, bf16[16,768]{1,0:T(8,128)(2,1)S(1)}, u32[]{:S(2)}) copy-start(bf16[16,768]{1,0:T(8,128)(2,1)S(1)} %collective-permute-done.2.refs_2_.refs_3_) | copy-start | bytes 73732
  18.3 16.2 %copy-start = (bf16[1,128,768]{2,1,0:T(8,128)(2,1)S(1)}, bf16[1,128,768]{2,1,0:T(8,128)(2,1)}, u32[]{:S(2)}) copy-start(bf16[1,128,768]{2,1,0:T(8,128)(2,1)} %vectors_ref.1) | copy-start | bytes 589828
  18.3 16.2 %copy-start.9 = (s32[1,64]{1,0:T(1,128)S(1)}, s32[1,64]{1,0:T(1,128)}, u32[]{:S(2)}) copy-start(s32[1,64]{1,0:T(1,128)} %ids_ref.1) | copy-start | bytes 772
  19.7 0.6 %copy-start.5 = (bf16[16,768]{1,0:T(8,128)(2,1)}, bf16[16,768]{1,0:T(8,128)(2,1)S(1)}, u32[]{:S(2)}) copy-start(bf16[16,768]{1,0:T(8,128)(2,1)S(1)} %collective-permute-done.1.refs_1_.refs_2_) | copy-start | bytes 73732
  20.3 11.6 %all-to-all-start.1 = ((bf16[8,16,768]{2,1,0:T(8,128)(2,1)}), bf16[8,16,768]{2,1,0:T(8,128)(2,1)S(1)}, u32[]{:S(2)}, u32[]{:S(2)}) async-start(bf16[8,16,768]{2,1,0:T(8,128)(2,1)} %bitcast.3), calls=%async_computation.1 | async-start | bytes 393216 | tf_op jit(solution)/shard_map/all_to_all | solution.py:22
  24.1 0.7 %copy-start.2 = (bf16[16,768]{1,0:T(8,128)(2,1)S(1)}, bf16[16,768]{1,0:T(8,128)(2,1)}, u32[]{:S(2)}) copy-start(bf16[16,768]{1,0:T(8,128)(2,1)} %copy-done.1) | copy-start | bytes 73732
  24.8 0.7 %copy-start.4 = (bf16[16,768]{1,0:T(8,128)(2,1)S(1)}, bf16[16,768]{1,0:T(8,128)(2,1)}, u32[]{:S(2)}) copy-start(bf16[16,768]{1,0:T(8,128)(2,1)} %copy-done.3) | copy-start | bytes 73732
  25.6 0.7 %copy-start.6 = (bf16[16,768]{1,0:T(8,128)(2,1)S(1)}, bf16[16,768]{1,0:T(8,128)(2,1)}, u32[]{:S(2)}) copy-start(bf16[16,768]{1,0:T(8,128)(2,1)} %copy-done.5) | copy-start | bytes 73732
  26.3 0.7 %copy-start.8 = (bf16[16,768]{1,0:T(8,128)(2,1)S(1)}, bf16[16,768]{1,0:T(8,128)(2,1)}, u32[]{:S(2)}) copy-start(bf16[16,768]{1,0:T(8,128)(2,1)} %copy-done.7) | copy-start | bytes 73732
  31.9 9.7 %all-to-all-start = ((f32[32,1,128]{2,1,0:T(1,128)}), f32[32,1,128]{2,1,0:T(1,128)S(1)}, u32[]{:S(2)}, u32[]{:S(2)}) async-start(f32[32,1,128]{2,1,0:T(1,128)} %bitcast.1), calls=%async_computation | async-start | bytes 32768 | tf_op jit(solution)/shard_map/all_to_all | solution.py:22

commit v7 on v3

v7 whole, which is shorter than its diff:
```python
import functools

import jax
import jax.numpy as jnp
from jax import lax
from jax.experimental import pallas as pl
from jax.experimental.pallas import tpu as pltpu
from jax.sharding import PartitionSpec as P

VMEM = pltpu.MemorySpace.VMEM
HBM = pltpu.MemorySpace.HBM
LANES = 128
PACK = 16
PARTS = 3
LIMIT = 24 * 2**20


def from_partner(value, axis, mask):
    count = lax.axis_size(axis)
    return lax.ppermute(value, axis, [(source, source ^ mask) for source in range(count)])


def in_hbm(value):
    return pltpu.with_memory_space_constraint(value, HBM)


def call(body, shapes, operands, cost, scratch=(), spaces=None):
    return pl.pallas_call(
        body,
        out_shape=shapes,
        in_specs=[pl.BlockSpec(memory_space=space) for space in spaces or [VMEM] * len(operands)],
        out_specs=jax.tree.map(lambda unused: pl.BlockSpec(memory_space=VMEM), shapes),
        scratch_shapes=scratch,
        compiler_params=pltpu.CompilerParams(vmem_limit_bytes=LIMIT),
        cost_estimate=pl.CostEstimate(flops=cost[0], bytes_accessed=cost[1], transcendentals=0),
    )(*operands)


def iota(shape, dim):
    return lax.broadcasted_iota(jnp.int32, shape, dim)


def early_kernel(
    heads_ref, new_ref, ids_ref, other_ref, kept_ref, head_sq_ref, pair_ref, kept_ids_ref, sems
):
    head_dev, width = heads_ref.shape
    new_count = new_ref.shape[0]
    tiles = 4
    tile = head_dev // tiles
    parts = [pl.ds(i * tile, tile) for i in range(tiles)]
    copies = [
        pltpu.make_async_copy(heads_ref.at[part], kept_ref.at[part], sems.at[i])
        for i, part in enumerate(parts)
    ]
    copies += [
        pltpu.make_async_copy(new_ref, pair_ref.at[pl.ds(0, new_count)], sems.at[tiles]),
        pltpu.make_async_copy(ids_ref, kept_ids_ref, sems.at[tiles + 1]),
    ]
    for copy in copies:
        copy.start()
    pair_ref[new_count:, :] = other_ref[...]
    for i in range(tiles):
        copies[i].wait()
        for first in range(i * tile, (i + 1) * tile, LANES):
            block = jnp.square(kept_ref[first:first + LANES, :].astype(jnp.float32))
            folded = block[:, :LANES]
            for column in range(LANES, width, LANES):
                folded = folded + block[:, column:column + LANES]
            head_sq_ref[:, first:first + LANES] = jnp.sum(folded.T, axis=0, keepdims=True)
    for copy in copies[tiles:]:
        copy.wait()


def listed_rows(ids, me, slots, heads_ref):
    members, near = ids.shape
    head_dev = heads_ref.shape[0]
    local = ids - me * head_dev
    owned = (local >= 0) & (local < head_dev)
    earlier = (iota((near, near), 0) < iota((near, near), 1)).astype(jnp.bfloat16)
    rank = jnp.dot(owned.astype(jnp.bfloat16), earlier, preferred_element_type=jnp.float32)
    rank = jnp.where(owned, rank.astype(jnp.int32), -1)
    shape = (members, slots, near)
    pick = jnp.broadcast_to(rank[:, None, :], shape) == iota(shape, 1)
    wanted = jnp.sum(
        jnp.where(pick, jnp.broadcast_to(local[:, None, :] + 1, shape), 0), axis=2, keepdims=True
    ).reshape(members * slots, 1)
    onehot = (wanted == iota((members * slots, head_dev), 1) + 1).astype(jnp.bfloat16)
    return jnp.dot(
        onehot, heads_ref[...], preferred_element_type=jnp.float32
    ).astype(jnp.bfloat16)


def crowding(queries, heads_ref, head_sq_ref):
    head_dev, width = heads_ref.shape
    query_sq = jnp.sum(jnp.square(queries.astype(jnp.float32)), axis=1, keepdims=True)
    total_w = jnp.zeros((queries.shape[0], 1), jnp.float32)
    total_we = jnp.zeros((queries.shape[0], 1), jnp.float32)
    tile = 512
    for start in range(0, head_dev, tile):
        dots = lax.dot_general(
            queries, heads_ref[start:start + tile, :], (((1,), (1,)), ((), ())),
            preferred_element_type=jnp.float32,
        )
        head_sq = head_sq_ref[:, start:start + tile]
        excess = (query_sq + head_sq - 2.0 * dots) * (1.0 / width)
        inverse = 1.0 / (1.0 + excess)
        weight = inverse * inverse
        total_w = total_w + jnp.sum(weight, axis=1, keepdims=True)
        total_we = total_we + jnp.sum(weight * excess, axis=1, keepdims=True)
    return total_w, total_we


def message_kernel(groups, members, slots, ids_ref, heads_ref, head_sq_ref, *refs):
    query_refs, out_ref = refs[:-1], refs[-1]
    width = heads_ref.shape[1]
    here = lax.axis_index("group")
    me = lax.axis_index("member")
    ids = jnp.concatenate([ids_ref[pl.ds(me ^ member, 1), :] for member in range(members)], axis=0)
    rows = listed_rows(ids, me, slots, heads_ref)
    chunks = width // LANES
    for member in range(members):
        for chunk in range(chunks):
            out_ref[member, chunk * slots:(chunk + 1) * slots, :] = rows[
                member * slots:(member + 1) * slots, chunk * LANES:(chunk + 1) * LANES
            ]

    queries = jnp.concatenate([ref[...] for ref in query_refs], axis=0)
    new_count = queries.shape[0] // groups
    totals = crowding(queries, heads_ref, head_sq_ref)
    lines = 2 * groups * new_count // LANES
    lane = iota((new_count, LANES), 1)
    row = iota((new_count, LANES), 0)
    line = iota((lines, LANES), 0)
    sums = jnp.zeros((lines, LANES), jnp.float32)
    for mask in range(groups):
        part = slice(mask * new_count, (mask + 1) * new_count)
        for kind in range(2):
            place = (kind * groups + (here ^ mask)) * new_count
            spread_out = jnp.where(lane == row + place % LANES, totals[kind][part], 0.0)
            spread_out = jnp.sum(spread_out, axis=0, keepdims=True)
            sums = sums + jnp.where(line == place // LANES, spread_out, 0.0)
    coded = []
    for unused in range(PARTS):
        coded.append(sums.astype(jnp.bfloat16).astype(jnp.float32))
        sums = sums - coded[-1]
    extra = out_ref.shape[1] - chunks * slots
    if extra > PARTS * lines:
        coded.append(jnp.zeros((extra - PARTS * lines, LANES), jnp.float32))
    tail = jnp.concatenate(coded, axis=0).astype(jnp.bfloat16)
    for member in range(members):
        out_ref[member, chunks * slots:, :] = tail


def near_kernel(most, slots, head_dev, ids_ref, listed_ref, vectors_ref, out_ref):
    near = ids_ref.shape[1]
    members = listed_ref.shape[0]
    block, width = vectors_ref.shape[1:]
    square = (near, near)
    owner_row = jnp.broadcast_to(lax.div(ids_ref[...], head_dev), square)
    eye = iota(square, 0) == iota(square, 1)
    owner = jnp.sum(jnp.where(eye, owner_row, 0), axis=1, keepdims=True)
    before = (owner_row == owner) & (iota(square, 1) < iota(square, 0))
    place = jnp.sum(before.astype(jnp.int32), axis=1, keepdims=True)
    source = owner * slots + place
    back = (source == iota((near, members * slots), 1)).astype(jnp.bfloat16)
    rows = []
    for chunk in range(width // LANES):
        part = listed_ref[:, chunk * slots:(chunk + 1) * slots, :].reshape(members * slots, LANES)
        rows.append(jnp.dot(back, part, preferred_element_type=jnp.float32))
    rows = jnp.concatenate(rows, axis=1)
    row_sq = jnp.sum(jnp.square(rows), axis=1, keepdims=True)
    vec = vectors_ref[0]
    vec_sq = jnp.sum(jnp.square(vec.astype(jnp.float32)), axis=1, keepdims=True)
    turned = iota((block, block), 0) == iota((block, block), 1)
    vec_sq = jnp.sum(jnp.where(turned, vec_sq, 0.0), axis=0, keepdims=True)
    dots = lax.dot_general(
        rows.astype(jnp.bfloat16), vec, (((1,), (1,)), ((), ())),
        preferred_element_type=jnp.float32,
    )
    out_ref[0] = (row_sq + vec_sq - 2.0 * dots) * (1.0 / width)


def final_kernel(groups, new_count, total_heads, mine_ref, other_ref, density_ref, spread_ref):
    here = lax.axis_index("group")
    total = mine_ref[...] + other_ref[...]
    lines = total.shape[0]
    shape = (new_count, LANES)
    eye = iota((new_count, new_count), 0) == iota((new_count, new_count), 1)
    found = []
    for kind in range(2):
        place = (kind * groups + here) * new_count
        line = jnp.sum(
            jnp.where(iota((lines, LANES), 0) == place // LANES, total, 0.0), axis=0, keepdims=True
        )
        column = jnp.sum(
            jnp.where(iota(shape, 1) == iota(shape, 0) + place % LANES, line, 0.0),
            axis=1, keepdims=True,
        )
        found.append(jnp.sum(jnp.where(eye, column, 0.0), axis=0, keepdims=True))
    density_ref[...] = jnp.log(found[0] * (1.0 / total_heads))
    spread_ref[...] = found[1] / found[0]


def per_device(heads, new_heads, vectors, near_ids):
    head_dev, width = heads.shape
    new_count = new_heads.shape[0]
    near = near_ids.shape[1]
    groups = lax.axis_size("group")
    members = lax.axis_size("member")
    most = 2 * near // members
    slots = -(-most // PACK) * PACK

    partner_ids = from_partner(near_ids, "member", 1)
    partner_new = from_partner(new_heads, "group", 1)
    kept, head_sq, pair, ids = call(
        early_kernel,
        (
            jax.ShapeDtypeStruct(heads.shape, heads.dtype),
            jax.ShapeDtypeStruct((1, head_dev), jnp.float32),
            jax.ShapeDtypeStruct((2 * new_count, width), new_heads.dtype),
            jax.ShapeDtypeStruct(near_ids.shape, near_ids.dtype),
        ),
        (in_hbm(heads), in_hbm(new_heads), in_hbm(near_ids), partner_new),
        (heads.size * 2, heads.size * 2),
        scratch=[pltpu.SemaphoreType.DMA((6,))],
        spaces=[HBM, HBM, HBM, VMEM],
    )
    ids = jnp.concatenate([ids, partner_ids], axis=0)
    mask = 2
    while mask < members:
        ids = jnp.concatenate([ids, from_partner(ids, "member", mask)], axis=0)
        mask *= 2
    blocks = [pair]
    mask = 2
    while mask < groups:
        blocks.append(from_partner(jnp.concatenate(blocks, axis=0), "group", mask))
        mask *= 2

    lines = 2 * groups * new_count // LANES
    chunks = width // LANES
    extra = -(-PARTS * lines // PACK) * PACK
    message = call(
        functools.partial(message_kernel, groups, members, slots),
        jax.ShapeDtypeStruct((members, chunks * slots + extra, LANES), jnp.bfloat16),
        (ids, kept, head_sq, *blocks),
        (2 * (members * slots + groups * new_count) * head_dev * width, heads.size * 4),
    )
    message = lax.all_to_all(message, "member", 0, 0, tiled=True)

    coded = message[:, chunks * slots:chunks * slots + PARTS * lines, :].astype(jnp.float32)
    total = jnp.sum(coded.reshape(members * PARTS, lines, LANES), axis=0)
    mask = groups // 2
    while mask > 1:
        total = total + from_partner(total, "group", mask)
        mask //= 2
    density, spread = call(
        functools.partial(
            final_kernel, groups, new_count, float(head_dev * groups * members)
        ),
        (jax.ShapeDtypeStruct((1, new_count), jnp.float32),) * 2,
        (total, from_partner(total, "group", 1)),
        (lines * LANES, lines * LANES * 4),
    )
    reassign = call(
        functools.partial(near_kernel, most, slots, head_dev),
        jax.ShapeDtypeStruct((1, near, vectors.shape[1]), jnp.float32),
        (near_ids, message, vectors),
        (4 * near * vectors.shape[1] * width, vectors.size * 4),
    )
    return (density[0], spread[0], reassign)


def solution(mesh):
    placed = (
        P(("group", "member"), None),
        P("group", None),
        P(("group", "member"), None, None),
        P(("group", "member"), None),
    )
    return jax.shard_map(
        per_device,
        mesh=mesh,
        in_specs=placed,
        out_specs=(P("group"), P("group"), P(("group", "member"), None, None)),
        check_vma=False,
    )
```

time: 46.7 us -> 35.4 us (0.76)
  waiting for transfers between devices: 18.7 us -> 6.55 us
  blocking collectives: 0 us -> 11.6 us
  starting transfers between devices: 16.9 us -> 10.5 us
  local copies, waits for them, and re-layouts: 2.64 us -> 0.01 us
  other arithmetic: 2.07 us -> 0.06 us
    all_to_all x2 -> x0, waiting for transfers between devices: 13.1 us -> none  [to_each(): return lax.all_to_all(value, axis, 0, 0, tiled=True)]
    all_to_all x0 -> x1, blocking collectives: none -> 11.6 us  [per_device(): message = lax.all_to_all(message, 'member', 0, 0, tiled=True)]
    all_to_all x2 -> x0, starting transfers between devices: 6.92 us -> none  [to_each(): return lax.all_to_all(value, axis, 0, 0, tiled=True)]
    unnamed x10 -> x4, local copies, waits for them, and re-layouts: 2.64 us -> 0.01 us
    concatenate x3 -> x2, other arithmetic: 2.07 us -> 0.02 us  [per_device(): ids = jnp.concatenate([ids, from_partner(ids, 'member', mask)], axis=0)]
    ppermute x6 -> x7, waiting for transfers between devices: 5.58 us -> 6.55 us  [from_partner(): lax.ppermute(value, axis, [(source, source ^ mask) for source in range(co...]
    ppermute x6 -> x7, starting transfers between devices: 10 us -> 10.5 us  [from_partner(): lax.ppermute(value, axis, [(source, source ^ mask) for source in range(co...]
  transfers between devices with their start and end apart: 8 -> 7, of which waited for: 6 -> 4; matrix products, arithmetic and copies ran while one was open for 2% -> 0% of each run, Pallas kernels for 5% -> 9%
where the time goes in v7:
time: 35.4 us; the launch traced here: 35.1 us
  blocking collectives  11.6 us (33%)
  starting transfers between devices  10.5 us (30%)
  waiting for transfers between devices  6.55 us (19%)
  Pallas kernels  5.7 us (16%)
  between operations  0.69 us (2%)
    all_to_all x1, blocking collectives, per_device(): message = lax.all_to_all(message, 'member', 0, 0, tiled=True)  11.6 us
    ppermute x7, starting transfers between devices, from_partner(): lax.ppermute(value, axis, [(source, source ^ mask) for source in range(co...  10.5 us
    ppermute x7, waiting for transfers between devices, from_partner(): lax.ppermute(value, axis, [(source, source ^ mask) for source in range(co...  6.55 us
    pallas_call x4, Pallas kernels, call(): pl.pallas_call(body, out_shape=shapes, in_specs=[pl.BlockSpec(memory_spac...  5.7 us
  transfers between devices with their start and end apart: 7, of which 4 were waited for; matrix products, arithmetic and copies ran while one was open for 0% of the time, Pallas kernels for 9%

profile of v7, /device:TPU:0, one launch (start us, length us, event | category | flops | bytes accessed | tf_op | source)
XLA Modules:
  0.0 35.1 jit_solution(14887528686270455056)
XLA Ops:
  0.6 0.0 copy-start.1
  0.6 0.0 copy-start
  0.7 0.5 %collective-permute-start = (bf16[16,768]{1,0:T(8,128)(2,1)}, bf16[16,768]{1,0:T(8,128)(2,1)S(1)}, u32[]{:S(2)}, u32[]{:S(2)}) collective-permute-start(bf16[16,768]{1,0:T(8,128)(2,1)} %new_ref.1), channel_id=1, source_target_pairs={{0,8},{8,0},{16,24},{24,16},{1,9},{9,1},{17,25},{25,17},{2,10},{10... | collective-permute-start | bytes 73736 | tf_op jit(solution)/shard_map/ppermute | solution.py:20
  1.2 2.6 %collective-permute-start.1 = (s32[1,64]{1,0:T(1,128)}, s32[1,64]{1,0:T(1,128)S(1)}, u32[]{:S(2)}, u32[]{:S(2)}) collective-permute-start(s32[1,64]{1,0:T(1,128)} %ids_ref.3), channel_id=1, source_target_pairs={{0,1},{1,0},{2,3},{3,2},{4,5},{5,4},{6,7},{7,6},{8,9},{9,8},{10,11... | collective-permute-start | bytes 776 | tf_op jit(solution)/shard_map/ppermute | solution.py:20
  3.7 0.0 collective-permute-done.other_ref
  3.7 2.1 %shard_map.67 = (bf16[2048,768]{1,0:T(8,128)(2,1)S(1)}, f32[1,2048]{1,0:T(1,128)S(1)}, bf16[32,768]{1,0:T(8,128)(2,1)S(1)}, s32[1,64]{1,0:T(1,128)S(1)}) custom-call(bf16[2048,768]{1,0:T(8,128)(2,1)} %heads_ref.1, bf16[16,768]{1,0:T(8,128)(2,1)} %new_ref.1, s32[1,64]{1,0:T(1,128)} %ids_ref.3, bf16[16,768]{1,0:T(8,128)(2,1)S(1)} %collective-permute-done.other_ref), custom_call_target="tpu_custom_call" | custom-call | flops 3145728 | bytes 3145728 | tf_op jit(solution)/shard_map/pallas_call | solution.py:28
  5.9 0.0 collective-permute-done.1
  5.9 1.7 %collective-permute-start.2 = (s32[2,64]{1,0:T(2,128)S(1)}, s32[2,64]{1,0:T(2,128)S(1)}, u32[]{:S(2)}, u32[]{:S(2)}) collective-permute-start(s32[2,64]{1,0:T(2,128)S(1)} %pad_add_fusion.2), channel_id=1, source_target_pairs={{0,2},{1,3},{2,0},{3,1},{4,6},{5,7},{6,4},{7,5},{8,10},{9,11},{10,... | collective-permute-start | bytes 1544 | tf_op jit(solution)/shard_map/ppermute | solution.py:20
  7.6 2.0 %collective-permute-done.2 = s32[2,64]{1,0:T(2,128)S(1)} collective-permute-done((s32[2,64]{1,0:T(2,128)S(1)}, s32[2,64]{1,0:T(2,128)S(1)}, u32[]{:S(2)}, u32[]{:S(2)}) %collective-permute-start.2) | collective-permute-done | bytes 544 | tf_op jit(solution)/shard_map/ppermute | solution.py:20
  9.5 2.7 %collective-permute-start.3 = (s32[4,64]{1,0:T(4,128)S(1)}, s32[4,64]{1,0:T(4,128)S(1)}, u32[]{:S(2)}, u32[]{:S(2)}) collective-permute-start(s32[4,64]{1,0:T(4,128)S(1)} %pad_add_fusion.1), channel_id=1, source_target_pairs={{0,4},{1,5},{2,6},{3,7},{4,0},{5,1},{6,2},{7,3},{8,12},{9,13},{10,... | collective-permute-start | bytes 3080 | tf_op jit(solution)/shard_map/ppermute | solution.py:20
  12.2 1.5 %collective-permute-start.4 = (bf16[32,768]{1,0:T(8,128)(2,1)S(1)}, bf16[32,768]{1,0:T(8,128)(2,1)S(1)}, u32[]{:S(2)}, u32[]{:S(2)}) collective-permute-start(bf16[32,768]{1,0:T(8,128)(2,1)S(1)} %get-tuple-element.12.refs_0_), channel_id=1, source_target_pairs={{0,16},{8,24},{16,0},{24,8},{1,17},{9,25},{17,1},{25,9},{2,18},{10... | collective-permute-start | bytes 147464 | tf_op jit(solution)/shard_map/ppermute | solution.py:20
  13.7 0.3 collective-permute-done.3
  14.1 2.2 %collective-permute-done.4.refs_1_ = bf16[32,768]{1,0:T(8,128)(2,1)S(1)} collective-permute-done((bf16[32,768]{1,0:T(8,128)(2,1)S(1)}, bf16[32,768]{1,0:T(8,128)(2,1)S(1)}, u32[]{:S(2)}, u32[]{:S(2)}) %collective-permute-start.4) | collective-permute-done | bytes 49184 | tf_op jit(solution)/shard_map/ppermute | solution.py:20
  16.3 1.8 %shard_map.68 = bf16[8,112,128]{2,1,0:T(8,128)(2,1)S(1)} custom-call(s32[8,64]{1,0:T(8,128)S(1)} %pad_add_fusion.ids_ref, bf16[2048,768]{1,0:T(8,128)(2,1)S(1)} %get-tuple-element.10.heads_ref, f32[1,2048]{1,0:T(1,128)S(1)} %get-tuple-element.11.head_sq_ref, bf16[32,768]{1,0:T(8,128)(2,1)S(1)} %get-tuple-element.12.refs_0_, ...), custom_call_target="tpu_custom_call" | custom-call | flops 603979776 | bytes 6291456 | tf_op jit(solution)/shard_map/pallas_call | solution.py:28
  18.2 11.6 %all_to_all.5.listed_ref = bf16[8,112,128]{2,1,0:T(8,128)(2,1)S(1)} all-to-all(bf16[8,112,128]{2,1,0:T(8,128)(2,1)S(1)} %shard_map.68), channel_id=1, replica_groups=mesh['group'=4,'member'=8] {'member'}, dimensions={0} | all-to-all | bytes 458752 | tf_op jit(solution)/shard_map/all_to_all | solution.py:248
  29.8 1.6 %collective-permute-start.5 = (f32[1,128]{1,0:T(1,128)S(1)}, f32[1,128]{1,0:T(1,128)S(1)}, u32[]{:S(2)}, u32[]{:S(2)}) collective-permute-start(f32[1,128]{1,0:T(1,128)S(1)} %bitcast.4), channel_id=1, source_target_pairs={{0,16},{8,24},{16,0},{24,8},{1,17},{9,25},{17,1},{25,9},{2,18},{10... | collective-permute-start | bytes 1544 | tf_op jit(solution)/shard_map/ppermute | solution.py:20
  31.3 2.0 %collective-permute-done.5 = f32[1,128]{1,0:T(1,128)S(1)} collective-permute-done((f32[1,128]{1,0:T(1,128)S(1)}, f32[1,128]{1,0:T(1,128)S(1)}, u32[]{:S(2)}, u32[]{:S(2)}) %collective-permute-start.5) | collective-permute-done | bytes 544 | tf_op jit(solution)/shard_map/ppermute | solution.py:20
  33.4 0.0 collective-permute-start.6
  33.4 0.0 copy-done.1
  33.4 0.0 copy-done
  33.4 1.1 %shard_map.70 = f32[1,64,128]{2,1,0:T(8,128)} custom-call(s32[1,64]{1,0:T(1,128)S(1)} %copy-done.1, bf16[8,112,128]{2,1,0:T(8,128)(2,1)S(1)} %all_to_all.5.listed_ref, bf16[1,128,768]{2,1,0:T(8,128)(2,1)S(1)} %copy-done), custom_call_target="tpu_custom_call" | custom-call | flops 25165824 | bytes 393216 | tf_op jit(solution)/shard_map/pallas_call | solution.py:28
  34.5 0.0 collective-permute-done.6.other_ref
  34.5 0.6 %shard_map.69 = (f32[1,16]{1,0:T(1,128)}, f32[1,16]{1,0:T(1,128)}) custom-call(f32[1,128]{1,0:T(1,128)S(1)} %bitcast_add_fusion.mine_ref, f32[1,128]{1,0:T(1,128)S(1)} %collective-permute-done.6.other_ref), custom_call_target="tpu_custom_call" | custom-call | flops 128 | bytes 512 | tf_op jit(solution)/shard_map/pallas_call | solution.py:28
  (5 shorter events, 0.1 us)
Async XLA Ops:
  0.6 32.7 %copy-start.1 = (s32[1,64]{1,0:T(1,128)S(1)}, s32[1,64]{1,0:T(1,128)}, u32[]{:S(2)}) copy-start(s32[1,64]{1,0:T(1,128)} %ids_ref.3) | copy-start | bytes 772
  0.6 32.7 %copy-start = (bf16[1,128,768]{2,1,0:T(8,128)(2,1)S(1)}, bf16[1,128,768]{2,1,0:T(8,128)(2,1)}, u32[]{:S(2)}) copy-start(bf16[1,128,768]{2,1,0:T(8,128)(2,1)} %vectors_ref.1) | copy-start | bytes 589828
  0.7 3.1 %collective-permute-start = (bf16[16,768]{1,0:T(8,128)(2,1)}, bf16[16,768]{1,0:T(8,128)(2,1)S(1)}, u32[]{:S(2)}, u32[]{:S(2)}) collective-permute-start(bf16[16,768]{1,0:T(8,128)(2,1)} %new_ref.1), channel_id=1, source_target_pairs={{0,8},{8,0},{16,24},{24,16},{1,9},{9,1},{17,25},{25,17},{2,10},{10... | collective-permute-start | bytes 73736 | tf_op jit(solution)/shard_map/ppermute | solution.py:20
  1.2 4.7 %collective-permute-start.1 = (s32[1,64]{1,0:T(1,128)}, s32[1,64]{1,0:T(1,128)S(1)}, u32[]{:S(2)}, u32[]{:S(2)}) collective-permute-start(s32[1,64]{1,0:T(1,128)} %ids_ref.3), channel_id=1, source_target_pairs={{0,1},{1,0},{2,3},{3,2},{4,5},{5,4},{6,7},{7,6},{8,9},{9,8},{10,11... | collective-permute-start | bytes 776 | tf_op jit(solution)/shard_map/ppermute | solution.py:20
  5.9 3.6 %collective-permute-start.2 = (s32[2,64]{1,0:T(2,128)S(1)}, s32[2,64]{1,0:T(2,128)S(1)}, u32[]{:S(2)}, u32[]{:S(2)}) collective-permute-start(s32[2,64]{1,0:T(2,128)S(1)} %pad_add_fusion.2), channel_id=1, source_target_pairs={{0,2},{1,3},{2,0},{3,1},{4,6},{5,7},{6,4},{7,5},{8,10},{9,11},{10,... | collective-permute-start | bytes 1544 | tf_op jit(solution)/shard_map/ppermute | solution.py:20
  9.5 4.5 %collective-permute-start.3 = (s32[4,64]{1,0:T(4,128)S(1)}, s32[4,64]{1,0:T(4,128)S(1)}, u32[]{:S(2)}, u32[]{:S(2)}) collective-permute-start(s32[4,64]{1,0:T(4,128)S(1)} %pad_add_fusion.1), channel_id=1, source_target_pairs={{0,4},{1,5},{2,6},{3,7},{4,0},{5,1},{6,2},{7,3},{8,12},{9,13},{10,... | collective-permute-start | bytes 3080 | tf_op jit(solution)/shard_map/ppermute | solution.py:20
  12.2 4.1 %collective-permute-start.4 = (bf16[32,768]{1,0:T(8,128)(2,1)S(1)}, bf16[32,768]{1,0:T(8,128)(2,1)S(1)}, u32[]{:S(2)}, u32[]{:S(2)}) collective-permute-start(bf16[32,768]{1,0:T(8,128)(2,1)S(1)} %get-tuple-element.12.refs_0_), channel_id=1, source_target_pairs={{0,16},{8,24},{16,0},{24,8},{1,17},{9,25},{17,1},{25,9},{2,18},{10... | collective-permute-start | bytes 147464 | tf_op jit(solution)/shard_map/ppermute | solution.py:20
  29.8 3.6 %collective-permute-start.5 = (f32[1,128]{1,0:T(1,128)S(1)}, f32[1,128]{1,0:T(1,128)S(1)}, u32[]{:S(2)}, u32[]{:S(2)}) collective-permute-start(f32[1,128]{1,0:T(1,128)S(1)} %bitcast.4), channel_id=1, source_target_pairs={{0,16},{8,24},{16,0},{24,8},{1,17},{9,25},{17,1},{25,9},{2,18},{10... | collective-permute-start | bytes 1544 | tf_op jit(solution)/shard_map/ppermute | solution.py:20
  33.4 1.1 %collective-permute-start.6 = (f32[1,128]{1,0:T(1,128)S(1)}, f32[1,128]{1,0:T(1,128)S(1)}, u32[]{:S(2)}, u32[]{:S(2)}) collective-permute-start(f32[1,128]{1,0:T(1,128)S(1)} %bitcast_add_fusion.mine_ref), channel_id=1, source_target_pairs={{0,8},{8,0},{16,24},{24,16},{1,9},{9,1},{17,25},{25,17},{2,10},{10... | collective-permute-start | bytes 1544 | tf_op jit(solution)/shard_map/ppermute | solution.py:20

commit v8 on v7

--- a/solution.py
+++ b/solution.py
@@ -110,28 +110,16 @@
     return total_w, total_we
 
 
-def message_kernel(groups, members, slots, ids_ref, heads_ref, head_sq_ref, *refs):
-    query_refs, out_ref = refs[:-1], refs[-1]
-    width = heads_ref.shape[1]
+def crowd_kernel(groups, heads_ref, head_sq_ref, *refs):
+    query_refs, sums_ref = refs[:-1], refs[-1]
     here = lax.axis_index("group")
-    me = lax.axis_index("member")
-    ids = jnp.concatenate([ids_ref[pl.ds(me ^ member, 1), :] for member in range(members)], axis=0)
-    rows = listed_rows(ids, me, slots, heads_ref)
-    chunks = width // LANES
-    for member in range(members):
-        for chunk in range(chunks):
-            out_ref[member, chunk * slots:(chunk + 1) * slots, :] = rows[
-                member * slots:(member + 1) * slots, chunk * LANES:(chunk + 1) * LANES
-            ]
-
     queries = jnp.concatenate([ref[...] for ref in query_refs], axis=0)
     new_count = queries.shape[0] // groups
     totals = crowding(queries, heads_ref, head_sq_ref)
-    lines = 2 * groups * new_count // LANES
     lane = iota((new_count, LANES), 1)
     row = iota((new_count, LANES), 0)
-    line = iota((lines, LANES), 0)
-    sums = jnp.zeros((lines, LANES), jnp.float32)
+    line = iota(sums_ref.shape, 0)
+    sums = jnp.zeros(sums_ref.shape, jnp.float32)
     for mask in range(groups):
         part = slice(mask * new_count, (mask + 1) * new_count)
         for kind in range(2):
@@ -139,19 +127,36 @@
             spread_out = jnp.where(lane == row + place % LANES, totals[kind][part], 0.0)
             spread_out = jnp.sum(spread_out, axis=0, keepdims=True)
             sums = sums + jnp.where(line == place // LANES, spread_out, 0.0)
+    sums_ref[...] = sums
+
+
+def gather_kernel(members, slots, ids_ref, heads_ref, unused, rows_ref):
+    me = lax.axis_index("member")
+    ids = jnp.concatenate([ids_ref[pl.ds(me ^ member, 1), :] for member in range(members)], axis=0)
+    rows_ref[...] = listed_rows(ids, me, slots, heads_ref)
+
+
+def pack_kernel(members, slots, rows_ref, mine_ref, other_ref, out_ref):
+    chunks = rows_ref.shape[1] // LANES
+    for member in range(members):
+        for chunk in range(chunks):
+            out_ref[member, chunk * slots:(chunk + 1) * slots, :] = rows_ref[
+                member * slots:(member + 1) * slots, chunk * LANES:(chunk + 1) * LANES
+            ]
+    sums = mine_ref[...] + other_ref[...]
     coded = []
     for unused in range(PARTS):
         coded.append(sums.astype(jnp.bfloat16).astype(jnp.float32))
         sums = sums - coded[-1]
-    extra = out_ref.shape[1] - chunks * slots
-    if extra > PARTS * lines:
-        coded.append(jnp.zeros((extra - PARTS * lines, LANES), jnp.float32))
+    missing = out_ref.shape[1] - chunks * slots - PARTS * sums.shape[0]
+    if missing:
+        coded.append(jnp.zeros((missing, LANES), jnp.float32))
     tail = jnp.concatenate(coded, axis=0).astype(jnp.bfloat16)
     for member in range(members):
         out_ref[member, chunks * slots:, :] = tail
 
 
-def near_kernel(most, slots, head_dev, ids_ref, listed_ref, vectors_ref, out_ref):
+def distances(slots, head_dev, ids_ref, listed_ref, vectors_ref, out_ref):
     near = ids_ref.shape[1]
     members = listed_ref.shape[0]
     block, width = vectors_ref.shape[1:]
@@ -180,10 +185,18 @@
     out_ref[0] = (row_sq + vec_sq - 2.0 * dots) * (1.0 / width)
 
 
-def final_kernel(groups, new_count, total_heads, mine_ref, other_ref, density_ref, spread_ref):
+def tail_kernel(
+    groups, slots, head_dev, total_heads, ids_ref, listed_ref, vectors_ref,
+    density_ref, spread_ref, out_ref,
+):
+    distances(slots, head_dev, ids_ref, listed_ref, vectors_ref, out_ref)
     here = lax.axis_index("group")
-    total = mine_ref[...] + other_ref[...]
-    lines = total.shape[0]
+    members = listed_ref.shape[0]
+    new_count = density_ref.shape[1]
+    lines = 2 * groups * new_count // LANES
+    first = vectors_ref.shape[2] // LANES * slots
+    coded = jnp.sum(listed_ref[:, first:, :].astype(jnp.float32), axis=0)
+    total = sum(coded[part * lines:(part + 1) * lines] for part in range(PARTS))
     shape = (new_count, LANES)
     eye = iota((new_count, new_count), 0) == iota((new_count, new_count), 1)
     found = []
@@ -239,31 +252,40 @@
     lines = 2 * groups * new_count // LANES
     chunks = width // LANES
     extra = -(-PARTS * lines // PACK) * PACK
+    sums = call(
+        functools.partial(crowd_kernel, groups),
+        jax.ShapeDtypeStruct((lines, LANES), jnp.float32),
+        (kept, head_sq, *blocks),
+        (2 * groups * new_count * head_dev * width, heads.size * 2),
+    )
+    mask = 1
+    while mask < groups // 2:
+        sums = sums + from_partner(sums, "group", mask)
+        mask *= 2
+    rows = call(
+        functools.partial(gather_kernel, members, slots),
+        jax.ShapeDtypeStruct((members * slots, width), jnp.bfloat16),
+        (ids, kept, sums),
+        (2 * members * slots * head_dev * width, heads.size * 2),
+        spaces=[VMEM, VMEM, pl.ANY],
+    )
     message = call(
-        functools.partial(message_kernel, groups, members, slots),
+        functools.partial(pack_kernel, members, slots),
         jax.ShapeDtypeStruct((members, chunks * slots + extra, LANES), jnp.bfloat16),
-        (ids, kept, head_sq, *blocks),
-        (2 * (members * slots + groups * new_count) * head_dev * width, heads.size * 4),
+        (rows, sums, from_partner(sums, "group", mask)),
+        (0, members * slots * width * 4),
     )
     message = lax.all_to_all(message, "member", 0, 0, tiled=True)
 
-    coded = message[:, chunks * slots:chunks * slots + PARTS * lines, :].astype(jnp.float32)
-    total = jnp.sum(coded.reshape(members * PARTS, lines, LANES), axis=0)
-    mask = groups // 2
-    while mask > 1:
-        total = total + from_partner(total, "group", mask)
-        mask //= 2
-    density, spread = call(
+    density, spread, reassign = call(
         functools.partial(
-            final_kernel, groups, new_count, float(head_dev * groups * members)
+            tail_kernel, groups, slots, head_dev, float(head_dev * groups * members)
         ),
-        (jax.ShapeDtypeStruct((1, new_count), jnp.float32),) * 2,
-        (total, from_partner(total, "group", 1)),
-        (lines * LANES, lines * LANES * 4),
-    )
-    reassign = call(
-        functools.partial(near_kernel, most, slots, head_dev),
-        jax.ShapeDtypeStruct((1, near, vectors.shape[1]), jnp.float32),
+        (
+            jax.ShapeDtypeStruct((1, new_count), jnp.float32),
+            jax.ShapeDtypeStruct((1, new_count), jnp.float32),
+            jax.ShapeDtypeStruct((1, near, vectors.shape[1]), jnp.float32),
+        ),
         (near_ids, message, vectors),
         (4 * near * vectors.shape[1] * width, vectors.size * 4),
     )

time: 35.4 us -> 32.7 us (0.924)
  waiting for transfers between devices: 6.55 us -> 2.77 us
  blocking collectives: 11.6 us -> 13.2 us
  Pallas kernels: 5.7 us -> 5.29 us
    ppermute x7, waiting for transfers between devices: 6.55 us -> 2.77 us  [from_partner(): lax.ppermute(value, axis, [(source, source ^ mask) for source in range(co...]
    all_to_all x1, blocking collectives: 11.6 us -> 13.2 us  [per_device(): message = lax.all_to_all(message, 'member', 0, 0, tiled=True)]
    pallas_call x4 -> x5, Pallas kernels: 5.7 us -> 5.29 us  [call(): pl.pallas_call(body, out_shape=shapes, in_specs=[pl.BlockSpec(memory_spac...]
  transfers between devices with their start and end apart: 7 -> 7, of which waited for: 4 -> 4; matrix products, arithmetic and copies ran while one was open for 0% -> 0% of each run, Pallas kernels for 9% -> 13%
where the time goes in v8:
time: 32.7 us; the launch traced here: 32.5 us
  blocking collectives  13.2 us (40%)
  starting transfers between devices  10.5 us (32%)
  Pallas kernels  5.29 us (16%)
  waiting for transfers between devices  2.77 us (8%)
  between operations  0.68 us (2%)
    all_to_all x1, blocking collectives, per_device(): message = lax.all_to_all(message, 'member', 0, 0, tiled=True)  13.2 us
    ppermute x7, starting transfers between devices, from_partner(): lax.ppermute(value, axis, [(source, source ^ mask) for source in range(co...  10.5 us
    pallas_call x5, Pallas kernels, call(): pl.pallas_call(body, out_shape=shapes, in_specs=[pl.BlockSpec(memory_spac...  5.29 us
    ppermute x7, waiting for transfers between devices, from_partner(): lax.ppermute(value, axis, [(source, source ^ mask) for source in range(co...  2.77 us
  transfers between devices with their start and end apart: 7, of which 4 were waited for; matrix products, arithmetic and copies ran while one was open for 0% of the time, Pallas kernels for 13%

profile of v8, /device:TPU:0, one launch (start us, length us, event | category | flops | bytes accessed | tf_op | source)
XLA Modules:
  0.0 32.5 jit_solution(13425605089949824847)
XLA Ops:
  0.6 0.5 %collective-permute-start = (bf16[16,768]{1,0:T(8,128)(2,1)}, bf16[16,768]{1,0:T(8,128)(2,1)S(1)}, u32[]{:S(2)}, u32[]{:S(2)}) collective-permute-start(bf16[16,768]{1,0:T(8,128)(2,1)} %new_ref.1), channel_id=1, source_target_pairs={{0,8},{8,0},{16,24},{24,16},{1,9},{9,1},{17,25},{25,17},{2,10},{10... | collective-permute-start | bytes 73736 | tf_op jit(solution)/shard_map/ppermute | solution.py:20
  1.1 2.6 %collective-permute-start.1 = (s32[1,64]{1,0:T(1,128)}, s32[1,64]{1,0:T(1,128)S(1)}, u32[]{:S(2)}, u32[]{:S(2)}) collective-permute-start(s32[1,64]{1,0:T(1,128)} %ids_ref.3), channel_id=1, source_target_pairs={{0,1},{1,0},{2,3},{3,2},{4,5},{5,4},{6,7},{7,6},{8,9},{9,8},{10,11... | collective-permute-start | bytes 776 | tf_op jit(solution)/shard_map/ppermute | solution.py:20
  3.7 0.0 collective-permute-done.other_ref
  3.7 2.1 %shard_map.67 = (bf16[2048,768]{1,0:T(8,128)(2,1)S(1)}, f32[1,2048]{1,0:T(1,128)S(1)}, bf16[32,768]{1,0:T(8,128)(2,1)S(1)}, s32[1,64]{1,0:T(1,128)S(1)}) custom-call(bf16[2048,768]{1,0:T(8,128)(2,1)} %heads_ref.1, bf16[16,768]{1,0:T(8,128)(2,1)} %new_ref.1, s32[1,64]{1,0:T(1,128)} %ids_ref.3, bf16[16,768]{1,0:T(8,128)(2,1)S(1)} %collective-permute-done.other_ref), custom_call_target="tpu_custom_call" | custom-call | flops 3145728 | bytes 3145728 | tf_op jit(solution)/shard_map/pallas_call | solution.py:28
  5.8 0.0 collective-permute-done.1
  5.9 1.7 %collective-permute-start.2 = (s32[2,64]{1,0:T(2,128)S(1)}, s32[2,64]{1,0:T(2,128)S(1)}, u32[]{:S(2)}, u32[]{:S(2)}) collective-permute-start(s32[2,64]{1,0:T(2,128)S(1)} %pad_add_fusion.2), channel_id=1, source_target_pairs={{0,2},{1,3},{2,0},{3,1},{4,6},{5,7},{6,4},{7,5},{8,10},{9,11},{10,... | collective-permute-start | bytes 1544 | tf_op jit(solution)/shard_map/ppermute | solution.py:20
  7.5 1.5 %collective-permute-start.4 = (bf16[32,768]{1,0:T(8,128)(2,1)S(1)}, bf16[32,768]{1,0:T(8,128)(2,1)S(1)}, u32[]{:S(2)}, u32[]{:S(2)}) collective-permute-start(bf16[32,768]{1,0:T(8,128)(2,1)S(1)} %get-tuple-element.13.refs_0_), channel_id=1, source_target_pairs={{0,16},{8,24},{16,0},{24,8},{1,17},{9,25},{17,1},{25,9},{2,18},{10... | collective-permute-start | bytes 147464 | tf_op jit(solution)/shard_map/ppermute | solution.py:20
  9.1 0.4 %collective-permute-done.2 = s32[2,64]{1,0:T(2,128)S(1)} collective-permute-done((s32[2,64]{1,0:T(2,128)S(1)}, s32[2,64]{1,0:T(2,128)S(1)}, u32[]{:S(2)}, u32[]{:S(2)}) %collective-permute-start.2) | collective-permute-done | bytes 544 | tf_op jit(solution)/shard_map/ppermute | solution.py:20
  9.5 2.7 %collective-permute-start.3 = (s32[4,64]{1,0:T(4,128)S(1)}, s32[4,64]{1,0:T(4,128)S(1)}, u32[]{:S(2)}, u32[]{:S(2)}) collective-permute-start(s32[4,64]{1,0:T(4,128)S(1)} %pad_add_fusion.1), channel_id=1, source_target_pairs={{0,4},{1,5},{2,6},{3,7},{4,0},{5,1},{6,2},{7,3},{8,12},{9,13},{10,... | collective-permute-start | bytes 3080 | tf_op jit(solution)/shard_map/ppermute | solution.py:20
  12.2 0.0 collective-permute-done.4.refs_1_
  12.2 0.0 copy-start
  12.2 0.0 copy-start.1
  12.2 1.2 %shard_map.68 = f32[1,128]{1,0:T(1,128)S(1)} custom-call(bf16[2048,768]{1,0:T(8,128)(2,1)S(1)} %get-tuple-element.11.heads_ref, f32[1,2048]{1,0:T(1,128)S(1)} %get-tuple-element.12.head_sq_ref, bf16[32,768]{1,0:T(8,128)(2,1)S(1)} %get-tuple-element.13.refs_0_, bf16[32,768]{1,0:T(8,128)(2,1)S(1)} %collective-permute-done.4.refs_1_), custom_call_target="tpu_custom_call" | custom-call | flops 201326592 | bytes 3145728 | tf_op jit(solution)/shard_map/pallas_call | solution.py:28
  13.4 0.1 collective-permute-start.5
  13.5 0.6 %collective-permute-done.3 = s32[4,64]{1,0:T(4,128)S(1)} collective-permute-done((s32[4,64]{1,0:T(4,128)S(1)}, s32[4,64]{1,0:T(4,128)S(1)}, u32[]{:S(2)}, u32[]{:S(2)}) %collective-permute-start.3) | collective-permute-done | bytes 1056 | tf_op jit(solution)/shard_map/ppermute | solution.py:20
  14.1 0.5 %collective-permute-done.5 = f32[1,128]{1,0:T(1,128)S(1)} collective-permute-done((f32[1,128]{1,0:T(1,128)S(1)}, f32[1,128]{1,0:T(1,128)S(1)}, u32[]{:S(2)}, u32[]{:S(2)}) %collective-permute-start.5) | collective-permute-done | bytes 544 | tf_op jit(solution)/shard_map/ppermute | solution.py:20
  14.6 1.5 %collective-permute-start.6 = (f32[1,128]{1,0:T(1,128)S(1)}, f32[1,128]{1,0:T(1,128)S(1)}, u32[]{:S(2)}, u32[]{:S(2)}) collective-permute-start(f32[1,128]{1,0:T(1,128)S(1)} %add.3.unused.mine_ref), channel_id=1, source_target_pairs={{0,16},{8,24},{16,0},{24,8},{1,17},{9,25},{17,1},{25,9},{2,18},{10... | collective-permute-start | bytes 1544 | tf_op jit(solution)/shard_map/ppermute | solution.py:20
  16.1 0.8 %shard_map.69.rows_ref = bf16[128,768]{1,0:T(8,128)(2,1)S(1)} custom-call(s32[8,64]{1,0:T(8,128)S(1)} %pad_add_fusion.ids_ref, bf16[2048,768]{1,0:T(8,128)(2,1)S(1)} %get-tuple-element.11.heads_ref, f32[1,128]{1,0:T(1,128)S(1)} %add.3.unused.mine_ref), custom_call_target="tpu_custom_call" | custom-call | flops 402653184 | bytes 3145728 | tf_op jit(solution)/shard_map/pallas_call | solution.py:28
  16.9 1.2 %collective-permute-done.6.other_ref = f32[1,128]{1,0:T(1,128)S(1)} collective-permute-done((f32[1,128]{1,0:T(1,128)S(1)}, f32[1,128]{1,0:T(1,128)S(1)}, u32[]{:S(2)}, u32[]{:S(2)}) %collective-permute-start.6) | collective-permute-done | bytes 544 | tf_op jit(solution)/shard_map/ppermute | solution.py:20
  18.2 13.2 %all_to_all.5.listed_ref = bf16[8,112,128]{2,1,0:T(8,128)(2,1)S(1)} all-to-all(bf16[8,112,128]{2,1,0:T(8,128)(2,1)S(1)} %shard_map.70), channel_id=1, replica_groups=mesh['group'=4,'member'=8] {'member'}, dimensions={0} | all-to-all | bytes 458752 | tf_op jit(solution)/shard_map/all_to_all | solution.py:278
  31.4 0.0 copy-done
  31.4 0.0 copy-done.1
  31.4 1.1 %shard_map.71 = (f32[1,16]{1,0:T(1,128)}, f32[1,16]{1,0:T(1,128)}, f32[1,64,128]{2,1,0:T(8,128)}) custom-call(s32[1,64]{1,0:T(1,128)S(1)} %copy-done.1, bf16[8,112,128]{2,1,0:T(8,128)(2,1)S(1)} %all_to_all.5.listed_ref, bf16[1,128,768]{2,1,0:T(8,128)(2,1)S(1)} %copy-done), custom_call_target="tpu_custom_call" | custom-call | flops 25165824 | bytes 393216 | tf_op jit(solution)/shard_map/pallas_call | solution.py:28
  (5 shorter events, 0.1 us)
Async XLA Ops:
  0.6 3.1 %collective-permute-start = (bf16[16,768]{1,0:T(8,128)(2,1)}, bf16[16,768]{1,0:T(8,128)(2,1)S(1)}, u32[]{:S(2)}, u32[]{:S(2)}) collective-permute-start(bf16[16,768]{1,0:T(8,128)(2,1)} %new_ref.1), channel_id=1, source_target_pairs={{0,8},{8,0},{16,24},{24,16},{1,9},{9,1},{17,25},{25,17},{2,10},{10... | collective-permute-start | bytes 73736 | tf_op jit(solution)/shard_map/ppermute | solution.py:20
  1.1 4.7 %collective-permute-start.1 = (s32[1,64]{1,0:T(1,128)}, s32[1,64]{1,0:T(1,128)S(1)}, u32[]{:S(2)}, u32[]{:S(2)}) collective-permute-start(s32[1,64]{1,0:T(1,128)} %ids_ref.3), channel_id=1, source_target_pairs={{0,1},{1,0},{2,3},{3,2},{4,5},{5,4},{6,7},{7,6},{8,9},{9,8},{10,11... | collective-permute-start | bytes 776 | tf_op jit(solution)/shard_map/ppermute | solution.py:20
  5.9 3.6 %collective-permute-start.2 = (s32[2,64]{1,0:T(2,128)S(1)}, s32[2,64]{1,0:T(2,128)S(1)}, u32[]{:S(2)}, u32[]{:S(2)}) collective-permute-start(s32[2,64]{1,0:T(2,128)S(1)} %pad_add_fusion.2), channel_id=1, source_target_pairs={{0,2},{1,3},{2,0},{3,1},{4,6},{5,7},{6,4},{7,5},{8,10},{9,11},{10,... | collective-permute-start | bytes 1544 | tf_op jit(solution)/shard_map/ppermute | solution.py:20
  7.5 4.7 %collective-permute-start.4 = (bf16[32,768]{1,0:T(8,128)(2,1)S(1)}, bf16[32,768]{1,0:T(8,128)(2,1)S(1)}, u32[]{:S(2)}, u32[]{:S(2)}) collective-permute-start(bf16[32,768]{1,0:T(8,128)(2,1)S(1)} %get-tuple-element.13.refs_0_), channel_id=1, source_target_pairs={{0,16},{8,24},{16,0},{24,8},{1,17},{9,25},{17,1},{25,9},{2,18},{10... | collective-permute-start | bytes 147464 | tf_op jit(solution)/shard_map/ppermute | solution.py:20
  9.5 4.5 %collective-permute-start.3 = (s32[4,64]{1,0:T(4,128)S(1)}, s32[4,64]{1,0:T(4,128)S(1)}, u32[]{:S(2)}, u32[]{:S(2)}) collective-permute-start(s32[4,64]{1,0:T(4,128)S(1)} %pad_add_fusion.1), channel_id=1, source_target_pairs={{0,4},{1,5},{2,6},{3,7},{4,0},{5,1},{6,2},{7,3},{8,12},{9,13},{10,... | collective-permute-start | bytes 3080 | tf_op jit(solution)/shard_map/ppermute | solution.py:20
  12.2 19.2 %copy-start = (bf16[1,128,768]{2,1,0:T(8,128)(2,1)S(1)}, bf16[1,128,768]{2,1,0:T(8,128)(2,1)}, u32[]{:S(2)}) copy-start(bf16[1,128,768]{2,1,0:T(8,128)(2,1)} %vectors_ref.1) | copy-start | bytes 589828
  12.2 19.2 %copy-start.1 = (s32[1,64]{1,0:T(1,128)S(1)}, s32[1,64]{1,0:T(1,128)}, u32[]{:S(2)}) copy-start(s32[1,64]{1,0:T(1,128)} %ids_ref.3) | copy-start | bytes 772
  13.4 1.2 %collective-permute-start.5 = (f32[1,128]{1,0:T(1,128)S(1)}, f32[1,128]{1,0:T(1,128)S(1)}, u32[]{:S(2)}, u32[]{:S(2)}) collective-permute-start(f32[1,128]{1,0:T(1,128)S(1)} %shard_map.68), channel_id=1, source_target_pairs={{0,8},{8,0},{16,24},{24,16},{1,9},{9,1},{17,25},{25,17},{2,10},{10... | collective-permute-start | bytes 1544 | tf_op jit(solution)/shard_map/ppermute | solution.py:20
  14.6 3.5 %collective-permute-start.6 = (f32[1,128]{1,0:T(1,128)S(1)}, f32[1,128]{1,0:T(1,128)S(1)}, u32[]{:S(2)}, u32[]{:S(2)}) collective-permute-start(f32[1,128]{1,0:T(1,128)S(1)} %add.3.unused.mine_ref), channel_id=1, source_target_pairs={{0,16},{8,24},{16,0},{24,8},{1,17},{9,25},{17,1},{25,9},{2,18},{10... | collective-permute-start | bytes 1544 | tf_op jit(solution)/shard_map/ppermute | solution.py:20

commit v9 on v8

--- a/solution.py
+++ b/solution.py
@@ -130,8 +130,11 @@
     sums_ref[...] = sums
 
 
-def gather_kernel(members, slots, ids_ref, heads_ref, unused, rows_ref):
+def gather_kernel(members, slots, near_ref, far_ref, heads_ref, unused, rows_ref, ids_ref):
     me = lax.axis_index("member")
+    half = members // 2
+    ids_ref[:half, :] = near_ref[...]
+    ids_ref[half:, :] = far_ref[...]
     ids = jnp.concatenate([ids_ref[pl.ds(me ^ member, 1), :] for member in range(members)], axis=0)
     rows_ref[...] = listed_rows(ids, me, slots, heads_ref)
 
@@ -240,9 +243,10 @@
     )
     ids = jnp.concatenate([ids, partner_ids], axis=0)
     mask = 2
-    while mask < members:
+    while mask < members // 2:
         ids = jnp.concatenate([ids, from_partner(ids, "member", mask)], axis=0)
         mask *= 2
+    far_ids = from_partner(ids, "member", mask)
     blocks = [pair]
     mask = 2
     while mask < groups:
@@ -265,9 +269,10 @@
     rows = call(
         functools.partial(gather_kernel, members, slots),
         jax.ShapeDtypeStruct((members * slots, width), jnp.bfloat16),
-        (ids, kept, sums),
+        (ids, far_ids, kept, sums),
         (2 * members * slots * head_dev * width, heads.size * 2),
-        spaces=[VMEM, VMEM, pl.ANY],
+        scratch=[pltpu.VMEM((members, near), jnp.int32)],
+        spaces=[VMEM, VMEM, VMEM, pl.ANY],
     )
     message = call(
         functools.partial(pack_kernel, members, slots),

time: 32.7 us -> 31.5 us (0.963)
  blocking collectives: 13.2 us -> 12 us
    all_to_all x1, blocking collectives: 13.2 us -> 12 us  [per_device(): message = lax.all_to_all(message, 'member', 0, 0, tiled=True)]
  transfers between devices with their start and end apart: 7 -> 7, of which waited for: 4 -> 3; matrix products, arithmetic and copies ran while one was open for 0% -> 0% of each run, Pallas kernels for 13% -> 13%
where the time goes in v9:
time: 31.5 us; the launch traced here: 31.3 us
  blocking collectives  12 us (38%)
  starting transfers between devices  10.5 us (33%)
  Pallas kernels  5.28 us (17%)
  waiting for transfers between devices  2.78 us (9%)
  between operations  0.68 us (2%)
    all_to_all x1, blocking collectives, per_device(): message = lax.all_to_all(message, 'member', 0, 0, tiled=True)  12 us
    ppermute x7, starting transfers between devices, from_partner(): lax.ppermute(value, axis, [(source, source ^ mask) for source in range(co...  10.5 us
    pallas_call x5, Pallas kernels, call(): pl.pallas_call(body, out_shape=shapes, in_specs=[pl.BlockSpec(memory_spac...  5.28 us
    ppermute x7, waiting for transfers between devices, from_partner(): lax.ppermute(value, axis, [(source, source ^ mask) for source in range(co...  2.78 us
  transfers between devices with their start and end apart: 7, of which 3 were waited for; matrix products, arithmetic and copies ran while one was open for 0% of the time, Pallas kernels for 13%

profile of v9, /device:TPU:0, one launch (start us, length us, event | category | flops | bytes accessed | tf_op | source)
XLA Modules:
  0.0 31.3 jit_solution(6804070789563904354)
XLA Ops:
  0.6 0.5 %collective-permute-start = (bf16[16,768]{1,0:T(8,128)(2,1)}, bf16[16,768]{1,0:T(8,128)(2,1)S(1)}, u32[]{:S(2)}, u32[]{:S(2)}) collective-permute-start(bf16[16,768]{1,0:T(8,128)(2,1)} %new_ref.1), channel_id=1, source_target_pairs={{0,8},{8,0},{16,24},{24,16},{1,9},{9,1},{17,25},{25,17},{2,10},{10... | collective-permute-start | bytes 73736 | tf_op jit(solution)/shard_map/ppermute | solution.py:20
  1.1 2.6 %collective-permute-start.1 = (s32[1,64]{1,0:T(1,128)}, s32[1,64]{1,0:T(1,128)S(1)}, u32[]{:S(2)}, u32[]{:S(2)}) collective-permute-start(s32[1,64]{1,0:T(1,128)} %ids_ref.3), channel_id=1, source_target_pairs={{0,1},{1,0},{2,3},{3,2},{4,5},{5,4},{6,7},{7,6},{8,9},{9,8},{10,11... | collective-permute-start | bytes 776 | tf_op jit(solution)/shard_map/ppermute | solution.py:20
  3.7 0.0 collective-permute-done.other_ref
  3.7 2.1 %shard_map.67 = (bf16[2048,768]{1,0:T(8,128)(2,1)S(1)}, f32[1,2048]{1,0:T(1,128)S(1)}, bf16[32,768]{1,0:T(8,128)(2,1)S(1)}, s32[1,64]{1,0:T(1,128)S(1)}) custom-call(bf16[2048,768]{1,0:T(8,128)(2,1)} %heads_ref.1, bf16[16,768]{1,0:T(8,128)(2,1)} %new_ref.1, s32[1,64]{1,0:T(1,128)} %ids_ref.3, bf16[16,768]{1,0:T(8,128)(2,1)S(1)} %collective-permute-done.other_ref), custom_call_target="tpu_custom_call" | custom-call | flops 3145728 | bytes 3145728 | tf_op jit(solution)/shard_map/pallas_call | solution.py:28
  5.8 0.0 collective-permute-done.1
  5.9 1.7 %collective-permute-start.2 = (s32[2,64]{1,0:T(2,128)S(1)}, s32[2,64]{1,0:T(2,128)S(1)}, u32[]{:S(2)}, u32[]{:S(2)}) collective-permute-start(s32[2,64]{1,0:T(2,128)S(1)} %pad_add_fusion.1), channel_id=1, source_target_pairs={{0,2},{1,3},{2,0},{3,1},{4,6},{5,7},{6,4},{7,5},{8,10},{9,11},{10,... | collective-permute-start | bytes 1544 | tf_op jit(solution)/shard_map/ppermute | solution.py:20
  7.5 1.5 %collective-permute-start.4 = (bf16[32,768]{1,0:T(8,128)(2,1)S(1)}, bf16[32,768]{1,0:T(8,128)(2,1)S(1)}, u32[]{:S(2)}, u32[]{:S(2)}) collective-permute-start(bf16[32,768]{1,0:T(8,128)(2,1)S(1)} %get-tuple-element.13.refs_0_), channel_id=1, source_target_pairs={{0,16},{8,24},{16,0},{24,8},{1,17},{9,25},{17,1},{25,9},{2,18},{10... | collective-permute-start | bytes 147464 | tf_op jit(solution)/shard_map/ppermute | solution.py:20
  9.1 0.4 %collective-permute-done.2 = s32[2,64]{1,0:T(2,128)S(1)} collective-permute-done((s32[2,64]{1,0:T(2,128)S(1)}, s32[2,64]{1,0:T(2,128)S(1)}, u32[]{:S(2)}, u32[]{:S(2)}) %collective-permute-start.2) | collective-permute-done | bytes 544 | tf_op jit(solution)/shard_map/ppermute | solution.py:20
  9.5 2.7 %collective-permute-start.3 = (s32[4,64]{1,0:T(4,128)S(1)}, s32[4,64]{1,0:T(4,128)S(1)}, u32[]{:S(2)}, u32[]{:S(2)}) collective-permute-start(s32[4,64]{1,0:T(4,128)S(1)} %pad_add_fusion.near_ref), channel_id=1, source_target_pairs={{0,4},{1,5},{2,6},{3,7},{4,0},{5,1},{6,2},{7,3},{8,12},{9,13},{10,... | collective-permute-start | bytes 3080 | tf_op jit(solution)/shard_map/ppermute | solution.py:20
  12.2 0.0 collective-permute-done.4.refs_1_
  12.2 0.0 copy-start
  12.2 0.0 copy-start.1
  12.2 1.2 %shard_map.68 = f32[1,128]{1,0:T(1,128)S(1)} custom-call(bf16[2048,768]{1,0:T(8,128)(2,1)S(1)} %get-tuple-element.11.heads_ref, f32[1,2048]{1,0:T(1,128)S(1)} %get-tuple-element.12.head_sq_ref, bf16[32,768]{1,0:T(8,128)(2,1)S(1)} %get-tuple-element.13.refs_0_, bf16[32,768]{1,0:T(8,128)(2,1)S(1)} %collective-permute-done.4.refs_1_), custom_call_target="tpu_custom_call" | custom-call | flops 201326592 | bytes 3145728 | tf_op jit(solution)/shard_map/pallas_call | solution.py:28
  13.4 0.1 collective-permute-start.5
  13.5 1.1 %collective-permute-done.5 = f32[1,128]{1,0:T(1,128)S(1)} collective-permute-done((f32[1,128]{1,0:T(1,128)S(1)}, f32[1,128]{1,0:T(1,128)S(1)}, u32[]{:S(2)}, u32[]{:S(2)}) %collective-permute-start.5) | collective-permute-done | bytes 544 | tf_op jit(solution)/shard_map/ppermute | solution.py:20
  14.6 1.5 %collective-permute-start.6 = (f32[1,128]{1,0:T(1,128)S(1)}, f32[1,128]{1,0:T(1,128)S(1)}, u32[]{:S(2)}, u32[]{:S(2)}) collective-permute-start(f32[1,128]{1,0:T(1,128)S(1)} %add.3.unused.mine_ref), channel_id=1, source_target_pairs={{0,16},{8,24},{16,0},{24,8},{1,17},{9,25},{17,1},{25,9},{2,18},{10... | collective-permute-start | bytes 1544 | tf_op jit(solution)/shard_map/ppermute | solution.py:20
  16.1 0.0 collective-permute-done.3.far_ref
  16.1 0.8 %shard_map.69.rows_ref = bf16[128,768]{1,0:T(8,128)(2,1)S(1)} custom-call(s32[4,64]{1,0:T(4,128)S(1)} %pad_add_fusion.near_ref, s32[4,64]{1,0:T(4,128)S(1)} %collective-permute-done.3.far_ref, bf16[2048,768]{1,0:T(8,128)(2,1)S(1)} %get-tuple-element.11.heads_ref, f32[1,128]{1,0:T(1,128)S(1)} %add.3.unused.mine_ref), custom_call_target="tpu_custom_call" | custom-call | flops 402653184 | bytes 3145728 | tf_op jit(solution)/shard_map/pallas_call | solution.py:28
  16.9 1.2 %collective-permute-done.6.other_ref = f32[1,128]{1,0:T(1,128)S(1)} collective-permute-done((f32[1,128]{1,0:T(1,128)S(1)}, f32[1,128]{1,0:T(1,128)S(1)}, u32[]{:S(2)}, u32[]{:S(2)}) %collective-permute-start.6) | collective-permute-done | bytes 544 | tf_op jit(solution)/shard_map/ppermute | solution.py:20
  18.2 12.0 %all_to_all.5.listed_ref = bf16[8,112,128]{2,1,0:T(8,128)(2,1)S(1)} all-to-all(bf16[8,112,128]{2,1,0:T(8,128)(2,1)S(1)} %shard_map.70), channel_id=1, replica_groups=mesh['group'=4,'member'=8] {'member'}, dimensions={0} | all-to-all | bytes 458752 | tf_op jit(solution)/shard_map/all_to_all | solution.py:283
  30.2 0.0 copy-done
  30.2 0.0 copy-done.1
  30.2 1.1 %shard_map.71 = (f32[1,16]{1,0:T(1,128)}, f32[1,16]{1,0:T(1,128)}, f32[1,64,128]{2,1,0:T(8,128)}) custom-call(s32[1,64]{1,0:T(1,128)S(1)} %copy-done.1, bf16[8,112,128]{2,1,0:T(8,128)(2,1)S(1)} %all_to_all.5.listed_ref, bf16[1,128,768]{2,1,0:T(8,128)(2,1)S(1)} %copy-done), custom_call_target="tpu_custom_call" | custom-call | flops 25165824 | bytes 393216 | tf_op jit(solution)/shard_map/pallas_call | solution.py:28
  (4 shorter events, 0.1 us)
Async XLA Ops:
  0.6 3.1 %collective-permute-start = (bf16[16,768]{1,0:T(8,128)(2,1)}, bf16[16,768]{1,0:T(8,128)(2,1)S(1)}, u32[]{:S(2)}, u32[]{:S(2)}) collective-permute-start(bf16[16,768]{1,0:T(8,128)(2,1)} %new_ref.1), channel_id=1, source_target_pairs={{0,8},{8,0},{16,24},{24,16},{1,9},{9,1},{17,25},{25,17},{2,10},{10... | collective-permute-start | bytes 73736 | tf_op jit(solution)/shard_map/ppermute | solution.py:20
  1.1 4.7 %collective-permute-start.1 = (s32[1,64]{1,0:T(1,128)}, s32[1,64]{1,0:T(1,128)S(1)}, u32[]{:S(2)}, u32[]{:S(2)}) collective-permute-start(s32[1,64]{1,0:T(1,128)} %ids_ref.3), channel_id=1, source_target_pairs={{0,1},{1,0},{2,3},{3,2},{4,5},{5,4},{6,7},{7,6},{8,9},{9,8},{10,11... | collective-permute-start | bytes 776 | tf_op jit(solution)/shard_map/ppermute | solution.py:20
  5.9 3.6 %collective-permute-start.2 = (s32[2,64]{1,0:T(2,128)S(1)}, s32[2,64]{1,0:T(2,128)S(1)}, u32[]{:S(2)}, u32[]{:S(2)}) collective-permute-start(s32[2,64]{1,0:T(2,128)S(1)} %pad_add_fusion.1), channel_id=1, source_target_pairs={{0,2},{1,3},{2,0},{3,1},{4,6},{5,7},{6,4},{7,5},{8,10},{9,11},{10,... | collective-permute-start | bytes 1544 | tf_op jit(solution)/shard_map/ppermute | solution.py:20
  7.5 4.7 %collective-permute-start.4 = (bf16[32,768]{1,0:T(8,128)(2,1)S(1)}, bf16[32,768]{1,0:T(8,128)(2,1)S(1)}, u32[]{:S(2)}, u32[]{:S(2)}) collective-permute-start(bf16[32,768]{1,0:T(8,128)(2,1)S(1)} %get-tuple-element.13.refs_0_), channel_id=1, source_target_pairs={{0,16},{8,24},{16,0},{24,8},{1,17},{9,25},{17,1},{25,9},{2,18},{10... | collective-permute-start | bytes 147464 | tf_op jit(solution)/shard_map/ppermute | solution.py:20
  9.5 6.6 %collective-permute-start.3 = (s32[4,64]{1,0:T(4,128)S(1)}, s32[4,64]{1,0:T(4,128)S(1)}, u32[]{:S(2)}, u32[]{:S(2)}) collective-permute-start(s32[4,64]{1,0:T(4,128)S(1)} %pad_add_fusion.near_ref), channel_id=1, source_target_pairs={{0,4},{1,5},{2,6},{3,7},{4,0},{5,1},{6,2},{7,3},{8,12},{9,13},{10,... | collective-permute-start | bytes 3080 | tf_op jit(solution)/shard_map/ppermute | solution.py:20
  12.2 18.0 %copy-start = (bf16[1,128,768]{2,1,0:T(8,128)(2,1)S(1)}, bf16[1,128,768]{2,1,0:T(8,128)(2,1)}, u32[]{:S(2)}) copy-start(bf16[1,128,768]{2,1,0:T(8,128)(2,1)} %vectors_ref.1) | copy-start | bytes 589828
  12.2 18.0 %copy-start.1 = (s32[1,64]{1,0:T(1,128)S(1)}, s32[1,64]{1,0:T(1,128)}, u32[]{:S(2)}) copy-start(s32[1,64]{1,0:T(1,128)} %ids_ref.3) | copy-start | bytes 772
  13.4 1.2 %collective-permute-start.5 = (f32[1,128]{1,0:T(1,128)S(1)}, f32[1,128]{1,0:T(1,128)S(1)}, u32[]{:S(2)}, u32[]{:S(2)}) collective-permute-start(f32[1,128]{1,0:T(1,128)S(1)} %shard_map.68), channel_id=1, source_target_pairs={{0,8},{8,0},{16,24},{24,16},{1,9},{9,1},{17,25},{25,17},{2,10},{10... | collective-permute-start | bytes 1544 | tf_op jit(solution)/shard_map/ppermute | solution.py:20
  14.6 3.5 %collective-permute-start.6 = (f32[1,128]{1,0:T(1,128)S(1)}, f32[1,128]{1,0:T(1,128)S(1)}, u32[]{:S(2)}, u32[]{:S(2)}) collective-permute-start(f32[1,128]{1,0:T(1,128)S(1)} %add.3.unused.mine_ref), channel_id=1, source_target_pairs={{0,16},{8,24},{16,0},{24,8},{1,17},{9,25},{17,1},{25,9},{2,18},{10... | collective-permute-start | bytes 1544 | tf_op jit(solution)/shard_map/ppermute | solution.py:20

commit v10 on v9

--- a/solution.py
+++ b/solution.py
@@ -41,10 +41,9 @@
 
 
 def early_kernel(
-    heads_ref, new_ref, ids_ref, other_ref, kept_ref, head_sq_ref, pair_ref, kept_ids_ref, sems
+    heads_ref, new_ref, ids_ref, kept_ref, head_sq_ref, kept_new_ref, kept_ids_ref, sems
 ):
     head_dev, width = heads_ref.shape
-    new_count = new_ref.shape[0]
     tiles = 4
     tile = head_dev // tiles
     parts = [pl.ds(i * tile, tile) for i in range(tiles)]
@@ -53,12 +52,11 @@
         for i, part in enumerate(parts)
     ]
     copies += [
-        pltpu.make_async_copy(new_ref, pair_ref.at[pl.ds(0, new_count)], sems.at[tiles]),
+        pltpu.make_async_copy(new_ref, kept_new_ref, sems.at[tiles]),
         pltpu.make_async_copy(ids_ref, kept_ids_ref, sems.at[tiles + 1]),
     ]
     for copy in copies:
         copy.start()
-    pair_ref[new_count:, :] = other_ref[...]
     for i in range(tiles):
         copies[i].wait()
         for first in range(i * tile, (i + 1) * tile, LANES):
@@ -110,8 +108,9 @@
     return total_w, total_we
 
 
-def crowd_kernel(groups, heads_ref, head_sq_ref, *refs):
-    query_refs, sums_ref = refs[:-1], refs[-1]
+def crowd_kernel(groups, ids_ref, heads_ref, head_sq_ref, *refs):
+    query_refs, (sums_ref, kept_ids_ref) = refs[:-2], refs[-2:]
+    kept_ids_ref[...] = ids_ref[...]
     here = lax.axis_index("group")
     queries = jnp.concatenate([ref[...] for ref in query_refs], axis=0)
     new_count = queries.shape[0] // groups
@@ -227,41 +226,39 @@
     slots = -(-most // PACK) * PACK
 
     partner_ids = from_partner(near_ids, "member", 1)
-    partner_new = from_partner(new_heads, "group", 1)
-    kept, head_sq, pair, ids = call(
+    others = [from_partner(new_heads, "group", mask) for mask in range(1, groups)]
+    kept, head_sq, new_heads, ids = call(
         early_kernel,
         (
             jax.ShapeDtypeStruct(heads.shape, heads.dtype),
             jax.ShapeDtypeStruct((1, head_dev), jnp.float32),
-            jax.ShapeDtypeStruct((2 * new_count, width), new_heads.dtype),
+            jax.ShapeDtypeStruct(new_heads.shape, new_heads.dtype),
             jax.ShapeDtypeStruct(near_ids.shape, near_ids.dtype),
         ),
-        (in_hbm(heads), in_hbm(new_heads), in_hbm(near_ids), partner_new),
-        (heads.size * 2, heads.size * 2),
+        (in_hbm(heads), in_hbm(new_heads), in_hbm(near_ids)),
+        (0, 0),
         scratch=[pltpu.SemaphoreType.DMA((6,))],
-        spaces=[HBM, HBM, HBM, VMEM],
+        spaces=[HBM, HBM, HBM],
     )
     ids = jnp.concatenate([ids, partner_ids], axis=0)
-    mask = 2
-    while mask < members // 2:
-        ids = jnp.concatenate([ids, from_partner(ids, "member", mask)], axis=0)
-        mask *= 2
-    far_ids = from_partner(ids, "member", mask)
-    blocks = [pair]
-    mask = 2
-    while mask < groups:
-        blocks.append(from_partner(jnp.concatenate(blocks, axis=0), "group", mask))
-        mask *= 2
-
     lines = 2 * groups * new_count // LANES
     chunks = width // LANES
     extra = -(-PARTS * lines // PACK) * PACK
-    sums = call(
+    sums, kept_ids = call(
         functools.partial(crowd_kernel, groups),
-        jax.ShapeDtypeStruct((lines, LANES), jnp.float32),
-        (kept, head_sq, *blocks),
-        (2 * groups * new_count * head_dev * width, heads.size * 2),
-    )
+        (
+            jax.ShapeDtypeStruct((lines, LANES), jnp.float32),
+            jax.ShapeDtypeStruct(ids.shape, ids.dtype),
+        ),
+        (ids, kept, head_sq, new_heads, *others),
+        (0, 0),
+    )
+    mask = 2
+    while mask < members // 2:
+        kept_ids = jnp.concatenate([kept_ids, from_partner(ids, "member", mask)], axis=0)
+        ids = kept_ids
+        mask *= 2
+    far_ids = from_partner(ids, "member", mask)
     mask = 1
     while mask < groups // 2:
         sums = sums + from_partner(sums, "group", mask)

time: 31.5 us -> 30.7 us (0.975)
  blocking collectives: 12 us -> 10.7 us
  waiting for transfers between devices: 2.78 us -> 3.1 us
    all_to_all x1, blocking collectives: 12 us -> 10.7 us  [per_device(): message = lax.all_to_all(message, 'member', 0, 0, tiled=True)]
    ppermute x7 -> x8, waiting for transfers between devices: 2.78 us -> 3.1 us  [from_partner(): lax.ppermute(value, axis, [(source, source ^ mask) for source in range(co...]
    ppermute x7 -> x8, starting transfers between devices: 10.5 us -> 10.7 us  [from_partner(): lax.ppermute(value, axis, [(source, source ^ mask) for source in range(co...]
  transfers between devices with their start and end apart: 7 -> 8, of which waited for: 3 -> 3; matrix products, arithmetic and copies ran while one was open for 0% -> 0% of each run, Pallas kernels for 13% -> 13%
where the time goes in v10:
time: 30.7 us; the launch traced here: 30.5 us
  starting transfers between devices  10.7 us (35%)
  blocking collectives  10.7 us (35%)
  Pallas kernels  5.29 us (17%)
  waiting for transfers between devices  3.1 us (10%)
  between operations  0.69 us (2%)
    all_to_all x1, blocking collectives, per_device(): message = lax.all_to_all(message, 'member', 0, 0, tiled=True)  10.7 us
    ppermute x8, starting transfers between devices, from_partner(): lax.ppermute(value, axis, [(source, source ^ mask) for source in range(co...  10.7 us
    pallas_call x5, Pallas kernels, call(): pl.pallas_call(body, out_shape=shapes, in_specs=[pl.BlockSpec(memory_spac...  5.29 us
    ppermute x8, waiting for transfers between devices, from_partner(): lax.ppermute(value, axis, [(source, source ^ mask) for source in range(co...  3.1 us
  transfers between devices with their start and end apart: 8, of which 3 were waited for; matrix products, arithmetic and copies ran while one was open for 0% of the time, Pallas kernels for 13%

profile of v10, /device:TPU:0, one launch (start us, length us, event | category | flops | bytes accessed | tf_op | source)
XLA Modules:
  0.0 30.5 jit_solution(9526364467566196869)
XLA Ops:
  0.6 3.0 %collective-permute-start = (s32[1,64]{1,0:T(1,128)}, s32[1,64]{1,0:T(1,128)S(1)}, u32[]{:S(2)}, u32[]{:S(2)}) collective-permute-start(s32[1,64]{1,0:T(1,128)} %ids_ref.3), channel_id=1, source_target_pairs={{0,1},{1,0},{2,3},{3,2},{4,5},{5,4},{6,7},{7,6},{8,9},{9,8},{10,11... | collective-permute-start | bytes 776 | tf_op jit(solution)/shard_map/ppermute | solution.py:20
  3.6 0.0 collective-permute-start.1
  3.6 1.5 %collective-permute-start.2 = (bf16[16,768]{1,0:T(8,128)(2,1)}, bf16[16,768]{1,0:T(8,128)(2,1)S(1)}, u32[]{:S(2)}, u32[]{:S(2)}) collective-permute-start(bf16[16,768]{1,0:T(8,128)(2,1)} %new_ref.1), channel_id=1, source_target_pairs={{0,16},{8,24},{16,0},{24,8},{1,17},{9,25},{17,1},{25,9},{2,18},{10... | collective-permute-start | bytes 73736 | tf_op jit(solution)/shard_map/ppermute | solution.py:20
  5.2 0.3 %collective-permute-start.3 = (bf16[16,768]{1,0:T(8,128)(2,1)}, bf16[16,768]{1,0:T(8,128)(2,1)S(1)}, u32[]{:S(2)}, u32[]{:S(2)}) collective-permute-start(bf16[16,768]{1,0:T(8,128)(2,1)} %new_ref.1), channel_id=1, source_target_pairs={{0,24},{8,16},{16,8},{24,0},{1,25},{9,17},{17,9},{25,1},{2,26},{10... | collective-permute-start | bytes 73736 | tf_op jit(solution)/shard_map/ppermute | solution.py:20
  5.5 2.1 %shard_map.67 = (bf16[2048,768]{1,0:T(8,128)(2,1)S(1)}, f32[1,2048]{1,0:T(1,128)S(1)}, bf16[16,768]{1,0:T(8,128)(2,1)S(1)}, s32[1,64]{1,0:T(1,128)S(1)}) custom-call(bf16[2048,768]{1,0:T(8,128)(2,1)} %heads_ref.1, bf16[16,768]{1,0:T(8,128)(2,1)} %new_ref.1, s32[1,64]{1,0:T(1,128)} %ids_ref.3), custom_call_target="tpu_custom_call" | custom-call | tf_op jit(solution)/shard_map/pallas_call | solution.py:28
  7.6 0.0 collective-permute-done
  7.6 1.6 %collective-permute-start.4 = (s32[2,64]{1,0:T(2,128)S(1)}, s32[2,64]{1,0:T(2,128)S(1)}, u32[]{:S(2)}, u32[]{:S(2)}) collective-permute-start(s32[2,64]{1,0:T(2,128)S(1)} %pad_add_fusion.1.ids_ref), channel_id=1, source_target_pairs={{0,2},{1,3},{2,0},{3,1},{4,6},{5,7},{6,4},{7,5},{8,10},{9,11},{10,... | collective-permute-start | bytes 1544 | tf_op jit(solution)/shard_map/ppermute | solution.py:20
  9.3 0.0 collective-permute-done.1.refs_1_
  9.3 0.0 collective-permute-done.2.refs_2_
  9.3 0.0 collective-permute-done.3.refs_3_
  9.3 0.0 copy-start
  9.3 0.0 copy-start.1
  9.3 1.2 %shard_map.68 = (f32[1,128]{1,0:T(1,128)S(1)}, s32[2,64]{1,0:T(2,128)S(1)}) custom-call(s32[2,64]{1,0:T(2,128)S(1)} %pad_add_fusion.1.ids_ref, bf16[2048,768]{1,0:T(8,128)(2,1)S(1)} %get-tuple-element.13.heads_ref, f32[1,2048]{1,0:T(1,128)S(1)} %get-tuple-element.14.head_sq_ref, bf16[16,768]{1,0:T(8,128)(2,1)S(1)} %get-tuple-element.15.refs_0_, ...), custom_call_target="tpu_custom_call" | custom-call | tf_op jit(solution)/shard_map/pallas_call | solution.py:28
  10.5 0.7 %collective-permute-done.4 = s32[2,64]{1,0:T(2,128)S(1)} collective-permute-done((s32[2,64]{1,0:T(2,128)S(1)}, s32[2,64]{1,0:T(2,128)S(1)}, u32[]{:S(2)}, u32[]{:S(2)}) %collective-permute-start.4) | collective-permute-done | bytes 544 | tf_op jit(solution)/shard_map/ppermute | solution.py:20
  11.3 2.6 %collective-permute-start.5 = (s32[4,64]{1,0:T(4,128)S(1)}, s32[4,64]{1,0:T(4,128)S(1)}, u32[]{:S(2)}, u32[]{:S(2)}) collective-permute-start(s32[4,64]{1,0:T(4,128)S(1)} %pad_add_fusion.near_ref), channel_id=1, source_target_pairs={{0,4},{1,5},{2,6},{3,7},{4,0},{5,1},{6,2},{7,3},{8,12},{9,13},{10,... | collective-permute-start | bytes 3080 | tf_op jit(solution)/shard_map/ppermute | solution.py:20
  13.9 0.0 collective-permute-start.6
  13.9 1.1 %collective-permute-done.6 = f32[1,128]{1,0:T(1,128)S(1)} collective-permute-done((f32[1,128]{1,0:T(1,128)S(1)}, f32[1,128]{1,0:T(1,128)S(1)}, u32[]{:S(2)}, u32[]{:S(2)}) %collective-permute-start.6) | collective-permute-done | bytes 544 | tf_op jit(solution)/shard_map/ppermute | solution.py:20
  15.1 1.5 %collective-permute-start.7 = (f32[1,128]{1,0:T(1,128)S(1)}, f32[1,128]{1,0:T(1,128)S(1)}, u32[]{:S(2)}, u32[]{:S(2)}) collective-permute-start(f32[1,128]{1,0:T(1,128)S(1)} %add.3.unused.mine_ref), channel_id=1, source_target_pairs={{0,16},{8,24},{16,0},{24,8},{1,17},{9,25},{17,1},{25,9},{2,18},{10... | collective-permute-start | bytes 1544 | tf_op jit(solution)/shard_map/ppermute | solution.py:20
  16.6 0.0 collective-permute-done.5.far_ref
  16.6 0.8 %shard_map.69.rows_ref = bf16[128,768]{1,0:T(8,128)(2,1)S(1)} custom-call(s32[4,64]{1,0:T(4,128)S(1)} %pad_add_fusion.near_ref, s32[4,64]{1,0:T(4,128)S(1)} %collective-permute-done.5.far_ref, bf16[2048,768]{1,0:T(8,128)(2,1)S(1)} %get-tuple-element.13.heads_ref, f32[1,128]{1,0:T(1,128)S(1)} %add.3.unused.mine_ref), custom_call_target="tpu_custom_call" | custom-call | flops 402653184 | bytes 3145728 | tf_op jit(solution)/shard_map/pallas_call | solution.py:28
  17.4 1.2 %collective-permute-done.7.other_ref = f32[1,128]{1,0:T(1,128)S(1)} collective-permute-done((f32[1,128]{1,0:T(1,128)S(1)}, f32[1,128]{1,0:T(1,128)S(1)}, u32[]{:S(2)}, u32[]{:S(2)}) %collective-permute-start.7) | collective-permute-done | bytes 544 | tf_op jit(solution)/shard_map/ppermute | solution.py:20
  18.7 10.7 %all_to_all.5.listed_ref = bf16[8,112,128]{2,1,0:T(8,128)(2,1)S(1)} all-to-all(bf16[8,112,128]{2,1,0:T(8,128)(2,1)S(1)} %shard_map.70), channel_id=1, replica_groups=mesh['group'=4,'member'=8] {'member'}, dimensions={0} | all-to-all | bytes 458752 | tf_op jit(solution)/shard_map/all_to_all | solution.py:280
  29.4 0.0 copy-done
  29.4 0.0 copy-done.1
  29.4 1.1 %shard_map.71 = (f32[1,16]{1,0:T(1,128)}, f32[1,16]{1,0:T(1,128)}, f32[1,64,128]{2,1,0:T(8,128)}) custom-call(s32[1,64]{1,0:T(1,128)S(1)} %copy-done.1, bf16[8,112,128]{2,1,0:T(8,128)(2,1)S(1)} %all_to_all.5.listed_ref, bf16[1,128,768]{2,1,0:T(8,128)(2,1)S(1)} %copy-done), custom_call_target="tpu_custom_call" | custom-call | flops 25165824 | bytes 393216 | tf_op jit(solution)/shard_map/pallas_call | solution.py:28
  (4 shorter events, 0.1 us)
Async XLA Ops:
  0.6 7.0 %collective-permute-start = (s32[1,64]{1,0:T(1,128)}, s32[1,64]{1,0:T(1,128)S(1)}, u32[]{:S(2)}, u32[]{:S(2)}) collective-permute-start(s32[1,64]{1,0:T(1,128)} %ids_ref.3), channel_id=1, source_target_pairs={{0,1},{1,0},{2,3},{3,2},{4,5},{5,4},{6,7},{7,6},{8,9},{9,8},{10,11... | collective-permute-start | bytes 776 | tf_op jit(solution)/shard_map/ppermute | solution.py:20
  3.6 5.7 %collective-permute-start.1 = (bf16[16,768]{1,0:T(8,128)(2,1)}, bf16[16,768]{1,0:T(8,128)(2,1)S(1)}, u32[]{:S(2)}, u32[]{:S(2)}) collective-permute-start(bf16[16,768]{1,0:T(8,128)(2,1)} %new_ref.1), channel_id=1, source_target_pairs={{0,8},{8,0},{16,24},{24,16},{1,9},{9,1},{17,25},{25,17},{2,10},{10... | collective-permute-start | bytes 73736 | tf_op jit(solution)/shard_map/ppermute | solution.py:20
  3.6 5.7 %collective-permute-start.2 = (bf16[16,768]{1,0:T(8,128)(2,1)}, bf16[16,768]{1,0:T(8,128)(2,1)S(1)}, u32[]{:S(2)}, u32[]{:S(2)}) collective-permute-start(bf16[16,768]{1,0:T(8,128)(2,1)} %new_ref.1), channel_id=1, source_target_pairs={{0,16},{8,24},{16,0},{24,8},{1,17},{9,25},{17,1},{25,9},{2,18},{10... | collective-permute-start | bytes 73736 | tf_op jit(solution)/shard_map/ppermute | solution.py:20
  5.2 4.1 %collective-permute-start.3 = (bf16[16,768]{1,0:T(8,128)(2,1)}, bf16[16,768]{1,0:T(8,128)(2,1)S(1)}, u32[]{:S(2)}, u32[]{:S(2)}) collective-permute-start(bf16[16,768]{1,0:T(8,128)(2,1)} %new_ref.1), channel_id=1, source_target_pairs={{0,24},{8,16},{16,8},{24,0},{1,25},{9,17},{17,9},{25,1},{2,26},{10... | collective-permute-start | bytes 73736 | tf_op jit(solution)/shard_map/ppermute | solution.py:20
  7.6 3.6 %collective-permute-start.4 = (s32[2,64]{1,0:T(2,128)S(1)}, s32[2,64]{1,0:T(2,128)S(1)}, u32[]{:S(2)}, u32[]{:S(2)}) collective-permute-start(s32[2,64]{1,0:T(2,128)S(1)} %pad_add_fusion.1.ids_ref), channel_id=1, source_target_pairs={{0,2},{1,3},{2,0},{3,1},{4,6},{5,7},{6,4},{7,5},{8,10},{9,11},{10,... | collective-permute-start | bytes 1544 | tf_op jit(solution)/shard_map/ppermute | solution.py:20
  9.3 20.1 %copy-start = (bf16[1,128,768]{2,1,0:T(8,128)(2,1)S(1)}, bf16[1,128,768]{2,1,0:T(8,128)(2,1)}, u32[]{:S(2)}) copy-start(bf16[1,128,768]{2,1,0:T(8,128)(2,1)} %vectors_ref.1) | copy-start | bytes 589828
  9.3 20.1 %copy-start.1 = (s32[1,64]{1,0:T(1,128)S(1)}, s32[1,64]{1,0:T(1,128)}, u32[]{:S(2)}) copy-start(s32[1,64]{1,0:T(1,128)} %ids_ref.3) | copy-start | bytes 772
  11.3 5.3 %collective-permute-start.5 = (s32[4,64]{1,0:T(4,128)S(1)}, s32[4,64]{1,0:T(4,128)S(1)}, u32[]{:S(2)}, u32[]{:S(2)}) collective-permute-start(s32[4,64]{1,0:T(4,128)S(1)} %pad_add_fusion.near_ref), channel_id=1, source_target_pairs={{0,4},{1,5},{2,6},{3,7},{4,0},{5,1},{6,2},{7,3},{8,12},{9,13},{10,... | collective-permute-start | bytes 3080 | tf_op jit(solution)/shard_map/ppermute | solution.py:20
  13.9 1.1 %collective-permute-start.6 = (f32[1,128]{1,0:T(1,128)S(1)}, f32[1,128]{1,0:T(1,128)S(1)}, u32[]{:S(2)}, u32[]{:S(2)}) collective-permute-start(f32[1,128]{1,0:T(1,128)S(1)} %get-tuple-element.17), channel_id=1, source_target_pairs={{0,8},{8,0},{16,24},{24,16},{1,9},{9,1},{17,25},{25,17},{2,10},{10... | collective-permute-start | bytes 1544 | tf_op jit(solution)/shard_map/ppermute | solution.py:20
  15.1 3.5 %collective-permute-start.7 = (f32[1,128]{1,0:T(1,128)S(1)}, f32[1,128]{1,0:T(1,128)S(1)}, u32[]{:S(2)}, u32[]{:S(2)}) collective-permute-start(f32[1,128]{1,0:T(1,128)S(1)} %add.3.unused.mine_ref), channel_id=1, source_target_pairs={{0,16},{8,24},{16,0},{24,8},{1,17},{9,25},{17,1},{25,9},{2,18},{10... | collective-permute-start | bytes 1544 | tf_op jit(solution)/shard_map/ppermute | solution.py:20

commit v11 on v10

--- a/solution.py
+++ b/solution.py
@@ -38,35 +38,6 @@
 
 def iota(shape, dim):
     return lax.broadcasted_iota(jnp.int32, shape, dim)
-
-
-def early_kernel(
-    heads_ref, new_ref, ids_ref, kept_ref, head_sq_ref, kept_new_ref, kept_ids_ref, sems
-):
-    head_dev, width = heads_ref.shape
-    tiles = 4
-    tile = head_dev // tiles
-    parts = [pl.ds(i * tile, tile) for i in range(tiles)]
-    copies = [
-        pltpu.make_async_copy(heads_ref.at[part], kept_ref.at[part], sems.at[i])
-        for i, part in enumerate(parts)
-    ]
-    copies += [
-        pltpu.make_async_copy(new_ref, kept_new_ref, sems.at[tiles]),
-        pltpu.make_async_copy(ids_ref, kept_ids_ref, sems.at[tiles + 1]),
-    ]
-    for copy in copies:
-        copy.start()
-    for i in range(tiles):
-        copies[i].wait()
-        for first in range(i * tile, (i + 1) * tile, LANES):
-            block = jnp.square(kept_ref[first:first + LANES, :].astype(jnp.float32))
-            folded = block[:, :LANES]
-            for column in range(LANES, width, LANES):
-                folded = folded + block[:, column:column + LANES]
-            head_sq_ref[:, first:first + LANES] = jnp.sum(folded.T, axis=0, keepdims=True)
-    for copy in copies[tiles:]:
-        copy.wait()
 
 
 def listed_rows(ids, me, slots, heads_ref):
@@ -88,33 +59,61 @@
     ).astype(jnp.bfloat16)
 
 
-def crowding(queries, heads_ref, head_sq_ref):
+def stage_kernel(ids_ref, kept_ref, sem):
+    copy = pltpu.make_async_copy(ids_ref, kept_ref, sem)
+    copy.start()
+    copy.wait()
+
+
+def squares(block):
+    width = block.shape[1]
+    block = jnp.square(block.astype(jnp.float32))
+    folded = block[:, :LANES]
+    for column in range(LANES, width, LANES):
+        folded = folded + block[:, column:column + LANES]
+    return jnp.sum(folded.T, axis=0, keepdims=True)
+
+
+def crowd_kernel(groups, unused, heads_ref, new_ref, *refs):
+    other_refs, (sums_ref, kept_ref, queries_ref, sems) = refs[:-4], refs[-4:]
     head_dev, width = heads_ref.shape
+    new_count = new_ref.shape[0]
+    tiles = sems.shape[0] - 1
+    tile = head_dev // tiles
+    parts = [pl.ds(i * tile, tile) for i in range(tiles)]
+    new_copy = pltpu.make_async_copy(new_ref, queries_ref.at[pl.ds(0, new_count)], sems.at[tiles])
+    new_copy.start()
+    copies = [
+        pltpu.make_async_copy(heads_ref.at[part], kept_ref.at[part], sems.at[i])
+        for i, part in enumerate(parts)
+    ]
+    for copy in copies:
+        copy.start()
+    for i, ref in enumerate(other_refs):
+        queries_ref[(i + 1) * new_count:(i + 2) * new_count, :] = ref[...]
+    new_copy.wait()
+    queries = queries_ref[...]
     query_sq = jnp.sum(jnp.square(queries.astype(jnp.float32)), axis=1, keepdims=True)
-    total_w = jnp.zeros((queries.shape[0], 1), jnp.float32)
-    total_we = jnp.zeros((queries.shape[0], 1), jnp.float32)
-    tile = 512
-    for start in range(0, head_dev, tile):
+    total_w = jnp.zeros((groups * new_count, 1), jnp.float32)
+    total_we = jnp.zeros((groups * new_count, 1), jnp.float32)
+    for i, copy in enumerate(copies):
+        copy.wait()
+        first = i * tile
+        head_sq = jnp.concatenate(
+            [squares(kept_ref[row:row + LANES, :]) for row in range(first, first + tile, LANES)],
+            axis=1,
+        )
         dots = lax.dot_general(
-            queries, heads_ref[start:start + tile, :], (((1,), (1,)), ((), ())),
+            queries, kept_ref[first:first + tile, :], (((1,), (1,)), ((), ())),
             preferred_element_type=jnp.float32,
         )
-        head_sq = head_sq_ref[:, start:start + tile]
         excess = (query_sq + head_sq - 2.0 * dots) * (1.0 / width)
         inverse = 1.0 / (1.0 + excess)
         weight = inverse * inverse
         total_w = total_w + jnp.sum(weight, axis=1, keepdims=True)
         total_we = total_we + jnp.sum(weight * excess, axis=1, keepdims=True)
-    return total_w, total_we
-
-
-def crowd_kernel(groups, ids_ref, heads_ref, head_sq_ref, *refs):
-    query_refs, (sums_ref, kept_ids_ref) = refs[:-2], refs[-2:]
-    kept_ids_ref[...] = ids_ref[...]
+    totals = (total_w, total_we)
     here = lax.axis_index("group")
-    queries = jnp.concatenate([ref[...] for ref in query_refs], axis=0)
-    new_count = queries.shape[0] // groups
-    totals = crowding(queries, heads_ref, head_sq_ref)
     lane = iota((new_count, LANES), 1)
     row = iota((new_count, LANES), 0)
     line = iota(sums_ref.shape, 0)
@@ -127,6 +126,13 @@
             spread_out = jnp.sum(spread_out, axis=0, keepdims=True)
             sums = sums + jnp.where(line == place // LANES, spread_out, 0.0)
     sums_ref[...] = sums
+
+
+def join_kernel(mine_ref, other_ref, low_ref, high_ref, sums_ref, ids_ref):
+    half = low_ref.shape[0]
+    sums_ref[...] = mine_ref[...] + other_ref[...]
+    ids_ref[:half, :] = low_ref[...]
+    ids_ref[half:, :] = high_ref[...]
 
 
 def gather_kernel(members, slots, near_ref, far_ref, heads_ref, unused, rows_ref, ids_ref):
@@ -227,39 +233,47 @@
 
     partner_ids = from_partner(near_ids, "member", 1)
     others = [from_partner(new_heads, "group", mask) for mask in range(1, groups)]
-    kept, head_sq, new_heads, ids = call(
-        early_kernel,
-        (
-            jax.ShapeDtypeStruct(heads.shape, heads.dtype),
-            jax.ShapeDtypeStruct((1, head_dev), jnp.float32),
-            jax.ShapeDtypeStruct(new_heads.shape, new_heads.dtype),
-            jax.ShapeDtypeStruct(near_ids.shape, near_ids.dtype),
-        ),
-        (in_hbm(heads), in_hbm(new_heads), in_hbm(near_ids)),
+    ids = call(
+        stage_kernel,
+        jax.ShapeDtypeStruct(near_ids.shape, near_ids.dtype),
+        (in_hbm(near_ids),),
         (0, 0),
-        scratch=[pltpu.SemaphoreType.DMA((6,))],
-        spaces=[HBM, HBM, HBM],
+        scratch=[pltpu.SemaphoreType.DMA],
+        spaces=[HBM],
     )
     ids = jnp.concatenate([ids, partner_ids], axis=0)
     lines = 2 * groups * new_count // LANES
     chunks = width // LANES
     extra = -(-PARTS * lines // PACK) * PACK
-    sums, kept_ids = call(
+    sums, kept = call(
         functools.partial(crowd_kernel, groups),
         (
             jax.ShapeDtypeStruct((lines, LANES), jnp.float32),
-            jax.ShapeDtypeStruct(ids.shape, ids.dtype),
+            jax.ShapeDtypeStruct(heads.shape, heads.dtype),
         ),
-        (ids, kept, head_sq, new_heads, *others),
+        (ids, in_hbm(heads), in_hbm(new_heads), *others),
         (0, 0),
+        scratch=[
+            pltpu.VMEM((groups * new_count, width), new_heads.dtype),
+            pltpu.SemaphoreType.DMA((5,)),
+        ],
+        spaces=[pl.ANY, HBM, HBM] + [VMEM] * len(others),
     )
     mask = 2
-    while mask < members // 2:
-        kept_ids = jnp.concatenate([kept_ids, from_partner(ids, "member", mask)], axis=0)
-        ids = kept_ids
+    while mask < members // 4:
+        ids = jnp.concatenate([ids, from_partner(ids, "member", mask)], axis=0)
         mask *= 2
-    far_ids = from_partner(ids, "member", mask)
-    mask = 1
+    sums, ids = call(
+        join_kernel,
+        (
+            jax.ShapeDtypeStruct(sums.shape, sums.dtype),
+            jax.ShapeDtypeStruct((2 * mask, near), ids.dtype),
+        ),
+        (sums, from_partner(sums, "group", 1), ids, from_partner(ids, "member", mask)),
+        (0, 0),
+    )
+    far_ids = from_partner(ids, "member", 2 * mask)
+    mask = 2
     while mask < groups // 2:
         sums = sums + from_partner(sums, "group", mask)
         mask *= 2

time: 30.7 us -> 32.3 us (1.052)
  blocking collectives: 10.7 us -> 11.8 us
  waiting for transfers between devices: 3.1 us -> 3.62 us
  starting transfers between devices: 10.7 us -> 10.2 us
  Pallas kernels: 5.29 us -> 5.78 us
    all_to_all x1, blocking collectives: 10.7 us -> 11.8 us  [per_device(): message = lax.all_to_all(message, 'member', 0, 0, tiled=True)]
    ppermute x8, waiting for transfers between devices: 3.1 us -> 3.62 us  [from_partner(): lax.ppermute(value, axis, [(source, source ^ mask) for source in range(co...]
    ppermute x8, starting transfers between devices: 10.7 us -> 10.2 us  [from_partner(): lax.ppermute(value, axis, [(source, source ^ mask) for source in range(co...]
    pallas_call x5 -> x6, Pallas kernels: 5.29 us -> 5.78 us  [call(): pl.pallas_call(body, out_shape=shapes, in_specs=[pl.BlockSpec(memory_spac...]
  transfers between devices with their start and end apart: 8 -> 8, of which waited for: 3 -> 4; matrix products, arithmetic and copies ran while one was open for 0% -> 0% of each run, Pallas kernels for 13% -> 14%
where the time goes in v11:
time: 32.3 us; the launch traced here: 32.1 us
  blocking collectives  11.8 us (37%)
  starting transfers between devices  10.2 us (32%)
  Pallas kernels  5.78 us (18%)
  waiting for transfers between devices  3.62 us (11%)
  between operations  0.69 us (2%)
    all_to_all x1, blocking collectives, per_device(): message = lax.all_to_all(message, 'member', 0, 0, tiled=True)  11.8 us
    ppermute x8, starting transfers between devices, from_partner(): lax.ppermute(value, axis, [(source, source ^ mask) for source in range(co...  10.2 us
    pallas_call x6, Pallas kernels, call(): pl.pallas_call(body, out_shape=shapes, in_specs=[pl.BlockSpec(memory_spac...  5.78 us
    ppermute x8, waiting for transfers between devices, from_partner(): lax.ppermute(value, axis, [(source, source ^ mask) for source in range(co...  3.62 us
  transfers between devices with their start and end apart: 8, of which 4 were waited for; matrix products, arithmetic and copies ran while one was open for 0% of the time, Pallas kernels for 14%

profile of v11, /device:TPU:0, one launch (start us, length us, event | category | flops | bytes accessed | tf_op | source)
XLA Modules:
  0.0 32.1 jit_solution(12646455598018158998)
XLA Ops:
  0.6 3.0 %collective-permute-start = (s32[1,64]{1,0:T(1,128)}, s32[1,64]{1,0:T(1,128)S(1)}, u32[]{:S(2)}, u32[]{:S(2)}) collective-permute-start(s32[1,64]{1,0:T(1,128)} %ids_ref.3), channel_id=1, source_target_pairs={{0,1},{1,0},{2,3},{3,2},{4,5},{5,4},{6,7},{7,6},{8,9},{9,8},{10,11... | collective-permute-start | bytes 776 | tf_op jit(solution)/shard_map/ppermute | solution.py:20
  3.6 0.0 collective-permute-start.1
  3.6 1.5 %collective-permute-start.2 = (bf16[16,768]{1,0:T(8,128)(2,1)}, bf16[16,768]{1,0:T(8,128)(2,1)S(1)}, u32[]{:S(2)}, u32[]{:S(2)}) collective-permute-start(bf16[16,768]{1,0:T(8,128)(2,1)} %new_ref.1), channel_id=1, source_target_pairs={{0,16},{8,24},{16,0},{24,8},{1,17},{9,25},{17,1},{25,9},{2,18},{10... | collective-permute-start | bytes 73736 | tf_op jit(solution)/shard_map/ppermute | solution.py:20
  5.2 0.3 %collective-permute-start.3 = (bf16[16,768]{1,0:T(8,128)(2,1)}, bf16[16,768]{1,0:T(8,128)(2,1)S(1)}, u32[]{:S(2)}, u32[]{:S(2)}) collective-permute-start(bf16[16,768]{1,0:T(8,128)(2,1)} %new_ref.1), channel_id=1, source_target_pairs={{0,24},{8,16},{16,8},{24,0},{1,25},{9,17},{17,9},{25,1},{2,26},{10... | collective-permute-start | bytes 73736 | tf_op jit(solution)/shard_map/ppermute | solution.py:20
  5.5 0.7 %shard_map.67 = s32[1,64]{1,0:T(1,128)S(1)} custom-call(s32[1,64]{1,0:T(1,128)} %ids_ref.3), custom_call_target="tpu_custom_call" | custom-call | tf_op jit(solution)/shard_map/pallas_call | solution.py:28
  6.2 0.0 collective-permute-done
  6.2 0.0 copy-start
  6.2 0.0 copy-start.1
  6.2 1.6 %collective-permute-start.5 = (s32[2,64]{1,0:T(2,128)S(1)}, s32[2,64]{1,0:T(2,128)S(1)}, u32[]{:S(2)}, u32[]{:S(2)}) collective-permute-start(s32[2,64]{1,0:T(2,128)S(1)} %pad_add_fusion.unused.low_ref), channel_id=1, source_target_pairs={{0,2},{1,3},{2,0},{3,1},{4,6},{5,7},{6,4},{7,5},{8,10},{9,11},{10,... | collective-permute-start | bytes 1544 | tf_op jit(solution)/shard_map/ppermute | solution.py:20
  7.9 0.0 collective-permute-done.1.refs_0_
  7.9 0.0 collective-permute-done.2.refs_1_
  7.9 0.8 %collective-permute-done.3.refs_2_ = bf16[16,768]{1,0:T(8,128)(2,1)S(1)} collective-permute-done((bf16[16,768]{1,0:T(8,128)(2,1)}, bf16[16,768]{1,0:T(8,128)(2,1)S(1)}, u32[]{:S(2)}, u32[]{:S(2)}) %collective-permute-start.3) | collective-permute-done | bytes 24608 | tf_op jit(solution)/shard_map/ppermute | solution.py:20
  8.6 3.1 %shard_map.68 = (f32[1,128]{1,0:T(1,128)S(1)}, bf16[2048,768]{1,0:T(8,128)(2,1)S(1)}) custom-call(s32[2,64]{1,0:T(2,128)S(1)} %pad_add_fusion.unused.low_ref, bf16[2048,768]{1,0:T(8,128)(2,1)} %heads_ref.1, bf16[16,768]{1,0:T(8,128)(2,1)} %new_ref.1, bf16[16,768]{1,0:T(8,128)(2,1)S(1)} %collective-permute-done.1.refs_0_, ...), custom_call_target="tpu_custom_call" | custom-call | tf_op jit(solution)/shard_map/pallas_call | solution.py:28
  11.8 0.3 collective-permute-start.4
  12.1 0.0 collective-permute-done.5.high_ref
  12.1 0.9 %collective-permute-done.4.other_ref = f32[1,128]{1,0:T(1,128)S(1)} collective-permute-done((f32[1,128]{1,0:T(1,128)S(1)}, f32[1,128]{1,0:T(1,128)S(1)}, u32[]{:S(2)}, u32[]{:S(2)}) %collective-permute-start.4) | collective-permute-done | bytes 544 | tf_op jit(solution)/shard_map/ppermute | solution.py:20
  13.0 2.6 %collective-permute-start.6 = (s32[4,64]{1,0:T(4,128)S(1)}, s32[4,64]{1,0:T(4,128)S(1)}, u32[]{:S(2)}, u32[]{:S(2)}) collective-permute-start(s32[4,64]{1,0:T(4,128)S(1)} %get-tuple-element.11.near_ref), channel_id=1, source_target_pairs={{0,4},{1,5},{2,6},{3,7},{4,0},{5,1},{6,2},{7,3},{8,12},{9,13},{10,... | collective-permute-start | bytes 3080 | tf_op jit(solution)/shard_map/ppermute | solution.py:20
  15.6 0.8 %collective-permute-start.7 = (f32[1,128]{1,0:T(1,128)S(1)}, f32[1,128]{1,0:T(1,128)S(1)}, u32[]{:S(2)}, u32[]{:S(2)}) collective-permute-start(f32[1,128]{1,0:T(1,128)S(1)} %get-tuple-element.13.unused.mine_ref), channel_id=1, source_target_pairs={{0,16},{8,24},{16,0},{24,8},{1,17},{9,25},{17,1},{25,9},{2,18},{10... | collective-permute-start | bytes 1544 | tf_op jit(solution)/shard_map/ppermute | solution.py:20
  16.3 1.1 %collective-permute-done.6.far_ref = s32[4,64]{1,0:T(4,128)S(1)} collective-permute-done((s32[4,64]{1,0:T(4,128)S(1)}, s32[4,64]{1,0:T(4,128)S(1)}, u32[]{:S(2)}, u32[]{:S(2)}) %collective-permute-start.6) | collective-permute-done | bytes 1056 | tf_op jit(solution)/shard_map/ppermute | solution.py:20
  17.5 0.8 %shard_map.70.rows_ref = bf16[128,768]{1,0:T(8,128)(2,1)S(1)} custom-call(s32[4,64]{1,0:T(4,128)S(1)} %get-tuple-element.11.near_ref, s32[4,64]{1,0:T(4,128)S(1)} %collective-permute-done.6.far_ref, bf16[2048,768]{1,0:T(8,128)(2,1)S(1)} %get-tuple-element.12.heads_ref, f32[1,128]{1,0:T(1,128)S(1)} %get-tuple-element.13.unused.mine_ref), custom_call_target="tpu_custom_call" | custom-call | flops 402653184 | bytes 3145728 | tf_op jit(solution)/shard_map/pallas_call | solution.py:28
  18.2 0.8 %collective-permute-done.7.other_ref = f32[1,128]{1,0:T(1,128)S(1)} collective-permute-done((f32[1,128]{1,0:T(1,128)S(1)}, f32[1,128]{1,0:T(1,128)S(1)}, u32[]{:S(2)}, u32[]{:S(2)}) %collective-permute-start.7) | collective-permute-done | bytes 544 | tf_op jit(solution)/shard_map/ppermute | solution.py:20
  19.1 11.8 %all_to_all.5.listed_ref = bf16[8,112,128]{2,1,0:T(8,128)(2,1)S(1)} all-to-all(bf16[8,112,128]{2,1,0:T(8,128)(2,1)S(1)} %shard_map.71), channel_id=1, replica_groups=mesh['group'=4,'member'=8] {'member'}, dimensions={0} | all-to-all | bytes 458752 | tf_op jit(solution)/shard_map/all_to_all | solution.py:294
  31.0 0.0 copy-done
  31.0 0.0 copy-done.1
  31.0 1.1 %shard_map.72 = (f32[1,16]{1,0:T(1,128)}, f32[1,16]{1,0:T(1,128)}, f32[1,64,128]{2,1,0:T(8,128)}) custom-call(s32[1,64]{1,0:T(1,128)S(1)} %copy-done.1, bf16[8,112,128]{2,1,0:T(8,128)(2,1)S(1)} %all_to_all.5.listed_ref, bf16[1,128,768]{2,1,0:T(8,128)(2,1)S(1)} %copy-done), custom_call_target="tpu_custom_call" | custom-call | flops 25165824 | bytes 393216 | tf_op jit(solution)/shard_map/pallas_call | solution.py:28
  (3 shorter events, 0.1 us)
Async XLA Ops:
  0.6 5.5 %collective-permute-start = (s32[1,64]{1,0:T(1,128)}, s32[1,64]{1,0:T(1,128)S(1)}, u32[]{:S(2)}, u32[]{:S(2)}) collective-permute-start(s32[1,64]{1,0:T(1,128)} %ids_ref.3), channel_id=1, source_target_pairs={{0,1},{1,0},{2,3},{3,2},{4,5},{5,4},{6,7},{7,6},{8,9},{9,8},{10,11... | collective-permute-start | bytes 776 | tf_op jit(solution)/shard_map/ppermute | solution.py:20
  3.6 4.2 %collective-permute-start.1 = (bf16[16,768]{1,0:T(8,128)(2,1)}, bf16[16,768]{1,0:T(8,128)(2,1)S(1)}, u32[]{:S(2)}, u32[]{:S(2)}) collective-permute-start(bf16[16,768]{1,0:T(8,128)(2,1)} %new_ref.1), channel_id=1, source_target_pairs={{0,8},{8,0},{16,24},{24,16},{1,9},{9,1},{17,25},{25,17},{2,10},{10... | collective-permute-start | bytes 73736 | tf_op jit(solution)/shard_map/ppermute | solution.py:20
  3.6 4.2 %collective-permute-start.2 = (bf16[16,768]{1,0:T(8,128)(2,1)}, bf16[16,768]{1,0:T(8,128)(2,1)S(1)}, u32[]{:S(2)}, u32[]{:S(2)}) collective-permute-start(bf16[16,768]{1,0:T(8,128)(2,1)} %new_ref.1), channel_id=1, source_target_pairs={{0,16},{8,24},{16,0},{24,8},{1,17},{9,25},{17,1},{25,9},{2,18},{10... | collective-permute-start | bytes 73736 | tf_op jit(solution)/shard_map/ppermute | solution.py:20
  5.2 3.5 %collective-permute-start.3 = (bf16[16,768]{1,0:T(8,128)(2,1)}, bf16[16,768]{1,0:T(8,128)(2,1)S(1)}, u32[]{:S(2)}, u32[]{:S(2)}) collective-permute-start(bf16[16,768]{1,0:T(8,128)(2,1)} %new_ref.1), channel_id=1, source_target_pairs={{0,24},{8,16},{16,8},{24,0},{1,25},{9,17},{17,9},{25,1},{2,26},{10... | collective-permute-start | bytes 73736 | tf_op jit(solution)/shard_map/ppermute | solution.py:20
  6.2 24.8 %copy-start = (bf16[1,128,768]{2,1,0:T(8,128)(2,1)S(1)}, bf16[1,128,768]{2,1,0:T(8,128)(2,1)}, u32[]{:S(2)}) copy-start(bf16[1,128,768]{2,1,0:T(8,128)(2,1)} %vectors_ref.1) | copy-start | bytes 589828
  6.2 24.8 %copy-start.1 = (s32[1,64]{1,0:T(1,128)S(1)}, s32[1,64]{1,0:T(1,128)}, u32[]{:S(2)}) copy-start(s32[1,64]{1,0:T(1,128)} %ids_ref.3) | copy-start | bytes 772
  6.2 5.9 %collective-permute-start.5 = (s32[2,64]{1,0:T(2,128)S(1)}, s32[2,64]{1,0:T(2,128)S(1)}, u32[]{:S(2)}, u32[]{:S(2)}) collective-permute-start(s32[2,64]{1,0:T(2,128)S(1)} %pad_add_fusion.unused.low_ref), channel_id=1, source_target_pairs={{0,2},{1,3},{2,0},{3,1},{4,6},{5,7},{6,4},{7,5},{8,10},{9,11},{10,... | collective-permute-start | bytes 1544 | tf_op jit(solution)/shard_map/ppermute | solution.py:20
  11.8 1.2 %collective-permute-start.4 = (f32[1,128]{1,0:T(1,128)S(1)}, f32[1,128]{1,0:T(1,128)S(1)}, u32[]{:S(2)}, u32[]{:S(2)}) collective-permute-start(f32[1,128]{1,0:T(1,128)S(1)} %get-tuple-element.10.mine_ref), channel_id=1, source_target_pairs={{0,8},{8,0},{16,24},{24,16},{1,9},{9,1},{17,25},{25,17},{2,10},{10... | collective-permute-start | bytes 1544 | tf_op jit(solution)/shard_map/ppermute | solution.py:20
  13.0 4.5 %collective-permute-start.6 = (s32[4,64]{1,0:T(4,128)S(1)}, s32[4,64]{1,0:T(4,128)S(1)}, u32[]{:S(2)}, u32[]{:S(2)}) collective-permute-start(s32[4,64]{1,0:T(4,128)S(1)} %get-tuple-element.11.near_ref), channel_id=1, source_target_pairs={{0,4},{1,5},{2,6},{3,7},{4,0},{5,1},{6,2},{7,3},{8,12},{9,13},{10,... | collective-permute-start | bytes 3080 | tf_op jit(solution)/shard_map/ppermute | solution.py:20
  15.6 3.5 %collective-permute-start.7 = (f32[1,128]{1,0:T(1,128)S(1)}, f32[1,128]{1,0:T(1,128)S(1)}, u32[]{:S(2)}, u32[]{:S(2)}) collective-permute-start(f32[1,128]{1,0:T(1,128)S(1)} %get-tuple-element.13.unused.mine_ref), channel_id=1, source_target_pairs={{0,16},{8,24},{16,0},{24,8},{1,17},{9,25},{17,1},{25,9},{2,18},{10... | collective-permute-start | bytes 1544 | tf_op jit(solution)/shard_map/ppermute | solution.py:20

commit v12 on v10

--- a/solution.py
+++ b/solution.py
@@ -40,33 +40,22 @@
     return lax.broadcasted_iota(jnp.int32, shape, dim)
 
 
-def early_kernel(
-    heads_ref, new_ref, ids_ref, kept_ref, head_sq_ref, kept_new_ref, kept_ids_ref, sems
-):
-    head_dev, width = heads_ref.shape
-    tiles = 4
-    tile = head_dev // tiles
-    parts = [pl.ds(i * tile, tile) for i in range(tiles)]
-    copies = [
-        pltpu.make_async_copy(heads_ref.at[part], kept_ref.at[part], sems.at[i])
-        for i, part in enumerate(parts)
-    ]
-    copies += [
-        pltpu.make_async_copy(new_ref, kept_new_ref, sems.at[tiles]),
-        pltpu.make_async_copy(ids_ref, kept_ids_ref, sems.at[tiles + 1]),
-    ]
+def early_kernel(heads_ref, new_ref, ids_ref, kept_ref, kept_new_ref, kept_ids_ref, sems):
+    pairs = [(heads_ref, kept_ref), (new_ref, kept_new_ref), (ids_ref, kept_ids_ref)]
+    copies = [pltpu.make_async_copy(*pair, sems.at[i]) for i, pair in enumerate(pairs)]
     for copy in copies:
         copy.start()
-    for i in range(tiles):
-        copies[i].wait()
-        for first in range(i * tile, (i + 1) * tile, LANES):
-            block = jnp.square(kept_ref[first:first + LANES, :].astype(jnp.float32))
-            folded = block[:, :LANES]
-            for column in range(LANES, width, LANES):
-                folded = folded + block[:, column:column + LANES]
-            head_sq_ref[:, first:first + LANES] = jnp.sum(folded.T, axis=0, keepdims=True)
-    for copy in copies[tiles:]:
+    for copy in copies:
         copy.wait()
+
+
+def squares(block):
+    width = block.shape[1]
+    block = jnp.square(block.astype(jnp.float32))
+    folded = block[:, :LANES]
+    for column in range(LANES, width, LANES):
+        folded = folded + block[:, column:column + LANES]
+    return jnp.sum(folded.T, axis=0, keepdims=True)
 
 
 def listed_rows(ids, me, slots, heads_ref):
@@ -88,7 +77,7 @@
     ).astype(jnp.bfloat16)
 
 
-def crowding(queries, heads_ref, head_sq_ref):
+def crowding(queries, heads_ref):
     head_dev, width = heads_ref.shape
     query_sq = jnp.sum(jnp.square(queries.astype(jnp.float32)), axis=1, keepdims=True)
     total_w = jnp.zeros((queries.shape[0], 1), jnp.float32)
@@ -99,7 +88,10 @@
             queries, heads_ref[start:start + tile, :], (((1,), (1,)), ((), ())),
             preferred_element_type=jnp.float32,
         )
-        head_sq = head_sq_ref[:, start:start + tile]
+        head_sq = jnp.concatenate(
+            [squares(heads_ref[row:row + LANES, :]) for row in range(start, start + tile, LANES)],
+            axis=1,
+        )
         excess = (query_sq + head_sq - 2.0 * dots) * (1.0 / width)
         inverse = 1.0 / (1.0 + excess)
         weight = inverse * inverse
@@ -108,13 +100,12 @@
     return total_w, total_we
 
 
-def crowd_kernel(groups, ids_ref, heads_ref, head_sq_ref, *refs):
-    query_refs, (sums_ref, kept_ids_ref) = refs[:-2], refs[-2:]
-    kept_ids_ref[...] = ids_ref[...]
+def crowd_kernel(groups, unused, heads_ref, *refs):
+    query_refs, sums_ref = refs[:-1], refs[-1]
     here = lax.axis_index("group")
     queries = jnp.concatenate([ref[...] for ref in query_refs], axis=0)
     new_count = queries.shape[0] // groups
-    totals = crowding(queries, heads_ref, head_sq_ref)
+    totals = crowding(queries, heads_ref)
     lane = iota((new_count, LANES), 1)
     row = iota((new_count, LANES), 0)
     line = iota(sums_ref.shape, 0)
@@ -127,6 +118,13 @@
             spread_out = jnp.sum(spread_out, axis=0, keepdims=True)
             sums = sums + jnp.where(line == place // LANES, spread_out, 0.0)
     sums_ref[...] = sums
+
+
+def join_kernel(mine_ref, other_ref, low_ref, high_ref, sums_ref, ids_ref):
+    half = low_ref.shape[0]
+    sums_ref[...] = mine_ref[...] + other_ref[...]
+    ids_ref[:half, :] = low_ref[...]
+    ids_ref[half:, :] = high_ref[...]
 
 
 def gather_kernel(members, slots, near_ref, far_ref, heads_ref, unused, rows_ref, ids_ref):
@@ -227,39 +225,44 @@
 
     partner_ids = from_partner(near_ids, "member", 1)
     others = [from_partner(new_heads, "group", mask) for mask in range(1, groups)]
-    kept, head_sq, new_heads, ids = call(
+    kept, new_heads, ids = call(
         early_kernel,
         (
             jax.ShapeDtypeStruct(heads.shape, heads.dtype),
-            jax.ShapeDtypeStruct((1, head_dev), jnp.float32),
             jax.ShapeDtypeStruct(new_heads.shape, new_heads.dtype),
             jax.ShapeDtypeStruct(near_ids.shape, near_ids.dtype),
         ),
         (in_hbm(heads), in_hbm(new_heads), in_hbm(near_ids)),
         (0, 0),
-        scratch=[pltpu.SemaphoreType.DMA((6,))],
+        scratch=[pltpu.SemaphoreType.DMA((3,))],
         spaces=[HBM, HBM, HBM],
     )
     ids = jnp.concatenate([ids, partner_ids], axis=0)
     lines = 2 * groups * new_count // LANES
     chunks = width // LANES
     extra = -(-PARTS * lines // PACK) * PACK
-    sums, kept_ids = call(
+    sums = call(
         functools.partial(crowd_kernel, groups),
+        jax.ShapeDtypeStruct((lines, LANES), jnp.float32),
+        (ids, kept, new_heads, *others),
+        (0, 0),
+        spaces=[pl.ANY] + [VMEM] * (2 + len(others)),
+    )
+    mask = 2
+    while mask < members // 4:
+        ids = jnp.concatenate([ids, from_partner(ids, "member", mask)], axis=0)
+        mask *= 2
+    sums, ids = call(
+        join_kernel,
         (
-            jax.ShapeDtypeStruct((lines, LANES), jnp.float32),
-            jax.ShapeDtypeStruct(ids.shape, ids.dtype),
+            jax.ShapeDtypeStruct(sums.shape, sums.dtype),
+            jax.ShapeDtypeStruct((2 * mask, near), ids.dtype),
         ),
-        (ids, kept, head_sq, new_heads, *others),
+        (sums, from_partner(sums, "group", 1), ids, from_partner(ids, "member", mask)),
         (0, 0),
     )
+    far_ids = from_partner(ids, "member", 2 * mask)
     mask = 2
-    while mask < members // 2:
-        kept_ids = jnp.concatenate([kept_ids, from_partner(ids, "member", mask)], axis=0)
-        ids = kept_ids
-        mask *= 2
-    far_ids = from_partner(ids, "member", mask)
-    mask = 1
     while mask < groups // 2:
         sums = sums + from_partner(sums, "group", mask)
         mask *= 2

time: 30.7 us -> 30.6 us (level)
  waiting for transfers between devices: 3.1 us -> 2.35 us
  blocking collectives: 10.7 us -> 11.3 us
    ppermute x8, waiting for transfers between devices: 3.1 us -> 2.35 us  [from_partner(): lax.ppermute(value, axis, [(source, source ^ mask) for source in range(co...]
    all_to_all x1, blocking collectives: 10.7 us -> 11.3 us  [per_device(): message = lax.all_to_all(message, 'member', 0, 0, tiled=True)]
    pallas_call x5 -> x6, Pallas kernels: 5.29 us -> 5.35 us  [call(): pl.pallas_call(body, out_shape=shapes, in_specs=[pl.BlockSpec(memory_spac...]
  transfers between devices with their start and end apart: 8 -> 8, of which waited for: 3 -> 4; matrix products, arithmetic and copies ran while one was open for 0% -> 0% of each run, Pallas kernels for 13% -> 14%
where the time goes in v12:
time: 30.6 us; the launch traced here: 30.4 us
  blocking collectives  11.3 us (37%)
  starting transfers between devices  10.7 us (35%)
  Pallas kernels  5.35 us (17%)
  waiting for transfers between devices  2.35 us (8%)
  between operations  0.7 us (2%)
    all_to_all x1, blocking collectives, per_device(): message = lax.all_to_all(message, 'member', 0, 0, tiled=True)  11.3 us
    ppermute x8, starting transfers between devices, from_partner(): lax.ppermute(value, axis, [(source, source ^ mask) for source in range(co...  10.7 us
    pallas_call x6, Pallas kernels, call(): pl.pallas_call(body, out_shape=shapes, in_specs=[pl.BlockSpec(memory_spac...  5.35 us
    ppermute x8, waiting for transfers between devices, from_partner(): lax.ppermute(value, axis, [(source, source ^ mask) for source in range(co...  2.35 us
  transfers between devices with their start and end apart: 8, of which 4 were waited for; matrix products, arithmetic and copies ran while one was open for 0% of the time, Pallas kernels for 14%

profile of v12, /device:TPU:0, one launch (start us, length us, event | category | flops | bytes accessed | tf_op | source)
XLA Modules:
  0.0 30.4 jit_solution(10392378440657717637)
XLA Ops:
  0.6 3.0 %collective-permute-start = (s32[1,64]{1,0:T(1,128)}, s32[1,64]{1,0:T(1,128)S(1)}, u32[]{:S(2)}, u32[]{:S(2)}) collective-permute-start(s32[1,64]{1,0:T(1,128)} %ids_ref.3), channel_id=1, source_target_pairs={{0,1},{1,0},{2,3},{3,2},{4,5},{5,4},{6,7},{7,6},{8,9},{9,8},{10,11... | collective-permute-start | bytes 776 | tf_op jit(solution)/shard_map/ppermute | solution.py:20
  3.6 0.0 collective-permute-start.1
  3.6 1.5 %collective-permute-start.2 = (bf16[16,768]{1,0:T(8,128)(2,1)}, bf16[16,768]{1,0:T(8,128)(2,1)S(1)}, u32[]{:S(2)}, u32[]{:S(2)}) collective-permute-start(bf16[16,768]{1,0:T(8,128)(2,1)} %new_ref.1), channel_id=1, source_target_pairs={{0,16},{8,24},{16,0},{24,8},{1,17},{9,25},{17,1},{25,9},{2,18},{10... | collective-permute-start | bytes 73736 | tf_op jit(solution)/shard_map/ppermute | solution.py:20
  5.2 0.3 %collective-permute-start.3 = (bf16[16,768]{1,0:T(8,128)(2,1)}, bf16[16,768]{1,0:T(8,128)(2,1)S(1)}, u32[]{:S(2)}, u32[]{:S(2)}) collective-permute-start(bf16[16,768]{1,0:T(8,128)(2,1)} %new_ref.1), channel_id=1, source_target_pairs={{0,24},{8,16},{16,8},{24,0},{1,25},{9,17},{17,9},{25,1},{2,26},{10... | collective-permute-start | bytes 73736 | tf_op jit(solution)/shard_map/ppermute | solution.py:20
  5.5 1.9 %shard_map.67 = (bf16[2048,768]{1,0:T(8,128)(2,1)S(1)}, bf16[16,768]{1,0:T(8,128)(2,1)S(1)}, s32[1,64]{1,0:T(1,128)S(1)}) custom-call(bf16[2048,768]{1,0:T(8,128)(2,1)} %heads_ref.1, bf16[16,768]{1,0:T(8,128)(2,1)} %new_ref.1, s32[1,64]{1,0:T(1,128)} %ids_ref.3), custom_call_target="tpu_custom_call" | custom-call | tf_op jit(solution)/shard_map/pallas_call | solution.py:28
  7.4 0.0 collective-permute-done
  7.4 1.6 %collective-permute-start.5 = (s32[2,64]{1,0:T(2,128)S(1)}, s32[2,64]{1,0:T(2,128)S(1)}, u32[]{:S(2)}, u32[]{:S(2)}) collective-permute-start(s32[2,64]{1,0:T(2,128)S(1)} %pad_add_fusion.unused.low_ref), channel_id=1, source_target_pairs={{0,2},{1,3},{2,0},{3,1},{4,6},{5,7},{6,4},{7,5},{8,10},{9,11},{10,... | collective-permute-start | bytes 1544 | tf_op jit(solution)/shard_map/ppermute | solution.py:20
  9.1 0.0 collective-permute-done.1.refs_1_
  9.1 0.0 collective-permute-done.2.refs_2_
  9.1 0.0 collective-permute-done.3.refs_3_
  9.1 0.0 copy-start
  9.1 0.0 copy-start.1
  9.1 1.5 %shard_map.68.mine_ref = f32[1,128]{1,0:T(1,128)S(1)} custom-call(s32[2,64]{1,0:T(2,128)S(1)} %pad_add_fusion.unused.low_ref, bf16[2048,768]{1,0:T(8,128)(2,1)S(1)} %get-tuple-element.12.heads_ref, bf16[16,768]{1,0:T(8,128)(2,1)S(1)} %get-tuple-element.13.refs_0_, bf16[16,768]{1,0:T(8,128)(2,1)S(1)} %collective-permute-done.1.refs_1_, ...), custom_call_target="tpu_custom_call" | custom-call | tf_op jit(solution)/shard_map/pallas_call | solution.py:28
  10.6 0.1 collective-permute-start.4
  10.7 0.4 %collective-permute-done.5.high_ref = s32[2,64]{1,0:T(2,128)S(1)} collective-permute-done((s32[2,64]{1,0:T(2,128)S(1)}, s32[2,64]{1,0:T(2,128)S(1)}, u32[]{:S(2)}, u32[]{:S(2)}) %collective-permute-start.5) | collective-permute-done | bytes 544 | tf_op jit(solution)/shard_map/ppermute | solution.py:20
  11.1 0.7 %collective-permute-done.4.other_ref = f32[1,128]{1,0:T(1,128)S(1)} collective-permute-done((f32[1,128]{1,0:T(1,128)S(1)}, f32[1,128]{1,0:T(1,128)S(1)}, u32[]{:S(2)}, u32[]{:S(2)}) %collective-permute-start.4) | collective-permute-done | bytes 544 | tf_op jit(solution)/shard_map/ppermute | solution.py:20
  11.8 2.6 %collective-permute-start.6 = (s32[4,64]{1,0:T(4,128)S(1)}, s32[4,64]{1,0:T(4,128)S(1)}, u32[]{:S(2)}, u32[]{:S(2)}) collective-permute-start(s32[4,64]{1,0:T(4,128)S(1)} %get-tuple-element.14.near_ref), channel_id=1, source_target_pairs={{0,4},{1,5},{2,6},{3,7},{4,0},{5,1},{6,2},{7,3},{8,12},{9,13},{10,... | collective-permute-start | bytes 3080 | tf_op jit(solution)/shard_map/ppermute | solution.py:20
  14.4 1.5 %collective-permute-start.7 = (f32[1,128]{1,0:T(1,128)S(1)}, f32[1,128]{1,0:T(1,128)S(1)}, u32[]{:S(2)}, u32[]{:S(2)}) collective-permute-start(f32[1,128]{1,0:T(1,128)S(1)} %get-tuple-element.15.unused.mine_ref), channel_id=1, source_target_pairs={{0,16},{8,24},{16,0},{24,8},{1,17},{9,25},{17,1},{25,9},{2,18},{10... | collective-permute-start | bytes 1544 | tf_op jit(solution)/shard_map/ppermute | solution.py:20
  15.9 0.4 %collective-permute-done.6.far_ref = s32[4,64]{1,0:T(4,128)S(1)} collective-permute-done((s32[4,64]{1,0:T(4,128)S(1)}, s32[4,64]{1,0:T(4,128)S(1)}, u32[]{:S(2)}, u32[]{:S(2)}) %collective-permute-start.6) | collective-permute-done | bytes 1056 | tf_op jit(solution)/shard_map/ppermute | solution.py:20
  16.3 0.8 %shard_map.70.rows_ref = bf16[128,768]{1,0:T(8,128)(2,1)S(1)} custom-call(s32[4,64]{1,0:T(4,128)S(1)} %get-tuple-element.14.near_ref, s32[4,64]{1,0:T(4,128)S(1)} %collective-permute-done.6.far_ref, bf16[2048,768]{1,0:T(8,128)(2,1)S(1)} %get-tuple-element.12.heads_ref, f32[1,128]{1,0:T(1,128)S(1)} %get-tuple-element.15.unused.mine_ref), custom_call_target="tpu_custom_call" | custom-call | flops 402653184 | bytes 3145728 | tf_op jit(solution)/shard_map/pallas_call | solution.py:28
  17.1 0.9 %collective-permute-done.7.other_ref = f32[1,128]{1,0:T(1,128)S(1)} collective-permute-done((f32[1,128]{1,0:T(1,128)S(1)}, f32[1,128]{1,0:T(1,128)S(1)}, u32[]{:S(2)}, u32[]{:S(2)}) %collective-permute-start.7) | collective-permute-done | bytes 544 | tf_op jit(solution)/shard_map/ppermute | solution.py:20
  18.0 11.3 %all_to_all.5.listed_ref = bf16[8,112,128]{2,1,0:T(8,128)(2,1)S(1)} all-to-all(bf16[8,112,128]{2,1,0:T(8,128)(2,1)S(1)} %shard_map.71), channel_id=1, replica_groups=mesh['group'=4,'member'=8] {'member'}, dimensions={0} | all-to-all | bytes 458752 | tf_op jit(solution)/shard_map/all_to_all | solution.py:283
  29.3 0.0 copy-done
  29.3 0.0 copy-done.1
  29.3 1.1 %shard_map.72 = (f32[1,16]{1,0:T(1,128)}, f32[1,16]{1,0:T(1,128)}, f32[1,64,128]{2,1,0:T(8,128)}) custom-call(s32[1,64]{1,0:T(1,128)S(1)} %copy-done.1, bf16[8,112,128]{2,1,0:T(8,128)(2,1)S(1)} %all_to_all.5.listed_ref, bf16[1,128,768]{2,1,0:T(8,128)(2,1)S(1)} %copy-done), custom_call_target="tpu_custom_call" | custom-call | flops 25165824 | bytes 393216 | tf_op jit(solution)/shard_map/pallas_call | solution.py:28
  (3 shorter events, 0.1 us)
Async XLA Ops:
  0.6 6.8 %collective-permute-start = (s32[1,64]{1,0:T(1,128)}, s32[1,64]{1,0:T(1,128)S(1)}, u32[]{:S(2)}, u32[]{:S(2)}) collective-permute-start(s32[1,64]{1,0:T(1,128)} %ids_ref.3), channel_id=1, source_target_pairs={{0,1},{1,0},{2,3},{3,2},{4,5},{5,4},{6,7},{7,6},{8,9},{9,8},{10,11... | collective-permute-start | bytes 776 | tf_op jit(solution)/shard_map/ppermute | solution.py:20
  3.6 5.5 %collective-permute-start.1 = (bf16[16,768]{1,0:T(8,128)(2,1)}, bf16[16,768]{1,0:T(8,128)(2,1)S(1)}, u32[]{:S(2)}, u32[]{:S(2)}) collective-permute-start(bf16[16,768]{1,0:T(8,128)(2,1)} %new_ref.1), channel_id=1, source_target_pairs={{0,8},{8,0},{16,24},{24,16},{1,9},{9,1},{17,25},{25,17},{2,10},{10... | collective-permute-start | bytes 73736 | tf_op jit(solution)/shard_map/ppermute | solution.py:20
  3.6 5.5 %collective-permute-start.2 = (bf16[16,768]{1,0:T(8,128)(2,1)}, bf16[16,768]{1,0:T(8,128)(2,1)S(1)}, u32[]{:S(2)}, u32[]{:S(2)}) collective-permute-start(bf16[16,768]{1,0:T(8,128)(2,1)} %new_ref.1), channel_id=1, source_target_pairs={{0,16},{8,24},{16,0},{24,8},{1,17},{9,25},{17,1},{25,9},{2,18},{10... | collective-permute-start | bytes 73736 | tf_op jit(solution)/shard_map/ppermute | solution.py:20
  5.2 3.9 %collective-permute-start.3 = (bf16[16,768]{1,0:T(8,128)(2,1)}, bf16[16,768]{1,0:T(8,128)(2,1)S(1)}, u32[]{:S(2)}, u32[]{:S(2)}) collective-permute-start(bf16[16,768]{1,0:T(8,128)(2,1)} %new_ref.1), channel_id=1, source_target_pairs={{0,24},{8,16},{16,8},{24,0},{1,25},{9,17},{17,9},{25,1},{2,26},{10... | collective-permute-start | bytes 73736 | tf_op jit(solution)/shard_map/ppermute | solution.py:20
  7.4 3.6 %collective-permute-start.5 = (s32[2,64]{1,0:T(2,128)S(1)}, s32[2,64]{1,0:T(2,128)S(1)}, u32[]{:S(2)}, u32[]{:S(2)}) collective-permute-start(s32[2,64]{1,0:T(2,128)S(1)} %pad_add_fusion.unused.low_ref), channel_id=1, source_target_pairs={{0,2},{1,3},{2,0},{3,1},{4,6},{5,7},{6,4},{7,5},{8,10},{9,11},{10,... | collective-permute-start | bytes 1544 | tf_op jit(solution)/shard_map/ppermute | solution.py:20
  9.1 20.2 %copy-start = (bf16[1,128,768]{2,1,0:T(8,128)(2,1)S(1)}, bf16[1,128,768]{2,1,0:T(8,128)(2,1)}, u32[]{:S(2)}) copy-start(bf16[1,128,768]{2,1,0:T(8,128)(2,1)} %vectors_ref.1) | copy-start | bytes 589828
  9.1 20.2 %copy-start.1 = (s32[1,64]{1,0:T(1,128)S(1)}, s32[1,64]{1,0:T(1,128)}, u32[]{:S(2)}) copy-start(s32[1,64]{1,0:T(1,128)} %ids_ref.3) | copy-start | bytes 772
  10.6 1.2 %collective-permute-start.4 = (f32[1,128]{1,0:T(1,128)S(1)}, f32[1,128]{1,0:T(1,128)S(1)}, u32[]{:S(2)}, u32[]{:S(2)}) collective-permute-start(f32[1,128]{1,0:T(1,128)S(1)} %shard_map.68.mine_ref), channel_id=1, source_target_pairs={{0,8},{8,0},{16,24},{24,16},{1,9},{9,1},{17,25},{25,17},{2,10},{10... | collective-permute-start | bytes 1544 | tf_op jit(solution)/shard_map/ppermute | solution.py:20
  11.8 4.5 %collective-permute-start.6 = (s32[4,64]{1,0:T(4,128)S(1)}, s32[4,64]{1,0:T(4,128)S(1)}, u32[]{:S(2)}, u32[]{:S(2)}) collective-permute-start(s32[4,64]{1,0:T(4,128)S(1)} %get-tuple-element.14.near_ref), channel_id=1, source_target_pairs={{0,4},{1,5},{2,6},{3,7},{4,0},{5,1},{6,2},{7,3},{8,12},{9,13},{10,... | collective-permute-start | bytes 3080 | tf_op jit(solution)/shard_map/ppermute | solution.py:20
  14.4 3.5 %collective-permute-start.7 = (f32[1,128]{1,0:T(1,128)S(1)}, f32[1,128]{1,0:T(1,128)S(1)}, u32[]{:S(2)}, u32[]{:S(2)}) collective-permute-start(f32[1,128]{1,0:T(1,128)S(1)} %get-tuple-element.15.unused.mine_ref), channel_id=1, source_target_pairs={{0,16},{8,24},{16,0},{24,8},{1,17},{9,25},{17,1},{25,9},{2,18},{10... | collective-permute-start | bytes 1544 | tf_op jit(solution)/shard_map/ppermute | solution.py:20

commit v13 on v12

--- a/solution.py
+++ b/solution.py
@@ -18,6 +18,20 @@
 def from_partner(value, axis, mask):
     count = lax.axis_size(axis)
     return lax.ppermute(value, axis, [(source, source ^ mask) for source in range(count)])
+
+
+def on_odd(value, mask):
+    groups, members = lax.axis_size("group"), lax.axis_size("member")
+    pairs = [
+        (group * members + member, group * members + (member ^ mask))
+        for group in range(1, groups, 2) for member in range(members)
+    ]
+    return lax.ppermute(value, ("group", "member"), pairs)
+
+
+def across_core(value, first):
+    groups = lax.axis_size("group")
+    return lax.ppermute(value, "group", [(group, group ^ 1) for group in range(first, groups, 2)])
 
 
 def in_hbm(value):
@@ -40,8 +54,19 @@
     return lax.broadcasted_iota(jnp.int32, shape, dim)
 
 
+def stage_kernel(ids_ref, kept_ref, sem):
+    copy = pltpu.make_async_copy(ids_ref, kept_ref, sem)
+    copy.start()
+    copy.wait()
+
+
 def early_kernel(heads_ref, new_ref, ids_ref, kept_ref, kept_new_ref, kept_ids_ref, sems):
-    pairs = [(heads_ref, kept_ref), (new_ref, kept_new_ref), (ids_ref, kept_ids_ref)]
+    kept_ids_ref[...] = ids_ref[...]
+    tiles = sems.shape[0] - 1
+    tile = heads_ref.shape[0] // tiles
+    parts = [pl.ds(i * tile, tile) for i in range(tiles)]
+    pairs = [(heads_ref.at[part], kept_ref.at[part]) for part in parts]
+    pairs.append((new_ref, kept_new_ref))
     copies = [pltpu.make_async_copy(*pair, sems.at[i]) for i, pair in enumerate(pairs)]
     for copy in copies:
         copy.start()
@@ -127,23 +152,31 @@
     ids_ref[half:, :] = high_ref[...]
 
 
-def gather_kernel(members, slots, near_ref, far_ref, heads_ref, unused, rows_ref, ids_ref):
+def joined(mine, other, low, high):
+    shapes = (
+        jax.ShapeDtypeStruct(mine.shape, mine.dtype),
+        jax.ShapeDtypeStruct((2 * low.shape[0], low.shape[1]), low.dtype),
+    )
+    return call(join_kernel, shapes, (mine, other, low, high), (0, 0))
+
+
+def gather_kernel(members, slots, mine_ref, handed_ref, heads_ref, rows_ref):
     me = lax.axis_index("member")
-    half = members // 2
-    ids_ref[:half, :] = near_ref[...]
-    ids_ref[half:, :] = far_ref[...]
-    ids = jnp.concatenate([ids_ref[pl.ds(me ^ member, 1), :] for member in range(members)], axis=0)
+    odd = lax.axis_index("group") % 2 == 1
+    mine = [mine_ref[pl.ds(2 * (me ^ member), 1), :] for member in range(members)]
+    handed = [handed_ref[pl.ds(2 * (me ^ member) + 1, 1), :] for member in range(members)]
+    ids = jnp.where(odd, jnp.concatenate(mine, axis=0), jnp.concatenate(handed, axis=0))
     rows_ref[...] = listed_rows(ids, me, slots, heads_ref)
 
 
-def pack_kernel(members, slots, rows_ref, mine_ref, other_ref, out_ref):
+def pack_kernel(members, slots, rows_ref, sums_ref, out_ref):
     chunks = rows_ref.shape[1] // LANES
     for member in range(members):
         for chunk in range(chunks):
             out_ref[member, chunk * slots:(chunk + 1) * slots, :] = rows_ref[
                 member * slots:(member + 1) * slots, chunk * LANES:(chunk + 1) * LANES
             ]
-    sums = mine_ref[...] + other_ref[...]
+    sums = sums_ref[...]
     coded = []
     for unused in range(PARTS):
         coded.append(sums.astype(jnp.bfloat16).astype(jnp.float32))
@@ -223,21 +256,30 @@
     most = 2 * near // members
     slots = -(-most // PACK) * PACK
 
-    partner_ids = from_partner(near_ids, "member", 1)
+    neighbour_ids = across_core(near_ids, 0)
     others = [from_partner(new_heads, "group", mask) for mask in range(1, groups)]
-    kept, new_heads, ids = call(
+    ids = call(
+        stage_kernel,
+        jax.ShapeDtypeStruct(near_ids.shape, near_ids.dtype),
+        (in_hbm(near_ids),),
+        (0, 0),
+        scratch=[pltpu.SemaphoreType.DMA],
+        spaces=[HBM],
+    )
+    ids = jnp.concatenate([ids, neighbour_ids], axis=0)
+    kept, new_heads, kept_ids = call(
         early_kernel,
         (
             jax.ShapeDtypeStruct(heads.shape, heads.dtype),
             jax.ShapeDtypeStruct(new_heads.shape, new_heads.dtype),
-            jax.ShapeDtypeStruct(near_ids.shape, near_ids.dtype),
+            jax.ShapeDtypeStruct(ids.shape, ids.dtype),
         ),
-        (in_hbm(heads), in_hbm(new_heads), in_hbm(near_ids)),
-        (0, 0),
-        scratch=[pltpu.SemaphoreType.DMA((3,))],
-        spaces=[HBM, HBM, HBM],
-    )
-    ids = jnp.concatenate([ids, partner_ids], axis=0)
+        (in_hbm(heads), in_hbm(new_heads), ids),
+        (0, heads.size * 4),
+        scratch=[pltpu.SemaphoreType.DMA((9,))],
+        spaces=[HBM, HBM, VMEM],
+    )
+    ids = jnp.concatenate([kept_ids, on_odd(ids, 1)], axis=0)
     lines = 2 * groups * new_count // LANES
     chunks = width // LANES
     extra = -(-PARTS * lines // PACK) * PACK
@@ -250,35 +292,26 @@
     )
     mask = 2
     while mask < members // 4:
-        ids = jnp.concatenate([ids, from_partner(ids, "member", mask)], axis=0)
+        ids = jnp.concatenate([ids, on_odd(ids, mask)], axis=0)
         mask *= 2
-    sums, ids = call(
-        join_kernel,
-        (
-            jax.ShapeDtypeStruct(sums.shape, sums.dtype),
-            jax.ShapeDtypeStruct((2 * mask, near), ids.dtype),
-        ),
-        (sums, from_partner(sums, "group", 1), ids, from_partner(ids, "member", mask)),
-        (0, 0),
-    )
-    far_ids = from_partner(ids, "member", 2 * mask)
+    sums, ids = joined(sums, from_partner(sums, "group", 1), ids, on_odd(ids, mask))
+    far_ids = on_odd(ids, 2 * mask)
     mask = 2
     while mask < groups // 2:
         sums = sums + from_partner(sums, "group", mask)
         mask *= 2
+    sums, ids = joined(sums, from_partner(sums, "group", mask), ids, far_ids)
     rows = call(
         functools.partial(gather_kernel, members, slots),
         jax.ShapeDtypeStruct((members * slots, width), jnp.bfloat16),
-        (ids, far_ids, kept, sums),
-        (2 * members * slots * head_dev * width, heads.size * 2),
-        scratch=[pltpu.VMEM((members, near), jnp.int32)],
-        spaces=[VMEM, VMEM, VMEM, pl.ANY],
+        (ids, across_core(ids, 1), kept),
+        (0, 0),
     )
     message = call(
         functools.partial(pack_kernel, members, slots),
         jax.ShapeDtypeStruct((members, chunks * slots + extra, LANES), jnp.bfloat16),
-        (rows, sums, from_partner(sums, "group", mask)),
-        (0, members * slots * width * 4),
+        (rows, sums),
+        (0, 0),
     )
     message = lax.all_to_all(message, "member", 0, 0, tiled=True)
 

time: 30.6 us -> 40.3 us (1.32)
  waiting for transfers between devices: 2.35 us -> 7.36 us
  starting transfers between devices: 10.7 us -> 14.5 us
  Pallas kernels: 5.35 us -> 5.99 us
    ppermute x0 -> x5, starting transfers between devices: none -> 5.61 us  [the longest x2 3.65 us: across_core(): lax.ppermute(value, 'group', [(group, group ^ 1) for group in range(first...]
    ppermute x0 -> x5, waiting for transfers between devices: none -> 3.62 us  [the longest x2 3.61 us: across_core(): lax.ppermute(value, 'group', [(group, group ^ 1) for group in range(first...]
    ppermute x8 -> x5, starting transfers between devices: 10.7 us -> 8.86 us  [from_partner(): lax.ppermute(value, axis, [(source, source ^ mask) for source in range(co...]
    ppermute x8 -> x5, waiting for transfers between devices: 2.35 us -> 3.74 us  [from_partner(): lax.ppermute(value, axis, [(source, source ^ mask) for source in range(co...]
    pallas_call x6 -> x8, Pallas kernels: 5.35 us -> 5.99 us  [call(): pl.pallas_call(body, out_shape=shapes, in_specs=[pl.BlockSpec(memory_spac...]
  transfers between devices with their start and end apart: 8 -> 10, of which waited for: 4 -> 5; matrix products, arithmetic and copies ran while one was open for 0% -> 0% of each run, Pallas kernels for 14% -> 10%
where the time goes in v13:
time: 40.3 us; the launch traced here: 40 us
  starting transfers between devices  14.5 us (36%)
  blocking collectives  11.5 us (29%)
  waiting for transfers between devices  7.36 us (18%)
  Pallas kernels  5.99 us (15%)
  between operations  0.74 us (2%)
    all_to_all x1, blocking collectives, per_device(): message = lax.all_to_all(message, 'member', 0, 0, tiled=True)  11.5 us
    ppermute x5, starting transfers between devices, from_partner(): lax.ppermute(value, axis, [(source, source ^ mask) for source in range(co...  8.86 us
    pallas_call x8, Pallas kernels, call(): pl.pallas_call(body, out_shape=shapes, in_specs=[pl.BlockSpec(memory_spac...  5.99 us
    ppermute x5, waiting for transfers between devices, from_partner(): lax.ppermute(value, axis, [(source, source ^ mask) for source in range(co...  3.74 us
    ppermute x2, starting transfers between devices, across_core(): lax.ppermute(value, 'group', [(group, group ^ 1) for group in range(first...  3.65 us
    ppermute x2, waiting for transfers between devices, across_core(): lax.ppermute(value, 'group', [(group, group ^ 1) for group in range(first...  3.61 us
    ppermute x3, starting transfers between devices, on_odd(): return lax.ppermute(value, ('group', 'member'), pairs)  1.96 us
  transfers between devices with their start and end apart: 10, of which 5 were waited for; matrix products, arithmetic and copies ran while one was open for 0% of the time, Pallas kernels for 10%

profile of v13, /device:TPU:0, one launch (start us, length us, event | category | flops | bytes accessed | tf_op | source)
XLA Modules:
  0.0 40.0 jit_solution(4241002090464974110)
XLA Ops:
  0.6 2.4 %collective-permute-start = (s32[1,64]{1,0:T(1,128)}, s32[1,64]{1,0:T(1,128)S(1)}, u32[]{:S(2)}, u32[]{:S(2)}) collective-permute-start(s32[1,64]{1,0:T(1,128)} %ids_ref.3), channel_id=1, source_target_pairs={{0,8},{16,24},{1,9},{17,25},{2,10},{18,26},{3,11},{19,27},{4,12},{... | collective-permute-start | bytes 776 | tf_op jit(solution)/shard_map/ppermute | solution.py:34
  3.0 0.7 %shard_map.67 = s32[1,64]{1,0:T(1,128)S(1)} custom-call(s32[1,64]{1,0:T(1,128)} %ids_ref.3), custom_call_target="tpu_custom_call" | custom-call | tf_op jit(solution)/shard_map/pallas_call | solution.py:42
  3.7 0.3 collective-permute-done
  3.9 0.6 %collective-permute-start.1 = (s32[2,64]{1,0:T(2,128)S(1)}, s32[2,64]{1,0:T(2,128)S(1)}, u32[]{:S(2)}, u32[]{:S(2)}) collective-permute-start(s32[2,64]{1,0:T(2,128)S(1)} %pad_add_fusion.1.ids_ref), channel_id=1, source_target_pairs={{8,9},{9,8},{10,11},{11,10},{12,13},{13,12},{14,15},{15,14},{24,25... | collective-permute-start | bytes 1544 | tf_op jit(solution)/shard_map/ppermute | solution.py:29
  4.6 3.7 %collective-permute-start.2 = (bf16[16,768]{1,0:T(8,128)(2,1)}, bf16[16,768]{1,0:T(8,128)(2,1)S(1)}, u32[]{:S(2)}, u32[]{:S(2)}) collective-permute-start(bf16[16,768]{1,0:T(8,128)(2,1)} %new_ref.1), channel_id=1, source_target_pairs={{0,8},{8,0},{16,24},{24,16},{1,9},{9,1},{17,25},{25,17},{2,10},{10... | collective-permute-start | bytes 73736 | tf_op jit(solution)/shard_map/ppermute | solution.py:20
  8.3 1.2 %collective-permute-start.4 = (bf16[16,768]{1,0:T(8,128)(2,1)}, bf16[16,768]{1,0:T(8,128)(2,1)S(1)}, u32[]{:S(2)}, u32[]{:S(2)}) collective-permute-start(bf16[16,768]{1,0:T(8,128)(2,1)} %new_ref.1), channel_id=1, source_target_pairs={{0,24},{8,16},{16,8},{24,0},{1,25},{9,17},{17,9},{25,1},{2,26},{10... | collective-permute-start | bytes 73736 | tf_op jit(solution)/shard_map/ppermute | solution.py:20
  9.5 0.5 %collective-permute-start.3 = (bf16[16,768]{1,0:T(8,128)(2,1)}, bf16[16,768]{1,0:T(8,128)(2,1)S(1)}, u32[]{:S(2)}, u32[]{:S(2)}) collective-permute-start(bf16[16,768]{1,0:T(8,128)(2,1)} %new_ref.1), channel_id=1, source_target_pairs={{0,16},{8,24},{16,0},{24,8},{1,17},{9,25},{17,1},{25,9},{2,18},{10... | collective-permute-start | bytes 73736 | tf_op jit(solution)/shard_map/ppermute | solution.py:20
  10.0 1.9 %shard_map.68 = (bf16[2048,768]{1,0:T(8,128)(2,1)S(1)}, bf16[16,768]{1,0:T(8,128)(2,1)S(1)}, s32[2,64]{1,0:T(2,128)S(1)}) custom-call(bf16[2048,768]{1,0:T(8,128)(2,1)} %heads_ref.1, bf16[16,768]{1,0:T(8,128)(2,1)} %new_ref.1, s32[2,64]{1,0:T(2,128)S(1)} %pad_add_fusion.1.ids_ref), custom_call_target="tpu_custom_call" | custom-call | bytes 6291456 | tf_op jit(solution)/shard_map/pallas_call | solution.py:42
  11.9 0.0 collective-permute-done.1
  11.9 0.7 %collective-permute-start.6 = (s32[4,64]{1,0:T(4,128)S(1)}, s32[4,64]{1,0:T(4,128)S(1)}, u32[]{:S(2)}, u32[]{:S(2)}) collective-permute-start(s32[4,64]{1,0:T(4,128)S(1)} %pad_add_fusion.unused.low_ref), channel_id=1, source_target_pairs={{8,10},{9,11},{10,8},{11,9},{12,14},{13,15},{14,12},{15,13},{24,26... | collective-permute-start | bytes 3080 | tf_op jit(solution)/shard_map/ppermute | solution.py:29
  12.6 0.0 collective-permute-done.2.refs_1_
  12.6 0.0 collective-permute-done.4.refs_3_
  12.6 0.9 %collective-permute-done.3.refs_2_ = bf16[16,768]{1,0:T(8,128)(2,1)S(1)} collective-permute-done((bf16[16,768]{1,0:T(8,128)(2,1)}, bf16[16,768]{1,0:T(8,128)(2,1)S(1)}, u32[]{:S(2)}, u32[]{:S(2)}) %collective-permute-start.3) | collective-permute-done | bytes 24608 | tf_op jit(solution)/shard_map/ppermute | solution.py:20
  13.5 0.0 copy-start
  13.5 0.0 copy-start.1
  13.5 1.5 %shard_map.69.mine_ref = f32[1,128]{1,0:T(1,128)S(1)} custom-call(s32[4,64]{1,0:T(4,128)S(1)} %pad_add_fusion.unused.low_ref, bf16[2048,768]{1,0:T(8,128)(2,1)S(1)} %get-tuple-element.14.heads_ref, bf16[16,768]{1,0:T(8,128)(2,1)S(1)} %get-tuple-element.15.refs_0_, bf16[16,768]{1,0:T(8,128)(2,1)S(1)} %collective-permute-done.2.refs_1_, ...), custom_call_target="tpu_custom_call" | custom-call | tf_op jit(solution)/shard_map/pallas_call | solution.py:42
  15.0 1.9 %collective-permute-start.5 = (f32[1,128]{1,0:T(1,128)S(1)}, f32[1,128]{1,0:T(1,128)S(1)}, u32[]{:S(2)}, u32[]{:S(2)}) collective-permute-start(f32[1,128]{1,0:T(1,128)S(1)} %shard_map.69.mine_ref), channel_id=1, source_target_pairs={{0,8},{8,0},{16,24},{24,16},{1,9},{9,1},{17,25},{25,17},{2,10},{10... | collective-permute-start | bytes 1544 | tf_op jit(solution)/shard_map/ppermute | solution.py:20
  16.9 0.0 collective-permute-done.6.high_ref
  16.9 0.8 %collective-permute-done.5.other_ref = f32[1,128]{1,0:T(1,128)S(1)} collective-permute-done((f32[1,128]{1,0:T(1,128)S(1)}, f32[1,128]{1,0:T(1,128)S(1)}, u32[]{:S(2)}, u32[]{:S(2)}) %collective-permute-start.5) | collective-permute-done | bytes 544 | tf_op jit(solution)/shard_map/ppermute | solution.py:20
  17.7 0.6 %collective-permute-start.8 = (s32[8,64]{1,0:T(8,128)S(1)}, s32[8,64]{1,0:T(8,128)S(1)}, u32[]{:S(2)}, u32[]{:S(2)}) collective-permute-start(s32[8,64]{1,0:T(8,128)S(1)} %get-tuple-element.17.low_ref), channel_id=1, source_target_pairs={{8,12},{9,13},{10,14},{11,15},{12,8},{13,9},{14,10},{15,11},{24,28... | collective-permute-start | bytes 6152 | tf_op jit(solution)/shard_map/ppermute | solution.py:29
  18.4 1.6 %collective-permute-start.7 = (f32[1,128]{1,0:T(1,128)S(1)}, f32[1,128]{1,0:T(1,128)S(1)}, u32[]{:S(2)}, u32[]{:S(2)}) collective-permute-start(f32[1,128]{1,0:T(1,128)S(1)} %get-tuple-element.16.mine_ref), channel_id=1, source_target_pairs={{0,16},{8,24},{16,0},{24,8},{1,17},{9,25},{17,1},{25,9},{2,18},{10... | collective-permute-start | bytes 1544 | tf_op jit(solution)/shard_map/ppermute | solution.py:20
  19.9 2.0 %collective-permute-done.7.other_ref = f32[1,128]{1,0:T(1,128)S(1)} collective-permute-done((f32[1,128]{1,0:T(1,128)S(1)}, f32[1,128]{1,0:T(1,128)S(1)}, u32[]{:S(2)}, u32[]{:S(2)}) %collective-permute-start.7) | collective-permute-done | bytes 544 | tf_op jit(solution)/shard_map/ppermute | solution.py:20
  22.0 0.0 collective-permute-done.8.high_ref
  22.0 1.3 %collective-permute-start.9 = (s32[16,64]{1,0:T(8,128)S(1)}, s32[16,64]{1,0:T(8,128)S(1)}, u32[]{:S(2)}, u32[]{:S(2)}) collective-permute-start(s32[16,64]{1,0:T(8,128)S(1)} %get-tuple-element.18.mine_ref), channel_id=1, source_target_pairs={{8,0},{24,16},{9,1},{25,17},{10,2},{26,18},{11,3},{27,19},{12,4},{... | collective-permute-start | bytes 12296 | tf_op jit(solution)/shard_map/ppermute | solution.py:34
  23.3 3.3 %collective-permute-done.9.handed_ref = s32[16,64]{1,0:T(8,128)S(1)} collective-permute-done((s32[16,64]{1,0:T(8,128)S(1)}, s32[16,64]{1,0:T(8,128)S(1)}, u32[]{:S(2)}, u32[]{:S(2)}) %collective-permute-start.9) | collective-permute-done | bytes 4128 | tf_op jit(solution)/shard_map/ppermute | solution.py:34
  26.6 0.8 %shard_map.72.rows_ref = bf16[128,768]{1,0:T(8,128)(2,1)S(1)} custom-call(s32[16,64]{1,0:T(8,128)S(1)} %get-tuple-element.18.mine_ref, s32[16,64]{1,0:T(8,128)S(1)} %collective-permute-done.9.handed_ref, bf16[2048,768]{1,0:T(8,128)(2,1)S(1)} %get-tuple-element.14.heads_ref), custom_call_target="tpu_custom_call" | custom-call | tf_op jit(solution)/shard_map/pallas_call | solution.py:42
  27.5 11.5 %all_to_all.5.listed_ref = bf16[8,112,128]{2,1,0:T(8,128)(2,1)S(1)} all-to-all(bf16[8,112,128]{2,1,0:T(8,128)(2,1)S(1)} %shard_map.73), channel_id=1, replica_groups=mesh['group'=4,'member'=8] {'member'}, dimensions={0} | all-to-all | bytes 458752 | tf_op jit(solution)/shard_map/all_to_all | solution.py:316
  38.9 0.0 copy-done
  38.9 0.0 copy-done.1
  38.9 1.1 %shard_map.74 = (f32[1,16]{1,0:T(1,128)}, f32[1,16]{1,0:T(1,128)}, f32[1,64,128]{2,1,0:T(8,128)}) custom-call(s32[1,64]{1,0:T(1,128)S(1)} %copy-done.1, bf16[8,112,128]{2,1,0:T(8,128)(2,1)S(1)} %all_to_all.5.listed_ref, bf16[1,128,768]{2,1,0:T(8,128)(2,1)S(1)} %copy-done), custom_call_target="tpu_custom_call" | custom-call | flops 25165824 | bytes 393216 | tf_op jit(solution)/shard_map/pallas_call | solution.py:42
  (5 shorter events, 0.1 us)
Async XLA Ops:
  0.6 3.3 %collective-permute-start = (s32[1,64]{1,0:T(1,128)}, s32[1,64]{1,0:T(1,128)S(1)}, u32[]{:S(2)}, u32[]{:S(2)}) collective-permute-start(s32[1,64]{1,0:T(1,128)} %ids_ref.3), channel_id=1, source_target_pairs={{0,8},{16,24},{1,9},{17,25},{2,10},{18,26},{3,11},{19,27},{4,12},{... | collective-permute-start | bytes 776 | tf_op jit(solution)/shard_map/ppermute | solution.py:34
  3.9 7.9 %collective-permute-start.1 = (s32[2,64]{1,0:T(2,128)S(1)}, s32[2,64]{1,0:T(2,128)S(1)}, u32[]{:S(2)}, u32[]{:S(2)}) collective-permute-start(s32[2,64]{1,0:T(2,128)S(1)} %pad_add_fusion.1.ids_ref), channel_id=1, source_target_pairs={{8,9},{9,8},{10,11},{11,10},{12,13},{13,12},{14,15},{15,14},{24,25... | collective-permute-start | bytes 1544 | tf_op jit(solution)/shard_map/ppermute | solution.py:29
  4.6 8.0 %collective-permute-start.2 = (bf16[16,768]{1,0:T(8,128)(2,1)}, bf16[16,768]{1,0:T(8,128)(2,1)S(1)}, u32[]{:S(2)}, u32[]{:S(2)}) collective-permute-start(bf16[16,768]{1,0:T(8,128)(2,1)} %new_ref.1), channel_id=1, source_target_pairs={{0,8},{8,0},{16,24},{24,16},{1,9},{9,1},{17,25},{25,17},{2,10},{10... | collective-permute-start | bytes 73736 | tf_op jit(solution)/shard_map/ppermute | solution.py:20
  8.3 4.3 %collective-permute-start.4 = (bf16[16,768]{1,0:T(8,128)(2,1)}, bf16[16,768]{1,0:T(8,128)(2,1)S(1)}, u32[]{:S(2)}, u32[]{:S(2)}) collective-permute-start(bf16[16,768]{1,0:T(8,128)(2,1)} %new_ref.1), channel_id=1, source_target_pairs={{0,24},{8,16},{16,8},{24,0},{1,25},{9,17},{17,9},{25,1},{2,26},{10... | collective-permute-start | bytes 73736 | tf_op jit(solution)/shard_map/ppermute | solution.py:20
  9.5 4.0 %collective-permute-start.3 = (bf16[16,768]{1,0:T(8,128)(2,1)}, bf16[16,768]{1,0:T(8,128)(2,1)S(1)}, u32[]{:S(2)}, u32[]{:S(2)}) collective-permute-start(bf16[16,768]{1,0:T(8,128)(2,1)} %new_ref.1), channel_id=1, source_target_pairs={{0,16},{8,24},{16,0},{24,8},{1,17},{9,25},{17,1},{25,9},{2,18},{10... | collective-permute-start | bytes 73736 | tf_op jit(solution)/shard_map/ppermute | solution.py:20
  11.9 5.0 %collective-permute-start.6 = (s32[4,64]{1,0:T(4,128)S(1)}, s32[4,64]{1,0:T(4,128)S(1)}, u32[]{:S(2)}, u32[]{:S(2)}) collective-permute-start(s32[4,64]{1,0:T(4,128)S(1)} %pad_add_fusion.unused.low_ref), channel_id=1, source_target_pairs={{8,10},{9,11},{10,8},{11,9},{12,14},{13,15},{14,12},{15,13},{24,26... | collective-permute-start | bytes 3080 | tf_op jit(solution)/shard_map/ppermute | solution.py:29
  13.5 25.4 %copy-start = (bf16[1,128,768]{2,1,0:T(8,128)(2,1)S(1)}, bf16[1,128,768]{2,1,0:T(8,128)(2,1)}, u32[]{:S(2)}) copy-start(bf16[1,128,768]{2,1,0:T(8,128)(2,1)} %vectors_ref.1) | copy-start | bytes 589828
  13.5 25.4 %copy-start.1 = (s32[1,64]{1,0:T(1,128)S(1)}, s32[1,64]{1,0:T(1,128)}, u32[]{:S(2)}) copy-start(s32[1,64]{1,0:T(1,128)} %ids_ref.3) | copy-start | bytes 772
  15.0 2.7 %collective-permute-start.5 = (f32[1,128]{1,0:T(1,128)S(1)}, f32[1,128]{1,0:T(1,128)S(1)}, u32[]{:S(2)}, u32[]{:S(2)}) collective-permute-start(f32[1,128]{1,0:T(1,128)S(1)} %shard_map.69.mine_ref), channel_id=1, source_target_pairs={{0,8},{8,0},{16,24},{24,16},{1,9},{9,1},{17,25},{25,17},{2,10},{10... | collective-permute-start | bytes 1544 | tf_op jit(solution)/shard_map/ppermute | solution.py:20
  17.7 4.3 %collective-permute-start.8 = (s32[8,64]{1,0:T(8,128)S(1)}, s32[8,64]{1,0:T(8,128)S(1)}, u32[]{:S(2)}, u32[]{:S(2)}) collective-permute-start(s32[8,64]{1,0:T(8,128)S(1)} %get-tuple-element.17.low_ref), channel_id=1, source_target_pairs={{8,12},{9,13},{10,14},{11,15},{12,8},{13,9},{14,10},{15,11},{24,28... | collective-permute-start | bytes 6152 | tf_op jit(solution)/shard_map/ppermute | solution.py:29
  18.4 3.6 %collective-permute-start.7 = (f32[1,128]{1,0:T(1,128)S(1)}, f32[1,128]{1,0:T(1,128)S(1)}, u32[]{:S(2)}, u32[]{:S(2)}) collective-permute-start(f32[1,128]{1,0:T(1,128)S(1)} %get-tuple-element.16.mine_ref), channel_id=1, source_target_pairs={{0,16},{8,24},{16,0},{24,8},{1,17},{9,25},{17,1},{25,9},{2,18},{10... | collective-permute-start | bytes 1544 | tf_op jit(solution)/shard_map/ppermute | solution.py:20
  22.0 4.6 %collective-permute-start.9 = (s32[16,64]{1,0:T(8,128)S(1)}, s32[16,64]{1,0:T(8,128)S(1)}, u32[]{:S(2)}, u32[]{:S(2)}) collective-permute-start(s32[16,64]{1,0:T(8,128)S(1)} %get-tuple-element.18.mine_ref), channel_id=1, source_target_pairs={{8,0},{24,16},{9,1},{25,17},{10,2},{26,18},{11,3},{27,19},{12,4},{... | collective-permute-start | bytes 12296 | tf_op jit(solution)/shard_map/ppermute | solution.py:34

commit v14 on v10

--- a/solution.py
+++ b/solution.py
@@ -40,9 +40,13 @@
     return lax.broadcasted_iota(jnp.int32, shape, dim)
 
 
-def early_kernel(
-    heads_ref, new_ref, ids_ref, kept_ref, head_sq_ref, kept_new_ref, kept_ids_ref, sems
-):
+def stage_kernel(ids_ref, kept_ref, sem):
+    copy = pltpu.make_async_copy(ids_ref, kept_ref, sem)
+    copy.start()
+    copy.wait()
+
+
+def early_kernel(heads_ref, new_ref, unused, kept_ref, head_sq_ref, kept_new_ref, sems):
     head_dev, width = heads_ref.shape
     tiles = 4
     tile = head_dev // tiles
@@ -51,10 +55,7 @@
         pltpu.make_async_copy(heads_ref.at[part], kept_ref.at[part], sems.at[i])
         for i, part in enumerate(parts)
     ]
-    copies += [
-        pltpu.make_async_copy(new_ref, kept_new_ref, sems.at[tiles]),
-        pltpu.make_async_copy(ids_ref, kept_ids_ref, sems.at[tiles + 1]),
-    ]
+    copies.append(pltpu.make_async_copy(new_ref, kept_new_ref, sems.at[tiles]))
     for copy in copies:
         copy.start()
     for i in range(tiles):
@@ -227,20 +228,27 @@
 
     partner_ids = from_partner(near_ids, "member", 1)
     others = [from_partner(new_heads, "group", mask) for mask in range(1, groups)]
-    kept, head_sq, new_heads, ids = call(
+    ids = call(
+        stage_kernel,
+        jax.ShapeDtypeStruct(near_ids.shape, near_ids.dtype),
+        (in_hbm(near_ids),),
+        (0, 0),
+        scratch=[pltpu.SemaphoreType.DMA],
+        spaces=[HBM],
+    )
+    ids = jnp.concatenate([ids, partner_ids], axis=0)
+    kept, head_sq, new_heads = call(
         early_kernel,
         (
             jax.ShapeDtypeStruct(heads.shape, heads.dtype),
             jax.ShapeDtypeStruct((1, head_dev), jnp.float32),
             jax.ShapeDtypeStruct(new_heads.shape, new_heads.dtype),
-            jax.ShapeDtypeStruct(near_ids.shape, near_ids.dtype),
         ),
-        (in_hbm(heads), in_hbm(new_heads), in_hbm(near_ids)),
+        (in_hbm(heads), in_hbm(new_heads), ids),
         (0, 0),
-        scratch=[pltpu.SemaphoreType.DMA((6,))],
-        spaces=[HBM, HBM, HBM],
-    )
-    ids = jnp.concatenate([ids, partner_ids], axis=0)
+        scratch=[pltpu.SemaphoreType.DMA((5,))],
+        spaces=[HBM, HBM, pl.ANY],
+    )
     lines = 2 * groups * new_count // LANES
     chunks = width // LANES
     extra = -(-PARTS * lines // PACK) * PACK

time: 30.7 us -> 30.3 us (0.987)
  waiting for transfers between devices: 3.1 us -> 2.36 us
  Pallas kernels: 5.29 us -> 5.94 us
    ppermute x8, waiting for transfers between devices: 3.1 us -> 2.36 us  [from_partner(): lax.ppermute(value, axis, [(source, source ^ mask) for source in range(co...]
    pallas_call x5 -> x6, Pallas kernels: 5.29 us -> 5.94 us  [call(): pl.pallas_call(body, out_shape=shapes, in_specs=[pl.BlockSpec(memory_spac...]
  transfers between devices with their start and end apart: 8 -> 8, of which waited for: 3 -> 2; matrix products, arithmetic and copies ran while one was open for 0% -> 0% of each run, Pallas kernels for 13% -> 16%
where the time goes in v14:
time: 30.3 us; the launch traced here: 30.2 us
  starting transfers between devices  10.7 us (35%)
  blocking collectives  10.4 us (34%)
  Pallas kernels  5.94 us (20%)
  waiting for transfers between devices  2.36 us (8%)
  between operations  0.73 us (2%)
    ppermute x8, starting transfers between devices, from_partner(): lax.ppermute(value, axis, [(source, source ^ mask) for source in range(co...  10.7 us
    all_to_all x1, blocking collectives, per_device(): message = lax.all_to_all(message, 'member', 0, 0, tiled=True)  10.4 us
    pallas_call x6, Pallas kernels, call(): pl.pallas_call(body, out_shape=shapes, in_specs=[pl.BlockSpec(memory_spac...  5.94 us
    ppermute x8, waiting for transfers between devices, from_partner(): lax.ppermute(value, axis, [(source, source ^ mask) for source in range(co...  2.36 us
  transfers between devices with their start and end apart: 8, of which 2 were waited for; matrix products, arithmetic and copies ran while one was open for 0% of the time, Pallas kernels for 16%

profile of v14, /device:TPU:0, one launch (start us, length us, event | category | flops | bytes accessed | tf_op | source)
XLA Modules:
  0.0 30.2 jit_solution(1649132046135451941)
XLA Ops:
  0.6 3.0 %collective-permute-start = (s32[1,64]{1,0:T(1,128)}, s32[1,64]{1,0:T(1,128)S(1)}, u32[]{:S(2)}, u32[]{:S(2)}) collective-permute-start(s32[1,64]{1,0:T(1,128)} %ids_ref.3), channel_id=1, source_target_pairs={{0,1},{1,0},{2,3},{3,2},{4,5},{5,4},{6,7},{7,6},{8,9},{9,8},{10,11... | collective-permute-start | bytes 776 | tf_op jit(solution)/shard_map/ppermute | solution.py:20
  3.6 0.0 collective-permute-start.1
  3.6 1.5 %collective-permute-start.2 = (bf16[16,768]{1,0:T(8,128)(2,1)}, bf16[16,768]{1,0:T(8,128)(2,1)S(1)}, u32[]{:S(2)}, u32[]{:S(2)}) collective-permute-start(bf16[16,768]{1,0:T(8,128)(2,1)} %new_ref.1), channel_id=1, source_target_pairs={{0,16},{8,24},{16,0},{24,8},{1,17},{9,25},{17,1},{25,9},{2,18},{10... | collective-permute-start | bytes 73736 | tf_op jit(solution)/shard_map/ppermute | solution.py:20
  5.2 0.3 %collective-permute-start.3 = (bf16[16,768]{1,0:T(8,128)(2,1)}, bf16[16,768]{1,0:T(8,128)(2,1)S(1)}, u32[]{:S(2)}, u32[]{:S(2)}) collective-permute-start(bf16[16,768]{1,0:T(8,128)(2,1)} %new_ref.1), channel_id=1, source_target_pairs={{0,24},{8,16},{16,8},{24,0},{1,25},{9,17},{17,9},{25,1},{2,26},{10... | collective-permute-start | bytes 73736 | tf_op jit(solution)/shard_map/ppermute | solution.py:20
  5.5 0.7 %shard_map.67 = s32[1,64]{1,0:T(1,128)S(1)} custom-call(s32[1,64]{1,0:T(1,128)} %ids_ref.3), custom_call_target="tpu_custom_call" | custom-call | tf_op jit(solution)/shard_map/pallas_call | solution.py:28
  6.2 0.0 collective-permute-done
  6.2 1.6 %collective-permute-start.4 = (s32[2,64]{1,0:T(2,128)S(1)}, s32[2,64]{1,0:T(2,128)S(1)}, u32[]{:S(2)}, u32[]{:S(2)}) collective-permute-start(s32[2,64]{1,0:T(2,128)S(1)} %pad_add_fusion.1.unused.ids_ref), channel_id=1, source_target_pairs={{0,2},{1,3},{2,0},{3,1},{4,6},{5,7},{6,4},{7,5},{8,10},{9,11},{10,... | collective-permute-start | bytes 1544 | tf_op jit(solution)/shard_map/ppermute | solution.py:20
  7.8 2.1 %shard_map.68 = (bf16[2048,768]{1,0:T(8,128)(2,1)S(1)}, f32[1,2048]{1,0:T(1,128)S(1)}, bf16[16,768]{1,0:T(8,128)(2,1)S(1)}) custom-call(bf16[2048,768]{1,0:T(8,128)(2,1)} %heads_ref.1, bf16[16,768]{1,0:T(8,128)(2,1)} %new_ref.1, s32[2,64]{1,0:T(2,128)S(1)} %pad_add_fusion.1.unused.ids_ref), custom_call_target="tpu_custom_call" | custom-call | tf_op jit(solution)/shard_map/pallas_call | solution.py:28
  10.0 0.0 collective-permute-done.1.refs_1_
  10.0 0.0 collective-permute-done.2.refs_2_
  10.0 0.0 collective-permute-done.3.refs_3_
  10.0 0.0 copy-start
  10.0 0.0 copy-start.1
  10.0 1.2 %shard_map.69 = (f32[1,128]{1,0:T(1,128)S(1)}, s32[2,64]{1,0:T(2,128)S(1)}) custom-call(s32[2,64]{1,0:T(2,128)S(1)} %pad_add_fusion.1.unused.ids_ref, bf16[2048,768]{1,0:T(8,128)(2,1)S(1)} %get-tuple-element.11.heads_ref, f32[1,2048]{1,0:T(1,128)S(1)} %get-tuple-element.12.head_sq_ref, bf16[16,768]{1,0:T(8,128)(2,1)S(1)} %get-tuple-element.13.refs_0_, ...), custom_call_target="tpu_custom_call" | custom-call | tf_op jit(solution)/shard_map/pallas_call | solution.py:28
  11.2 0.0 collective-permute-done.4
  11.2 2.7 %collective-permute-start.5 = (s32[4,64]{1,0:T(4,128)S(1)}, s32[4,64]{1,0:T(4,128)S(1)}, u32[]{:S(2)}, u32[]{:S(2)}) collective-permute-start(s32[4,64]{1,0:T(4,128)S(1)} %pad_add_fusion.near_ref), channel_id=1, source_target_pairs={{0,4},{1,5},{2,6},{3,7},{4,0},{5,1},{6,2},{7,3},{8,12},{9,13},{10,... | collective-permute-start | bytes 3080 | tf_op jit(solution)/shard_map/ppermute | solution.py:20
  13.9 0.0 collective-permute-start.6
  13.9 1.1 %collective-permute-done.6 = f32[1,128]{1,0:T(1,128)S(1)} collective-permute-done((f32[1,128]{1,0:T(1,128)S(1)}, f32[1,128]{1,0:T(1,128)S(1)}, u32[]{:S(2)}, u32[]{:S(2)}) %collective-permute-start.6) | collective-permute-done | bytes 544 | tf_op jit(solution)/shard_map/ppermute | solution.py:20
  15.0 1.5 %collective-permute-start.7 = (f32[1,128]{1,0:T(1,128)S(1)}, f32[1,128]{1,0:T(1,128)S(1)}, u32[]{:S(2)}, u32[]{:S(2)}) collective-permute-start(f32[1,128]{1,0:T(1,128)S(1)} %add.3.unused.mine_ref), channel_id=1, source_target_pairs={{0,16},{8,24},{16,0},{24,8},{1,17},{9,25},{17,1},{25,9},{2,18},{10... | collective-permute-start | bytes 1544 | tf_op jit(solution)/shard_map/ppermute | solution.py:20
  16.5 0.0 collective-permute-done.5.far_ref
  16.5 0.8 %shard_map.70.rows_ref = bf16[128,768]{1,0:T(8,128)(2,1)S(1)} custom-call(s32[4,64]{1,0:T(4,128)S(1)} %pad_add_fusion.near_ref, s32[4,64]{1,0:T(4,128)S(1)} %collective-permute-done.5.far_ref, bf16[2048,768]{1,0:T(8,128)(2,1)S(1)} %get-tuple-element.11.heads_ref, f32[1,128]{1,0:T(1,128)S(1)} %add.3.unused.mine_ref), custom_call_target="tpu_custom_call" | custom-call | flops 402653184 | bytes 3145728 | tf_op jit(solution)/shard_map/pallas_call | solution.py:28
  17.3 1.2 %collective-permute-done.7.other_ref = f32[1,128]{1,0:T(1,128)S(1)} collective-permute-done((f32[1,128]{1,0:T(1,128)S(1)}, f32[1,128]{1,0:T(1,128)S(1)}, u32[]{:S(2)}, u32[]{:S(2)}) %collective-permute-start.7) | collective-permute-done | bytes 544 | tf_op jit(solution)/shard_map/ppermute | solution.py:20
  18.6 10.4 %all_to_all.5.listed_ref = bf16[8,112,128]{2,1,0:T(8,128)(2,1)S(1)} all-to-all(bf16[8,112,128]{2,1,0:T(8,128)(2,1)S(1)} %shard_map.71), channel_id=1, replica_groups=mesh['group'=4,'member'=8] {'member'}, dimensions={0} | all-to-all | bytes 458752 | tf_op jit(solution)/shard_map/all_to_all | solution.py:288
  29.0 0.0 copy-done
  29.0 0.0 copy-done.1
  29.0 1.1 %shard_map.72 = (f32[1,16]{1,0:T(1,128)}, f32[1,16]{1,0:T(1,128)}, f32[1,64,128]{2,1,0:T(8,128)}) custom-call(s32[1,64]{1,0:T(1,128)S(1)} %copy-done.1, bf16[8,112,128]{2,1,0:T(8,128)(2,1)S(1)} %all_to_all.5.listed_ref, bf16[1,128,768]{2,1,0:T(8,128)(2,1)S(1)} %copy-done), custom_call_target="tpu_custom_call" | custom-call | flops 25165824 | bytes 393216 | tf_op jit(solution)/shard_map/pallas_call | solution.py:28
  (4 shorter events, 0.1 us)
Async XLA Ops:
  0.6 5.5 %collective-permute-start = (s32[1,64]{1,0:T(1,128)}, s32[1,64]{1,0:T(1,128)S(1)}, u32[]{:S(2)}, u32[]{:S(2)}) collective-permute-start(s32[1,64]{1,0:T(1,128)} %ids_ref.3), channel_id=1, source_target_pairs={{0,1},{1,0},{2,3},{3,2},{4,5},{5,4},{6,7},{7,6},{8,9},{9,8},{10,11... | collective-permute-start | bytes 776 | tf_op jit(solution)/shard_map/ppermute | solution.py:20
  3.6 6.3 %collective-permute-start.1 = (bf16[16,768]{1,0:T(8,128)(2,1)}, bf16[16,768]{1,0:T(8,128)(2,1)S(1)}, u32[]{:S(2)}, u32[]{:S(2)}) collective-permute-start(bf16[16,768]{1,0:T(8,128)(2,1)} %new_ref.1), channel_id=1, source_target_pairs={{0,8},{8,0},{16,24},{24,16},{1,9},{9,1},{17,25},{25,17},{2,10},{10... | collective-permute-start | bytes 73736 | tf_op jit(solution)/shard_map/ppermute | solution.py:20
  3.6 6.3 %collective-permute-start.2 = (bf16[16,768]{1,0:T(8,128)(2,1)}, bf16[16,768]{1,0:T(8,128)(2,1)S(1)}, u32[]{:S(2)}, u32[]{:S(2)}) collective-permute-start(bf16[16,768]{1,0:T(8,128)(2,1)} %new_ref.1), channel_id=1, source_target_pairs={{0,16},{8,24},{16,0},{24,8},{1,17},{9,25},{17,1},{25,9},{2,18},{10... | collective-permute-start | bytes 73736 | tf_op jit(solution)/shard_map/ppermute | solution.py:20
  5.2 4.8 %collective-permute-start.3 = (bf16[16,768]{1,0:T(8,128)(2,1)}, bf16[16,768]{1,0:T(8,128)(2,1)S(1)}, u32[]{:S(2)}, u32[]{:S(2)}) collective-permute-start(bf16[16,768]{1,0:T(8,128)(2,1)} %new_ref.1), channel_id=1, source_target_pairs={{0,24},{8,16},{16,8},{24,0},{1,25},{9,17},{17,9},{25,1},{2,26},{10... | collective-permute-start | bytes 73736 | tf_op jit(solution)/shard_map/ppermute | solution.py:20
  6.2 5.0 %collective-permute-start.4 = (s32[2,64]{1,0:T(2,128)S(1)}, s32[2,64]{1,0:T(2,128)S(1)}, u32[]{:S(2)}, u32[]{:S(2)}) collective-permute-start(s32[2,64]{1,0:T(2,128)S(1)} %pad_add_fusion.1.unused.ids_ref), channel_id=1, source_target_pairs={{0,2},{1,3},{2,0},{3,1},{4,6},{5,7},{6,4},{7,5},{8,10},{9,11},{10,... | collective-permute-start | bytes 1544 | tf_op jit(solution)/shard_map/ppermute | solution.py:20
  10.0 19.0 %copy-start = (bf16[1,128,768]{2,1,0:T(8,128)(2,1)S(1)}, bf16[1,128,768]{2,1,0:T(8,128)(2,1)}, u32[]{:S(2)}) copy-start(bf16[1,128,768]{2,1,0:T(8,128)(2,1)} %vectors_ref.1) | copy-start | bytes 589828
  10.0 19.0 %copy-start.1 = (s32[1,64]{1,0:T(1,128)S(1)}, s32[1,64]{1,0:T(1,128)}, u32[]{:S(2)}) copy-start(s32[1,64]{1,0:T(1,128)} %ids_ref.3) | copy-start | bytes 772
  11.2 5.3 %collective-permute-start.5 = (s32[4,64]{1,0:T(4,128)S(1)}, s32[4,64]{1,0:T(4,128)S(1)}, u32[]{:S(2)}, u32[]{:S(2)}) collective-permute-start(s32[4,64]{1,0:T(4,128)S(1)} %pad_add_fusion.near_ref), channel_id=1, source_target_pairs={{0,4},{1,5},{2,6},{3,7},{4,0},{5,1},{6,2},{7,3},{8,12},{9,13},{10,... | collective-permute-start | bytes 3080 | tf_op jit(solution)/shard_map/ppermute | solution.py:20
  13.9 1.1 %collective-permute-start.6 = (f32[1,128]{1,0:T(1,128)S(1)}, f32[1,128]{1,0:T(1,128)S(1)}, u32[]{:S(2)}, u32[]{:S(2)}) collective-permute-start(f32[1,128]{1,0:T(1,128)S(1)} %get-tuple-element.15), channel_id=1, source_target_pairs={{0,8},{8,0},{16,24},{24,16},{1,9},{9,1},{17,25},{25,17},{2,10},{10... | collective-permute-start | bytes 1544 | tf_op jit(solution)/shard_map/ppermute | solution.py:20
  15.0 3.5 %collective-permute-start.7 = (f32[1,128]{1,0:T(1,128)S(1)}, f32[1,128]{1,0:T(1,128)S(1)}, u32[]{:S(2)}, u32[]{:S(2)}) collective-permute-start(f32[1,128]{1,0:T(1,128)S(1)} %add.3.unused.mine_ref), channel_id=1, source_target_pairs={{0,16},{8,24},{16,0},{24,8},{1,17},{9,25},{17,1},{25,9},{2,18},{10... | collective-permute-start | bytes 1544 | tf_op jit(solution)/shard_map/ppermute | solution.py:20

commit v15 on v14

--- a/solution.py
+++ b/solution.py
@@ -11,6 +11,7 @@
 HBM = pltpu.MemorySpace.HBM
 LANES = 128
 PACK = 16
+TILE = 8
 PARTS = 3
 LIMIT = 24 * 2**20
 
@@ -139,19 +140,19 @@
     rows_ref[...] = listed_rows(ids, me, slots, heads_ref)
 
 
-def pack_kernel(members, slots, rows_ref, mine_ref, other_ref, out_ref):
+def pack_kernel(members, slots, lines, rows_ref, mine_ref, other_ref, out_ref):
     chunks = rows_ref.shape[1] // LANES
     for member in range(members):
         for chunk in range(chunks):
             out_ref[member, chunk * slots:(chunk + 1) * slots, :] = rows_ref[
                 member * slots:(member + 1) * slots, chunk * LANES:(chunk + 1) * LANES
             ]
-    sums = mine_ref[...] + other_ref[...]
+    sums = (mine_ref[...] + other_ref[...])[:lines]
     coded = []
     for unused in range(PARTS):
         coded.append(sums.astype(jnp.bfloat16).astype(jnp.float32))
         sums = sums - coded[-1]
-    missing = out_ref.shape[1] - chunks * slots - PARTS * sums.shape[0]
+    missing = out_ref.shape[1] - chunks * slots - PARTS * lines
     if missing:
         coded.append(jnp.zeros((missing, LANES), jnp.float32))
     tail = jnp.concatenate(coded, axis=0).astype(jnp.bfloat16)
@@ -251,11 +252,11 @@
     )
     lines = 2 * groups * new_count // LANES
     chunks = width // LANES
-    extra = -(-PARTS * lines // PACK) * PACK
+    extra = -(-PARTS * lines // TILE) * TILE
     sums, kept_ids = call(
         functools.partial(crowd_kernel, groups),
         (
-            jax.ShapeDtypeStruct((lines, LANES), jnp.float32),
+            jax.ShapeDtypeStruct((-(-lines // TILE) * TILE, LANES), jnp.float32),
             jax.ShapeDtypeStruct(ids.shape, ids.dtype),
         ),
         (ids, kept, head_sq, new_heads, *others),
@@ -280,7 +281,7 @@
         spaces=[VMEM, VMEM, VMEM, pl.ANY],
     )
     message = call(
-        functools.partial(pack_kernel, members, slots),
+        functools.partial(pack_kernel, members, slots, lines),
         jax.ShapeDtypeStruct((members, chunks * slots + extra, LANES), jnp.bfloat16),
         (rows, sums, from_partner(sums, "group", mask)),
         (0, members * slots * width * 4),

time: 30.3 us -> 30.1 us (level)
  waiting for transfers between devices: 2.36 us -> 1.31 us
  blocking collectives: 10.4 us -> 10.9 us
    ppermute x8, waiting for transfers between devices: 2.36 us -> 1.31 us  [from_partner(): lax.ppermute(value, axis, [(source, source ^ mask) for source in range(co...]
    all_to_all x1, blocking collectives: 10.4 us -> 10.9 us  [per_device(): message = lax.all_to_all(message, 'member', 0, 0, tiled=True)]
    ppermute x8, starting transfers between devices: 10.7 us -> 11 us  [from_partner(): lax.ppermute(value, axis, [(source, source ^ mask) for source in range(co...]
where the time goes in v15:
time: 30.1 us; the launch traced here: 30 us
  starting transfers between devices  11 us (37%)
  blocking collectives  10.9 us (36%)
  Pallas kernels  5.94 us (20%)
  waiting for transfers between devices  1.31 us (4%)
  between operations  0.74 us (2%)
    ppermute x8, starting transfers between devices, from_partner(): lax.ppermute(value, axis, [(source, source ^ mask) for source in range(co...  11 us
    all_to_all x1, blocking collectives, per_device(): message = lax.all_to_all(message, 'member', 0, 0, tiled=True)  10.9 us
    pallas_call x6, Pallas kernels, call(): pl.pallas_call(body, out_shape=shapes, in_specs=[pl.BlockSpec(memory_spac...  5.94 us
    ppermute x8, waiting for transfers between devices, from_partner(): lax.ppermute(value, axis, [(source, source ^ mask) for source in range(co...  1.31 us
  transfers between devices with their start and end apart: 8, of which 2 were waited for; matrix products, arithmetic and copies ran while one was open for 0% of the time, Pallas kernels for 16%

profile of v15, /device:TPU:0, one launch (start us, length us, event | category | flops | bytes accessed | tf_op | source)
XLA Modules:
  0.0 30.0 jit_solution(18072077393711253228)
XLA Ops:
  0.6 3.0 %collective-permute-start = (s32[1,64]{1,0:T(1,128)}, s32[1,64]{1,0:T(1,128)S(1)}, u32[]{:S(2)}, u32[]{:S(2)}) collective-permute-start(s32[1,64]{1,0:T(1,128)} %ids_ref.3), channel_id=1, source_target_pairs={{0,1},{1,0},{2,3},{3,2},{4,5},{5,4},{6,7},{7,6},{8,9},{9,8},{10,11... | collective-permute-start | bytes 776 | tf_op jit(solution)/shard_map/ppermute | solution.py:21
  3.6 0.0 collective-permute-start.1
  3.6 1.6 %collective-permute-start.3 = (bf16[16,768]{1,0:T(8,128)(2,1)}, bf16[16,768]{1,0:T(8,128)(2,1)S(1)}, u32[]{:S(2)}, u32[]{:S(2)}) collective-permute-start(bf16[16,768]{1,0:T(8,128)(2,1)} %new_ref.1), channel_id=1, source_target_pairs={{0,24},{8,16},{16,8},{24,0},{1,25},{9,17},{17,9},{25,1},{2,26},{10... | collective-permute-start | bytes 73736 | tf_op jit(solution)/shard_map/ppermute | solution.py:21
  5.3 0.5 %collective-permute-start.2 = (bf16[16,768]{1,0:T(8,128)(2,1)}, bf16[16,768]{1,0:T(8,128)(2,1)S(1)}, u32[]{:S(2)}, u32[]{:S(2)}) collective-permute-start(bf16[16,768]{1,0:T(8,128)(2,1)} %new_ref.1), channel_id=1, source_target_pairs={{0,16},{8,24},{16,0},{24,8},{1,17},{9,25},{17,1},{25,9},{2,18},{10... | collective-permute-start | bytes 73736 | tf_op jit(solution)/shard_map/ppermute | solution.py:21
  5.8 0.7 %shard_map.67 = s32[1,64]{1,0:T(1,128)S(1)} custom-call(s32[1,64]{1,0:T(1,128)} %ids_ref.3), custom_call_target="tpu_custom_call" | custom-call | tf_op jit(solution)/shard_map/pallas_call | solution.py:29
  6.4 0.0 collective-permute-done
  6.5 1.6 %collective-permute-start.4 = (s32[2,64]{1,0:T(2,128)S(1)}, s32[2,64]{1,0:T(2,128)S(1)}, u32[]{:S(2)}, u32[]{:S(2)}) collective-permute-start(s32[2,64]{1,0:T(2,128)S(1)} %pad_add_fusion.1.unused.ids_ref), channel_id=1, source_target_pairs={{0,2},{1,3},{2,0},{3,1},{4,6},{5,7},{6,4},{7,5},{8,10},{9,11},{10,... | collective-permute-start | bytes 1544 | tf_op jit(solution)/shard_map/ppermute | solution.py:21
  8.1 2.1 %shard_map.68 = (bf16[2048,768]{1,0:T(8,128)(2,1)S(1)}, f32[1,2048]{1,0:T(1,128)S(1)}, bf16[16,768]{1,0:T(8,128)(2,1)S(1)}) custom-call(bf16[2048,768]{1,0:T(8,128)(2,1)} %heads_ref.1, bf16[16,768]{1,0:T(8,128)(2,1)} %new_ref.1, s32[2,64]{1,0:T(2,128)S(1)} %pad_add_fusion.1.unused.ids_ref), custom_call_target="tpu_custom_call" | custom-call | tf_op jit(solution)/shard_map/pallas_call | solution.py:29
  10.2 0.0 collective-permute-done.1.refs_1_
  10.2 0.0 collective-permute-done.3.refs_3_
  10.3 0.0 collective-permute-done.2.refs_2_
  10.3 0.0 copy-start
  10.3 0.0 copy-start.1
  10.3 1.2 %shard_map.69 = (f32[8,128]{1,0:T(8,128)S(1)}, s32[2,64]{1,0:T(2,128)S(1)}) custom-call(s32[2,64]{1,0:T(2,128)S(1)} %pad_add_fusion.1.unused.ids_ref, bf16[2048,768]{1,0:T(8,128)(2,1)S(1)} %get-tuple-element.11.heads_ref, f32[1,2048]{1,0:T(1,128)S(1)} %get-tuple-element.12.head_sq_ref, bf16[16,768]{1,0:T(8,128)(2,1)S(1)} %get-tuple-element.13.refs_0_, ...), custom_call_target="tpu_custom_call" | custom-call | tf_op jit(solution)/shard_map/pallas_call | solution.py:29
  11.5 0.1 collective-permute-start.6
  11.6 0.0 collective-permute-done.4
  11.6 2.7 %collective-permute-start.5 = (s32[4,64]{1,0:T(4,128)S(1)}, s32[4,64]{1,0:T(4,128)S(1)}, u32[]{:S(2)}, u32[]{:S(2)}) collective-permute-start(s32[4,64]{1,0:T(4,128)S(1)} %pad_add_fusion.near_ref), channel_id=1, source_target_pairs={{0,4},{1,5},{2,6},{3,7},{4,0},{5,1},{6,2},{7,3},{8,12},{9,13},{10,... | collective-permute-start | bytes 3080 | tf_op jit(solution)/shard_map/ppermute | solution.py:21
  14.3 0.0 collective-permute-done.6
  14.3 1.5 %collective-permute-start.7 = (f32[8,128]{1,0:T(8,128)S(1)}, f32[8,128]{1,0:T(8,128)S(1)}, u32[]{:S(2)}, u32[]{:S(2)}) collective-permute-start(f32[8,128]{1,0:T(8,128)S(1)} %add.3.unused.mine_ref), channel_id=1, source_target_pairs={{0,16},{8,24},{16,0},{24,8},{1,17},{9,25},{17,1},{25,9},{2,18},{10... | collective-permute-start | bytes 12296 | tf_op jit(solution)/shard_map/ppermute | solution.py:21
  15.8 0.4 %collective-permute-done.5.far_ref = s32[4,64]{1,0:T(4,128)S(1)} collective-permute-done((s32[4,64]{1,0:T(4,128)S(1)}, s32[4,64]{1,0:T(4,128)S(1)}, u32[]{:S(2)}, u32[]{:S(2)}) %collective-permute-start.5) | collective-permute-done | bytes 1056 | tf_op jit(solution)/shard_map/ppermute | solution.py:21
  16.2 0.8 %shard_map.70.rows_ref = bf16[128,768]{1,0:T(8,128)(2,1)S(1)} custom-call(s32[4,64]{1,0:T(4,128)S(1)} %pad_add_fusion.near_ref, s32[4,64]{1,0:T(4,128)S(1)} %collective-permute-done.5.far_ref, bf16[2048,768]{1,0:T(8,128)(2,1)S(1)} %get-tuple-element.11.heads_ref, f32[8,128]{1,0:T(8,128)S(1)} %add.3.unused.mine_ref), custom_call_target="tpu_custom_call" | custom-call | flops 402653184 | bytes 3145728 | tf_op jit(solution)/shard_map/pallas_call | solution.py:29
  16.9 0.9 %collective-permute-done.7.other_ref = f32[8,128]{1,0:T(8,128)S(1)} collective-permute-done((f32[8,128]{1,0:T(8,128)S(1)}, f32[8,128]{1,0:T(8,128)S(1)}, u32[]{:S(2)}, u32[]{:S(2)}) %collective-permute-start.7) | collective-permute-done | bytes 4128 | tf_op jit(solution)/shard_map/ppermute | solution.py:21
  17.9 10.9 %all_to_all.5.listed_ref = bf16[8,104,128]{2,1,0:T(8,128)(2,1)S(1)} all-to-all(bf16[8,104,128]{2,1,0:T(8,128)(2,1)S(1)} %shard_map.71), channel_id=1, replica_groups=mesh['group'=4,'member'=8] {'member'}, dimensions={0} | all-to-all | bytes 425984 | tf_op jit(solution)/shard_map/all_to_all | solution.py:289
  28.8 0.0 copy-done
  28.8 0.0 copy-done.1
  28.9 1.1 %shard_map.72 = (f32[1,16]{1,0:T(1,128)}, f32[1,16]{1,0:T(1,128)}, f32[1,64,128]{2,1,0:T(8,128)}) custom-call(s32[1,64]{1,0:T(1,128)S(1)} %copy-done.1, bf16[8,104,128]{2,1,0:T(8,128)(2,1)S(1)} %all_to_all.5.listed_ref, bf16[1,128,768]{2,1,0:T(8,128)(2,1)S(1)} %copy-done), custom_call_target="tpu_custom_call" | custom-call | flops 25165824 | bytes 393216 | tf_op jit(solution)/shard_map/pallas_call | solution.py:29
  (4 shorter events, 0.1 us)
Async XLA Ops:
  0.6 5.8 %collective-permute-start = (s32[1,64]{1,0:T(1,128)}, s32[1,64]{1,0:T(1,128)S(1)}, u32[]{:S(2)}, u32[]{:S(2)}) collective-permute-start(s32[1,64]{1,0:T(1,128)} %ids_ref.3), channel_id=1, source_target_pairs={{0,1},{1,0},{2,3},{3,2},{4,5},{5,4},{6,7},{7,6},{8,9},{9,8},{10,11... | collective-permute-start | bytes 776 | tf_op jit(solution)/shard_map/ppermute | solution.py:21
  3.6 6.6 %collective-permute-start.1 = (bf16[16,768]{1,0:T(8,128)(2,1)}, bf16[16,768]{1,0:T(8,128)(2,1)S(1)}, u32[]{:S(2)}, u32[]{:S(2)}) collective-permute-start(bf16[16,768]{1,0:T(8,128)(2,1)} %new_ref.1), channel_id=1, source_target_pairs={{0,8},{8,0},{16,24},{24,16},{1,9},{9,1},{17,25},{25,17},{2,10},{10... | collective-permute-start | bytes 73736 | tf_op jit(solution)/shard_map/ppermute | solution.py:21
  3.6 6.6 %collective-permute-start.3 = (bf16[16,768]{1,0:T(8,128)(2,1)}, bf16[16,768]{1,0:T(8,128)(2,1)S(1)}, u32[]{:S(2)}, u32[]{:S(2)}) collective-permute-start(bf16[16,768]{1,0:T(8,128)(2,1)} %new_ref.1), channel_id=1, source_target_pairs={{0,24},{8,16},{16,8},{24,0},{1,25},{9,17},{17,9},{25,1},{2,26},{10... | collective-permute-start | bytes 73736 | tf_op jit(solution)/shard_map/ppermute | solution.py:21
  5.3 5.0 %collective-permute-start.2 = (bf16[16,768]{1,0:T(8,128)(2,1)}, bf16[16,768]{1,0:T(8,128)(2,1)S(1)}, u32[]{:S(2)}, u32[]{:S(2)}) collective-permute-start(bf16[16,768]{1,0:T(8,128)(2,1)} %new_ref.1), channel_id=1, source_target_pairs={{0,16},{8,24},{16,0},{24,8},{1,17},{9,25},{17,1},{25,9},{2,18},{10... | collective-permute-start | bytes 73736 | tf_op jit(solution)/shard_map/ppermute | solution.py:21
  6.5 5.1 %collective-permute-start.4 = (s32[2,64]{1,0:T(2,128)S(1)}, s32[2,64]{1,0:T(2,128)S(1)}, u32[]{:S(2)}, u32[]{:S(2)}) collective-permute-start(s32[2,64]{1,0:T(2,128)S(1)} %pad_add_fusion.1.unused.ids_ref), channel_id=1, source_target_pairs={{0,2},{1,3},{2,0},{3,1},{4,6},{5,7},{6,4},{7,5},{8,10},{9,11},{10,... | collective-permute-start | bytes 1544 | tf_op jit(solution)/shard_map/ppermute | solution.py:21
  10.3 18.6 %copy-start = (bf16[1,128,768]{2,1,0:T(8,128)(2,1)S(1)}, bf16[1,128,768]{2,1,0:T(8,128)(2,1)}, u32[]{:S(2)}) copy-start(bf16[1,128,768]{2,1,0:T(8,128)(2,1)} %vectors_ref.1) | copy-start | bytes 589828
  10.3 18.6 %copy-start.1 = (s32[1,64]{1,0:T(1,128)S(1)}, s32[1,64]{1,0:T(1,128)}, u32[]{:S(2)}) copy-start(s32[1,64]{1,0:T(1,128)} %ids_ref.3) | copy-start | bytes 772
  11.5 2.8 %collective-permute-start.6 = (f32[8,128]{1,0:T(8,128)S(1)}, f32[8,128]{1,0:T(8,128)S(1)}, u32[]{:S(2)}, u32[]{:S(2)}) collective-permute-start(f32[8,128]{1,0:T(8,128)S(1)} %get-tuple-element.15), channel_id=1, source_target_pairs={{0,8},{8,0},{16,24},{24,16},{1,9},{9,1},{17,25},{25,17},{2,10},{10... | collective-permute-start | bytes 12296 | tf_op jit(solution)/shard_map/ppermute | solution.py:21
  11.6 4.5 %collective-permute-start.5 = (s32[4,64]{1,0:T(4,128)S(1)}, s32[4,64]{1,0:T(4,128)S(1)}, u32[]{:S(2)}, u32[]{:S(2)}) collective-permute-start(s32[4,64]{1,0:T(4,128)S(1)} %pad_add_fusion.near_ref), channel_id=1, source_target_pairs={{0,4},{1,5},{2,6},{3,7},{4,0},{5,1},{6,2},{7,3},{8,12},{9,13},{10,... | collective-permute-start | bytes 3080 | tf_op jit(solution)/shard_map/ppermute | solution.py:21
  14.3 3.6 %collective-permute-start.7 = (f32[8,128]{1,0:T(8,128)S(1)}, f32[8,128]{1,0:T(8,128)S(1)}, u32[]{:S(2)}, u32[]{:S(2)}) collective-permute-start(f32[8,128]{1,0:T(8,128)S(1)} %add.3.unused.mine_ref), channel_id=1, source_target_pairs={{0,16},{8,24},{16,0},{24,8},{1,17},{9,25},{17,1},{25,9},{2,18},{10... | collective-permute-start | bytes 12296 | tf_op jit(solution)/shard_map/ppermute | solution.py:21

commit v16 on v15

--- a/solution.py
+++ b/solution.py
@@ -19,6 +19,14 @@
 def from_partner(value, axis, mask):
     count = lax.axis_size(axis)
     return lax.ppermute(value, axis, [(source, source ^ mask) for source in range(count)])
+
+
+def ring(members):
+    return [*range(0, members, 2), *range(members - 1, 0, -2)]
+
+
+def ring_place(member, members):
+    return jnp.where(member % 2 == 0, member // 2, members - 1 - member // 2)
 
 
 def in_hbm(value):
@@ -136,7 +144,7 @@
     half = members // 2
     ids_ref[:half, :] = near_ref[...]
     ids_ref[half:, :] = far_ref[...]
-    ids = jnp.concatenate([ids_ref[pl.ds(me ^ member, 1), :] for member in range(members)], axis=0)
+    ids = jnp.concatenate([ids_ref[pl.ds(me ^ member, 1), :] for member in ring(members)], axis=0)
     rows_ref[...] = listed_rows(ids, me, slots, heads_ref)
 
 
@@ -170,7 +178,7 @@
     owner = jnp.sum(jnp.where(eye, owner_row, 0), axis=1, keepdims=True)
     before = (owner_row == owner) & (iota(square, 1) < iota(square, 0))
     place = jnp.sum(before.astype(jnp.int32), axis=1, keepdims=True)
-    source = owner * slots + place
+    source = ring_place(owner, members) * slots + place
     back = (source == iota((near, members * slots), 1)).astype(jnp.bfloat16)
     rows = []
     for chunk in range(width // LANES):
@@ -286,7 +294,9 @@
         (rows, sums, from_partner(sums, "group", mask)),
         (0, members * slots * width * 4),
     )
-    message = lax.all_to_all(message, "member", 0, 0, tiled=True)
+    message = lax.all_to_all(
+        message, "member", 0, 0, tiled=True, axis_index_groups=[ring(members)]
+    )
 
     density, spread, reassign = call(
         functools.partial(

time: 30.1 us -> 30.4 us (level)
  no operation moved by 1% of the time
where the time goes in v16:
time: 30.4 us; the launch traced here: 30.3 us
  blocking collectives  11.2 us (37%)
  starting transfers between devices  11 us (36%)
  Pallas kernels  5.94 us (20%)
  waiting for transfers between devices  1.31 us (4%)
  between operations  0.74 us (2%)
    all_to_all x1, blocking collectives, per_device(): lax.all_to_all(message, 'member', 0, 0, tiled=True, axis_index_groups=[ri...  11.2 us
    ppermute x8, starting transfers between devices, from_partner(): lax.ppermute(value, axis, [(source, source ^ mask) for source in range(co...  11 us
    pallas_call x6, Pallas kernels, call(): pl.pallas_call(body, out_shape=shapes, in_specs=[pl.BlockSpec(memory_spac...  5.94 us
    ppermute x8, waiting for transfers between devices, from_partner(): lax.ppermute(value, axis, [(source, source ^ mask) for source in range(co...  1.31 us
  transfers between devices with their start and end apart: 8, of which 2 were waited for; matrix products, arithmetic and copies ran while one was open for 0% of the time, Pallas kernels for 16%

profile of v16, /device:TPU:0, one launch (start us, length us, event | category | flops | bytes accessed | tf_op | source)
XLA Modules:
  0.0 30.3 jit_solution(11539477122400944662)
XLA Ops:
  0.6 3.0 %collective-permute-start = (s32[1,64]{1,0:T(1,128)}, s32[1,64]{1,0:T(1,128)S(1)}, u32[]{:S(2)}, u32[]{:S(2)}) collective-permute-start(s32[1,64]{1,0:T(1,128)} %ids_ref.3), channel_id=1, source_target_pairs={{0,1},{1,0},{2,3},{3,2},{4,5},{5,4},{6,7},{7,6},{8,9},{9,8},{10,11... | collective-permute-start | bytes 776 | tf_op jit(solution)/shard_map/ppermute | solution.py:21
  3.6 0.0 collective-permute-start.1
  3.6 1.6 %collective-permute-start.3 = (bf16[16,768]{1,0:T(8,128)(2,1)}, bf16[16,768]{1,0:T(8,128)(2,1)S(1)}, u32[]{:S(2)}, u32[]{:S(2)}) collective-permute-start(bf16[16,768]{1,0:T(8,128)(2,1)} %new_ref.1), channel_id=1, source_target_pairs={{0,24},{8,16},{16,8},{24,0},{1,25},{9,17},{17,9},{25,1},{2,26},{10... | collective-permute-start | bytes 73736 | tf_op jit(solution)/shard_map/ppermute | solution.py:21
  5.3 0.5 %collective-permute-start.2 = (bf16[16,768]{1,0:T(8,128)(2,1)}, bf16[16,768]{1,0:T(8,128)(2,1)S(1)}, u32[]{:S(2)}, u32[]{:S(2)}) collective-permute-start(bf16[16,768]{1,0:T(8,128)(2,1)} %new_ref.1), channel_id=1, source_target_pairs={{0,16},{8,24},{16,0},{24,8},{1,17},{9,25},{17,1},{25,9},{2,18},{10... | collective-permute-start | bytes 73736 | tf_op jit(solution)/shard_map/ppermute | solution.py:21
  5.8 0.7 %shard_map.67 = s32[1,64]{1,0:T(1,128)S(1)} custom-call(s32[1,64]{1,0:T(1,128)} %ids_ref.3), custom_call_target="tpu_custom_call" | custom-call | tf_op jit(solution)/shard_map/pallas_call | solution.py:37
  6.4 0.0 collective-permute-done
  6.5 1.6 %collective-permute-start.4 = (s32[2,64]{1,0:T(2,128)S(1)}, s32[2,64]{1,0:T(2,128)S(1)}, u32[]{:S(2)}, u32[]{:S(2)}) collective-permute-start(s32[2,64]{1,0:T(2,128)S(1)} %pad_add_fusion.1.unused.ids_ref), channel_id=1, source_target_pairs={{0,2},{1,3},{2,0},{3,1},{4,6},{5,7},{6,4},{7,5},{8,10},{9,11},{10,... | collective-permute-start | bytes 1544 | tf_op jit(solution)/shard_map/ppermute | solution.py:21
  8.1 2.1 %shard_map.68 = (bf16[2048,768]{1,0:T(8,128)(2,1)S(1)}, f32[1,2048]{1,0:T(1,128)S(1)}, bf16[16,768]{1,0:T(8,128)(2,1)S(1)}) custom-call(bf16[2048,768]{1,0:T(8,128)(2,1)} %heads_ref.1, bf16[16,768]{1,0:T(8,128)(2,1)} %new_ref.1, s32[2,64]{1,0:T(2,128)S(1)} %pad_add_fusion.1.unused.ids_ref), custom_call_target="tpu_custom_call" | custom-call | tf_op jit(solution)/shard_map/pallas_call | solution.py:37
  10.2 0.0 collective-permute-done.1.refs_1_
  10.2 0.0 collective-permute-done.3.refs_3_
  10.3 0.0 collective-permute-done.2.refs_2_
  10.3 0.0 copy-start
  10.3 0.0 copy-start.1
  10.3 1.2 %shard_map.69 = (f32[8,128]{1,0:T(8,128)S(1)}, s32[2,64]{1,0:T(2,128)S(1)}) custom-call(s32[2,64]{1,0:T(2,128)S(1)} %pad_add_fusion.1.unused.ids_ref, bf16[2048,768]{1,0:T(8,128)(2,1)S(1)} %get-tuple-element.11.heads_ref, f32[1,2048]{1,0:T(1,128)S(1)} %get-tuple-element.12.head_sq_ref, bf16[16,768]{1,0:T(8,128)(2,1)S(1)} %get-tuple-element.13.refs_0_, ...), custom_call_target="tpu_custom_call" | custom-call | tf_op jit(solution)/shard_map/pallas_call | solution.py:37
  11.5 0.1 collective-permute-start.6
  11.6 0.0 collective-permute-done.4
  11.6 2.7 %collective-permute-start.5 = (s32[4,64]{1,0:T(4,128)S(1)}, s32[4,64]{1,0:T(4,128)S(1)}, u32[]{:S(2)}, u32[]{:S(2)}) collective-permute-start(s32[4,64]{1,0:T(4,128)S(1)} %pad_add_fusion.near_ref), channel_id=1, source_target_pairs={{0,4},{1,5},{2,6},{3,7},{4,0},{5,1},{6,2},{7,3},{8,12},{9,13},{10,... | collective-permute-start | bytes 3080 | tf_op jit(solution)/shard_map/ppermute | solution.py:21
  14.3 0.0 collective-permute-done.6
  14.3 1.5 %collective-permute-start.7 = (f32[8,128]{1,0:T(8,128)S(1)}, f32[8,128]{1,0:T(8,128)S(1)}, u32[]{:S(2)}, u32[]{:S(2)}) collective-permute-start(f32[8,128]{1,0:T(8,128)S(1)} %add.3.unused.mine_ref), channel_id=1, source_target_pairs={{0,16},{8,24},{16,0},{24,8},{1,17},{9,25},{17,1},{25,9},{2,18},{10... | collective-permute-start | bytes 12296 | tf_op jit(solution)/shard_map/ppermute | solution.py:21
  15.8 0.4 %collective-permute-done.5.far_ref = s32[4,64]{1,0:T(4,128)S(1)} collective-permute-done((s32[4,64]{1,0:T(4,128)S(1)}, s32[4,64]{1,0:T(4,128)S(1)}, u32[]{:S(2)}, u32[]{:S(2)}) %collective-permute-start.5) | collective-permute-done | bytes 1056 | tf_op jit(solution)/shard_map/ppermute | solution.py:21
  16.2 0.8 %shard_map.70.rows_ref = bf16[128,768]{1,0:T(8,128)(2,1)S(1)} custom-call(s32[4,64]{1,0:T(4,128)S(1)} %pad_add_fusion.near_ref, s32[4,64]{1,0:T(4,128)S(1)} %collective-permute-done.5.far_ref, bf16[2048,768]{1,0:T(8,128)(2,1)S(1)} %get-tuple-element.11.heads_ref, f32[8,128]{1,0:T(8,128)S(1)} %add.3.unused.mine_ref), custom_call_target="tpu_custom_call" | custom-call | flops 402653184 | bytes 3145728 | tf_op jit(solution)/shard_map/pallas_call | solution.py:37
  16.9 0.9 %collective-permute-done.7.other_ref = f32[8,128]{1,0:T(8,128)S(1)} collective-permute-done((f32[8,128]{1,0:T(8,128)S(1)}, f32[8,128]{1,0:T(8,128)S(1)}, u32[]{:S(2)}, u32[]{:S(2)}) %collective-permute-start.7) | collective-permute-done | bytes 4128 | tf_op jit(solution)/shard_map/ppermute | solution.py:21
  17.9 11.2 %all_to_all.5.listed_ref = bf16[8,104,128]{2,1,0:T(8,128)(2,1)S(1)} all-to-all(bf16[8,104,128]{2,1,0:T(8,128)(2,1)S(1)} %shard_map.71), channel_id=1, replica_groups={{0,2,4,6,7,5,3,1},{8,10,12,14,15,13,11,9},{16,18,20,22,23,21,19,17},{24..., dimensions={0} | all-to-all | bytes 425984 | tf_op jit(solution)/shard_map/all_to_all | solution.py:297
  29.1 0.0 copy-done
  29.1 0.0 copy-done.1
  29.1 1.1 %shard_map.72 = (f32[1,16]{1,0:T(1,128)}, f32[1,16]{1,0:T(1,128)}, f32[1,64,128]{2,1,0:T(8,128)}) custom-call(s32[1,64]{1,0:T(1,128)S(1)} %copy-done.1, bf16[8,104,128]{2,1,0:T(8,128)(2,1)S(1)} %all_to_all.5.listed_ref, bf16[1,128,768]{2,1,0:T(8,128)(2,1)S(1)} %copy-done), custom_call_target="tpu_custom_call" | custom-call | flops 25165824 | bytes 393216 | tf_op jit(solution)/shard_map/pallas_call | solution.py:37
  (4 shorter events, 0.1 us)
Async XLA Ops:
  0.6 5.8 %collective-permute-start = (s32[1,64]{1,0:T(1,128)}, s32[1,64]{1,0:T(1,128)S(1)}, u32[]{:S(2)}, u32[]{:S(2)}) collective-permute-start(s32[1,64]{1,0:T(1,128)} %ids_ref.3), channel_id=1, source_target_pairs={{0,1},{1,0},{2,3},{3,2},{4,5},{5,4},{6,7},{7,6},{8,9},{9,8},{10,11... | collective-permute-start | bytes 776 | tf_op jit(solution)/shard_map/ppermute | solution.py:21
  3.6 6.6 %collective-permute-start.1 = (bf16[16,768]{1,0:T(8,128)(2,1)}, bf16[16,768]{1,0:T(8,128)(2,1)S(1)}, u32[]{:S(2)}, u32[]{:S(2)}) collective-permute-start(bf16[16,768]{1,0:T(8,128)(2,1)} %new_ref.1), channel_id=1, source_target_pairs={{0,8},{8,0},{16,24},{24,16},{1,9},{9,1},{17,25},{25,17},{2,10},{10... | collective-permute-start | bytes 73736 | tf_op jit(solution)/shard_map/ppermute | solution.py:21
  3.6 6.6 %collective-permute-start.3 = (bf16[16,768]{1,0:T(8,128)(2,1)}, bf16[16,768]{1,0:T(8,128)(2,1)S(1)}, u32[]{:S(2)}, u32[]{:S(2)}) collective-permute-start(bf16[16,768]{1,0:T(8,128)(2,1)} %new_ref.1), channel_id=1, source_target_pairs={{0,24},{8,16},{16,8},{24,0},{1,25},{9,17},{17,9},{25,1},{2,26},{10... | collective-permute-start | bytes 73736 | tf_op jit(solution)/shard_map/ppermute | solution.py:21
  5.3 5.0 %collective-permute-start.2 = (bf16[16,768]{1,0:T(8,128)(2,1)}, bf16[16,768]{1,0:T(8,128)(2,1)S(1)}, u32[]{:S(2)}, u32[]{:S(2)}) collective-permute-start(bf16[16,768]{1,0:T(8,128)(2,1)} %new_ref.1), channel_id=1, source_target_pairs={{0,16},{8,24},{16,0},{24,8},{1,17},{9,25},{17,1},{25,9},{2,18},{10... | collective-permute-start | bytes 73736 | tf_op jit(solution)/shard_map/ppermute | solution.py:21
  6.5 5.1 %collective-permute-start.4 = (s32[2,64]{1,0:T(2,128)S(1)}, s32[2,64]{1,0:T(2,128)S(1)}, u32[]{:S(2)}, u32[]{:S(2)}) collective-permute-start(s32[2,64]{1,0:T(2,128)S(1)} %pad_add_fusion.1.unused.ids_ref), channel_id=1, source_target_pairs={{0,2},{1,3},{2,0},{3,1},{4,6},{5,7},{6,4},{7,5},{8,10},{9,11},{10,... | collective-permute-start | bytes 1544 | tf_op jit(solution)/shard_map/ppermute | solution.py:21
  10.3 18.9 %copy-start = (bf16[1,128,768]{2,1,0:T(8,128)(2,1)S(1)}, bf16[1,128,768]{2,1,0:T(8,128)(2,1)}, u32[]{:S(2)}) copy-start(bf16[1,128,768]{2,1,0:T(8,128)(2,1)} %vectors_ref.1) | copy-start | bytes 589828
  10.3 18.9 %copy-start.1 = (s32[1,64]{1,0:T(1,128)S(1)}, s32[1,64]{1,0:T(1,128)}, u32[]{:S(2)}) copy-start(s32[1,64]{1,0:T(1,128)} %ids_ref.3) | copy-start | bytes 772
  11.5 2.8 %collective-permute-start.6 = (f32[8,128]{1,0:T(8,128)S(1)}, f32[8,128]{1,0:T(8,128)S(1)}, u32[]{:S(2)}, u32[]{:S(2)}) collective-permute-start(f32[8,128]{1,0:T(8,128)S(1)} %get-tuple-element.15), channel_id=1, source_target_pairs={{0,8},{8,0},{16,24},{24,16},{1,9},{9,1},{17,25},{25,17},{2,10},{10... | collective-permute-start | bytes 12296 | tf_op jit(solution)/shard_map/ppermute | solution.py:21
  11.6 4.5 %collective-permute-start.5 = (s32[4,64]{1,0:T(4,128)S(1)}, s32[4,64]{1,0:T(4,128)S(1)}, u32[]{:S(2)}, u32[]{:S(2)}) collective-permute-start(s32[4,64]{1,0:T(4,128)S(1)} %pad_add_fusion.near_ref), channel_id=1, source_target_pairs={{0,4},{1,5},{2,6},{3,7},{4,0},{5,1},{6,2},{7,3},{8,12},{9,13},{10,... | collective-permute-start | bytes 3080 | tf_op jit(solution)/shard_map/ppermute | solution.py:21
  14.3 3.6 %collective-permute-start.7 = (f32[8,128]{1,0:T(8,128)S(1)}, f32[8,128]{1,0:T(8,128)S(1)}, u32[]{:S(2)}, u32[]{:S(2)}) collective-permute-start(f32[8,128]{1,0:T(8,128)S(1)} %add.3.unused.mine_ref), channel_id=1, source_target_pairs={{0,16},{8,24},{16,0},{24,8},{1,17},{9,25},{17,1},{25,9},{2,18},{10... | collective-permute-start | bytes 12296 | tf_op jit(solution)/shard_map/ppermute | solution.py:21

commit v17 on v15

--- a/solution.py
+++ b/solution.py
@@ -19,6 +19,10 @@
 def from_partner(value, axis, mask):
     count = lax.axis_size(axis)
     return lax.ppermute(value, axis, [(source, source ^ mask) for source in range(count)])
+
+
+def turned(members):
+    return [member ^ (members // 2) for member in range(members)]
 
 
 def in_hbm(value):
@@ -136,7 +140,7 @@
     half = members // 2
     ids_ref[:half, :] = near_ref[...]
     ids_ref[half:, :] = far_ref[...]
-    ids = jnp.concatenate([ids_ref[pl.ds(me ^ member, 1), :] for member in range(members)], axis=0)
+    ids = jnp.concatenate([ids_ref[pl.ds(me ^ member, 1), :] for member in turned(members)], axis=0)
     rows_ref[...] = listed_rows(ids, me, slots, heads_ref)
 
 
@@ -170,7 +174,7 @@
     owner = jnp.sum(jnp.where(eye, owner_row, 0), axis=1, keepdims=True)
     before = (owner_row == owner) & (iota(square, 1) < iota(square, 0))
     place = jnp.sum(before.astype(jnp.int32), axis=1, keepdims=True)
-    source = owner * slots + place
+    source = (owner ^ (members // 2)) * slots + place
     back = (source == iota((near, members * slots), 1)).astype(jnp.bfloat16)
     rows = []
     for chunk in range(width // LANES):
@@ -180,8 +184,8 @@
     row_sq = jnp.sum(jnp.square(rows), axis=1, keepdims=True)
     vec = vectors_ref[0]
     vec_sq = jnp.sum(jnp.square(vec.astype(jnp.float32)), axis=1, keepdims=True)
-    turned = iota((block, block), 0) == iota((block, block), 1)
-    vec_sq = jnp.sum(jnp.where(turned, vec_sq, 0.0), axis=0, keepdims=True)
+    diagonal = iota((block, block), 0) == iota((block, block), 1)
+    vec_sq = jnp.sum(jnp.where(diagonal, vec_sq, 0.0), axis=0, keepdims=True)
     dots = lax.dot_general(
         rows.astype(jnp.bfloat16), vec, (((1,), (1,)), ((), ())),
         preferred_element_type=jnp.float32,
@@ -286,7 +290,9 @@
         (rows, sums, from_partner(sums, "group", mask)),
         (0, members * slots * width * 4),
     )
-    message = lax.all_to_all(message, "member", 0, 0, tiled=True)
+    message = lax.all_to_all(
+        message, "member", 0, 0, tiled=True, axis_index_groups=[turned(members)]
+    )
 
     density, spread, reassign = call(
         functools.partial(

time: 30.1 us -> 29 us (0.963)
  blocking collectives: 10.9 us -> 9.81 us
    all_to_all x1, blocking collectives: 10.9 us -> 9.81 us  [per_device(): lax.all_to_all(message, 'member', 0, 0, tiled=True, axis_index_groups=[tu...]
where the time goes in v17:
time: 29 us; the launch traced here: 28.9 us
  starting transfers between devices  11 us (38%)
  blocking collectives  9.81 us (34%)
  Pallas kernels  5.94 us (20%)
  waiting for transfers between devices  1.31 us (5%)
  between operations  0.74 us (3%)
    ppermute x8, starting transfers between devices, from_partner(): lax.ppermute(value, axis, [(source, source ^ mask) for source in range(co...  11 us
    all_to_all x1, blocking collectives, per_device(): lax.all_to_all(message, 'member', 0, 0, tiled=True, axis_index_groups=[tu...  9.81 us
    pallas_call x6, Pallas kernels, call(): pl.pallas_call(body, out_shape=shapes, in_specs=[pl.BlockSpec(memory_spac...  5.94 us
    ppermute x8, waiting for transfers between devices, from_partner(): lax.ppermute(value, axis, [(source, source ^ mask) for source in range(co...  1.31 us
  transfers between devices with their start and end apart: 8, of which 2 were waited for; matrix products, arithmetic and copies ran while one was open for 0% of the time, Pallas kernels for 16%

profile of v17, /device:TPU:0, one launch (start us, length us, event | category | flops | bytes accessed | tf_op | source)
XLA Modules:
  0.0 28.9 jit_solution(3778220106829033956)
XLA Ops:
  0.6 3.0 %collective-permute-start = (s32[1,64]{1,0:T(1,128)}, s32[1,64]{1,0:T(1,128)S(1)}, u32[]{:S(2)}, u32[]{:S(2)}) collective-permute-start(s32[1,64]{1,0:T(1,128)} %ids_ref.3), channel_id=1, source_target_pairs={{0,1},{1,0},{2,3},{3,2},{4,5},{5,4},{6,7},{7,6},{8,9},{9,8},{10,11... | collective-permute-start | bytes 776 | tf_op jit(solution)/shard_map/ppermute | solution.py:21
  3.6 0.0 collective-permute-start.1
  3.6 1.6 %collective-permute-start.3 = (bf16[16,768]{1,0:T(8,128)(2,1)}, bf16[16,768]{1,0:T(8,128)(2,1)S(1)}, u32[]{:S(2)}, u32[]{:S(2)}) collective-permute-start(bf16[16,768]{1,0:T(8,128)(2,1)} %new_ref.1), channel_id=1, source_target_pairs={{0,24},{8,16},{16,8},{24,0},{1,25},{9,17},{17,9},{25,1},{2,26},{10... | collective-permute-start | bytes 73736 | tf_op jit(solution)/shard_map/ppermute | solution.py:21
  5.3 0.5 %collective-permute-start.2 = (bf16[16,768]{1,0:T(8,128)(2,1)}, bf16[16,768]{1,0:T(8,128)(2,1)S(1)}, u32[]{:S(2)}, u32[]{:S(2)}) collective-permute-start(bf16[16,768]{1,0:T(8,128)(2,1)} %new_ref.1), channel_id=1, source_target_pairs={{0,16},{8,24},{16,0},{24,8},{1,17},{9,25},{17,1},{25,9},{2,18},{10... | collective-permute-start | bytes 73736 | tf_op jit(solution)/shard_map/ppermute | solution.py:21
  5.8 0.7 %shard_map.67 = s32[1,64]{1,0:T(1,128)S(1)} custom-call(s32[1,64]{1,0:T(1,128)} %ids_ref.3), custom_call_target="tpu_custom_call" | custom-call | tf_op jit(solution)/shard_map/pallas_call | solution.py:33
  6.4 0.0 collective-permute-done
  6.5 1.6 %collective-permute-start.4 = (s32[2,64]{1,0:T(2,128)S(1)}, s32[2,64]{1,0:T(2,128)S(1)}, u32[]{:S(2)}, u32[]{:S(2)}) collective-permute-start(s32[2,64]{1,0:T(2,128)S(1)} %pad_add_fusion.1.unused.ids_ref), channel_id=1, source_target_pairs={{0,2},{1,3},{2,0},{3,1},{4,6},{5,7},{6,4},{7,5},{8,10},{9,11},{10,... | collective-permute-start | bytes 1544 | tf_op jit(solution)/shard_map/ppermute | solution.py:21
  8.1 2.1 %shard_map.68 = (bf16[2048,768]{1,0:T(8,128)(2,1)S(1)}, f32[1,2048]{1,0:T(1,128)S(1)}, bf16[16,768]{1,0:T(8,128)(2,1)S(1)}) custom-call(bf16[2048,768]{1,0:T(8,128)(2,1)} %heads_ref.1, bf16[16,768]{1,0:T(8,128)(2,1)} %new_ref.1, s32[2,64]{1,0:T(2,128)S(1)} %pad_add_fusion.1.unused.ids_ref), custom_call_target="tpu_custom_call" | custom-call | tf_op jit(solution)/shard_map/pallas_call | solution.py:33
  10.2 0.0 collective-permute-done.1.refs_1_
  10.2 0.0 collective-permute-done.3.refs_3_
  10.3 0.0 collective-permute-done.2.refs_2_
  10.3 0.0 copy-start
  10.3 0.0 copy-start.1
  10.3 1.2 %shard_map.69 = (f32[8,128]{1,0:T(8,128)S(1)}, s32[2,64]{1,0:T(2,128)S(1)}) custom-call(s32[2,64]{1,0:T(2,128)S(1)} %pad_add_fusion.1.unused.ids_ref, bf16[2048,768]{1,0:T(8,128)(2,1)S(1)} %get-tuple-element.11.heads_ref, f32[1,2048]{1,0:T(1,128)S(1)} %get-tuple-element.12.head_sq_ref, bf16[16,768]{1,0:T(8,128)(2,1)S(1)} %get-tuple-element.13.refs_0_, ...), custom_call_target="tpu_custom_call" | custom-call | tf_op jit(solution)/shard_map/pallas_call | solution.py:33
  11.5 0.1 collective-permute-start.6
  11.6 0.0 collective-permute-done.4
  11.6 2.7 %collective-permute-start.5 = (s32[4,64]{1,0:T(4,128)S(1)}, s32[4,64]{1,0:T(4,128)S(1)}, u32[]{:S(2)}, u32[]{:S(2)}) collective-permute-start(s32[4,64]{1,0:T(4,128)S(1)} %pad_add_fusion.near_ref), channel_id=1, source_target_pairs={{0,4},{1,5},{2,6},{3,7},{4,0},{5,1},{6,2},{7,3},{8,12},{9,13},{10,... | collective-permute-start | bytes 3080 | tf_op jit(solution)/shard_map/ppermute | solution.py:21
  14.3 0.0 collective-permute-done.6
  14.3 1.5 %collective-permute-start.7 = (f32[8,128]{1,0:T(8,128)S(1)}, f32[8,128]{1,0:T(8,128)S(1)}, u32[]{:S(2)}, u32[]{:S(2)}) collective-permute-start(f32[8,128]{1,0:T(8,128)S(1)} %add.3.unused.mine_ref), channel_id=1, source_target_pairs={{0,16},{8,24},{16,0},{24,8},{1,17},{9,25},{17,1},{25,9},{2,18},{10... | collective-permute-start | bytes 12296 | tf_op jit(solution)/shard_map/ppermute | solution.py:21
  15.8 0.4 %collective-permute-done.5.far_ref = s32[4,64]{1,0:T(4,128)S(1)} collective-permute-done((s32[4,64]{1,0:T(4,128)S(1)}, s32[4,64]{1,0:T(4,128)S(1)}, u32[]{:S(2)}, u32[]{:S(2)}) %collective-permute-start.5) | collective-permute-done | bytes 1056 | tf_op jit(solution)/shard_map/ppermute | solution.py:21
  16.2 0.8 %shard_map.70.rows_ref = bf16[128,768]{1,0:T(8,128)(2,1)S(1)} custom-call(s32[4,64]{1,0:T(4,128)S(1)} %pad_add_fusion.near_ref, s32[4,64]{1,0:T(4,128)S(1)} %collective-permute-done.5.far_ref, bf16[2048,768]{1,0:T(8,128)(2,1)S(1)} %get-tuple-element.11.heads_ref, f32[8,128]{1,0:T(8,128)S(1)} %add.3.unused.mine_ref), custom_call_target="tpu_custom_call" | custom-call | flops 402653184 | bytes 3145728 | tf_op jit(solution)/shard_map/pallas_call | solution.py:33
  16.9 0.9 %collective-permute-done.7.other_ref = f32[8,128]{1,0:T(8,128)S(1)} collective-permute-done((f32[8,128]{1,0:T(8,128)S(1)}, f32[8,128]{1,0:T(8,128)S(1)}, u32[]{:S(2)}, u32[]{:S(2)}) %collective-permute-start.7) | collective-permute-done | bytes 4128 | tf_op jit(solution)/shard_map/ppermute | solution.py:21
  17.9 9.8 %all_to_all.5.listed_ref = bf16[8,104,128]{2,1,0:T(8,128)(2,1)S(1)} all-to-all(bf16[8,104,128]{2,1,0:T(8,128)(2,1)S(1)} %shard_map.71), channel_id=1, replica_groups={{4,5,6,7,0,1,2,3},{12,13,14,15,8,9,10,11},{20,21,22,23,16,17,18,19},{28..., dimensions={0} | all-to-all | bytes 425984 | tf_op jit(solution)/shard_map/all_to_all | solution.py:293
  27.7 0.0 copy-done
  27.7 0.0 copy-done.1
  27.7 1.1 %shard_map.72 = (f32[1,16]{1,0:T(1,128)}, f32[1,16]{1,0:T(1,128)}, f32[1,64,128]{2,1,0:T(8,128)}) custom-call(s32[1,64]{1,0:T(1,128)S(1)} %copy-done.1, bf16[8,104,128]{2,1,0:T(8,128)(2,1)S(1)} %all_to_all.5.listed_ref, bf16[1,128,768]{2,1,0:T(8,128)(2,1)S(1)} %copy-done), custom_call_target="tpu_custom_call" | custom-call | flops 25165824 | bytes 393216 | tf_op jit(solution)/shard_map/pallas_call | solution.py:33
  (4 shorter events, 0.1 us)
Async XLA Ops:
  0.6 5.8 %collective-permute-start = (s32[1,64]{1,0:T(1,128)}, s32[1,64]{1,0:T(1,128)S(1)}, u32[]{:S(2)}, u32[]{:S(2)}) collective-permute-start(s32[1,64]{1,0:T(1,128)} %ids_ref.3), channel_id=1, source_target_pairs={{0,1},{1,0},{2,3},{3,2},{4,5},{5,4},{6,7},{7,6},{8,9},{9,8},{10,11... | collective-permute-start | bytes 776 | tf_op jit(solution)/shard_map/ppermute | solution.py:21
  3.6 6.6 %collective-permute-start.1 = (bf16[16,768]{1,0:T(8,128)(2,1)}, bf16[16,768]{1,0:T(8,128)(2,1)S(1)}, u32[]{:S(2)}, u32[]{:S(2)}) collective-permute-start(bf16[16,768]{1,0:T(8,128)(2,1)} %new_ref.1), channel_id=1, source_target_pairs={{0,8},{8,0},{16,24},{24,16},{1,9},{9,1},{17,25},{25,17},{2,10},{10... | collective-permute-start | bytes 73736 | tf_op jit(solution)/shard_map/ppermute | solution.py:21
  3.6 6.6 %collective-permute-start.3 = (bf16[16,768]{1,0:T(8,128)(2,1)}, bf16[16,768]{1,0:T(8,128)(2,1)S(1)}, u32[]{:S(2)}, u32[]{:S(2)}) collective-permute-start(bf16[16,768]{1,0:T(8,128)(2,1)} %new_ref.1), channel_id=1, source_target_pairs={{0,24},{8,16},{16,8},{24,0},{1,25},{9,17},{17,9},{25,1},{2,26},{10... | collective-permute-start | bytes 73736 | tf_op jit(solution)/shard_map/ppermute | solution.py:21
  5.3 5.0 %collective-permute-start.2 = (bf16[16,768]{1,0:T(8,128)(2,1)}, bf16[16,768]{1,0:T(8,128)(2,1)S(1)}, u32[]{:S(2)}, u32[]{:S(2)}) collective-permute-start(bf16[16,768]{1,0:T(8,128)(2,1)} %new_ref.1), channel_id=1, source_target_pairs={{0,16},{8,24},{16,0},{24,8},{1,17},{9,25},{17,1},{25,9},{2,18},{10... | collective-permute-start | bytes 73736 | tf_op jit(solution)/shard_map/ppermute | solution.py:21
  6.5 5.1 %collective-permute-start.4 = (s32[2,64]{1,0:T(2,128)S(1)}, s32[2,64]{1,0:T(2,128)S(1)}, u32[]{:S(2)}, u32[]{:S(2)}) collective-permute-start(s32[2,64]{1,0:T(2,128)S(1)} %pad_add_fusion.1.unused.ids_ref), channel_id=1, source_target_pairs={{0,2},{1,3},{2,0},{3,1},{4,6},{5,7},{6,4},{7,5},{8,10},{9,11},{10,... | collective-permute-start | bytes 1544 | tf_op jit(solution)/shard_map/ppermute | solution.py:21
  10.3 17.5 %copy-start = (bf16[1,128,768]{2,1,0:T(8,128)(2,1)S(1)}, bf16[1,128,768]{2,1,0:T(8,128)(2,1)}, u32[]{:S(2)}) copy-start(bf16[1,128,768]{2,1,0:T(8,128)(2,1)} %vectors_ref.1) | copy-start | bytes 589828
  10.3 17.5 %copy-start.1 = (s32[1,64]{1,0:T(1,128)S(1)}, s32[1,64]{1,0:T(1,128)}, u32[]{:S(2)}) copy-start(s32[1,64]{1,0:T(1,128)} %ids_ref.3) | copy-start | bytes 772
  11.5 2.8 %collective-permute-start.6 = (f32[8,128]{1,0:T(8,128)S(1)}, f32[8,128]{1,0:T(8,128)S(1)}, u32[]{:S(2)}, u32[]{:S(2)}) collective-permute-start(f32[8,128]{1,0:T(8,128)S(1)} %get-tuple-element.15), channel_id=1, source_target_pairs={{0,8},{8,0},{16,24},{24,16},{1,9},{9,1},{17,25},{25,17},{2,10},{10... | collective-permute-start | bytes 12296 | tf_op jit(solution)/shard_map/ppermute | solution.py:21
  11.6 4.5 %collective-permute-start.5 = (s32[4,64]{1,0:T(4,128)S(1)}, s32[4,64]{1,0:T(4,128)S(1)}, u32[]{:S(2)}, u32[]{:S(2)}) collective-permute-start(s32[4,64]{1,0:T(4,128)S(1)} %pad_add_fusion.near_ref), channel_id=1, source_target_pairs={{0,4},{1,5},{2,6},{3,7},{4,0},{5,1},{6,2},{7,3},{8,12},{9,13},{10,... | collective-permute-start | bytes 3080 | tf_op jit(solution)/shard_map/ppermute | solution.py:21
  14.3 3.6 %collective-permute-start.7 = (f32[8,128]{1,0:T(8,128)S(1)}, f32[8,128]{1,0:T(8,128)S(1)}, u32[]{:S(2)}, u32[]{:S(2)}) collective-permute-start(f32[8,128]{1,0:T(8,128)S(1)} %add.3.unused.mine_ref), channel_id=1, source_target_pairs={{0,16},{8,24},{16,0},{24,8},{1,17},{9,25},{17,1},{25,9},{2,18},{10... | collective-permute-start | bytes 12296 | tf_op jit(solution)/shard_map/ppermute | solution.py:21

commit v18 on v17

--- a/solution.py
+++ b/solution.py
@@ -22,7 +22,7 @@
 
 
 def turned(members):
-    return [member ^ (members // 2) for member in range(members)]
+    return [member ^ (members // 2 + 1) for member in range(members)]
 
 
 def in_hbm(value):
@@ -174,7 +174,7 @@
     owner = jnp.sum(jnp.where(eye, owner_row, 0), axis=1, keepdims=True)
     before = (owner_row == owner) & (iota(square, 1) < iota(square, 0))
     place = jnp.sum(before.astype(jnp.int32), axis=1, keepdims=True)
-    source = (owner ^ (members // 2)) * slots + place
+    source = (owner ^ (members // 2 + 1)) * slots + place
     back = (source == iota((near, members * slots), 1)).astype(jnp.bfloat16)
     rows = []
     for chunk in range(width // LANES):

time: 29 us -> 29.1 us (level)
  no operation moved by 1% of the time
where the time goes in v18:
time: 29.1 us; the launch traced here: 29 us
  starting transfers between devices  11 us (38%)
  blocking collectives  9.91 us (34%)
  Pallas kernels  5.94 us (20%)
  waiting for transfers between devices  1.31 us (5%)
  between operations  0.74 us (3%)
    ppermute x8, starting transfers between devices, from_partner(): lax.ppermute(value, axis, [(source, source ^ mask) for source in range(co...  11 us
    all_to_all x1, blocking collectives, per_device(): lax.all_to_all(message, 'member', 0, 0, tiled=True, axis_index_groups=[tu...  9.91 us
    pallas_call x6, Pallas kernels, call(): pl.pallas_call(body, out_shape=shapes, in_specs=[pl.BlockSpec(memory_spac...  5.94 us
    ppermute x8, waiting for transfers between devices, from_partner(): lax.ppermute(value, axis, [(source, source ^ mask) for source in range(co...  1.31 us
  transfers between devices with their start and end apart: 8, of which 2 were waited for; matrix products, arithmetic and copies ran while one was open for 0% of the time, Pallas kernels for 16%

profile of v18, /device:TPU:0, one launch (start us, length us, event | category | flops | bytes accessed | tf_op | source)
XLA Modules:
  0.0 29.0 jit_solution(14331748897465245658)
XLA Ops:
  0.6 3.0 %collective-permute-start = (s32[1,64]{1,0:T(1,128)}, s32[1,64]{1,0:T(1,128)S(1)}, u32[]{:S(2)}, u32[]{:S(2)}) collective-permute-start(s32[1,64]{1,0:T(1,128)} %ids_ref.3), channel_id=1, source_target_pairs={{0,1},{1,0},{2,3},{3,2},{4,5},{5,4},{6,7},{7,6},{8,9},{9,8},{10,11... | collective-permute-start | bytes 776 | tf_op jit(solution)/shard_map/ppermute | solution.py:21
  3.6 0.0 collective-permute-start.1
  3.6 1.6 %collective-permute-start.3 = (bf16[16,768]{1,0:T(8,128)(2,1)}, bf16[16,768]{1,0:T(8,128)(2,1)S(1)}, u32[]{:S(2)}, u32[]{:S(2)}) collective-permute-start(bf16[16,768]{1,0:T(8,128)(2,1)} %new_ref.1), channel_id=1, source_target_pairs={{0,24},{8,16},{16,8},{24,0},{1,25},{9,17},{17,9},{25,1},{2,26},{10... | collective-permute-start | bytes 73736 | tf_op jit(solution)/shard_map/ppermute | solution.py:21
  5.3 0.5 %collective-permute-start.2 = (bf16[16,768]{1,0:T(8,128)(2,1)}, bf16[16,768]{1,0:T(8,128)(2,1)S(1)}, u32[]{:S(2)}, u32[]{:S(2)}) collective-permute-start(bf16[16,768]{1,0:T(8,128)(2,1)} %new_ref.1), channel_id=1, source_target_pairs={{0,16},{8,24},{16,0},{24,8},{1,17},{9,25},{17,1},{25,9},{2,18},{10... | collective-permute-start | bytes 73736 | tf_op jit(solution)/shard_map/ppermute | solution.py:21
  5.8 0.7 %shard_map.67 = s32[1,64]{1,0:T(1,128)S(1)} custom-call(s32[1,64]{1,0:T(1,128)} %ids_ref.3), custom_call_target="tpu_custom_call" | custom-call | tf_op jit(solution)/shard_map/pallas_call | solution.py:33
  6.4 0.0 collective-permute-done
  6.5 1.6 %collective-permute-start.4 = (s32[2,64]{1,0:T(2,128)S(1)}, s32[2,64]{1,0:T(2,128)S(1)}, u32[]{:S(2)}, u32[]{:S(2)}) collective-permute-start(s32[2,64]{1,0:T(2,128)S(1)} %pad_add_fusion.1.unused.ids_ref), channel_id=1, source_target_pairs={{0,2},{1,3},{2,0},{3,1},{4,6},{5,7},{6,4},{7,5},{8,10},{9,11},{10,... | collective-permute-start | bytes 1544 | tf_op jit(solution)/shard_map/ppermute | solution.py:21
  8.1 2.1 %shard_map.68 = (bf16[2048,768]{1,0:T(8,128)(2,1)S(1)}, f32[1,2048]{1,0:T(1,128)S(1)}, bf16[16,768]{1,0:T(8,128)(2,1)S(1)}) custom-call(bf16[2048,768]{1,0:T(8,128)(2,1)} %heads_ref.1, bf16[16,768]{1,0:T(8,128)(2,1)} %new_ref.1, s32[2,64]{1,0:T(2,128)S(1)} %pad_add_fusion.1.unused.ids_ref), custom_call_target="tpu_custom_call" | custom-call | tf_op jit(solution)/shard_map/pallas_call | solution.py:33
  10.2 0.0 collective-permute-done.1.refs_1_
  10.2 0.0 collective-permute-done.3.refs_3_
  10.3 0.0 collective-permute-done.2.refs_2_
  10.3 0.0 copy-start
  10.3 0.0 copy-start.1
  10.3 1.2 %shard_map.69 = (f32[8,128]{1,0:T(8,128)S(1)}, s32[2,64]{1,0:T(2,128)S(1)}) custom-call(s32[2,64]{1,0:T(2,128)S(1)} %pad_add_fusion.1.unused.ids_ref, bf16[2048,768]{1,0:T(8,128)(2,1)S(1)} %get-tuple-element.11.heads_ref, f32[1,2048]{1,0:T(1,128)S(1)} %get-tuple-element.12.head_sq_ref, bf16[16,768]{1,0:T(8,128)(2,1)S(1)} %get-tuple-element.13.refs_0_, ...), custom_call_target="tpu_custom_call" | custom-call | tf_op jit(solution)/shard_map/pallas_call | solution.py:33
  11.5 0.1 collective-permute-start.6
  11.6 0.0 collective-permute-done.4
  11.6 2.7 %collective-permute-start.5 = (s32[4,64]{1,0:T(4,128)S(1)}, s32[4,64]{1,0:T(4,128)S(1)}, u32[]{:S(2)}, u32[]{:S(2)}) collective-permute-start(s32[4,64]{1,0:T(4,128)S(1)} %pad_add_fusion.near_ref), channel_id=1, source_target_pairs={{0,4},{1,5},{2,6},{3,7},{4,0},{5,1},{6,2},{7,3},{8,12},{9,13},{10,... | collective-permute-start | bytes 3080 | tf_op jit(solution)/shard_map/ppermute | solution.py:21
  14.3 0.0 collective-permute-done.6
  14.3 1.5 %collective-permute-start.7 = (f32[8,128]{1,0:T(8,128)S(1)}, f32[8,128]{1,0:T(8,128)S(1)}, u32[]{:S(2)}, u32[]{:S(2)}) collective-permute-start(f32[8,128]{1,0:T(8,128)S(1)} %add.3.unused.mine_ref), channel_id=1, source_target_pairs={{0,16},{8,24},{16,0},{24,8},{1,17},{9,25},{17,1},{25,9},{2,18},{10... | collective-permute-start | bytes 12296 | tf_op jit(solution)/shard_map/ppermute | solution.py:21
  15.8 0.4 %collective-permute-done.5.far_ref = s32[4,64]{1,0:T(4,128)S(1)} collective-permute-done((s32[4,64]{1,0:T(4,128)S(1)}, s32[4,64]{1,0:T(4,128)S(1)}, u32[]{:S(2)}, u32[]{:S(2)}) %collective-permute-start.5) | collective-permute-done | bytes 1056 | tf_op jit(solution)/shard_map/ppermute | solution.py:21
  16.2 0.8 %shard_map.70.rows_ref = bf16[128,768]{1,0:T(8,128)(2,1)S(1)} custom-call(s32[4,64]{1,0:T(4,128)S(1)} %pad_add_fusion.near_ref, s32[4,64]{1,0:T(4,128)S(1)} %collective-permute-done.5.far_ref, bf16[2048,768]{1,0:T(8,128)(2,1)S(1)} %get-tuple-element.11.heads_ref, f32[8,128]{1,0:T(8,128)S(1)} %add.3.unused.mine_ref), custom_call_target="tpu_custom_call" | custom-call | flops 402653184 | bytes 3145728 | tf_op jit(solution)/shard_map/pallas_call | solution.py:33
  16.9 0.9 %collective-permute-done.7.other_ref = f32[8,128]{1,0:T(8,128)S(1)} collective-permute-done((f32[8,128]{1,0:T(8,128)S(1)}, f32[8,128]{1,0:T(8,128)S(1)}, u32[]{:S(2)}, u32[]{:S(2)}) %collective-permute-start.7) | collective-permute-done | bytes 4128 | tf_op jit(solution)/shard_map/ppermute | solution.py:21
  17.9 9.9 %all_to_all.5.listed_ref = bf16[8,104,128]{2,1,0:T(8,128)(2,1)S(1)} all-to-all(bf16[8,104,128]{2,1,0:T(8,128)(2,1)S(1)} %shard_map.71), channel_id=1, replica_groups={{5,4,7,6,1,0,3,2},{13,12,15,14,9,8,11,10},{21,20,23,22,17,16,19,18},{29..., dimensions={0} | all-to-all | bytes 425984 | tf_op jit(solution)/shard_map/all_to_all | solution.py:293
  27.8 0.0 copy-done
  27.8 0.0 copy-done.1
  27.8 1.1 %shard_map.72 = (f32[1,16]{1,0:T(1,128)}, f32[1,16]{1,0:T(1,128)}, f32[1,64,128]{2,1,0:T(8,128)}) custom-call(s32[1,64]{1,0:T(1,128)S(1)} %copy-done.1, bf16[8,104,128]{2,1,0:T(8,128)(2,1)S(1)} %all_to_all.5.listed_ref, bf16[1,128,768]{2,1,0:T(8,128)(2,1)S(1)} %copy-done), custom_call_target="tpu_custom_call" | custom-call | flops 25165824 | bytes 393216 | tf_op jit(solution)/shard_map/pallas_call | solution.py:33
  (4 shorter events, 0.1 us)
Async XLA Ops:
  0.6 5.8 %collective-permute-start = (s32[1,64]{1,0:T(1,128)}, s32[1,64]{1,0:T(1,128)S(1)}, u32[]{:S(2)}, u32[]{:S(2)}) collective-permute-start(s32[1,64]{1,0:T(1,128)} %ids_ref.3), channel_id=1, source_target_pairs={{0,1},{1,0},{2,3},{3,2},{4,5},{5,4},{6,7},{7,6},{8,9},{9,8},{10,11... | collective-permute-start | bytes 776 | tf_op jit(solution)/shard_map/ppermute | solution.py:21
  3.6 6.6 %collective-permute-start.1 = (bf16[16,768]{1,0:T(8,128)(2,1)}, bf16[16,768]{1,0:T(8,128)(2,1)S(1)}, u32[]{:S(2)}, u32[]{:S(2)}) collective-permute-start(bf16[16,768]{1,0:T(8,128)(2,1)} %new_ref.1), channel_id=1, source_target_pairs={{0,8},{8,0},{16,24},{24,16},{1,9},{9,1},{17,25},{25,17},{2,10},{10... | collective-permute-start | bytes 73736 | tf_op jit(solution)/shard_map/ppermute | solution.py:21
  3.6 6.6 %collective-permute-start.3 = (bf16[16,768]{1,0:T(8,128)(2,1)}, bf16[16,768]{1,0:T(8,128)(2,1)S(1)}, u32[]{:S(2)}, u32[]{:S(2)}) collective-permute-start(bf16[16,768]{1,0:T(8,128)(2,1)} %new_ref.1), channel_id=1, source_target_pairs={{0,24},{8,16},{16,8},{24,0},{1,25},{9,17},{17,9},{25,1},{2,26},{10... | collective-permute-start | bytes 73736 | tf_op jit(solution)/shard_map/ppermute | solution.py:21
  5.3 5.0 %collective-permute-start.2 = (bf16[16,768]{1,0:T(8,128)(2,1)}, bf16[16,768]{1,0:T(8,128)(2,1)S(1)}, u32[]{:S(2)}, u32[]{:S(2)}) collective-permute-start(bf16[16,768]{1,0:T(8,128)(2,1)} %new_ref.1), channel_id=1, source_target_pairs={{0,16},{8,24},{16,0},{24,8},{1,17},{9,25},{17,1},{25,9},{2,18},{10... | collective-permute-start | bytes 73736 | tf_op jit(solution)/shard_map/ppermute | solution.py:21
  6.5 5.1 %collective-permute-start.4 = (s32[2,64]{1,0:T(2,128)S(1)}, s32[2,64]{1,0:T(2,128)S(1)}, u32[]{:S(2)}, u32[]{:S(2)}) collective-permute-start(s32[2,64]{1,0:T(2,128)S(1)} %pad_add_fusion.1.unused.ids_ref), channel_id=1, source_target_pairs={{0,2},{1,3},{2,0},{3,1},{4,6},{5,7},{6,4},{7,5},{8,10},{9,11},{10,... | collective-permute-start | bytes 1544 | tf_op jit(solution)/shard_map/ppermute | solution.py:21
  10.3 17.6 %copy-start = (bf16[1,128,768]{2,1,0:T(8,128)(2,1)S(1)}, bf16[1,128,768]{2,1,0:T(8,128)(2,1)}, u32[]{:S(2)}) copy-start(bf16[1,128,768]{2,1,0:T(8,128)(2,1)} %vectors_ref.1) | copy-start | bytes 589828
  10.3 17.6 %copy-start.1 = (s32[1,64]{1,0:T(1,128)S(1)}, s32[1,64]{1,0:T(1,128)}, u32[]{:S(2)}) copy-start(s32[1,64]{1,0:T(1,128)} %ids_ref.3) | copy-start | bytes 772
  11.5 2.8 %collective-permute-start.6 = (f32[8,128]{1,0:T(8,128)S(1)}, f32[8,128]{1,0:T(8,128)S(1)}, u32[]{:S(2)}, u32[]{:S(2)}) collective-permute-start(f32[8,128]{1,0:T(8,128)S(1)} %get-tuple-element.15), channel_id=1, source_target_pairs={{0,8},{8,0},{16,24},{24,16},{1,9},{9,1},{17,25},{25,17},{2,10},{10... | collective-permute-start | bytes 12296 | tf_op jit(solution)/shard_map/ppermute | solution.py:21
  11.6 4.5 %collective-permute-start.5 = (s32[4,64]{1,0:T(4,128)S(1)}, s32[4,64]{1,0:T(4,128)S(1)}, u32[]{:S(2)}, u32[]{:S(2)}) collective-permute-start(s32[4,64]{1,0:T(4,128)S(1)} %pad_add_fusion.near_ref), channel_id=1, source_target_pairs={{0,4},{1,5},{2,6},{3,7},{4,0},{5,1},{6,2},{7,3},{8,12},{9,13},{10,... | collective-permute-start | bytes 3080 | tf_op jit(solution)/shard_map/ppermute | solution.py:21
  14.3 3.6 %collective-permute-start.7 = (f32[8,128]{1,0:T(8,128)S(1)}, f32[8,128]{1,0:T(8,128)S(1)}, u32[]{:S(2)}, u32[]{:S(2)}) collective-permute-start(f32[8,128]{1,0:T(8,128)S(1)} %add.3.unused.mine_ref), channel_id=1, source_target_pairs={{0,16},{8,24},{16,0},{24,8},{1,17},{9,25},{17,1},{25,9},{2,18},{10... | collective-permute-start | bytes 12296 | tf_op jit(solution)/shard_map/ppermute | solution.py:21

commit v19 on v17

--- a/solution.py
+++ b/solution.py
@@ -88,17 +88,23 @@
     wanted = jnp.sum(
         jnp.where(pick, jnp.broadcast_to(local[:, None, :] + 1, shape), 0), axis=2, keepdims=True
     ).reshape(members * slots, 1)
-    onehot = (wanted == iota((members * slots, head_dev), 1) + 1).astype(jnp.bfloat16)
-    return jnp.dot(
-        onehot, heads_ref[...], preferred_element_type=jnp.float32
-    ).astype(jnp.bfloat16)
+    rows = None
+    tile = 512
+    for start in range(0, head_dev, tile):
+        onehot = wanted == iota((members * slots, tile), 1) + (start + 1)
+        part = jnp.dot(
+            onehot.astype(jnp.bfloat16), heads_ref[start:start + tile, :],
+            preferred_element_type=jnp.float32,
+        )
+        rows = part if rows is None else rows + part
+    return rows.astype(jnp.bfloat16)
 
 
 def crowding(queries, heads_ref, head_sq_ref):
     head_dev, width = heads_ref.shape
     query_sq = jnp.sum(jnp.square(queries.astype(jnp.float32)), axis=1, keepdims=True)
-    total_w = jnp.zeros((queries.shape[0], 1), jnp.float32)
-    total_we = jnp.zeros((queries.shape[0], 1), jnp.float32)
+    total_w = jnp.zeros((queries.shape[0], LANES), jnp.float32)
+    total_we = jnp.zeros((queries.shape[0], LANES), jnp.float32)
     tile = 512
     for start in range(0, head_dev, tile):
         dots = lax.dot_general(
@@ -109,8 +115,12 @@
         excess = (query_sq + head_sq - 2.0 * dots) * (1.0 / width)
         inverse = 1.0 / (1.0 + excess)
         weight = inverse * inverse
-        total_w = total_w + jnp.sum(weight, axis=1, keepdims=True)
-        total_we = total_we + jnp.sum(weight * excess, axis=1, keepdims=True)
+        weighted = weight * excess
+        for column in range(0, tile, LANES):
+            total_w = total_w + weight[:, column:column + LANES]
+            total_we = total_we + weighted[:, column:column + LANES]
+    total_w = jnp.sum(total_w, axis=1, keepdims=True)
+    total_we = jnp.sum(total_we, axis=1, keepdims=True)
     return total_w, total_we
 
 
@@ -121,18 +131,17 @@
     queries = jnp.concatenate([ref[...] for ref in query_refs], axis=0)
     new_count = queries.shape[0] // groups
     totals = crowding(queries, heads_ref, head_sq_ref)
-    lane = iota((new_count, LANES), 1)
-    row = iota((new_count, LANES), 0)
-    line = iota(sums_ref.shape, 0)
-    sums = jnp.zeros(sums_ref.shape, jnp.float32)
-    for mask in range(groups):
-        part = slice(mask * new_count, (mask + 1) * new_count)
-        for kind in range(2):
-            place = (kind * groups + (here ^ mask)) * new_count
-            spread_out = jnp.where(lane == row + place % LANES, totals[kind][part], 0.0)
-            spread_out = jnp.sum(spread_out, axis=0, keepdims=True)
-            sums = sums + jnp.where(line == place // LANES, spread_out, 0.0)
-    sums_ref[...] = sums
+    shape = (groups * new_count, LANES)
+    row = iota(shape, 0)
+    place = (here ^ (row // new_count)) * new_count + row % new_count
+    sums_ref[...] = jnp.zeros(sums_ref.shape, jnp.float32)
+    lines = 2 * groups * new_count // LANES
+    for line in range(lines):
+        lane = iota(shape, 1) + line * LANES
+        spread_out = jnp.where(lane == place, totals[0], 0.0) + jnp.where(
+            lane == place + groups * new_count, totals[1], 0.0
+        )
+        sums_ref[line:line + 1, :] = jnp.sum(spread_out, axis=0, keepdims=True)
 
 
 def gather_kernel(members, slots, near_ref, far_ref, heads_ref, unused, rows_ref, ids_ref):
@@ -164,10 +173,9 @@
         out_ref[member, chunks * slots:, :] = tail
 
 
-def distances(slots, head_dev, ids_ref, listed_ref, vectors_ref, out_ref):
+def prepare_kernel(members, slots, head_dev, ids_ref, vectors_ref, unused, back_ref, vec_sq_ref):
     near = ids_ref.shape[1]
-    members = listed_ref.shape[0]
-    block, width = vectors_ref.shape[1:]
+    block = vectors_ref.shape[1]
     square = (near, near)
     owner_row = jnp.broadcast_to(lax.div(ids_ref[...], head_dev), square)
     eye = iota(square, 0) == iota(square, 1)
@@ -175,29 +183,33 @@
     before = (owner_row == owner) & (iota(square, 1) < iota(square, 0))
     place = jnp.sum(before.astype(jnp.int32), axis=1, keepdims=True)
     source = (owner ^ (members // 2)) * slots + place
-    back = (source == iota((near, members * slots), 1)).astype(jnp.bfloat16)
+    back_ref[...] = (source == iota(back_ref.shape, 1)).astype(jnp.bfloat16)
+    vec_sq = jnp.sum(jnp.square(vectors_ref[0].astype(jnp.float32)), axis=1, keepdims=True)
+    diagonal = iota((block, block), 0) == iota((block, block), 1)
+    vec_sq_ref[...] = jnp.sum(jnp.where(diagonal, vec_sq, 0.0), axis=0, keepdims=True)
+
+
+def distances(slots, back_ref, vec_sq_ref, listed_ref, vectors_ref, out_ref):
+    members = listed_ref.shape[0]
+    width = vectors_ref.shape[2]
     rows = []
     for chunk in range(width // LANES):
         part = listed_ref[:, chunk * slots:(chunk + 1) * slots, :].reshape(members * slots, LANES)
-        rows.append(jnp.dot(back, part, preferred_element_type=jnp.float32))
+        rows.append(jnp.dot(back_ref[...], part, preferred_element_type=jnp.float32))
     rows = jnp.concatenate(rows, axis=1)
     row_sq = jnp.sum(jnp.square(rows), axis=1, keepdims=True)
-    vec = vectors_ref[0]
-    vec_sq = jnp.sum(jnp.square(vec.astype(jnp.float32)), axis=1, keepdims=True)
-    diagonal = iota((block, block), 0) == iota((block, block), 1)
-    vec_sq = jnp.sum(jnp.where(diagonal, vec_sq, 0.0), axis=0, keepdims=True)
     dots = lax.dot_general(
-        rows.astype(jnp.bfloat16), vec, (((1,), (1,)), ((), ())),
+        rows.astype(jnp.bfloat16), vectors_ref[0], (((1,), (1,)), ((), ())),
         preferred_element_type=jnp.float32,
     )
-    out_ref[0] = (row_sq + vec_sq - 2.0 * dots) * (1.0 / width)
+    out_ref[0] = (row_sq + vec_sq_ref[...] - 2.0 * dots) * (1.0 / width)
 
 
 def tail_kernel(
-    groups, slots, head_dev, total_heads, ids_ref, listed_ref, vectors_ref,
+    groups, slots, total_heads, back_ref, vec_sq_ref, listed_ref, vectors_ref,
     density_ref, spread_ref, out_ref,
 ):
-    distances(slots, head_dev, ids_ref, listed_ref, vectors_ref, out_ref)
+    distances(slots, back_ref, vec_sq_ref, listed_ref, vectors_ref, out_ref)
     here = lax.axis_index("group")
     members = listed_ref.shape[0]
     new_count = density_ref.shape[1]
@@ -290,20 +302,31 @@
         (rows, sums, from_partner(sums, "group", mask)),
         (0, members * slots * width * 4),
     )
+    sent = message
     message = lax.all_to_all(
-        message, "member", 0, 0, tiled=True, axis_index_groups=[turned(members)]
-    )
-
+        sent, "member", 0, 0, tiled=True, axis_index_groups=[turned(members)]
+    )
+
+    back, vec_sq = call(
+        functools.partial(prepare_kernel, members, slots, head_dev),
+        (
+            jax.ShapeDtypeStruct((near, members * slots), jnp.bfloat16),
+            jax.ShapeDtypeStruct((1, vectors.shape[1]), jnp.float32),
+        ),
+        (near_ids, vectors, sent),
+        (vectors.size * 2, vectors.size * 2),
+        spaces=[VMEM, VMEM, pl.ANY],
+    )
     density, spread, reassign = call(
         functools.partial(
-            tail_kernel, groups, slots, head_dev, float(head_dev * groups * members)
+            tail_kernel, groups, slots, float(head_dev * groups * members)
         ),
         (
             jax.ShapeDtypeStruct((1, new_count), jnp.float32),
             jax.ShapeDtypeStruct((1, new_count), jnp.float32),
             jax.ShapeDtypeStruct((1, near, vectors.shape[1]), jnp.float32),
         ),
-        (near_ids, message, vectors),
+        (back, vec_sq, message, vectors),
         (4 * near * vectors.shape[1] * width, vectors.size * 4),
     )
     return (density[0], spread[0], reassign)

time: 29 us -> 30.4 us (1.048)
  blocking collectives: 9.81 us -> 0 us
  waiting for transfers between devices: 1.31 us -> 6.69 us
  starting transfers between devices: 11 us -> 16 us
  Pallas kernels: 5.94 us -> 6.65 us
    all_to_all x1 -> x0, blocking collectives: 9.81 us -> none  [per_device(): lax.all_to_all(message, 'member', 0, 0, tiled=True, axis_index_groups=[tu...]
    all_to_all x0 -> x1, waiting for transfers between devices: none -> 5.38 us  [per_device(): lax.all_to_all(sent, 'member', 0, 0, tiled=True, axis_index_groups=[turne...]
    all_to_all x0 -> x1, starting transfers between devices: none -> 4.99 us  [per_device(): lax.all_to_all(sent, 'member', 0, 0, tiled=True, axis_index_groups=[turne...]
    pallas_call x6 -> x7, Pallas kernels: 5.94 us -> 6.65 us  [call(): pl.pallas_call(body, out_shape=shapes, in_specs=[pl.BlockSpec(memory_spac...]
  transfers between devices with their start and end apart: 8 -> 9, of which waited for: 2 -> 3; matrix products, arithmetic and copies ran while one was open for 0% -> 0% of each run, Pallas kernels for 16% -> 16%
where the time goes in v19:
time: 30.4 us; the launch traced here: 30.1 us
  starting transfers between devices  16 us (53%)
  waiting for transfers between devices  6.69 us (22%)
  Pallas kernels  6.65 us (22%)
  between operations  0.74 us (2%)
    ppermute x8, starting transfers between devices, from_partner(): lax.ppermute(value, axis, [(source, source ^ mask) for source in range(co...  11 us
    pallas_call x7, Pallas kernels, call(): pl.pallas_call(body, out_shape=shapes, in_specs=[pl.BlockSpec(memory_spac...  6.65 us
    all_to_all x1, waiting for transfers between devices, per_device(): lax.all_to_all(sent, 'member', 0, 0, tiled=True, axis_index_groups=[turne...  5.38 us
    all_to_all x1, starting transfers between devices, per_device(): lax.all_to_all(sent, 'member', 0, 0, tiled=True, axis_index_groups=[turne...  4.99 us
    ppermute x8, waiting for transfers between devices, from_partner(): lax.ppermute(value, axis, [(source, source ^ mask) for source in range(co...  1.31 us
  transfers between devices with their start and end apart: 9, of which 3 were waited for; matrix products, arithmetic and copies ran while one was open for 0% of the time, Pallas kernels for 16%

profile of v19, /device:TPU:0, one launch (start us, length us, event | category | flops | bytes accessed | tf_op | source)
XLA Modules:
  0.0 30.1 jit_solution(8560310298739979406)
XLA Ops:
  0.6 3.0 %collective-permute-start = (s32[1,64]{1,0:T(1,128)}, s32[1,64]{1,0:T(1,128)S(1)}, u32[]{:S(2)}, u32[]{:S(2)}) collective-permute-start(s32[1,64]{1,0:T(1,128)} %ids_ref.3), channel_id=1, source_target_pairs={{0,1},{1,0},{2,3},{3,2},{4,5},{5,4},{6,7},{7,6},{8,9},{9,8},{10,11... | collective-permute-start | bytes 776 | tf_op jit(solution)/shard_map/ppermute | solution.py:21
  3.6 0.0 collective-permute-start.1
  3.6 1.6 %collective-permute-start.3 = (bf16[16,768]{1,0:T(8,128)(2,1)}, bf16[16,768]{1,0:T(8,128)(2,1)S(1)}, u32[]{:S(2)}, u32[]{:S(2)}) collective-permute-start(bf16[16,768]{1,0:T(8,128)(2,1)} %new_ref.1), channel_id=1, source_target_pairs={{0,24},{8,16},{16,8},{24,0},{1,25},{9,17},{17,9},{25,1},{2,26},{10... | collective-permute-start | bytes 73736 | tf_op jit(solution)/shard_map/ppermute | solution.py:21
  5.3 0.5 %collective-permute-start.2 = (bf16[16,768]{1,0:T(8,128)(2,1)}, bf16[16,768]{1,0:T(8,128)(2,1)S(1)}, u32[]{:S(2)}, u32[]{:S(2)}) collective-permute-start(bf16[16,768]{1,0:T(8,128)(2,1)} %new_ref.1), channel_id=1, source_target_pairs={{0,16},{8,24},{16,0},{24,8},{1,17},{9,25},{17,1},{25,9},{2,18},{10... | collective-permute-start | bytes 73736 | tf_op jit(solution)/shard_map/ppermute | solution.py:21
  5.8 0.7 %shard_map.67 = s32[1,64]{1,0:T(1,128)S(1)} custom-call(s32[1,64]{1,0:T(1,128)} %ids_ref.3), custom_call_target="tpu_custom_call" | custom-call | tf_op jit(solution)/shard_map/pallas_call | solution.py:33
  6.4 0.0 collective-permute-done
  6.5 1.6 %collective-permute-start.4 = (s32[2,64]{1,0:T(2,128)S(1)}, s32[2,64]{1,0:T(2,128)S(1)}, u32[]{:S(2)}, u32[]{:S(2)}) collective-permute-start(s32[2,64]{1,0:T(2,128)S(1)} %pad_add_fusion.1.unused.ids_ref), channel_id=1, source_target_pairs={{0,2},{1,3},{2,0},{3,1},{4,6},{5,7},{6,4},{7,5},{8,10},{9,11},{10,... | collective-permute-start | bytes 1544 | tf_op jit(solution)/shard_map/ppermute | solution.py:21
  8.1 2.1 %shard_map.68 = (bf16[2048,768]{1,0:T(8,128)(2,1)S(1)}, f32[1,2048]{1,0:T(1,128)S(1)}, bf16[16,768]{1,0:T(8,128)(2,1)S(1)}) custom-call(bf16[2048,768]{1,0:T(8,128)(2,1)} %heads_ref.1, bf16[16,768]{1,0:T(8,128)(2,1)} %new_ref.1, s32[2,64]{1,0:T(2,128)S(1)} %pad_add_fusion.1.unused.ids_ref), custom_call_target="tpu_custom_call" | custom-call | tf_op jit(solution)/shard_map/pallas_call | solution.py:33
  10.2 0.0 collective-permute-done.1.refs_1_
  10.2 0.0 collective-permute-done.3.refs_3_
  10.3 0.0 collective-permute-done.2.refs_2_
  10.3 0.0 copy-start
  10.3 0.0 copy-start.1
  10.3 1.2 %shard_map.69 = (f32[8,128]{1,0:T(8,128)S(1)}, s32[2,64]{1,0:T(2,128)S(1)}) custom-call(s32[2,64]{1,0:T(2,128)S(1)} %pad_add_fusion.1.unused.ids_ref, bf16[2048,768]{1,0:T(8,128)(2,1)S(1)} %get-tuple-element.13.heads_ref, f32[1,2048]{1,0:T(1,128)S(1)} %get-tuple-element.14.head_sq_ref, bf16[16,768]{1,0:T(8,128)(2,1)S(1)} %get-tuple-element.15.refs_0_, ...), custom_call_target="tpu_custom_call" | custom-call | tf_op jit(solution)/shard_map/pallas_call | solution.py:33
  11.5 0.1 collective-permute-start.6
  11.6 0.0 collective-permute-done.4
  11.6 2.6 %collective-permute-start.5 = (s32[4,64]{1,0:T(4,128)S(1)}, s32[4,64]{1,0:T(4,128)S(1)}, u32[]{:S(2)}, u32[]{:S(2)}) collective-permute-start(s32[4,64]{1,0:T(4,128)S(1)} %pad_add_fusion.near_ref), channel_id=1, source_target_pairs={{0,4},{1,5},{2,6},{3,7},{4,0},{5,1},{6,2},{7,3},{8,12},{9,13},{10,... | collective-permute-start | bytes 3080 | tf_op jit(solution)/shard_map/ppermute | solution.py:21
  14.2 0.0 collective-permute-done.6
  14.2 1.5 %collective-permute-start.7 = (f32[8,128]{1,0:T(8,128)S(1)}, f32[8,128]{1,0:T(8,128)S(1)}, u32[]{:S(2)}, u32[]{:S(2)}) collective-permute-start(f32[8,128]{1,0:T(8,128)S(1)} %add.3.unused.mine_ref), channel_id=1, source_target_pairs={{0,16},{8,24},{16,0},{24,8},{1,17},{9,25},{17,1},{25,9},{2,18},{10... | collective-permute-start | bytes 12296 | tf_op jit(solution)/shard_map/ppermute | solution.py:21
  15.8 0.4 %collective-permute-done.5.far_ref = s32[4,64]{1,0:T(4,128)S(1)} collective-permute-done((s32[4,64]{1,0:T(4,128)S(1)}, s32[4,64]{1,0:T(4,128)S(1)}, u32[]{:S(2)}, u32[]{:S(2)}) %collective-permute-start.5) | collective-permute-done | bytes 1056 | tf_op jit(solution)/shard_map/ppermute | solution.py:21
  16.1 0.8 %shard_map.70.rows_ref = bf16[128,768]{1,0:T(8,128)(2,1)S(1)} custom-call(s32[4,64]{1,0:T(4,128)S(1)} %pad_add_fusion.near_ref, s32[4,64]{1,0:T(4,128)S(1)} %collective-permute-done.5.far_ref, bf16[2048,768]{1,0:T(8,128)(2,1)S(1)} %get-tuple-element.13.heads_ref, f32[8,128]{1,0:T(8,128)S(1)} %add.3.unused.mine_ref), custom_call_target="tpu_custom_call" | custom-call | flops 402653184 | bytes 3145728 | tf_op jit(solution)/shard_map/pallas_call | solution.py:33
  16.9 0.9 %collective-permute-done.7.other_ref = f32[8,128]{1,0:T(8,128)S(1)} collective-permute-done((f32[8,128]{1,0:T(8,128)S(1)}, f32[8,128]{1,0:T(8,128)S(1)}, u32[]{:S(2)}, u32[]{:S(2)}) %collective-permute-start.7) | collective-permute-done | bytes 4128 | tf_op jit(solution)/shard_map/ppermute | solution.py:21
  17.9 0.7 %shard_map.71.unused = bf16[8,104,128]{2,1,0:T(8,128)(2,1)} custom-call(bf16[128,768]{1,0:T(8,128)(2,1)S(1)} %shard_map.70.rows_ref, f32[8,128]{1,0:T(8,128)S(1)} %add.3.unused.mine_ref, f32[8,128]{1,0:T(8,128)S(1)} %collective-permute-done.7.other_ref), custom_call_target="tpu_custom_call" | custom-call | bytes 393216 | tf_op jit(solution)/shard_map/pallas_call | solution.py:33
  18.6 5.0 %all-to-all-start = ((bf16[8,104,128]{2,1,0:T(8,128)(2,1)}), bf16[8,104,128]{2,1,0:T(8,128)(2,1)S(1)}, u32[]{:S(2)}, u32[]{:S(2)}) async-start(bf16[8,104,128]{2,1,0:T(8,128)(2,1)} %shard_map.71.unused), calls=%async_computation | async-start | bytes 425984 | tf_op jit(solution)/shard_map/all_to_all | solution.py:306
  23.6 0.0 copy-done
  23.6 0.0 copy-done.1
  23.6 0.2 shard_map.72
  23.8 5.4 %all-to-all-done.listed_ref = bf16[8,104,128]{2,1,0:T(8,128)(2,1)S(1)} async-done(((bf16[8,104,128]{2,1,0:T(8,128)(2,1)}), bf16[8,104,128]{2,1,0:T(8,128)(2,1)S(1)}, u32[]{:S(2)}, u32[]{:S(2)}) %all-to-all-start) | async-done | bytes 213024 | tf_op jit(solution)/shard_map/all_to_all | solution.py:306
  29.2 1.0 %shard_map.73 = (f32[1,16]{1,0:T(1,128)}, f32[1,16]{1,0:T(1,128)}, f32[1,64,128]{2,1,0:T(8,128)}) custom-call(bf16[64,128]{1,0:T(8,128)(2,1)S(1)} %get-tuple-element.18.back_ref, f32[1,128]{1,0:T(1,128)S(1)} %get-tuple-element.19.vec_sq_ref, bf16[8,104,128]{2,1,0:T(8,128)(2,1)S(1)} %all-to-all-done.listed_ref, bf16[1,128,768]{2,1,0:T(8,128)(2,1)S(1)} %copy-done), custom_call_target="tpu_custom_call" | custom-call | flops 25165824 | bytes 393216 | tf_op jit(solution)/shard_map/pallas_call | solution.py:33
  (3 shorter events, 0.0 us)
Async XLA Ops:
  0.6 5.8 %collective-permute-start = (s32[1,64]{1,0:T(1,128)}, s32[1,64]{1,0:T(1,128)S(1)}, u32[]{:S(2)}, u32[]{:S(2)}) collective-permute-start(s32[1,64]{1,0:T(1,128)} %ids_ref.3), channel_id=1, source_target_pairs={{0,1},{1,0},{2,3},{3,2},{4,5},{5,4},{6,7},{7,6},{8,9},{9,8},{10,11... | collective-permute-start | bytes 776 | tf_op jit(solution)/shard_map/ppermute | solution.py:21
  3.6 6.6 %collective-permute-start.1 = (bf16[16,768]{1,0:T(8,128)(2,1)}, bf16[16,768]{1,0:T(8,128)(2,1)S(1)}, u32[]{:S(2)}, u32[]{:S(2)}) collective-permute-start(bf16[16,768]{1,0:T(8,128)(2,1)} %new_ref.1), channel_id=1, source_target_pairs={{0,8},{8,0},{16,24},{24,16},{1,9},{9,1},{17,25},{25,17},{2,10},{10... | collective-permute-start | bytes 73736 | tf_op jit(solution)/shard_map/ppermute | solution.py:21
  3.6 6.6 %collective-permute-start.3 = (bf16[16,768]{1,0:T(8,128)(2,1)}, bf16[16,768]{1,0:T(8,128)(2,1)S(1)}, u32[]{:S(2)}, u32[]{:S(2)}) collective-permute-start(bf16[16,768]{1,0:T(8,128)(2,1)} %new_ref.1), channel_id=1, source_target_pairs={{0,24},{8,16},{16,8},{24,0},{1,25},{9,17},{17,9},{25,1},{2,26},{10... | collective-permute-start | bytes 73736 | tf_op jit(solution)/shard_map/ppermute | solution.py:21
  5.3 5.0 %collective-permute-start.2 = (bf16[16,768]{1,0:T(8,128)(2,1)}, bf16[16,768]{1,0:T(8,128)(2,1)S(1)}, u32[]{:S(2)}, u32[]{:S(2)}) collective-permute-start(bf16[16,768]{1,0:T(8,128)(2,1)} %new_ref.1), channel_id=1, source_target_pairs={{0,16},{8,24},{16,0},{24,8},{1,17},{9,25},{17,1},{25,9},{2,18},{10... | collective-permute-start | bytes 73736 | tf_op jit(solution)/shard_map/ppermute | solution.py:21
  6.5 5.1 %collective-permute-start.4 = (s32[2,64]{1,0:T(2,128)S(1)}, s32[2,64]{1,0:T(2,128)S(1)}, u32[]{:S(2)}, u32[]{:S(2)}) collective-permute-start(s32[2,64]{1,0:T(2,128)S(1)} %pad_add_fusion.1.unused.ids_ref), channel_id=1, source_target_pairs={{0,2},{1,3},{2,0},{3,1},{4,6},{5,7},{6,4},{7,5},{8,10},{9,11},{10,... | collective-permute-start | bytes 1544 | tf_op jit(solution)/shard_map/ppermute | solution.py:21
  10.3 13.3 %copy-start = (bf16[1,128,768]{2,1,0:T(8,128)(2,1)S(1)}, bf16[1,128,768]{2,1,0:T(8,128)(2,1)}, u32[]{:S(2)}) copy-start(bf16[1,128,768]{2,1,0:T(8,128)(2,1)} %vectors_ref.3) | copy-start | bytes 589828
  10.3 13.3 %copy-start.1 = (s32[1,64]{1,0:T(1,128)S(1)}, s32[1,64]{1,0:T(1,128)}, u32[]{:S(2)}) copy-start(s32[1,64]{1,0:T(1,128)} %ids_ref.3) | copy-start | bytes 772
  11.5 2.8 %collective-permute-start.6 = (f32[8,128]{1,0:T(8,128)S(1)}, f32[8,128]{1,0:T(8,128)S(1)}, u32[]{:S(2)}, u32[]{:S(2)}) collective-permute-start(f32[8,128]{1,0:T(8,128)S(1)} %get-tuple-element.17), channel_id=1, source_target_pairs={{0,8},{8,0},{16,24},{24,16},{1,9},{9,1},{17,25},{25,17},{2,10},{10... | collective-permute-start | bytes 12296 | tf_op jit(solution)/shard_map/ppermute | solution.py:21
  11.6 4.5 %collective-permute-start.5 = (s32[4,64]{1,0:T(4,128)S(1)}, s32[4,64]{1,0:T(4,128)S(1)}, u32[]{:S(2)}, u32[]{:S(2)}) collective-permute-start(s32[4,64]{1,0:T(4,128)S(1)} %pad_add_fusion.near_ref), channel_id=1, source_target_pairs={{0,4},{1,5},{2,6},{3,7},{4,0},{5,1},{6,2},{7,3},{8,12},{9,13},{10,... | collective-permute-start | bytes 3080 | tf_op jit(solution)/shard_map/ppermute | solution.py:21
  14.2 3.6 %collective-permute-start.7 = (f32[8,128]{1,0:T(8,128)S(1)}, f32[8,128]{1,0:T(8,128)S(1)}, u32[]{:S(2)}, u32[]{:S(2)}) collective-permute-start(f32[8,128]{1,0:T(8,128)S(1)} %add.3.unused.mine_ref), channel_id=1, source_target_pairs={{0,16},{8,24},{16,0},{24,8},{1,17},{9,25},{17,1},{25,9},{2,18},{10... | collective-permute-start | bytes 12296 | tf_op jit(solution)/shard_map/ppermute | solution.py:21
  18.6 10.6 %all-to-all-start = ((bf16[8,104,128]{2,1,0:T(8,128)(2,1)}), bf16[8,104,128]{2,1,0:T(8,128)(2,1)S(1)}, u32[]{:S(2)}, u32[]{:S(2)}) async-start(bf16[8,104,128]{2,1,0:T(8,128)(2,1)} %shard_map.71.unused), calls=%async_computation | async-start | bytes 425984 | tf_op jit(solution)/shard_map/all_to_all | solution.py:306

commit v20 on v18

--- a/solution.py
+++ b/solution.py
@@ -21,8 +21,13 @@
     return lax.ppermute(value, axis, [(source, source ^ mask) for source in range(count)])
 
 
-def turned(members):
-    return [member ^ (members // 2 + 1) for member in range(members)]
+def middle_first(members):
+    return [members // 2] + [member for member in range(members) if member != members // 2]
+
+
+def first_middle(member, members):
+    middle = members // 2
+    return jnp.where(member == middle, 0, jnp.where(member < middle, member + 1, member))
 
 
 def in_hbm(value):
@@ -140,7 +145,7 @@
     half = members // 2
     ids_ref[:half, :] = near_ref[...]
     ids_ref[half:, :] = far_ref[...]
-    ids = jnp.concatenate([ids_ref[pl.ds(me ^ member, 1), :] for member in turned(members)], axis=0)
+    ids = jnp.concatenate([ids_ref[pl.ds(me ^ member, 1), :] for member in middle_first(members)], axis=0)
     rows_ref[...] = listed_rows(ids, me, slots, heads_ref)
 
 
@@ -164,40 +169,43 @@
         out_ref[member, chunks * slots:, :] = tail
 
 
-def distances(slots, head_dev, ids_ref, listed_ref, vectors_ref, out_ref):
+def prepare_kernel(members, slots, head_dev, ids_ref, vectors_ref, unused, back_ref, vec_sq_ref):
     near = ids_ref.shape[1]
-    members = listed_ref.shape[0]
-    block, width = vectors_ref.shape[1:]
+    block = vectors_ref.shape[1]
     square = (near, near)
     owner_row = jnp.broadcast_to(lax.div(ids_ref[...], head_dev), square)
     eye = iota(square, 0) == iota(square, 1)
     owner = jnp.sum(jnp.where(eye, owner_row, 0), axis=1, keepdims=True)
     before = (owner_row == owner) & (iota(square, 1) < iota(square, 0))
     place = jnp.sum(before.astype(jnp.int32), axis=1, keepdims=True)
-    source = (owner ^ (members // 2 + 1)) * slots + place
-    back = (source == iota((near, members * slots), 1)).astype(jnp.bfloat16)
+    source = first_middle(owner, members) * slots + place
+    back_ref[...] = (source == iota(back_ref.shape, 1)).astype(jnp.bfloat16)
+    vec_sq = jnp.sum(jnp.square(vectors_ref[0].astype(jnp.float32)), axis=1, keepdims=True)
+    diagonal = iota((block, block), 0) == iota((block, block), 1)
+    vec_sq_ref[...] = jnp.sum(jnp.where(diagonal, vec_sq, 0.0), axis=0, keepdims=True)
+
+
+def distances(slots, back_ref, vec_sq_ref, listed_ref, vectors_ref, out_ref):
+    members = listed_ref.shape[0]
+    width = vectors_ref.shape[2]
     rows = []
     for chunk in range(width // LANES):
         part = listed_ref[:, chunk * slots:(chunk + 1) * slots, :].reshape(members * slots, LANES)
-        rows.append(jnp.dot(back, part, preferred_element_type=jnp.float32))
+        rows.append(jnp.dot(back_ref[...], part, preferred_element_type=jnp.float32))
     rows = jnp.concatenate(rows, axis=1)
     row_sq = jnp.sum(jnp.square(rows), axis=1, keepdims=True)
-    vec = vectors_ref[0]
-    vec_sq = jnp.sum(jnp.square(vec.astype(jnp.float32)), axis=1, keepdims=True)
-    diagonal = iota((block, block), 0) == iota((block, block), 1)
-    vec_sq = jnp.sum(jnp.where(diagonal, vec_sq, 0.0), axis=0, keepdims=True)
     dots = lax.dot_general(
-        rows.astype(jnp.bfloat16), vec, (((1,), (1,)), ((), ())),
+        rows.astype(jnp.bfloat16), vectors_ref[0], (((1,), (1,)), ((), ())),
         preferred_element_type=jnp.float32,
     )
-    out_ref[0] = (row_sq + vec_sq - 2.0 * dots) * (1.0 / width)
+    out_ref[0] = (row_sq + vec_sq_ref[...] - 2.0 * dots) * (1.0 / width)
 
 
 def tail_kernel(
-    groups, slots, head_dev, total_heads, ids_ref, listed_ref, vectors_ref,
+    groups, slots, total_heads, back_ref, vec_sq_ref, listed_ref, vectors_ref,
     density_ref, spread_ref, out_ref,
 ):
-    distances(slots, head_dev, ids_ref, listed_ref, vectors_ref, out_ref)
+    distances(slots, back_ref, vec_sq_ref, listed_ref, vectors_ref, out_ref)
     here = lax.axis_index("group")
     members = listed_ref.shape[0]
     new_count = density_ref.shape[1]
@@ -276,10 +284,20 @@
     while mask < groups // 2:
         sums = sums + from_partner(sums, "group", mask)
         mask *= 2
+    back, vec_sq = call(
+        functools.partial(prepare_kernel, members, slots, head_dev),
+        (
+            jax.ShapeDtypeStruct((near, members * slots), jnp.bfloat16),
+            jax.ShapeDtypeStruct((1, vectors.shape[1]), jnp.float32),
+        ),
+        (near_ids, vectors, sums),
+        (0, 0),
+        spaces=[VMEM, VMEM, pl.ANY],
+    )
     rows = call(
         functools.partial(gather_kernel, members, slots),
         jax.ShapeDtypeStruct((members * slots, width), jnp.bfloat16),
-        (ids, far_ids, kept, sums),
+        (ids, far_ids, kept, back),
         (2 * members * slots * head_dev * width, heads.size * 2),
         scratch=[pltpu.VMEM((members, near), jnp.int32)],
         spaces=[VMEM, VMEM, VMEM, pl.ANY],
@@ -291,19 +309,19 @@
         (0, members * slots * width * 4),
     )
     message = lax.all_to_all(
-        message, "member", 0, 0, tiled=True, axis_index_groups=[turned(members)]
+        message, "member", 0, 0, tiled=True, axis_index_groups=[middle_first(members)]
     )
 
     density, spread, reassign = call(
         functools.partial(
-            tail_kernel, groups, slots, head_dev, float(head_dev * groups * members)
+            tail_kernel, groups, slots, float(head_dev * groups * members)
         ),
         (
             jax.ShapeDtypeStruct((1, new_count), jnp.float32),
             jax.ShapeDtypeStruct((1, new_count), jnp.float32),
             jax.ShapeDtypeStruct((1, near, vectors.shape[1]), jnp.float32),
         ),
-        (near_ids, message, vectors),
+        (back, vec_sq, message, vectors),
         (4 * near * vectors.shape[1] * width, vectors.size * 4),
     )
     return (density[0], spread[0], reassign)

time: 29.1 us -> 28.8 us (0.990)
    pallas_call x6 -> x7, Pallas kernels: 5.94 us -> 5.99 us  [call(): pl.pallas_call(body, out_shape=shapes, in_specs=[pl.BlockSpec(memory_spac...]
  transfers between devices with their start and end apart: 8 -> 8, of which waited for: 2 -> 2; matrix products, arithmetic and copies ran while one was open for 0% -> 0% of each run, Pallas kernels for 16% -> 17%
where the time goes in v20:
time: 28.8 us; the launch traced here: 28.6 us
  starting transfers between devices  10.8 us (38%)
  blocking collectives  10 us (35%)
  Pallas kernels  5.99 us (21%)
  waiting for transfers between devices  1.09 us (4%)
  between operations  0.74 us (3%)
    ppermute x8, starting transfers between devices, from_partner(): lax.ppermute(value, axis, [(source, source ^ mask) for source in range(co...  10.8 us
    all_to_all x1, blocking collectives, per_device(): lax.all_to_all(message, 'member', 0, 0, tiled=True, axis_index_groups=[mi...  10 us
    pallas_call x7, Pallas kernels, call(): pl.pallas_call(body, out_shape=shapes, in_specs=[pl.BlockSpec(memory_spac...  5.99 us
    ppermute x8, waiting for transfers between devices, from_partner(): lax.ppermute(value, axis, [(source, source ^ mask) for source in range(co...  1.09 us
  transfers between devices with their start and end apart: 8, of which 2 were waited for; matrix products, arithmetic and copies ran while one was open for 0% of the time, Pallas kernels for 17%

profile of v20, /device:TPU:0, one launch (start us, length us, event | category | flops | bytes accessed | tf_op | source)
XLA Modules:
  0.0 28.6 jit_solution(6685703717455462909)
XLA Ops:
  0.6 3.0 %collective-permute-start = (s32[1,64]{1,0:T(1,128)}, s32[1,64]{1,0:T(1,128)S(1)}, u32[]{:S(2)}, u32[]{:S(2)}) collective-permute-start(s32[1,64]{1,0:T(1,128)} %ids_ref.3), channel_id=1, source_target_pairs={{0,1},{1,0},{2,3},{3,2},{4,5},{5,4},{6,7},{7,6},{8,9},{9,8},{10,11... | collective-permute-start | bytes 776 | tf_op jit(solution)/shard_map/ppermute | solution.py:21
  3.6 0.0 collective-permute-start.1
  3.6 1.5 %collective-permute-start.2 = (bf16[16,768]{1,0:T(8,128)(2,1)}, bf16[16,768]{1,0:T(8,128)(2,1)S(1)}, u32[]{:S(2)}, u32[]{:S(2)}) collective-permute-start(bf16[16,768]{1,0:T(8,128)(2,1)} %new_ref.1), channel_id=1, source_target_pairs={{0,16},{8,24},{16,0},{24,8},{1,17},{9,25},{17,1},{25,9},{2,18},{10... | collective-permute-start | bytes 73736 | tf_op jit(solution)/shard_map/ppermute | solution.py:21
  5.2 0.3 %collective-permute-start.3 = (bf16[16,768]{1,0:T(8,128)(2,1)}, bf16[16,768]{1,0:T(8,128)(2,1)S(1)}, u32[]{:S(2)}, u32[]{:S(2)}) collective-permute-start(bf16[16,768]{1,0:T(8,128)(2,1)} %new_ref.1), channel_id=1, source_target_pairs={{0,24},{8,16},{16,8},{24,0},{1,25},{9,17},{17,9},{25,1},{2,26},{10... | collective-permute-start | bytes 73736 | tf_op jit(solution)/shard_map/ppermute | solution.py:21
  5.5 0.7 %shard_map.67 = s32[1,64]{1,0:T(1,128)S(1)} custom-call(s32[1,64]{1,0:T(1,128)} %ids_ref.3), custom_call_target="tpu_custom_call" | custom-call | tf_op jit(solution)/shard_map/pallas_call | solution.py:38
  6.2 0.0 collective-permute-done
  6.2 0.0 copy-start
  6.2 0.0 copy-start.1
  6.2 1.6 %collective-permute-start.5 = (s32[2,64]{1,0:T(2,128)S(1)}, s32[2,64]{1,0:T(2,128)S(1)}, u32[]{:S(2)}, u32[]{:S(2)}) collective-permute-start(s32[2,64]{1,0:T(2,128)S(1)} %pad_add_fusion.1.unused.ids_ref), channel_id=1, source_target_pairs={{0,2},{1,3},{2,0},{3,1},{4,6},{5,7},{6,4},{7,5},{8,10},{9,11},{10,... | collective-permute-start | bytes 1544 | tf_op jit(solution)/shard_map/ppermute | solution.py:21
  7.9 2.1 %shard_map.68 = (bf16[2048,768]{1,0:T(8,128)(2,1)S(1)}, f32[1,2048]{1,0:T(1,128)S(1)}, bf16[16,768]{1,0:T(8,128)(2,1)S(1)}) custom-call(bf16[2048,768]{1,0:T(8,128)(2,1)} %heads_ref.1, bf16[16,768]{1,0:T(8,128)(2,1)} %new_ref.1, s32[2,64]{1,0:T(2,128)S(1)} %pad_add_fusion.1.unused.ids_ref), custom_call_target="tpu_custom_call" | custom-call | tf_op jit(solution)/shard_map/pallas_call | solution.py:38
  10.0 0.0 collective-permute-done.1.refs_1_
  10.0 0.0 collective-permute-done.2.refs_2_
  10.0 0.0 collective-permute-done.3.refs_3_
  10.0 1.2 %shard_map.69 = (f32[8,128]{1,0:T(8,128)S(1)}, s32[2,64]{1,0:T(2,128)S(1)}) custom-call(s32[2,64]{1,0:T(2,128)S(1)} %pad_add_fusion.1.unused.ids_ref, bf16[2048,768]{1,0:T(8,128)(2,1)S(1)} %get-tuple-element.13.heads_ref, f32[1,2048]{1,0:T(1,128)S(1)} %get-tuple-element.14.head_sq_ref, bf16[16,768]{1,0:T(8,128)(2,1)S(1)} %get-tuple-element.15.refs_0_, ...), custom_call_target="tpu_custom_call" | custom-call | tf_op jit(solution)/shard_map/pallas_call | solution.py:38
  11.2 0.1 collective-permute-start.4
  11.3 0.0 collective-permute-done.5
  11.3 2.7 %collective-permute-start.6 = (s32[4,64]{1,0:T(4,128)S(1)}, s32[4,64]{1,0:T(4,128)S(1)}, u32[]{:S(2)}, u32[]{:S(2)}) collective-permute-start(s32[4,64]{1,0:T(4,128)S(1)} %pad_add_fusion.near_ref), channel_id=1, source_target_pairs={{0,4},{1,5},{2,6},{3,7},{4,0},{5,1},{6,2},{7,3},{8,12},{9,13},{10,... | collective-permute-start | bytes 3080 | tf_op jit(solution)/shard_map/ppermute | solution.py:21
  14.0 0.0 collective-permute-done.4
  14.0 1.5 %collective-permute-start.7 = (f32[8,128]{1,0:T(8,128)S(1)}, f32[8,128]{1,0:T(8,128)S(1)}, u32[]{:S(2)}, u32[]{:S(2)}) collective-permute-start(f32[8,128]{1,0:T(8,128)S(1)} %add.3.unused.mine_ref), channel_id=1, source_target_pairs={{0,16},{8,24},{16,0},{24,8},{1,17},{9,25},{17,1},{25,9},{2,18},{10... | collective-permute-start | bytes 12296 | tf_op jit(solution)/shard_map/ppermute | solution.py:21
  15.5 0.0 copy-done
  15.5 0.0 copy-done.1
  15.5 0.2 shard_map.70
  15.7 0.2 collective-permute-done.6.far_ref
  15.9 0.8 %shard_map.71.rows_ref = bf16[128,768]{1,0:T(8,128)(2,1)S(1)} custom-call(s32[4,64]{1,0:T(4,128)S(1)} %pad_add_fusion.near_ref, s32[4,64]{1,0:T(4,128)S(1)} %collective-permute-done.6.far_ref, bf16[2048,768]{1,0:T(8,128)(2,1)S(1)} %get-tuple-element.13.heads_ref, bf16[64,128]{1,0:T(8,128)(2,1)S(1)} %get-tuple-element.17.unused.back_ref), custom_call_target="tpu_custom_call" | custom-call | flops 402653184 | bytes 3145728 | tf_op jit(solution)/shard_map/pallas_call | solution.py:38
  16.7 0.9 %collective-permute-done.7.other_ref = f32[8,128]{1,0:T(8,128)S(1)} collective-permute-done((f32[8,128]{1,0:T(8,128)S(1)}, f32[8,128]{1,0:T(8,128)S(1)}, u32[]{:S(2)}, u32[]{:S(2)}) %collective-permute-start.7) | collective-permute-done | bytes 4128 | tf_op jit(solution)/shard_map/ppermute | solution.py:21
  17.6 10.0 %all_to_all.5.listed_ref = bf16[8,104,128]{2,1,0:T(8,128)(2,1)S(1)} all-to-all(bf16[8,104,128]{2,1,0:T(8,128)(2,1)S(1)} %shard_map.72), channel_id=1, replica_groups={{4,0,1,2,3,5,6,7},{12,8,9,10,11,13,14,15},{20,16,17,18,19,21,22,23},{28..., dimensions={0} | all-to-all | bytes 425984 | tf_op jit(solution)/shard_map/all_to_all | solution.py:311
  27.7 1.0 %shard_map.73 = (f32[1,16]{1,0:T(1,128)}, f32[1,16]{1,0:T(1,128)}, f32[1,64,128]{2,1,0:T(8,128)}) custom-call(bf16[64,128]{1,0:T(8,128)(2,1)S(1)} %get-tuple-element.17.unused.back_ref, f32[1,128]{1,0:T(1,128)S(1)} %get-tuple-element.18.vec_sq_ref, bf16[8,104,128]{2,1,0:T(8,128)(2,1)S(1)} %all_to_all.5.listed_ref, bf16[1,128,768]{2,1,0:T(8,128)(2,1)S(1)} %copy-done), custom_call_target="tpu_custom_call" | custom-call | flops 25165824 | bytes 393216 | tf_op jit(solution)/shard_map/pallas_call | solution.py:38
  (4 shorter events, 0.1 us)
Async XLA Ops:
  0.6 5.5 %collective-permute-start = (s32[1,64]{1,0:T(1,128)}, s32[1,64]{1,0:T(1,128)S(1)}, u32[]{:S(2)}, u32[]{:S(2)}) collective-permute-start(s32[1,64]{1,0:T(1,128)} %ids_ref.3), channel_id=1, source_target_pairs={{0,1},{1,0},{2,3},{3,2},{4,5},{5,4},{6,7},{7,6},{8,9},{9,8},{10,11... | collective-permute-start | bytes 776 | tf_op jit(solution)/shard_map/ppermute | solution.py:21
  3.6 6.3 %collective-permute-start.1 = (bf16[16,768]{1,0:T(8,128)(2,1)}, bf16[16,768]{1,0:T(8,128)(2,1)S(1)}, u32[]{:S(2)}, u32[]{:S(2)}) collective-permute-start(bf16[16,768]{1,0:T(8,128)(2,1)} %new_ref.1), channel_id=1, source_target_pairs={{0,8},{8,0},{16,24},{24,16},{1,9},{9,1},{17,25},{25,17},{2,10},{10... | collective-permute-start | bytes 73736 | tf_op jit(solution)/shard_map/ppermute | solution.py:21
  3.6 6.4 %collective-permute-start.2 = (bf16[16,768]{1,0:T(8,128)(2,1)}, bf16[16,768]{1,0:T(8,128)(2,1)S(1)}, u32[]{:S(2)}, u32[]{:S(2)}) collective-permute-start(bf16[16,768]{1,0:T(8,128)(2,1)} %new_ref.1), channel_id=1, source_target_pairs={{0,16},{8,24},{16,0},{24,8},{1,17},{9,25},{17,1},{25,9},{2,18},{10... | collective-permute-start | bytes 73736 | tf_op jit(solution)/shard_map/ppermute | solution.py:21
  5.2 4.8 %collective-permute-start.3 = (bf16[16,768]{1,0:T(8,128)(2,1)}, bf16[16,768]{1,0:T(8,128)(2,1)S(1)}, u32[]{:S(2)}, u32[]{:S(2)}) collective-permute-start(bf16[16,768]{1,0:T(8,128)(2,1)} %new_ref.1), channel_id=1, source_target_pairs={{0,24},{8,16},{16,8},{24,0},{1,25},{9,17},{17,9},{25,1},{2,26},{10... | collective-permute-start | bytes 73736 | tf_op jit(solution)/shard_map/ppermute | solution.py:21
  6.2 9.3 %copy-start = (bf16[1,128,768]{2,1,0:T(8,128)(2,1)S(1)}, bf16[1,128,768]{2,1,0:T(8,128)(2,1)}, u32[]{:S(2)}) copy-start(bf16[1,128,768]{2,1,0:T(8,128)(2,1)} %vectors_ref.3) | copy-start | bytes 589828
  6.2 9.3 %copy-start.1 = (s32[1,64]{1,0:T(1,128)S(1)}, s32[1,64]{1,0:T(1,128)}, u32[]{:S(2)}) copy-start(s32[1,64]{1,0:T(1,128)} %ids_ref.3) | copy-start | bytes 772
  6.2 5.1 %collective-permute-start.5 = (s32[2,64]{1,0:T(2,128)S(1)}, s32[2,64]{1,0:T(2,128)S(1)}, u32[]{:S(2)}, u32[]{:S(2)}) collective-permute-start(s32[2,64]{1,0:T(2,128)S(1)} %pad_add_fusion.1.unused.ids_ref), channel_id=1, source_target_pairs={{0,2},{1,3},{2,0},{3,1},{4,6},{5,7},{6,4},{7,5},{8,10},{9,11},{10,... | collective-permute-start | bytes 1544 | tf_op jit(solution)/shard_map/ppermute | solution.py:21
  11.2 2.8 %collective-permute-start.4 = (f32[8,128]{1,0:T(8,128)S(1)}, f32[8,128]{1,0:T(8,128)S(1)}, u32[]{:S(2)}, u32[]{:S(2)}) collective-permute-start(f32[8,128]{1,0:T(8,128)S(1)} %get-tuple-element.16), channel_id=1, source_target_pairs={{0,8},{8,0},{16,24},{24,16},{1,9},{9,1},{17,25},{25,17},{2,10},{10... | collective-permute-start | bytes 12296 | tf_op jit(solution)/shard_map/ppermute | solution.py:21
  11.3 4.5 %collective-permute-start.6 = (s32[4,64]{1,0:T(4,128)S(1)}, s32[4,64]{1,0:T(4,128)S(1)}, u32[]{:S(2)}, u32[]{:S(2)}) collective-permute-start(s32[4,64]{1,0:T(4,128)S(1)} %pad_add_fusion.near_ref), channel_id=1, source_target_pairs={{0,4},{1,5},{2,6},{3,7},{4,0},{5,1},{6,2},{7,3},{8,12},{9,13},{10,... | collective-permute-start | bytes 3080 | tf_op jit(solution)/shard_map/ppermute | solution.py:21
  14.0 3.6 %collective-permute-start.7 = (f32[8,128]{1,0:T(8,128)S(1)}, f32[8,128]{1,0:T(8,128)S(1)}, u32[]{:S(2)}, u32[]{:S(2)}) collective-permute-start(f32[8,128]{1,0:T(8,128)S(1)} %add.3.unused.mine_ref), channel_id=1, source_target_pairs={{0,16},{8,24},{16,0},{24,8},{1,17},{9,25},{17,1},{25,9},{2,18},{10... | collective-permute-start | bytes 12296 | tf_op jit(solution)/shard_map/ppermute | solution.py:21

commit v21 on v20

--- a/solution.py
+++ b/solution.py
@@ -22,11 +22,12 @@
 
 
 def middle_first(members):
-    return [members // 2] + [member for member in range(members) if member != members // 2]
+    middle = members // 2 + 1
+    return [middle] + [member for member in range(members) if member != middle]
 
 
 def first_middle(member, members):
-    middle = members // 2
+    middle = members // 2 + 1
     return jnp.where(member == middle, 0, jnp.where(member < middle, member + 1, member))
 
 
@@ -58,7 +59,7 @@
 
 def early_kernel(heads_ref, new_ref, unused, kept_ref, head_sq_ref, kept_new_ref, sems):
     head_dev, width = heads_ref.shape
-    tiles = 4
+    tiles = sems.shape[0] - 1
     tile = head_dev // tiles
     parts = [pl.ds(i * tile, tile) for i in range(tiles)]
     copies = [
@@ -259,7 +260,7 @@
         ),
         (in_hbm(heads), in_hbm(new_heads), ids),
         (0, 0),
-        scratch=[pltpu.SemaphoreType.DMA((5,))],
+        scratch=[pltpu.SemaphoreType.DMA((9,))],
         spaces=[HBM, HBM, pl.ANY],
     )
     lines = 2 * groups * new_count // LANES

time: 28.8 us -> 29 us (level)
  transfers between devices with their start and end apart: 8 -> 8, of which waited for: 2 -> 2; matrix products, arithmetic and copies ran while one was open for 0% -> 0% of each run, Pallas kernels for 17% -> 18%
where the time goes in v21:
time: 29 us; the launch traced here: 28.8 us
  starting transfers between devices  10.7 us (37%)
  blocking collectives  10.1 us (35%)
  Pallas kernels  6.18 us (21%)
  waiting for transfers between devices  1.1 us (4%)
  between operations  0.74 us (3%)
    ppermute x8, starting transfers between devices, from_partner(): lax.ppermute(value, axis, [(source, source ^ mask) for source in range(co...  10.7 us
    all_to_all x1, blocking collectives, per_device(): lax.all_to_all(message, 'member', 0, 0, tiled=True, axis_index_groups=[mi...  10.1 us
    pallas_call x7, Pallas kernels, call(): pl.pallas_call(body, out_shape=shapes, in_specs=[pl.BlockSpec(memory_spac...  6.18 us
    ppermute x8, waiting for transfers between devices, from_partner(): lax.ppermute(value, axis, [(source, source ^ mask) for source in range(co...  1.1 us
  transfers between devices with their start and end apart: 8, of which 2 were waited for; matrix products, arithmetic and copies ran while one was open for 0% of the time, Pallas kernels for 18%

profile of v21, /device:TPU:0, one launch (start us, length us, event | category | flops | bytes accessed | tf_op | source)
XLA Modules:
  0.0 28.8 jit_solution(10698411255848110730)
XLA Ops:
  0.6 3.0 %collective-permute-start = (s32[1,64]{1,0:T(1,128)}, s32[1,64]{1,0:T(1,128)S(1)}, u32[]{:S(2)}, u32[]{:S(2)}) collective-permute-start(s32[1,64]{1,0:T(1,128)} %ids_ref.3), channel_id=1, source_target_pairs={{0,1},{1,0},{2,3},{3,2},{4,5},{5,4},{6,7},{7,6},{8,9},{9,8},{10,11... | collective-permute-start | bytes 776 | tf_op jit(solution)/shard_map/ppermute | solution.py:21
  3.6 0.0 collective-permute-start.1
  3.6 1.5 %collective-permute-start.2 = (bf16[16,768]{1,0:T(8,128)(2,1)}, bf16[16,768]{1,0:T(8,128)(2,1)S(1)}, u32[]{:S(2)}, u32[]{:S(2)}) collective-permute-start(bf16[16,768]{1,0:T(8,128)(2,1)} %new_ref.1), channel_id=1, source_target_pairs={{0,16},{8,24},{16,0},{24,8},{1,17},{9,25},{17,1},{25,9},{2,18},{10... | collective-permute-start | bytes 73736 | tf_op jit(solution)/shard_map/ppermute | solution.py:21
  5.2 0.3 %collective-permute-start.3 = (bf16[16,768]{1,0:T(8,128)(2,1)}, bf16[16,768]{1,0:T(8,128)(2,1)S(1)}, u32[]{:S(2)}, u32[]{:S(2)}) collective-permute-start(bf16[16,768]{1,0:T(8,128)(2,1)} %new_ref.1), channel_id=1, source_target_pairs={{0,24},{8,16},{16,8},{24,0},{1,25},{9,17},{17,9},{25,1},{2,26},{10... | collective-permute-start | bytes 73736 | tf_op jit(solution)/shard_map/ppermute | solution.py:21
  5.5 0.7 %shard_map.67 = s32[1,64]{1,0:T(1,128)S(1)} custom-call(s32[1,64]{1,0:T(1,128)} %ids_ref.3), custom_call_target="tpu_custom_call" | custom-call | tf_op jit(solution)/shard_map/pallas_call | solution.py:39
  6.2 0.0 collective-permute-done
  6.2 0.0 copy-start
  6.2 0.0 copy-start.1
  6.2 1.6 %collective-permute-start.5 = (s32[2,64]{1,0:T(2,128)S(1)}, s32[2,64]{1,0:T(2,128)S(1)}, u32[]{:S(2)}, u32[]{:S(2)}) collective-permute-start(s32[2,64]{1,0:T(2,128)S(1)} %pad_add_fusion.1.unused.ids_ref), channel_id=1, source_target_pairs={{0,2},{1,3},{2,0},{3,1},{4,6},{5,7},{6,4},{7,5},{8,10},{9,11},{10,... | collective-permute-start | bytes 1544 | tf_op jit(solution)/shard_map/ppermute | solution.py:21
  7.9 2.3 %shard_map.68 = (bf16[2048,768]{1,0:T(8,128)(2,1)S(1)}, f32[1,2048]{1,0:T(1,128)S(1)}, bf16[16,768]{1,0:T(8,128)(2,1)S(1)}) custom-call(bf16[2048,768]{1,0:T(8,128)(2,1)} %heads_ref.1, bf16[16,768]{1,0:T(8,128)(2,1)} %new_ref.1, s32[2,64]{1,0:T(2,128)S(1)} %pad_add_fusion.1.unused.ids_ref), custom_call_target="tpu_custom_call" | custom-call | tf_op jit(solution)/shard_map/pallas_call | solution.py:39
  10.2 0.0 collective-permute-done.1.refs_1_
  10.2 0.0 collective-permute-done.2.refs_2_
  10.2 0.0 collective-permute-done.3.refs_3_
  10.2 1.2 %shard_map.69 = (f32[8,128]{1,0:T(8,128)S(1)}, s32[2,64]{1,0:T(2,128)S(1)}) custom-call(s32[2,64]{1,0:T(2,128)S(1)} %pad_add_fusion.1.unused.ids_ref, bf16[2048,768]{1,0:T(8,128)(2,1)S(1)} %get-tuple-element.13.heads_ref, f32[1,2048]{1,0:T(1,128)S(1)} %get-tuple-element.14.head_sq_ref, bf16[16,768]{1,0:T(8,128)(2,1)S(1)} %get-tuple-element.15.refs_0_, ...), custom_call_target="tpu_custom_call" | custom-call | tf_op jit(solution)/shard_map/pallas_call | solution.py:39
  11.4 0.1 collective-permute-start.4
  11.5 0.0 collective-permute-done.5
  11.5 2.7 %collective-permute-start.6 = (s32[4,64]{1,0:T(4,128)S(1)}, s32[4,64]{1,0:T(4,128)S(1)}, u32[]{:S(2)}, u32[]{:S(2)}) collective-permute-start(s32[4,64]{1,0:T(4,128)S(1)} %pad_add_fusion.near_ref), channel_id=1, source_target_pairs={{0,4},{1,5},{2,6},{3,7},{4,0},{5,1},{6,2},{7,3},{8,12},{9,13},{10,... | collective-permute-start | bytes 3080 | tf_op jit(solution)/shard_map/ppermute | solution.py:21
  14.2 0.0 collective-permute-done.4
  14.2 1.5 %collective-permute-start.7 = (f32[8,128]{1,0:T(8,128)S(1)}, f32[8,128]{1,0:T(8,128)S(1)}, u32[]{:S(2)}, u32[]{:S(2)}) collective-permute-start(f32[8,128]{1,0:T(8,128)S(1)} %add.3.unused.mine_ref), channel_id=1, source_target_pairs={{0,16},{8,24},{16,0},{24,8},{1,17},{9,25},{17,1},{25,9},{2,18},{10... | collective-permute-start | bytes 12296 | tf_op jit(solution)/shard_map/ppermute | solution.py:21
  15.7 0.0 copy-done
  15.7 0.0 copy-done.1
  15.7 0.2 shard_map.70
  15.9 0.2 collective-permute-done.6.far_ref
  16.1 0.8 %shard_map.71.rows_ref = bf16[128,768]{1,0:T(8,128)(2,1)S(1)} custom-call(s32[4,64]{1,0:T(4,128)S(1)} %pad_add_fusion.near_ref, s32[4,64]{1,0:T(4,128)S(1)} %collective-permute-done.6.far_ref, bf16[2048,768]{1,0:T(8,128)(2,1)S(1)} %get-tuple-element.13.heads_ref, bf16[64,128]{1,0:T(8,128)(2,1)S(1)} %get-tuple-element.17.unused.back_ref), custom_call_target="tpu_custom_call" | custom-call | flops 402653184 | bytes 3145728 | tf_op jit(solution)/shard_map/pallas_call | solution.py:39
  16.9 0.9 %collective-permute-done.7.other_ref = f32[8,128]{1,0:T(8,128)S(1)} collective-permute-done((f32[8,128]{1,0:T(8,128)S(1)}, f32[8,128]{1,0:T(8,128)S(1)}, u32[]{:S(2)}, u32[]{:S(2)}) %collective-permute-start.7) | collective-permute-done | bytes 4128 | tf_op jit(solution)/shard_map/ppermute | solution.py:21
  17.8 10.1 %all_to_all.5.listed_ref = bf16[8,104,128]{2,1,0:T(8,128)(2,1)S(1)} all-to-all(bf16[8,104,128]{2,1,0:T(8,128)(2,1)S(1)} %shard_map.72), channel_id=1, replica_groups={{5,0,1,2,3,4,6,7},{13,8,9,10,11,12,14,15},{21,16,17,18,19,20,22,23},{29..., dimensions={0} | all-to-all | bytes 425984 | tf_op jit(solution)/shard_map/all_to_all | solution.py:312
  27.9 1.0 %shard_map.73 = (f32[1,16]{1,0:T(1,128)}, f32[1,16]{1,0:T(1,128)}, f32[1,64,128]{2,1,0:T(8,128)}) custom-call(bf16[64,128]{1,0:T(8,128)(2,1)S(1)} %get-tuple-element.17.unused.back_ref, f32[1,128]{1,0:T(1,128)S(1)} %get-tuple-element.18.vec_sq_ref, bf16[8,104,128]{2,1,0:T(8,128)(2,1)S(1)} %all_to_all.5.listed_ref, bf16[1,128,768]{2,1,0:T(8,128)(2,1)S(1)} %copy-done), custom_call_target="tpu_custom_call" | custom-call | flops 25165824 | bytes 393216 | tf_op jit(solution)/shard_map/pallas_call | solution.py:39
  (4 shorter events, 0.1 us)
Async XLA Ops:
  0.6 5.5 %collective-permute-start = (s32[1,64]{1,0:T(1,128)}, s32[1,64]{1,0:T(1,128)S(1)}, u32[]{:S(2)}, u32[]{:S(2)}) collective-permute-start(s32[1,64]{1,0:T(1,128)} %ids_ref.3), channel_id=1, source_target_pairs={{0,1},{1,0},{2,3},{3,2},{4,5},{5,4},{6,7},{7,6},{8,9},{9,8},{10,11... | collective-permute-start | bytes 776 | tf_op jit(solution)/shard_map/ppermute | solution.py:21
  3.6 6.5 %collective-permute-start.1 = (bf16[16,768]{1,0:T(8,128)(2,1)}, bf16[16,768]{1,0:T(8,128)(2,1)S(1)}, u32[]{:S(2)}, u32[]{:S(2)}) collective-permute-start(bf16[16,768]{1,0:T(8,128)(2,1)} %new_ref.1), channel_id=1, source_target_pairs={{0,8},{8,0},{16,24},{24,16},{1,9},{9,1},{17,25},{25,17},{2,10},{10... | collective-permute-start | bytes 73736 | tf_op jit(solution)/shard_map/ppermute | solution.py:21
  3.6 6.5 %collective-permute-start.2 = (bf16[16,768]{1,0:T(8,128)(2,1)}, bf16[16,768]{1,0:T(8,128)(2,1)S(1)}, u32[]{:S(2)}, u32[]{:S(2)}) collective-permute-start(bf16[16,768]{1,0:T(8,128)(2,1)} %new_ref.1), channel_id=1, source_target_pairs={{0,16},{8,24},{16,0},{24,8},{1,17},{9,25},{17,1},{25,9},{2,18},{10... | collective-permute-start | bytes 73736 | tf_op jit(solution)/shard_map/ppermute | solution.py:21
  5.2 5.0 %collective-permute-start.3 = (bf16[16,768]{1,0:T(8,128)(2,1)}, bf16[16,768]{1,0:T(8,128)(2,1)S(1)}, u32[]{:S(2)}, u32[]{:S(2)}) collective-permute-start(bf16[16,768]{1,0:T(8,128)(2,1)} %new_ref.1), channel_id=1, source_target_pairs={{0,24},{8,16},{16,8},{24,0},{1,25},{9,17},{17,9},{25,1},{2,26},{10... | collective-permute-start | bytes 73736 | tf_op jit(solution)/shard_map/ppermute | solution.py:21
  6.2 9.5 %copy-start = (bf16[1,128,768]{2,1,0:T(8,128)(2,1)S(1)}, bf16[1,128,768]{2,1,0:T(8,128)(2,1)}, u32[]{:S(2)}) copy-start(bf16[1,128,768]{2,1,0:T(8,128)(2,1)} %vectors_ref.3) | copy-start | bytes 589828
  6.2 9.5 %copy-start.1 = (s32[1,64]{1,0:T(1,128)S(1)}, s32[1,64]{1,0:T(1,128)}, u32[]{:S(2)}) copy-start(s32[1,64]{1,0:T(1,128)} %ids_ref.3) | copy-start | bytes 772
  6.2 5.3 %collective-permute-start.5 = (s32[2,64]{1,0:T(2,128)S(1)}, s32[2,64]{1,0:T(2,128)S(1)}, u32[]{:S(2)}, u32[]{:S(2)}) collective-permute-start(s32[2,64]{1,0:T(2,128)S(1)} %pad_add_fusion.1.unused.ids_ref), channel_id=1, source_target_pairs={{0,2},{1,3},{2,0},{3,1},{4,6},{5,7},{6,4},{7,5},{8,10},{9,11},{10,... | collective-permute-start | bytes 1544 | tf_op jit(solution)/shard_map/ppermute | solution.py:21
  11.4 2.8 %collective-permute-start.4 = (f32[8,128]{1,0:T(8,128)S(1)}, f32[8,128]{1,0:T(8,128)S(1)}, u32[]{:S(2)}, u32[]{:S(2)}) collective-permute-start(f32[8,128]{1,0:T(8,128)S(1)} %get-tuple-element.16), channel_id=1, source_target_pairs={{0,8},{8,0},{16,24},{24,16},{1,9},{9,1},{17,25},{25,17},{2,10},{10... | collective-permute-start | bytes 12296 | tf_op jit(solution)/shard_map/ppermute | solution.py:21
  11.5 4.5 %collective-permute-start.6 = (s32[4,64]{1,0:T(4,128)S(1)}, s32[4,64]{1,0:T(4,128)S(1)}, u32[]{:S(2)}, u32[]{:S(2)}) collective-permute-start(s32[4,64]{1,0:T(4,128)S(1)} %pad_add_fusion.near_ref), channel_id=1, source_target_pairs={{0,4},{1,5},{2,6},{3,7},{4,0},{5,1},{6,2},{7,3},{8,12},{9,13},{10,... | collective-permute-start | bytes 3080 | tf_op jit(solution)/shard_map/ppermute | solution.py:21
  14.2 3.6 %collective-permute-start.7 = (f32[8,128]{1,0:T(8,128)S(1)}, f32[8,128]{1,0:T(8,128)S(1)}, u32[]{:S(2)}, u32[]{:S(2)}) collective-permute-start(f32[8,128]{1,0:T(8,128)S(1)} %add.3.unused.mine_ref), channel_id=1, source_target_pairs={{0,16},{8,24},{16,0},{24,8},{1,17},{9,25},{17,1},{25,9},{2,18},{10... | collective-permute-start | bytes 12296 | tf_op jit(solution)/shard_map/ppermute | solution.py:21

commit v22 on v20

--- a/solution.py
+++ b/solution.py
@@ -75,7 +75,7 @@
             folded = block[:, :LANES]
             for column in range(LANES, width, LANES):
                 folded = folded + block[:, column:column + LANES]
-            head_sq_ref[:, first:first + LANES] = jnp.sum(folded.T, axis=0, keepdims=True)
+            head_sq_ref[first:first + LANES, :] = jnp.sum(folded, axis=1, keepdims=True)
     for copy in copies[tiles:]:
         copy.wait()
 
@@ -99,24 +99,33 @@
     ).astype(jnp.bfloat16)
 
 
+def turned(vector):
+    count = max(vector.shape)
+    diagonal = iota((count, count), 0) == iota((count, count), 1)
+    return jnp.sum(jnp.where(diagonal, vector, 0.0), axis=vector.shape.index(count), keepdims=True)
+
+
 def crowding(queries, heads_ref, head_sq_ref):
     head_dev, width = heads_ref.shape
-    query_sq = jnp.sum(jnp.square(queries.astype(jnp.float32)), axis=1, keepdims=True)
-    total_w = jnp.zeros((queries.shape[0], 1), jnp.float32)
-    total_we = jnp.zeros((queries.shape[0], 1), jnp.float32)
-    tile = 512
+    query_sq = turned(jnp.sum(jnp.square(queries.astype(jnp.float32)), axis=1, keepdims=True))
+    total_w = jnp.zeros((TILE, queries.shape[0]), jnp.float32)
+    total_we = jnp.zeros((TILE, queries.shape[0]), jnp.float32)
+    tile = 256
     for start in range(0, head_dev, tile):
         dots = lax.dot_general(
-            queries, heads_ref[start:start + tile, :], (((1,), (1,)), ((), ())),
+            heads_ref[start:start + tile, :], queries, (((1,), (1,)), ((), ())),
             preferred_element_type=jnp.float32,
         )
-        head_sq = head_sq_ref[:, start:start + tile]
-        excess = (query_sq + head_sq - 2.0 * dots) * (1.0 / width)
+        excess = (query_sq + head_sq_ref[start:start + tile, :] - 2.0 * dots) * (1.0 / width)
         inverse = 1.0 / (1.0 + excess)
         weight = inverse * inverse
-        total_w = total_w + jnp.sum(weight, axis=1, keepdims=True)
-        total_we = total_we + jnp.sum(weight * excess, axis=1, keepdims=True)
-    return total_w, total_we
+        weighted = weight * excess
+        for row in range(0, tile, TILE):
+            total_w = total_w + weight[row:row + TILE, :]
+            total_we = total_we + weighted[row:row + TILE, :]
+    total_w = jnp.sum(total_w, axis=0, keepdims=True)
+    total_we = jnp.sum(total_we, axis=0, keepdims=True)
+    return turned(total_w), turned(total_we)
 
 
 def crowd_kernel(groups, ids_ref, heads_ref, head_sq_ref, *refs):
@@ -254,7 +263,7 @@
         early_kernel,
         (
             jax.ShapeDtypeStruct(heads.shape, heads.dtype),
-            jax.ShapeDtypeStruct((1, head_dev), jnp.float32),
+            jax.ShapeDtypeStruct((head_dev, 1), jnp.float32),
             jax.ShapeDtypeStruct(new_heads.shape, new_heads.dtype),
         ),
         (in_hbm(heads), in_hbm(new_heads), ids),

time: 28.8 us -> 29.3 us (1.017)
  blocking collectives: 10 us -> 10.3 us
where the time goes in v22:
time: 29.3 us; the launch traced here: 29.1 us
  starting transfers between devices  11 us (38%)
  blocking collectives  10.3 us (35%)
  Pallas kernels  5.95 us (20%)
  waiting for transfers between devices  1.1 us (4%)
  between operations  0.74 us (3%)
    ppermute x8, starting transfers between devices, from_partner(): lax.ppermute(value, axis, [(source, source ^ mask) for source in range(co...  11 us
    all_to_all x1, blocking collectives, per_device(): lax.all_to_all(message, 'member', 0, 0, tiled=True, axis_index_groups=[mi...  10.3 us
    pallas_call x7, Pallas kernels, call(): pl.pallas_call(body, out_shape=shapes, in_specs=[pl.BlockSpec(memory_spac...  5.95 us
    ppermute x8, waiting for transfers between devices, from_partner(): lax.ppermute(value, axis, [(source, source ^ mask) for source in range(co...  1.1 us
  transfers between devices with their start and end apart: 8, of which 2 were waited for; matrix products, arithmetic and copies ran while one was open for 0% of the time, Pallas kernels for 17%

profile of v22, /device:TPU:0, one launch (start us, length us, event | category | flops | bytes accessed | tf_op | source)
XLA Modules:
  0.0 29.1 jit_solution(8553076339534174850)
XLA Ops:
  0.6 3.0 %collective-permute-start = (s32[1,64]{1,0:T(1,128)}, s32[1,64]{1,0:T(1,128)S(1)}, u32[]{:S(2)}, u32[]{:S(2)}) collective-permute-start(s32[1,64]{1,0:T(1,128)} %ids_ref.3), channel_id=1, source_target_pairs={{0,1},{1,0},{2,3},{3,2},{4,5},{5,4},{6,7},{7,6},{8,9},{9,8},{10,11... | collective-permute-start | bytes 776 | tf_op jit(solution)/shard_map/ppermute | solution.py:21
  3.6 0.0 collective-permute-start.1
  3.6 1.6 %collective-permute-start.3 = (bf16[16,768]{1,0:T(8,128)(2,1)}, bf16[16,768]{1,0:T(8,128)(2,1)S(1)}, u32[]{:S(2)}, u32[]{:S(2)}) collective-permute-start(bf16[16,768]{1,0:T(8,128)(2,1)} %new_ref.1), channel_id=1, source_target_pairs={{0,24},{8,16},{16,8},{24,0},{1,25},{9,17},{17,9},{25,1},{2,26},{10... | collective-permute-start | bytes 73736 | tf_op jit(solution)/shard_map/ppermute | solution.py:21
  5.3 0.5 %collective-permute-start.2 = (bf16[16,768]{1,0:T(8,128)(2,1)}, bf16[16,768]{1,0:T(8,128)(2,1)S(1)}, u32[]{:S(2)}, u32[]{:S(2)}) collective-permute-start(bf16[16,768]{1,0:T(8,128)(2,1)} %new_ref.1), channel_id=1, source_target_pairs={{0,16},{8,24},{16,0},{24,8},{1,17},{9,25},{17,1},{25,9},{2,18},{10... | collective-permute-start | bytes 73736 | tf_op jit(solution)/shard_map/ppermute | solution.py:21
  5.8 0.7 %shard_map.67 = s32[1,64]{1,0:T(1,128)S(1)} custom-call(s32[1,64]{1,0:T(1,128)} %ids_ref.3), custom_call_target="tpu_custom_call" | custom-call | tf_op jit(solution)/shard_map/pallas_call | solution.py:38
  6.4 0.0 collective-permute-done
  6.5 0.0 copy-start
  6.5 0.0 copy-start.1
  6.5 1.6 %collective-permute-start.5 = (s32[2,64]{1,0:T(2,128)S(1)}, s32[2,64]{1,0:T(2,128)S(1)}, u32[]{:S(2)}, u32[]{:S(2)}) collective-permute-start(s32[2,64]{1,0:T(2,128)S(1)} %pad_add_fusion.1.unused.ids_ref), channel_id=1, source_target_pairs={{0,2},{1,3},{2,0},{3,1},{4,6},{5,7},{6,4},{7,5},{8,10},{9,11},{10,... | collective-permute-start | bytes 1544 | tf_op jit(solution)/shard_map/ppermute | solution.py:21
  8.1 2.1 %shard_map.68 = (bf16[2048,768]{1,0:T(8,128)(2,1)S(1)}, f32[2048,1]{1,0:T(8,128)S(1)}, bf16[16,768]{1,0:T(8,128)(2,1)S(1)}) custom-call(bf16[2048,768]{1,0:T(8,128)(2,1)} %heads_ref.1, bf16[16,768]{1,0:T(8,128)(2,1)} %new_ref.1, s32[2,64]{1,0:T(2,128)S(1)} %pad_add_fusion.1.unused.ids_ref), custom_call_target="tpu_custom_call" | custom-call | tf_op jit(solution)/shard_map/pallas_call | solution.py:38
  10.3 0.0 collective-permute-done.1.refs_1_
  10.3 0.0 collective-permute-done.3.refs_3_
  10.3 0.0 collective-permute-done.2.refs_2_
  10.3 1.2 %shard_map.69 = (f32[8,128]{1,0:T(8,128)S(1)}, s32[2,64]{1,0:T(2,128)S(1)}) custom-call(s32[2,64]{1,0:T(2,128)S(1)} %pad_add_fusion.1.unused.ids_ref, bf16[2048,768]{1,0:T(8,128)(2,1)S(1)} %get-tuple-element.13.heads_ref, f32[2048,1]{1,0:T(8,128)S(1)} %get-tuple-element.14.head_sq_ref, bf16[16,768]{1,0:T(8,128)(2,1)S(1)} %get-tuple-element.15.refs_0_, ...), custom_call_target="tpu_custom_call" | custom-call | tf_op jit(solution)/shard_map/pallas_call | solution.py:38
  11.5 0.1 collective-permute-start.4
  11.5 0.0 collective-permute-done.5
  11.6 2.6 %collective-permute-start.6 = (s32[4,64]{1,0:T(4,128)S(1)}, s32[4,64]{1,0:T(4,128)S(1)}, u32[]{:S(2)}, u32[]{:S(2)}) collective-permute-start(s32[4,64]{1,0:T(4,128)S(1)} %pad_add_fusion.near_ref), channel_id=1, source_target_pairs={{0,4},{1,5},{2,6},{3,7},{4,0},{5,1},{6,2},{7,3},{8,12},{9,13},{10,... | collective-permute-start | bytes 3080 | tf_op jit(solution)/shard_map/ppermute | solution.py:21
  14.2 0.0 collective-permute-done.4
  14.2 1.5 %collective-permute-start.7 = (f32[8,128]{1,0:T(8,128)S(1)}, f32[8,128]{1,0:T(8,128)S(1)}, u32[]{:S(2)}, u32[]{:S(2)}) collective-permute-start(f32[8,128]{1,0:T(8,128)S(1)} %add.3.unused.mine_ref), channel_id=1, source_target_pairs={{0,16},{8,24},{16,0},{24,8},{1,17},{9,25},{17,1},{25,9},{2,18},{10... | collective-permute-start | bytes 12296 | tf_op jit(solution)/shard_map/ppermute | solution.py:21
  15.7 0.0 copy-done
  15.7 0.0 copy-done.1
  15.8 0.2 shard_map.70
  15.9 0.2 collective-permute-done.6.far_ref
  16.1 0.8 %shard_map.71.rows_ref = bf16[128,768]{1,0:T(8,128)(2,1)S(1)} custom-call(s32[4,64]{1,0:T(4,128)S(1)} %pad_add_fusion.near_ref, s32[4,64]{1,0:T(4,128)S(1)} %collective-permute-done.6.far_ref, bf16[2048,768]{1,0:T(8,128)(2,1)S(1)} %get-tuple-element.13.heads_ref, bf16[64,128]{1,0:T(8,128)(2,1)S(1)} %get-tuple-element.17.unused.back_ref), custom_call_target="tpu_custom_call" | custom-call | flops 402653184 | bytes 3145728 | tf_op jit(solution)/shard_map/pallas_call | solution.py:38
  16.9 0.9 %collective-permute-done.7.other_ref = f32[8,128]{1,0:T(8,128)S(1)} collective-permute-done((f32[8,128]{1,0:T(8,128)S(1)}, f32[8,128]{1,0:T(8,128)S(1)}, u32[]{:S(2)}, u32[]{:S(2)}) %collective-permute-start.7) | collective-permute-done | bytes 4128 | tf_op jit(solution)/shard_map/ppermute | solution.py:21
  17.9 10.3 %all_to_all.5.listed_ref = bf16[8,104,128]{2,1,0:T(8,128)(2,1)S(1)} all-to-all(bf16[8,104,128]{2,1,0:T(8,128)(2,1)S(1)} %shard_map.72), channel_id=1, replica_groups={{4,0,1,2,3,5,6,7},{12,8,9,10,11,13,14,15},{20,16,17,18,19,21,22,23},{28..., dimensions={0} | all-to-all | bytes 425984 | tf_op jit(solution)/shard_map/all_to_all | solution.py:320
  28.1 1.0 %shard_map.73 = (f32[1,16]{1,0:T(1,128)}, f32[1,16]{1,0:T(1,128)}, f32[1,64,128]{2,1,0:T(8,128)}) custom-call(bf16[64,128]{1,0:T(8,128)(2,1)S(1)} %get-tuple-element.17.unused.back_ref, f32[1,128]{1,0:T(1,128)S(1)} %get-tuple-element.18.vec_sq_ref, bf16[8,104,128]{2,1,0:T(8,128)(2,1)S(1)} %all_to_all.5.listed_ref, bf16[1,128,768]{2,1,0:T(8,128)(2,1)S(1)} %copy-done), custom_call_target="tpu_custom_call" | custom-call | flops 25165824 | bytes 393216 | tf_op jit(solution)/shard_map/pallas_call | solution.py:38
  (4 shorter events, 0.1 us)
Async XLA Ops:
  0.6 5.8 %collective-permute-start = (s32[1,64]{1,0:T(1,128)}, s32[1,64]{1,0:T(1,128)S(1)}, u32[]{:S(2)}, u32[]{:S(2)}) collective-permute-start(s32[1,64]{1,0:T(1,128)} %ids_ref.3), channel_id=1, source_target_pairs={{0,1},{1,0},{2,3},{3,2},{4,5},{5,4},{6,7},{7,6},{8,9},{9,8},{10,11... | collective-permute-start | bytes 776 | tf_op jit(solution)/shard_map/ppermute | solution.py:21
  3.6 6.6 %collective-permute-start.1 = (bf16[16,768]{1,0:T(8,128)(2,1)}, bf16[16,768]{1,0:T(8,128)(2,1)S(1)}, u32[]{:S(2)}, u32[]{:S(2)}) collective-permute-start(bf16[16,768]{1,0:T(8,128)(2,1)} %new_ref.1), channel_id=1, source_target_pairs={{0,8},{8,0},{16,24},{24,16},{1,9},{9,1},{17,25},{25,17},{2,10},{10... | collective-permute-start | bytes 73736 | tf_op jit(solution)/shard_map/ppermute | solution.py:21
  3.6 6.6 %collective-permute-start.3 = (bf16[16,768]{1,0:T(8,128)(2,1)}, bf16[16,768]{1,0:T(8,128)(2,1)S(1)}, u32[]{:S(2)}, u32[]{:S(2)}) collective-permute-start(bf16[16,768]{1,0:T(8,128)(2,1)} %new_ref.1), channel_id=1, source_target_pairs={{0,24},{8,16},{16,8},{24,0},{1,25},{9,17},{17,9},{25,1},{2,26},{10... | collective-permute-start | bytes 73736 | tf_op jit(solution)/shard_map/ppermute | solution.py:21
  5.3 5.0 %collective-permute-start.2 = (bf16[16,768]{1,0:T(8,128)(2,1)}, bf16[16,768]{1,0:T(8,128)(2,1)S(1)}, u32[]{:S(2)}, u32[]{:S(2)}) collective-permute-start(bf16[16,768]{1,0:T(8,128)(2,1)} %new_ref.1), channel_id=1, source_target_pairs={{0,16},{8,24},{16,0},{24,8},{1,17},{9,25},{17,1},{25,9},{2,18},{10... | collective-permute-start | bytes 73736 | tf_op jit(solution)/shard_map/ppermute | solution.py:21
  6.5 9.3 %copy-start = (bf16[1,128,768]{2,1,0:T(8,128)(2,1)S(1)}, bf16[1,128,768]{2,1,0:T(8,128)(2,1)}, u32[]{:S(2)}) copy-start(bf16[1,128,768]{2,1,0:T(8,128)(2,1)} %vectors_ref.3) | copy-start | bytes 589828
  6.5 9.3 %copy-start.1 = (s32[1,64]{1,0:T(1,128)S(1)}, s32[1,64]{1,0:T(1,128)}, u32[]{:S(2)}) copy-start(s32[1,64]{1,0:T(1,128)} %ids_ref.3) | copy-start | bytes 772
  6.5 5.1 %collective-permute-start.5 = (s32[2,64]{1,0:T(2,128)S(1)}, s32[2,64]{1,0:T(2,128)S(1)}, u32[]{:S(2)}, u32[]{:S(2)}) collective-permute-start(s32[2,64]{1,0:T(2,128)S(1)} %pad_add_fusion.1.unused.ids_ref), channel_id=1, source_target_pairs={{0,2},{1,3},{2,0},{3,1},{4,6},{5,7},{6,4},{7,5},{8,10},{9,11},{10,... | collective-permute-start | bytes 1544 | tf_op jit(solution)/shard_map/ppermute | solution.py:21
  11.5 2.8 %collective-permute-start.4 = (f32[8,128]{1,0:T(8,128)S(1)}, f32[8,128]{1,0:T(8,128)S(1)}, u32[]{:S(2)}, u32[]{:S(2)}) collective-permute-start(f32[8,128]{1,0:T(8,128)S(1)} %get-tuple-element.16), channel_id=1, source_target_pairs={{0,8},{8,0},{16,24},{24,16},{1,9},{9,1},{17,25},{25,17},{2,10},{10... | collective-permute-start | bytes 12296 | tf_op jit(solution)/shard_map/ppermute | solution.py:21
  11.6 4.5 %collective-permute-start.6 = (s32[4,64]{1,0:T(4,128)S(1)}, s32[4,64]{1,0:T(4,128)S(1)}, u32[]{:S(2)}, u32[]{:S(2)}) collective-permute-start(s32[4,64]{1,0:T(4,128)S(1)} %pad_add_fusion.near_ref), channel_id=1, source_target_pairs={{0,4},{1,5},{2,6},{3,7},{4,0},{5,1},{6,2},{7,3},{8,12},{9,13},{10,... | collective-permute-start | bytes 3080 | tf_op jit(solution)/shard_map/ppermute | solution.py:21
  14.2 3.6 %collective-permute-start.7 = (f32[8,128]{1,0:T(8,128)S(1)}, f32[8,128]{1,0:T(8,128)S(1)}, u32[]{:S(2)}, u32[]{:S(2)}) collective-permute-start(f32[8,128]{1,0:T(8,128)S(1)} %add.3.unused.mine_ref), channel_id=1, source_target_pairs={{0,16},{8,24},{16,0},{24,8},{1,17},{9,25},{17,1},{25,9},{2,18},{10... | collective-permute-start | bytes 12296 | tf_op jit(solution)/shard_map/ppermute | solution.py:21

commit v23 on v20

--- a/solution.py
+++ b/solution.py
@@ -264,7 +264,7 @@
     )
     lines = 2 * groups * new_count // LANES
     chunks = width // LANES
-    extra = -(-PARTS * lines // TILE) * TILE
+    extra = -(-PARTS * lines // PACK) * PACK
     sums, kept_ids = call(
         functools.partial(crowd_kernel, groups),
         (

time: 28.8 us -> 29.4 us (1.021)
  blocking collectives: 10 us -> 10.6 us
    all_to_all x1, blocking collectives: 10 us -> 10.6 us  [per_device(): lax.all_to_all(message, 'member', 0, 0, tiled=True, axis_index_groups=[mi...]
where the time goes in v23:
time: 29.4 us; the launch traced here: 29.2 us
  starting transfers between devices  10.8 us (37%)
  blocking collectives  10.6 us (36%)
  Pallas kernels  5.99 us (20%)
  waiting for transfers between devices  1.09 us (4%)
  between operations  0.74 us (3%)
    ppermute x8, starting transfers between devices, from_partner(): lax.ppermute(value, axis, [(source, source ^ mask) for source in range(co...  10.8 us
    all_to_all x1, blocking collectives, per_device(): lax.all_to_all(message, 'member', 0, 0, tiled=True, axis_index_groups=[mi...  10.6 us
    pallas_call x7, Pallas kernels, call(): pl.pallas_call(body, out_shape=shapes, in_specs=[pl.BlockSpec(memory_spac...  5.99 us
    ppermute x8, waiting for transfers between devices, from_partner(): lax.ppermute(value, axis, [(source, source ^ mask) for source in range(co...  1.09 us
  transfers between devices with their start and end apart: 8, of which 2 were waited for; matrix products, arithmetic and copies ran while one was open for 0% of the time, Pallas kernels for 17%

profile of v23, /device:TPU:0, one launch (start us, length us, event | category | flops | bytes accessed | tf_op | source)
XLA Modules:
  0.0 29.2 jit_solution(8107451033645438173)
XLA Ops:
  0.6 3.0 %collective-permute-start = (s32[1,64]{1,0:T(1,128)}, s32[1,64]{1,0:T(1,128)S(1)}, u32[]{:S(2)}, u32[]{:S(2)}) collective-permute-start(s32[1,64]{1,0:T(1,128)} %ids_ref.3), channel_id=1, source_target_pairs={{0,1},{1,0},{2,3},{3,2},{4,5},{5,4},{6,7},{7,6},{8,9},{9,8},{10,11... | collective-permute-start | bytes 776 | tf_op jit(solution)/shard_map/ppermute | solution.py:21
  3.6 0.0 collective-permute-start.1
  3.6 1.5 %collective-permute-start.2 = (bf16[16,768]{1,0:T(8,128)(2,1)}, bf16[16,768]{1,0:T(8,128)(2,1)S(1)}, u32[]{:S(2)}, u32[]{:S(2)}) collective-permute-start(bf16[16,768]{1,0:T(8,128)(2,1)} %new_ref.1), channel_id=1, source_target_pairs={{0,16},{8,24},{16,0},{24,8},{1,17},{9,25},{17,1},{25,9},{2,18},{10... | collective-permute-start | bytes 73736 | tf_op jit(solution)/shard_map/ppermute | solution.py:21
  5.2 0.3 %collective-permute-start.3 = (bf16[16,768]{1,0:T(8,128)(2,1)}, bf16[16,768]{1,0:T(8,128)(2,1)S(1)}, u32[]{:S(2)}, u32[]{:S(2)}) collective-permute-start(bf16[16,768]{1,0:T(8,128)(2,1)} %new_ref.1), channel_id=1, source_target_pairs={{0,24},{8,16},{16,8},{24,0},{1,25},{9,17},{17,9},{25,1},{2,26},{10... | collective-permute-start | bytes 73736 | tf_op jit(solution)/shard_map/ppermute | solution.py:21
  5.5 0.7 %shard_map.67 = s32[1,64]{1,0:T(1,128)S(1)} custom-call(s32[1,64]{1,0:T(1,128)} %ids_ref.3), custom_call_target="tpu_custom_call" | custom-call | tf_op jit(solution)/shard_map/pallas_call | solution.py:38
  6.2 0.0 collective-permute-done
  6.2 0.0 copy-start
  6.2 0.0 copy-start.1
  6.2 1.6 %collective-permute-start.5 = (s32[2,64]{1,0:T(2,128)S(1)}, s32[2,64]{1,0:T(2,128)S(1)}, u32[]{:S(2)}, u32[]{:S(2)}) collective-permute-start(s32[2,64]{1,0:T(2,128)S(1)} %pad_add_fusion.1.unused.ids_ref), channel_id=1, source_target_pairs={{0,2},{1,3},{2,0},{3,1},{4,6},{5,7},{6,4},{7,5},{8,10},{9,11},{10,... | collective-permute-start | bytes 1544 | tf_op jit(solution)/shard_map/ppermute | solution.py:21
  7.9 2.1 %shard_map.68 = (bf16[2048,768]{1,0:T(8,128)(2,1)S(1)}, f32[1,2048]{1,0:T(1,128)S(1)}, bf16[16,768]{1,0:T(8,128)(2,1)S(1)}) custom-call(bf16[2048,768]{1,0:T(8,128)(2,1)} %heads_ref.1, bf16[16,768]{1,0:T(8,128)(2,1)} %new_ref.1, s32[2,64]{1,0:T(2,128)S(1)} %pad_add_fusion.1.unused.ids_ref), custom_call_target="tpu_custom_call" | custom-call | tf_op jit(solution)/shard_map/pallas_call | solution.py:38
  10.0 0.0 collective-permute-done.1.refs_1_
  10.0 0.0 collective-permute-done.2.refs_2_
  10.0 0.0 collective-permute-done.3.refs_3_
  10.0 1.2 %shard_map.69 = (f32[8,128]{1,0:T(8,128)S(1)}, s32[2,64]{1,0:T(2,128)S(1)}) custom-call(s32[2,64]{1,0:T(2,128)S(1)} %pad_add_fusion.1.unused.ids_ref, bf16[2048,768]{1,0:T(8,128)(2,1)S(1)} %get-tuple-element.13.heads_ref, f32[1,2048]{1,0:T(1,128)S(1)} %get-tuple-element.14.head_sq_ref, bf16[16,768]{1,0:T(8,128)(2,1)S(1)} %get-tuple-element.15.refs_0_, ...), custom_call_target="tpu_custom_call" | custom-call | tf_op jit(solution)/shard_map/pallas_call | solution.py:38
  11.2 0.1 collective-permute-start.4
  11.3 0.0 collective-permute-done.5
  11.3 2.7 %collective-permute-start.6 = (s32[4,64]{1,0:T(4,128)S(1)}, s32[4,64]{1,0:T(4,128)S(1)}, u32[]{:S(2)}, u32[]{:S(2)}) collective-permute-start(s32[4,64]{1,0:T(4,128)S(1)} %pad_add_fusion.near_ref), channel_id=1, source_target_pairs={{0,4},{1,5},{2,6},{3,7},{4,0},{5,1},{6,2},{7,3},{8,12},{9,13},{10,... | collective-permute-start | bytes 3080 | tf_op jit(solution)/shard_map/ppermute | solution.py:21
  14.0 0.0 collective-permute-done.4
  14.0 1.5 %collective-permute-start.7 = (f32[8,128]{1,0:T(8,128)S(1)}, f32[8,128]{1,0:T(8,128)S(1)}, u32[]{:S(2)}, u32[]{:S(2)}) collective-permute-start(f32[8,128]{1,0:T(8,128)S(1)} %add.3.unused.mine_ref), channel_id=1, source_target_pairs={{0,16},{8,24},{16,0},{24,8},{1,17},{9,25},{17,1},{25,9},{2,18},{10... | collective-permute-start | bytes 12296 | tf_op jit(solution)/shard_map/ppermute | solution.py:21
  15.5 0.0 copy-done
  15.5 0.0 copy-done.1
  15.5 0.2 shard_map.70
  15.7 0.2 collective-permute-done.6.far_ref
  15.9 0.8 %shard_map.71.rows_ref = bf16[128,768]{1,0:T(8,128)(2,1)S(1)} custom-call(s32[4,64]{1,0:T(4,128)S(1)} %pad_add_fusion.near_ref, s32[4,64]{1,0:T(4,128)S(1)} %collective-permute-done.6.far_ref, bf16[2048,768]{1,0:T(8,128)(2,1)S(1)} %get-tuple-element.13.heads_ref, bf16[64,128]{1,0:T(8,128)(2,1)S(1)} %get-tuple-element.17.unused.back_ref), custom_call_target="tpu_custom_call" | custom-call | flops 402653184 | bytes 3145728 | tf_op jit(solution)/shard_map/pallas_call | solution.py:38
  16.7 0.9 %collective-permute-done.7.other_ref = f32[8,128]{1,0:T(8,128)S(1)} collective-permute-done((f32[8,128]{1,0:T(8,128)S(1)}, f32[8,128]{1,0:T(8,128)S(1)}, u32[]{:S(2)}, u32[]{:S(2)}) %collective-permute-start.7) | collective-permute-done | bytes 4128 | tf_op jit(solution)/shard_map/ppermute | solution.py:21
  17.6 10.6 %all_to_all.5.listed_ref = bf16[8,112,128]{2,1,0:T(8,128)(2,1)S(1)} all-to-all(bf16[8,112,128]{2,1,0:T(8,128)(2,1)S(1)} %shard_map.72), channel_id=1, replica_groups={{4,0,1,2,3,5,6,7},{12,8,9,10,11,13,14,15},{20,16,17,18,19,21,22,23},{28..., dimensions={0} | all-to-all | bytes 458752 | tf_op jit(solution)/shard_map/all_to_all | solution.py:311
  28.2 1.0 %shard_map.73 = (f32[1,16]{1,0:T(1,128)}, f32[1,16]{1,0:T(1,128)}, f32[1,64,128]{2,1,0:T(8,128)}) custom-call(bf16[64,128]{1,0:T(8,128)(2,1)S(1)} %get-tuple-element.17.unused.back_ref, f32[1,128]{1,0:T(1,128)S(1)} %get-tuple-element.18.vec_sq_ref, bf16[8,112,128]{2,1,0:T(8,128)(2,1)S(1)} %all_to_all.5.listed_ref, bf16[1,128,768]{2,1,0:T(8,128)(2,1)S(1)} %copy-done), custom_call_target="tpu_custom_call" | custom-call | flops 25165824 | bytes 393216 | tf_op jit(solution)/shard_map/pallas_call | solution.py:38
  (4 shorter events, 0.1 us)
Async XLA Ops:
  0.6 5.5 %collective-permute-start = (s32[1,64]{1,0:T(1,128)}, s32[1,64]{1,0:T(1,128)S(1)}, u32[]{:S(2)}, u32[]{:S(2)}) collective-permute-start(s32[1,64]{1,0:T(1,128)} %ids_ref.3), channel_id=1, source_target_pairs={{0,1},{1,0},{2,3},{3,2},{4,5},{5,4},{6,7},{7,6},{8,9},{9,8},{10,11... | collective-permute-start | bytes 776 | tf_op jit(solution)/shard_map/ppermute | solution.py:21
  3.6 6.3 %collective-permute-start.1 = (bf16[16,768]{1,0:T(8,128)(2,1)}, bf16[16,768]{1,0:T(8,128)(2,1)S(1)}, u32[]{:S(2)}, u32[]{:S(2)}) collective-permute-start(bf16[16,768]{1,0:T(8,128)(2,1)} %new_ref.1), channel_id=1, source_target_pairs={{0,8},{8,0},{16,24},{24,16},{1,9},{9,1},{17,25},{25,17},{2,10},{10... | collective-permute-start | bytes 73736 | tf_op jit(solution)/shard_map/ppermute | solution.py:21
  3.6 6.4 %collective-permute-start.2 = (bf16[16,768]{1,0:T(8,128)(2,1)}, bf16[16,768]{1,0:T(8,128)(2,1)S(1)}, u32[]{:S(2)}, u32[]{:S(2)}) collective-permute-start(bf16[16,768]{1,0:T(8,128)(2,1)} %new_ref.1), channel_id=1, source_target_pairs={{0,16},{8,24},{16,0},{24,8},{1,17},{9,25},{17,1},{25,9},{2,18},{10... | collective-permute-start | bytes 73736 | tf_op jit(solution)/shard_map/ppermute | solution.py:21
  5.2 4.8 %collective-permute-start.3 = (bf16[16,768]{1,0:T(8,128)(2,1)}, bf16[16,768]{1,0:T(8,128)(2,1)S(1)}, u32[]{:S(2)}, u32[]{:S(2)}) collective-permute-start(bf16[16,768]{1,0:T(8,128)(2,1)} %new_ref.1), channel_id=1, source_target_pairs={{0,24},{8,16},{16,8},{24,0},{1,25},{9,17},{17,9},{25,1},{2,26},{10... | collective-permute-start | bytes 73736 | tf_op jit(solution)/shard_map/ppermute | solution.py:21
  6.2 9.3 %copy-start = (bf16[1,128,768]{2,1,0:T(8,128)(2,1)S(1)}, bf16[1,128,768]{2,1,0:T(8,128)(2,1)}, u32[]{:S(2)}) copy-start(bf16[1,128,768]{2,1,0:T(8,128)(2,1)} %vectors_ref.3) | copy-start | bytes 589828
  6.2 9.3 %copy-start.1 = (s32[1,64]{1,0:T(1,128)S(1)}, s32[1,64]{1,0:T(1,128)}, u32[]{:S(2)}) copy-start(s32[1,64]{1,0:T(1,128)} %ids_ref.3) | copy-start | bytes 772
  6.2 5.1 %collective-permute-start.5 = (s32[2,64]{1,0:T(2,128)S(1)}, s32[2,64]{1,0:T(2,128)S(1)}, u32[]{:S(2)}, u32[]{:S(2)}) collective-permute-start(s32[2,64]{1,0:T(2,128)S(1)} %pad_add_fusion.1.unused.ids_ref), channel_id=1, source_target_pairs={{0,2},{1,3},{2,0},{3,1},{4,6},{5,7},{6,4},{7,5},{8,10},{9,11},{10,... | collective-permute-start | bytes 1544 | tf_op jit(solution)/shard_map/ppermute | solution.py:21
  11.2 2.8 %collective-permute-start.4 = (f32[8,128]{1,0:T(8,128)S(1)}, f32[8,128]{1,0:T(8,128)S(1)}, u32[]{:S(2)}, u32[]{:S(2)}) collective-permute-start(f32[8,128]{1,0:T(8,128)S(1)} %get-tuple-element.16), channel_id=1, source_target_pairs={{0,8},{8,0},{16,24},{24,16},{1,9},{9,1},{17,25},{25,17},{2,10},{10... | collective-permute-start | bytes 12296 | tf_op jit(solution)/shard_map/ppermute | solution.py:21
  11.3 4.5 %collective-permute-start.6 = (s32[4,64]{1,0:T(4,128)S(1)}, s32[4,64]{1,0:T(4,128)S(1)}, u32[]{:S(2)}, u32[]{:S(2)}) collective-permute-start(s32[4,64]{1,0:T(4,128)S(1)} %pad_add_fusion.near_ref), channel_id=1, source_target_pairs={{0,4},{1,5},{2,6},{3,7},{4,0},{5,1},{6,2},{7,3},{8,12},{9,13},{10,... | collective-permute-start | bytes 3080 | tf_op jit(solution)/shard_map/ppermute | solution.py:21
  14.0 3.6 %collective-permute-start.7 = (f32[8,128]{1,0:T(8,128)S(1)}, f32[8,128]{1,0:T(8,128)S(1)}, u32[]{:S(2)}, u32[]{:S(2)}) collective-permute-start(f32[8,128]{1,0:T(8,128)S(1)} %add.3.unused.mine_ref), channel_id=1, source_target_pairs={{0,16},{8,24},{16,0},{24,8},{1,17},{9,25},{17,1},{25,9},{2,18},{10... | collective-permute-start | bytes 12296 | tf_op jit(solution)/shard_map/ppermute | solution.py:21

commit v24 on v20

--- a/solution.py
+++ b/solution.py
@@ -151,11 +151,6 @@
 
 def pack_kernel(members, slots, lines, rows_ref, mine_ref, other_ref, out_ref):
     chunks = rows_ref.shape[1] // LANES
-    for member in range(members):
-        for chunk in range(chunks):
-            out_ref[member, chunk * slots:(chunk + 1) * slots, :] = rows_ref[
-                member * slots:(member + 1) * slots, chunk * LANES:(chunk + 1) * LANES
-            ]
     sums = (mine_ref[...] + other_ref[...])[:lines]
     coded = []
     for unused in range(PARTS):
@@ -166,7 +161,9 @@
         coded.append(jnp.zeros((missing, LANES), jnp.float32))
     tail = jnp.concatenate(coded, axis=0).astype(jnp.bfloat16)
     for member in range(members):
-        out_ref[member, chunks * slots:, :] = tail
+        part = slice(member * slots, (member + 1) * slots)
+        pieces = [rows_ref[part, chunk * LANES:(chunk + 1) * LANES] for chunk in range(chunks)]
+        out_ref[member] = jnp.concatenate([*pieces, tail], axis=0)
 
 
 def prepare_kernel(members, slots, head_dev, ids_ref, vectors_ref, unused, back_ref, vec_sq_ref):
@@ -185,12 +182,12 @@
     vec_sq_ref[...] = jnp.sum(jnp.where(diagonal, vec_sq, 0.0), axis=0, keepdims=True)
 
 
-def distances(slots, back_ref, vec_sq_ref, listed_ref, vectors_ref, out_ref):
-    members = listed_ref.shape[0]
+def distances(slots, back_ref, vec_sq_ref, listed, vectors_ref, out_ref):
+    members = listed.shape[0]
     width = vectors_ref.shape[2]
     rows = []
     for chunk in range(width // LANES):
-        part = listed_ref[:, chunk * slots:(chunk + 1) * slots, :].reshape(members * slots, LANES)
+        part = listed[:, chunk * slots:(chunk + 1) * slots, :].reshape(members * slots, LANES)
         rows.append(jnp.dot(back_ref[...], part, preferred_element_type=jnp.float32))
     rows = jnp.concatenate(rows, axis=1)
     row_sq = jnp.sum(jnp.square(rows), axis=1, keepdims=True)
@@ -205,13 +202,14 @@
     groups, slots, total_heads, back_ref, vec_sq_ref, listed_ref, vectors_ref,
     density_ref, spread_ref, out_ref,
 ):
-    distances(slots, back_ref, vec_sq_ref, listed_ref, vectors_ref, out_ref)
+    listed = listed_ref[...]
+    distances(slots, back_ref, vec_sq_ref, listed, vectors_ref, out_ref)
     here = lax.axis_index("group")
     members = listed_ref.shape[0]
     new_count = density_ref.shape[1]
     lines = 2 * groups * new_count // LANES
     first = vectors_ref.shape[2] // LANES * slots
-    coded = jnp.sum(listed_ref[:, first:, :].astype(jnp.float32), axis=0)
+    coded = jnp.sum(listed[:, first:, :].astype(jnp.float32), axis=0)
     total = sum(coded[part * lines:(part + 1) * lines] for part in range(PARTS))
     shape = (new_count, LANES)
     eye = iota((new_count, new_count), 0) == iota((new_count, new_count), 1)

time: 28.8 us -> 28.8 us (level)
  no operation moved by 1% of the time
where the time goes in v24:
time: 28.8 us; the launch traced here: 28.6 us
  starting transfers between devices  10.8 us (38%)
  blocking collectives  10 us (35%)
  Pallas kernels  5.98 us (21%)
  waiting for transfers between devices  1.09 us (4%)
  between operations  0.74 us (3%)
    ppermute x8, starting transfers between devices, from_partner(): lax.ppermute(value, axis, [(source, source ^ mask) for source in range(co...  10.8 us
    all_to_all x1, blocking collectives, per_device(): lax.all_to_all(message, 'member', 0, 0, tiled=True, axis_index_groups=[mi...  10 us
    pallas_call x7, Pallas kernels, call(): pl.pallas_call(body, out_shape=shapes, in_specs=[pl.BlockSpec(memory_spac...  5.98 us
    ppermute x8, waiting for transfers between devices, from_partner(): lax.ppermute(value, axis, [(source, source ^ mask) for source in range(co...  1.09 us
  transfers between devices with their start and end apart: 8, of which 2 were waited for; matrix products, arithmetic and copies ran while one was open for 0% of the time, Pallas kernels for 17%

profile of v24, /device:TPU:0, one launch (start us, length us, event | category | flops | bytes accessed | tf_op | source)
XLA Modules:
  0.0 28.6 jit_solution(10430939903243293092)
XLA Ops:
  0.6 3.0 %collective-permute-start = (s32[1,64]{1,0:T(1,128)}, s32[1,64]{1,0:T(1,128)S(1)}, u32[]{:S(2)}, u32[]{:S(2)}) collective-permute-start(s32[1,64]{1,0:T(1,128)} %ids_ref.3), channel_id=1, source_target_pairs={{0,1},{1,0},{2,3},{3,2},{4,5},{5,4},{6,7},{7,6},{8,9},{9,8},{10,11... | collective-permute-start | bytes 776 | tf_op jit(solution)/shard_map/ppermute | solution.py:21
  3.6 0.0 collective-permute-start.1
  3.6 1.5 %collective-permute-start.2 = (bf16[16,768]{1,0:T(8,128)(2,1)}, bf16[16,768]{1,0:T(8,128)(2,1)S(1)}, u32[]{:S(2)}, u32[]{:S(2)}) collective-permute-start(bf16[16,768]{1,0:T(8,128)(2,1)} %new_ref.1), channel_id=1, source_target_pairs={{0,16},{8,24},{16,0},{24,8},{1,17},{9,25},{17,1},{25,9},{2,18},{10... | collective-permute-start | bytes 73736 | tf_op jit(solution)/shard_map/ppermute | solution.py:21
  5.2 0.3 %collective-permute-start.3 = (bf16[16,768]{1,0:T(8,128)(2,1)}, bf16[16,768]{1,0:T(8,128)(2,1)S(1)}, u32[]{:S(2)}, u32[]{:S(2)}) collective-permute-start(bf16[16,768]{1,0:T(8,128)(2,1)} %new_ref.1), channel_id=1, source_target_pairs={{0,24},{8,16},{16,8},{24,0},{1,25},{9,17},{17,9},{25,1},{2,26},{10... | collective-permute-start | bytes 73736 | tf_op jit(solution)/shard_map/ppermute | solution.py:21
  5.5 0.7 %shard_map.67 = s32[1,64]{1,0:T(1,128)S(1)} custom-call(s32[1,64]{1,0:T(1,128)} %ids_ref.3), custom_call_target="tpu_custom_call" | custom-call | tf_op jit(solution)/shard_map/pallas_call | solution.py:38
  6.2 0.0 collective-permute-done
  6.2 0.0 copy-start
  6.2 0.0 copy-start.1
  6.2 1.6 %collective-permute-start.5 = (s32[2,64]{1,0:T(2,128)S(1)}, s32[2,64]{1,0:T(2,128)S(1)}, u32[]{:S(2)}, u32[]{:S(2)}) collective-permute-start(s32[2,64]{1,0:T(2,128)S(1)} %pad_add_fusion.1.unused.ids_ref), channel_id=1, source_target_pairs={{0,2},{1,3},{2,0},{3,1},{4,6},{5,7},{6,4},{7,5},{8,10},{9,11},{10,... | collective-permute-start | bytes 1544 | tf_op jit(solution)/shard_map/ppermute | solution.py:21
  7.9 2.1 %shard_map.68 = (bf16[2048,768]{1,0:T(8,128)(2,1)S(1)}, f32[1,2048]{1,0:T(1,128)S(1)}, bf16[16,768]{1,0:T(8,128)(2,1)S(1)}) custom-call(bf16[2048,768]{1,0:T(8,128)(2,1)} %heads_ref.1, bf16[16,768]{1,0:T(8,128)(2,1)} %new_ref.1, s32[2,64]{1,0:T(2,128)S(1)} %pad_add_fusion.1.unused.ids_ref), custom_call_target="tpu_custom_call" | custom-call | tf_op jit(solution)/shard_map/pallas_call | solution.py:38
  10.0 0.0 collective-permute-done.1.refs_1_
  10.0 0.0 collective-permute-done.2.refs_2_
  10.0 0.0 collective-permute-done.3.refs_3_
  10.0 1.2 %shard_map.69 = (f32[8,128]{1,0:T(8,128)S(1)}, s32[2,64]{1,0:T(2,128)S(1)}) custom-call(s32[2,64]{1,0:T(2,128)S(1)} %pad_add_fusion.1.unused.ids_ref, bf16[2048,768]{1,0:T(8,128)(2,1)S(1)} %get-tuple-element.13.heads_ref, f32[1,2048]{1,0:T(1,128)S(1)} %get-tuple-element.14.head_sq_ref, bf16[16,768]{1,0:T(8,128)(2,1)S(1)} %get-tuple-element.15.refs_0_, ...), custom_call_target="tpu_custom_call" | custom-call | tf_op jit(solution)/shard_map/pallas_call | solution.py:38
  11.2 0.1 collective-permute-start.4
  11.3 0.0 collective-permute-done.5
  11.3 2.7 %collective-permute-start.6 = (s32[4,64]{1,0:T(4,128)S(1)}, s32[4,64]{1,0:T(4,128)S(1)}, u32[]{:S(2)}, u32[]{:S(2)}) collective-permute-start(s32[4,64]{1,0:T(4,128)S(1)} %pad_add_fusion.near_ref), channel_id=1, source_target_pairs={{0,4},{1,5},{2,6},{3,7},{4,0},{5,1},{6,2},{7,3},{8,12},{9,13},{10,... | collective-permute-start | bytes 3080 | tf_op jit(solution)/shard_map/ppermute | solution.py:21
  14.0 0.0 collective-permute-done.4
  14.0 1.5 %collective-permute-start.7 = (f32[8,128]{1,0:T(8,128)S(1)}, f32[8,128]{1,0:T(8,128)S(1)}, u32[]{:S(2)}, u32[]{:S(2)}) collective-permute-start(f32[8,128]{1,0:T(8,128)S(1)} %add.3.unused.mine_ref), channel_id=1, source_target_pairs={{0,16},{8,24},{16,0},{24,8},{1,17},{9,25},{17,1},{25,9},{2,18},{10... | collective-permute-start | bytes 12296 | tf_op jit(solution)/shard_map/ppermute | solution.py:21
  15.5 0.0 copy-done
  15.5 0.0 copy-done.1
  15.5 0.2 shard_map.70
  15.7 0.2 collective-permute-done.6.far_ref
  15.9 0.8 %shard_map.71.rows_ref = bf16[128,768]{1,0:T(8,128)(2,1)S(1)} custom-call(s32[4,64]{1,0:T(4,128)S(1)} %pad_add_fusion.near_ref, s32[4,64]{1,0:T(4,128)S(1)} %collective-permute-done.6.far_ref, bf16[2048,768]{1,0:T(8,128)(2,1)S(1)} %get-tuple-element.13.heads_ref, bf16[64,128]{1,0:T(8,128)(2,1)S(1)} %get-tuple-element.17.unused.back_ref), custom_call_target="tpu_custom_call" | custom-call | flops 402653184 | bytes 3145728 | tf_op jit(solution)/shard_map/pallas_call | solution.py:38
  16.7 0.9 %collective-permute-done.7.other_ref = f32[8,128]{1,0:T(8,128)S(1)} collective-permute-done((f32[8,128]{1,0:T(8,128)S(1)}, f32[8,128]{1,0:T(8,128)S(1)}, u32[]{:S(2)}, u32[]{:S(2)}) %collective-permute-start.7) | collective-permute-done | bytes 4128 | tf_op jit(solution)/shard_map/ppermute | solution.py:21
  17.6 10.0 %all_to_all.5.listed_ref = bf16[8,104,128]{2,1,0:T(8,128)(2,1)S(1)} all-to-all(bf16[8,104,128]{2,1,0:T(8,128)(2,1)S(1)} %shard_map.72), channel_id=1, replica_groups={{4,0,1,2,3,5,6,7},{12,8,9,10,11,13,14,15},{20,16,17,18,19,21,22,23},{28..., dimensions={0} | all-to-all | bytes 425984 | tf_op jit(solution)/shard_map/all_to_all | solution.py:309
  27.7 1.0 %shard_map.73 = (f32[1,16]{1,0:T(1,128)}, f32[1,16]{1,0:T(1,128)}, f32[1,64,128]{2,1,0:T(8,128)}) custom-call(bf16[64,128]{1,0:T(8,128)(2,1)S(1)} %get-tuple-element.17.unused.back_ref, f32[1,128]{1,0:T(1,128)S(1)} %get-tuple-element.18.vec_sq_ref, bf16[8,104,128]{2,1,0:T(8,128)(2,1)S(1)} %all_to_all.5.listed_ref, bf16[1,128,768]{2,1,0:T(8,128)(2,1)S(1)} %copy-done), custom_call_target="tpu_custom_call" | custom-call | flops 25165824 | bytes 393216 | tf_op jit(solution)/shard_map/pallas_call | solution.py:38
  (4 shorter events, 0.1 us)
Async XLA Ops:
  0.6 5.5 %collective-permute-start = (s32[1,64]{1,0:T(1,128)}, s32[1,64]{1,0:T(1,128)S(1)}, u32[]{:S(2)}, u32[]{:S(2)}) collective-permute-start(s32[1,64]{1,0:T(1,128)} %ids_ref.3), channel_id=1, source_target_pairs={{0,1},{1,0},{2,3},{3,2},{4,5},{5,4},{6,7},{7,6},{8,9},{9,8},{10,11... | collective-permute-start | bytes 776 | tf_op jit(solution)/shard_map/ppermute | solution.py:21
  3.6 6.3 %collective-permute-start.1 = (bf16[16,768]{1,0:T(8,128)(2,1)}, bf16[16,768]{1,0:T(8,128)(2,1)S(1)}, u32[]{:S(2)}, u32[]{:S(2)}) collective-permute-start(bf16[16,768]{1,0:T(8,128)(2,1)} %new_ref.1), channel_id=1, source_target_pairs={{0,8},{8,0},{16,24},{24,16},{1,9},{9,1},{17,25},{25,17},{2,10},{10... | collective-permute-start | bytes 73736 | tf_op jit(solution)/shard_map/ppermute | solution.py:21
  3.6 6.4 %collective-permute-start.2 = (bf16[16,768]{1,0:T(8,128)(2,1)}, bf16[16,768]{1,0:T(8,128)(2,1)S(1)}, u32[]{:S(2)}, u32[]{:S(2)}) collective-permute-start(bf16[16,768]{1,0:T(8,128)(2,1)} %new_ref.1), channel_id=1, source_target_pairs={{0,16},{8,24},{16,0},{24,8},{1,17},{9,25},{17,1},{25,9},{2,18},{10... | collective-permute-start | bytes 73736 | tf_op jit(solution)/shard_map/ppermute | solution.py:21
  5.2 4.8 %collective-permute-start.3 = (bf16[16,768]{1,0:T(8,128)(2,1)}, bf16[16,768]{1,0:T(8,128)(2,1)S(1)}, u32[]{:S(2)}, u32[]{:S(2)}) collective-permute-start(bf16[16,768]{1,0:T(8,128)(2,1)} %new_ref.1), channel_id=1, source_target_pairs={{0,24},{8,16},{16,8},{24,0},{1,25},{9,17},{17,9},{25,1},{2,26},{10... | collective-permute-start | bytes 73736 | tf_op jit(solution)/shard_map/ppermute | solution.py:21
  6.2 9.3 %copy-start = (bf16[1,128,768]{2,1,0:T(8,128)(2,1)S(1)}, bf16[1,128,768]{2,1,0:T(8,128)(2,1)}, u32[]{:S(2)}) copy-start(bf16[1,128,768]{2,1,0:T(8,128)(2,1)} %vectors_ref.3) | copy-start | bytes 589828
  6.2 9.3 %copy-start.1 = (s32[1,64]{1,0:T(1,128)S(1)}, s32[1,64]{1,0:T(1,128)}, u32[]{:S(2)}) copy-start(s32[1,64]{1,0:T(1,128)} %ids_ref.3) | copy-start | bytes 772
  6.2 5.1 %collective-permute-start.5 = (s32[2,64]{1,0:T(2,128)S(1)}, s32[2,64]{1,0:T(2,128)S(1)}, u32[]{:S(2)}, u32[]{:S(2)}) collective-permute-start(s32[2,64]{1,0:T(2,128)S(1)} %pad_add_fusion.1.unused.ids_ref), channel_id=1, source_target_pairs={{0,2},{1,3},{2,0},{3,1},{4,6},{5,7},{6,4},{7,5},{8,10},{9,11},{10,... | collective-permute-start | bytes 1544 | tf_op jit(solution)/shard_map/ppermute | solution.py:21
  11.2 2.8 %collective-permute-start.4 = (f32[8,128]{1,0:T(8,128)S(1)}, f32[8,128]{1,0:T(8,128)S(1)}, u32[]{:S(2)}, u32[]{:S(2)}) collective-permute-start(f32[8,128]{1,0:T(8,128)S(1)} %get-tuple-element.16), channel_id=1, source_target_pairs={{0,8},{8,0},{16,24},{24,16},{1,9},{9,1},{17,25},{25,17},{2,10},{10... | collective-permute-start | bytes 12296 | tf_op jit(solution)/shard_map/ppermute | solution.py:21
  11.3 4.5 %collective-permute-start.6 = (s32[4,64]{1,0:T(4,128)S(1)}, s32[4,64]{1,0:T(4,128)S(1)}, u32[]{:S(2)}, u32[]{:S(2)}) collective-permute-start(s32[4,64]{1,0:T(4,128)S(1)} %pad_add_fusion.near_ref), channel_id=1, source_target_pairs={{0,4},{1,5},{2,6},{3,7},{4,0},{5,1},{6,2},{7,3},{8,12},{9,13},{10,... | collective-permute-start | bytes 3080 | tf_op jit(solution)/shard_map/ppermute | solution.py:21
  14.0 3.6 %collective-permute-start.7 = (f32[8,128]{1,0:T(8,128)S(1)}, f32[8,128]{1,0:T(8,128)S(1)}, u32[]{:S(2)}, u32[]{:S(2)}) collective-permute-start(f32[8,128]{1,0:T(8,128)S(1)} %add.3.unused.mine_ref), channel_id=1, source_target_pairs={{0,16},{8,24},{16,0},{24,8},{1,17},{9,25},{17,1},{25,9},{2,18},{10... | collective-permute-start | bytes 12296 | tf_op jit(solution)/shard_map/ppermute | solution.py:21

commit v25 on v24

--- a/solution.py
+++ b/solution.py
@@ -21,13 +21,14 @@
     return lax.ppermute(value, axis, [(source, source ^ mask) for source in range(count)])
 
 
-def middle_first(members):
-    return [members // 2] + [member for member in range(members) if member != members // 2]
-
-
-def first_middle(member, members):
-    middle = members // 2
-    return jnp.where(member == middle, 0, jnp.where(member < middle, member + 1, member))
+def by_turns(members):
+    half = members // 2
+    return [place // 2 + (half if place % 2 == 0 else 0) for place in range(members)]
+
+
+def turn_of(member, members):
+    half = members // 2
+    return jnp.where(member < half, 2 * member + 1, 2 * (member - half))
 
 
 def in_hbm(value):
@@ -145,7 +146,7 @@
     half = members // 2
     ids_ref[:half, :] = near_ref[...]
     ids_ref[half:, :] = far_ref[...]
-    ids = jnp.concatenate([ids_ref[pl.ds(me ^ member, 1), :] for member in middle_first(members)], axis=0)
+    ids = jnp.concatenate([ids_ref[pl.ds(me ^ member, 1), :] for member in by_turns(members)], axis=0)
     rows_ref[...] = listed_rows(ids, me, slots, heads_ref)
 
 
@@ -175,7 +176,7 @@
     owner = jnp.sum(jnp.where(eye, owner_row, 0), axis=1, keepdims=True)
     before = (owner_row == owner) & (iota(square, 1) < iota(square, 0))
     place = jnp.sum(before.astype(jnp.int32), axis=1, keepdims=True)
-    source = first_middle(owner, members) * slots + place
+    source = turn_of(owner, members) * slots + place
     back_ref[...] = (source == iota(back_ref.shape, 1)).astype(jnp.bfloat16)
     vec_sq = jnp.sum(jnp.square(vectors_ref[0].astype(jnp.float32)), axis=1, keepdims=True)
     diagonal = iota((block, block), 0) == iota((block, block), 1)
@@ -307,7 +308,7 @@
         (0, members * slots * width * 4),
     )
     message = lax.all_to_all(
-        message, "member", 0, 0, tiled=True, axis_index_groups=[middle_first(members)]
+        message, "member", 0, 0, tiled=True, axis_index_groups=[by_turns(members)]
     )
 
     density, spread, reassign = call(

time: 28.8 us -> 28.1 us (0.976)
  blocking collectives: 10 us -> 9.34 us
    all_to_all x1, blocking collectives: 10 us -> 9.34 us  [per_device(): lax.all_to_all(message, 'member', 0, 0, tiled=True, axis_index_groups=[by...]
  transfers between devices with their start and end apart: 8 -> 8, of which waited for: 2 -> 2; matrix products, arithmetic and copies ran while one was open for 0% -> 0% of each run, Pallas kernels for 17% -> 18%
where the time goes in v25:
time: 28.1 us; the launch traced here: 27.9 us
  starting transfers between devices  10.8 us (38%)
  blocking collectives  9.34 us (33%)
  Pallas kernels  5.98 us (21%)
  waiting for transfers between devices  1.09 us (4%)
  between operations  0.74 us (3%)
    ppermute x8, starting transfers between devices, from_partner(): lax.ppermute(value, axis, [(source, source ^ mask) for source in range(co...  10.8 us
    all_to_all x1, blocking collectives, per_device(): lax.all_to_all(message, 'member', 0, 0, tiled=True, axis_index_groups=[by...  9.34 us
    pallas_call x7, Pallas kernels, call(): pl.pallas_call(body, out_shape=shapes, in_specs=[pl.BlockSpec(memory_spac...  5.98 us
    ppermute x8, waiting for transfers between devices, from_partner(): lax.ppermute(value, axis, [(source, source ^ mask) for source in range(co...  1.09 us
  transfers between devices with their start and end apart: 8, of which 2 were waited for; matrix products, arithmetic and copies ran while one was open for 0% of the time, Pallas kernels for 18%

profile of v25, /device:TPU:0, one launch (start us, length us, event | category | flops | bytes accessed | tf_op | source)
XLA Modules:
  0.0 27.9 jit_solution(14686711103777393700)
XLA Ops:
  0.6 3.0 %collective-permute-start = (s32[1,64]{1,0:T(1,128)}, s32[1,64]{1,0:T(1,128)S(1)}, u32[]{:S(2)}, u32[]{:S(2)}) collective-permute-start(s32[1,64]{1,0:T(1,128)} %ids_ref.3), channel_id=1, source_target_pairs={{0,1},{1,0},{2,3},{3,2},{4,5},{5,4},{6,7},{7,6},{8,9},{9,8},{10,11... | collective-permute-start | bytes 776 | tf_op jit(solution)/shard_map/ppermute | solution.py:21
  3.6 0.0 collective-permute-start.1
  3.6 1.5 %collective-permute-start.2 = (bf16[16,768]{1,0:T(8,128)(2,1)}, bf16[16,768]{1,0:T(8,128)(2,1)S(1)}, u32[]{:S(2)}, u32[]{:S(2)}) collective-permute-start(bf16[16,768]{1,0:T(8,128)(2,1)} %new_ref.1), channel_id=1, source_target_pairs={{0,16},{8,24},{16,0},{24,8},{1,17},{9,25},{17,1},{25,9},{2,18},{10... | collective-permute-start | bytes 73736 | tf_op jit(solution)/shard_map/ppermute | solution.py:21
  5.2 0.3 %collective-permute-start.3 = (bf16[16,768]{1,0:T(8,128)(2,1)}, bf16[16,768]{1,0:T(8,128)(2,1)S(1)}, u32[]{:S(2)}, u32[]{:S(2)}) collective-permute-start(bf16[16,768]{1,0:T(8,128)(2,1)} %new_ref.1), channel_id=1, source_target_pairs={{0,24},{8,16},{16,8},{24,0},{1,25},{9,17},{17,9},{25,1},{2,26},{10... | collective-permute-start | bytes 73736 | tf_op jit(solution)/shard_map/ppermute | solution.py:21
  5.5 0.7 %shard_map.67 = s32[1,64]{1,0:T(1,128)S(1)} custom-call(s32[1,64]{1,0:T(1,128)} %ids_ref.3), custom_call_target="tpu_custom_call" | custom-call | tf_op jit(solution)/shard_map/pallas_call | solution.py:39
  6.2 0.0 collective-permute-done
  6.2 0.0 copy-start
  6.2 0.0 copy-start.1
  6.2 1.6 %collective-permute-start.5 = (s32[2,64]{1,0:T(2,128)S(1)}, s32[2,64]{1,0:T(2,128)S(1)}, u32[]{:S(2)}, u32[]{:S(2)}) collective-permute-start(s32[2,64]{1,0:T(2,128)S(1)} %pad_add_fusion.1.unused.ids_ref), channel_id=1, source_target_pairs={{0,2},{1,3},{2,0},{3,1},{4,6},{5,7},{6,4},{7,5},{8,10},{9,11},{10,... | collective-permute-start | bytes 1544 | tf_op jit(solution)/shard_map/ppermute | solution.py:21
  7.9 2.1 %shard_map.68 = (bf16[2048,768]{1,0:T(8,128)(2,1)S(1)}, f32[1,2048]{1,0:T(1,128)S(1)}, bf16[16,768]{1,0:T(8,128)(2,1)S(1)}) custom-call(bf16[2048,768]{1,0:T(8,128)(2,1)} %heads_ref.1, bf16[16,768]{1,0:T(8,128)(2,1)} %new_ref.1, s32[2,64]{1,0:T(2,128)S(1)} %pad_add_fusion.1.unused.ids_ref), custom_call_target="tpu_custom_call" | custom-call | tf_op jit(solution)/shard_map/pallas_call | solution.py:39
  10.0 0.0 collective-permute-done.1.refs_1_
  10.0 0.0 collective-permute-done.2.refs_2_
  10.0 0.0 collective-permute-done.3.refs_3_
  10.0 1.2 %shard_map.69 = (f32[8,128]{1,0:T(8,128)S(1)}, s32[2,64]{1,0:T(2,128)S(1)}) custom-call(s32[2,64]{1,0:T(2,128)S(1)} %pad_add_fusion.1.unused.ids_ref, bf16[2048,768]{1,0:T(8,128)(2,1)S(1)} %get-tuple-element.13.heads_ref, f32[1,2048]{1,0:T(1,128)S(1)} %get-tuple-element.14.head_sq_ref, bf16[16,768]{1,0:T(8,128)(2,1)S(1)} %get-tuple-element.15.refs_0_, ...), custom_call_target="tpu_custom_call" | custom-call | tf_op jit(solution)/shard_map/pallas_call | solution.py:39
  11.2 0.1 collective-permute-start.4
  11.3 0.0 collective-permute-done.5
  11.3 2.7 %collective-permute-start.6 = (s32[4,64]{1,0:T(4,128)S(1)}, s32[4,64]{1,0:T(4,128)S(1)}, u32[]{:S(2)}, u32[]{:S(2)}) collective-permute-start(s32[4,64]{1,0:T(4,128)S(1)} %pad_add_fusion.near_ref), channel_id=1, source_target_pairs={{0,4},{1,5},{2,6},{3,7},{4,0},{5,1},{6,2},{7,3},{8,12},{9,13},{10,... | collective-permute-start | bytes 3080 | tf_op jit(solution)/shard_map/ppermute | solution.py:21
  14.0 0.0 collective-permute-done.4
  14.0 1.5 %collective-permute-start.7 = (f32[8,128]{1,0:T(8,128)S(1)}, f32[8,128]{1,0:T(8,128)S(1)}, u32[]{:S(2)}, u32[]{:S(2)}) collective-permute-start(f32[8,128]{1,0:T(8,128)S(1)} %add.3.unused.mine_ref), channel_id=1, source_target_pairs={{0,16},{8,24},{16,0},{24,8},{1,17},{9,25},{17,1},{25,9},{2,18},{10... | collective-permute-start | bytes 12296 | tf_op jit(solution)/shard_map/ppermute | solution.py:21
  15.5 0.0 copy-done
  15.5 0.0 copy-done.1
  15.5 0.2 shard_map.70
  15.7 0.2 collective-permute-done.6.far_ref
  15.9 0.8 %shard_map.71.rows_ref = bf16[128,768]{1,0:T(8,128)(2,1)S(1)} custom-call(s32[4,64]{1,0:T(4,128)S(1)} %pad_add_fusion.near_ref, s32[4,64]{1,0:T(4,128)S(1)} %collective-permute-done.6.far_ref, bf16[2048,768]{1,0:T(8,128)(2,1)S(1)} %get-tuple-element.13.heads_ref, bf16[64,128]{1,0:T(8,128)(2,1)S(1)} %get-tuple-element.17.unused.back_ref), custom_call_target="tpu_custom_call" | custom-call | flops 402653184 | bytes 3145728 | tf_op jit(solution)/shard_map/pallas_call | solution.py:39
  16.7 0.9 %collective-permute-done.7.other_ref = f32[8,128]{1,0:T(8,128)S(1)} collective-permute-done((f32[8,128]{1,0:T(8,128)S(1)}, f32[8,128]{1,0:T(8,128)S(1)}, u32[]{:S(2)}, u32[]{:S(2)}) %collective-permute-start.7) | collective-permute-done | bytes 4128 | tf_op jit(solution)/shard_map/ppermute | solution.py:21
  17.6 9.3 %all_to_all.5.listed_ref = bf16[8,104,128]{2,1,0:T(8,128)(2,1)S(1)} all-to-all(bf16[8,104,128]{2,1,0:T(8,128)(2,1)S(1)} %shard_map.72), channel_id=1, replica_groups={{4,0,5,1,6,2,7,3},{12,8,13,9,14,10,15,11},{20,16,21,17,22,18,23,19},{28..., dimensions={0} | all-to-all | bytes 425984 | tf_op jit(solution)/shard_map/all_to_all | solution.py:310
  27.0 1.0 %shard_map.73 = (f32[1,16]{1,0:T(1,128)}, f32[1,16]{1,0:T(1,128)}, f32[1,64,128]{2,1,0:T(8,128)}) custom-call(bf16[64,128]{1,0:T(8,128)(2,1)S(1)} %get-tuple-element.17.unused.back_ref, f32[1,128]{1,0:T(1,128)S(1)} %get-tuple-element.18.vec_sq_ref, bf16[8,104,128]{2,1,0:T(8,128)(2,1)S(1)} %all_to_all.5.listed_ref, bf16[1,128,768]{2,1,0:T(8,128)(2,1)S(1)} %copy-done), custom_call_target="tpu_custom_call" | custom-call | flops 25165824 | bytes 393216 | tf_op jit(solution)/shard_map/pallas_call | solution.py:39
  (4 shorter events, 0.1 us)
Async XLA Ops:
  0.6 5.5 %collective-permute-start = (s32[1,64]{1,0:T(1,128)}, s32[1,64]{1,0:T(1,128)S(1)}, u32[]{:S(2)}, u32[]{:S(2)}) collective-permute-start(s32[1,64]{1,0:T(1,128)} %ids_ref.3), channel_id=1, source_target_pairs={{0,1},{1,0},{2,3},{3,2},{4,5},{5,4},{6,7},{7,6},{8,9},{9,8},{10,11... | collective-permute-start | bytes 776 | tf_op jit(solution)/shard_map/ppermute | solution.py:21
  3.6 6.3 %collective-permute-start.1 = (bf16[16,768]{1,0:T(8,128)(2,1)}, bf16[16,768]{1,0:T(8,128)(2,1)S(1)}, u32[]{:S(2)}, u32[]{:S(2)}) collective-permute-start(bf16[16,768]{1,0:T(8,128)(2,1)} %new_ref.1), channel_id=1, source_target_pairs={{0,8},{8,0},{16,24},{24,16},{1,9},{9,1},{17,25},{25,17},{2,10},{10... | collective-permute-start | bytes 73736 | tf_op jit(solution)/shard_map/ppermute | solution.py:21
  3.6 6.4 %collective-permute-start.2 = (bf16[16,768]{1,0:T(8,128)(2,1)}, bf16[16,768]{1,0:T(8,128)(2,1)S(1)}, u32[]{:S(2)}, u32[]{:S(2)}) collective-permute-start(bf16[16,768]{1,0:T(8,128)(2,1)} %new_ref.1), channel_id=1, source_target_pairs={{0,16},{8,24},{16,0},{24,8},{1,17},{9,25},{17,1},{25,9},{2,18},{10... | collective-permute-start | bytes 73736 | tf_op jit(solution)/shard_map/ppermute | solution.py:21
  5.2 4.8 %collective-permute-start.3 = (bf16[16,768]{1,0:T(8,128)(2,1)}, bf16[16,768]{1,0:T(8,128)(2,1)S(1)}, u32[]{:S(2)}, u32[]{:S(2)}) collective-permute-start(bf16[16,768]{1,0:T(8,128)(2,1)} %new_ref.1), channel_id=1, source_target_pairs={{0,24},{8,16},{16,8},{24,0},{1,25},{9,17},{17,9},{25,1},{2,26},{10... | collective-permute-start | bytes 73736 | tf_op jit(solution)/shard_map/ppermute | solution.py:21
  6.2 9.3 %copy-start = (bf16[1,128,768]{2,1,0:T(8,128)(2,1)S(1)}, bf16[1,128,768]{2,1,0:T(8,128)(2,1)}, u32[]{:S(2)}) copy-start(bf16[1,128,768]{2,1,0:T(8,128)(2,1)} %vectors_ref.3) | copy-start | bytes 589828
  6.2 9.3 %copy-start.1 = (s32[1,64]{1,0:T(1,128)S(1)}, s32[1,64]{1,0:T(1,128)}, u32[]{:S(2)}) copy-start(s32[1,64]{1,0:T(1,128)} %ids_ref.3) | copy-start | bytes 772
  6.2 5.1 %collective-permute-start.5 = (s32[2,64]{1,0:T(2,128)S(1)}, s32[2,64]{1,0:T(2,128)S(1)}, u32[]{:S(2)}, u32[]{:S(2)}) collective-permute-start(s32[2,64]{1,0:T(2,128)S(1)} %pad_add_fusion.1.unused.ids_ref), channel_id=1, source_target_pairs={{0,2},{1,3},{2,0},{3,1},{4,6},{5,7},{6,4},{7,5},{8,10},{9,11},{10,... | collective-permute-start | bytes 1544 | tf_op jit(solution)/shard_map/ppermute | solution.py:21
  11.2 2.8 %collective-permute-start.4 = (f32[8,128]{1,0:T(8,128)S(1)}, f32[8,128]{1,0:T(8,128)S(1)}, u32[]{:S(2)}, u32[]{:S(2)}) collective-permute-start(f32[8,128]{1,0:T(8,128)S(1)} %get-tuple-element.16), channel_id=1, source_target_pairs={{0,8},{8,0},{16,24},{24,16},{1,9},{9,1},{17,25},{25,17},{2,10},{10... | collective-permute-start | bytes 12296 | tf_op jit(solution)/shard_map/ppermute | solution.py:21
  11.3 4.5 %collective-permute-start.6 = (s32[4,64]{1,0:T(4,128)S(1)}, s32[4,64]{1,0:T(4,128)S(1)}, u32[]{:S(2)}, u32[]{:S(2)}) collective-permute-start(s32[4,64]{1,0:T(4,128)S(1)} %pad_add_fusion.near_ref), channel_id=1, source_target_pairs={{0,4},{1,5},{2,6},{3,7},{4,0},{5,1},{6,2},{7,3},{8,12},{9,13},{10,... | collective-permute-start | bytes 3080 | tf_op jit(solution)/shard_map/ppermute | solution.py:21
  14.0 3.6 %collective-permute-start.7 = (f32[8,128]{1,0:T(8,128)S(1)}, f32[8,128]{1,0:T(8,128)S(1)}, u32[]{:S(2)}, u32[]{:S(2)}) collective-permute-start(f32[8,128]{1,0:T(8,128)S(1)} %add.3.unused.mine_ref), channel_id=1, source_target_pairs={{0,16},{8,24},{16,0},{24,8},{1,17},{9,25},{17,1},{25,9},{2,18},{10... | collective-permute-start | bytes 12296 | tf_op jit(solution)/shard_map/ppermute | solution.py:21

commit v26 on v25

--- a/solution.py
+++ b/solution.py
@@ -23,12 +23,14 @@
 
 def by_turns(members):
     half = members // 2
-    return [place // 2 + (half if place % 2 == 0 else 0) for place in range(members)]
+    order = [place // 2 + (half if place % 2 == 0 else 0) for place in range(members)]
+    return [order[2], order[1], order[0], *order[3:]]
 
 
 def turn_of(member, members):
     half = members // 2
-    return jnp.where(member < half, 2 * member + 1, 2 * (member - half))
+    high = member - half
+    return jnp.where(member < half, 2 * member + 1, 2 * jnp.where(high < 2, 1 - high, high))
 
 
 def in_hbm(value):

time: 28.1 us -> 28.4 us (1.011)
  blocking collectives: 9.34 us -> 9.64 us
    all_to_all x1, blocking collectives: 9.34 us -> 9.64 us  [per_device(): lax.all_to_all(message, 'member', 0, 0, tiled=True, axis_index_groups=[by...]
where the time goes in v26:
time: 28.4 us; the launch traced here: 28.2 us
  starting transfers between devices  10.8 us (38%)
  blocking collectives  9.64 us (34%)
  Pallas kernels  5.98 us (21%)
  waiting for transfers between devices  1.09 us (4%)
  between operations  0.74 us (3%)
    ppermute x8, starting transfers between devices, from_partner(): lax.ppermute(value, axis, [(source, source ^ mask) for source in range(co...  10.8 us
    all_to_all x1, blocking collectives, per_device(): lax.all_to_all(message, 'member', 0, 0, tiled=True, axis_index_groups=[by...  9.64 us
    pallas_call x7, Pallas kernels, call(): pl.pallas_call(body, out_shape=shapes, in_specs=[pl.BlockSpec(memory_spac...  5.98 us
    ppermute x8, waiting for transfers between devices, from_partner(): lax.ppermute(value, axis, [(source, source ^ mask) for source in range(co...  1.09 us
  transfers between devices with their start and end apart: 8, of which 2 were waited for; matrix products, arithmetic and copies ran while one was open for 0% of the time, Pallas kernels for 18%

profile of v26, /device:TPU:0, one launch (start us, length us, event | category | flops | bytes accessed | tf_op | source)
XLA Modules:
  0.0 28.2 jit_solution(8008164874805868676)
XLA Ops:
  0.6 3.0 %collective-permute-start = (s32[1,64]{1,0:T(1,128)}, s32[1,64]{1,0:T(1,128)S(1)}, u32[]{:S(2)}, u32[]{:S(2)}) collective-permute-start(s32[1,64]{1,0:T(1,128)} %ids_ref.3), channel_id=1, source_target_pairs={{0,1},{1,0},{2,3},{3,2},{4,5},{5,4},{6,7},{7,6},{8,9},{9,8},{10,11... | collective-permute-start | bytes 776 | tf_op jit(solution)/shard_map/ppermute | solution.py:21
  3.6 0.0 collective-permute-start.1
  3.6 1.5 %collective-permute-start.2 = (bf16[16,768]{1,0:T(8,128)(2,1)}, bf16[16,768]{1,0:T(8,128)(2,1)S(1)}, u32[]{:S(2)}, u32[]{:S(2)}) collective-permute-start(bf16[16,768]{1,0:T(8,128)(2,1)} %new_ref.1), channel_id=1, source_target_pairs={{0,16},{8,24},{16,0},{24,8},{1,17},{9,25},{17,1},{25,9},{2,18},{10... | collective-permute-start | bytes 73736 | tf_op jit(solution)/shard_map/ppermute | solution.py:21
  5.2 0.3 %collective-permute-start.3 = (bf16[16,768]{1,0:T(8,128)(2,1)}, bf16[16,768]{1,0:T(8,128)(2,1)S(1)}, u32[]{:S(2)}, u32[]{:S(2)}) collective-permute-start(bf16[16,768]{1,0:T(8,128)(2,1)} %new_ref.1), channel_id=1, source_target_pairs={{0,24},{8,16},{16,8},{24,0},{1,25},{9,17},{17,9},{25,1},{2,26},{10... | collective-permute-start | bytes 73736 | tf_op jit(solution)/shard_map/ppermute | solution.py:21
  5.5 0.7 %shard_map.67 = s32[1,64]{1,0:T(1,128)S(1)} custom-call(s32[1,64]{1,0:T(1,128)} %ids_ref.3), custom_call_target="tpu_custom_call" | custom-call | tf_op jit(solution)/shard_map/pallas_call | solution.py:41
  6.2 0.0 collective-permute-done
  6.2 0.0 copy-start
  6.2 0.0 copy-start.1
  6.2 1.6 %collective-permute-start.5 = (s32[2,64]{1,0:T(2,128)S(1)}, s32[2,64]{1,0:T(2,128)S(1)}, u32[]{:S(2)}, u32[]{:S(2)}) collective-permute-start(s32[2,64]{1,0:T(2,128)S(1)} %pad_add_fusion.1.unused.ids_ref), channel_id=1, source_target_pairs={{0,2},{1,3},{2,0},{3,1},{4,6},{5,7},{6,4},{7,5},{8,10},{9,11},{10,... | collective-permute-start | bytes 1544 | tf_op jit(solution)/shard_map/ppermute | solution.py:21
  7.9 2.1 %shard_map.68 = (bf16[2048,768]{1,0:T(8,128)(2,1)S(1)}, f32[1,2048]{1,0:T(1,128)S(1)}, bf16[16,768]{1,0:T(8,128)(2,1)S(1)}) custom-call(bf16[2048,768]{1,0:T(8,128)(2,1)} %heads_ref.1, bf16[16,768]{1,0:T(8,128)(2,1)} %new_ref.1, s32[2,64]{1,0:T(2,128)S(1)} %pad_add_fusion.1.unused.ids_ref), custom_call_target="tpu_custom_call" | custom-call | tf_op jit(solution)/shard_map/pallas_call | solution.py:41
  10.0 0.0 collective-permute-done.1.refs_1_
  10.0 0.0 collective-permute-done.2.refs_2_
  10.0 0.0 collective-permute-done.3.refs_3_
  10.0 1.2 %shard_map.69 = (f32[8,128]{1,0:T(8,128)S(1)}, s32[2,64]{1,0:T(2,128)S(1)}) custom-call(s32[2,64]{1,0:T(2,128)S(1)} %pad_add_fusion.1.unused.ids_ref, bf16[2048,768]{1,0:T(8,128)(2,1)S(1)} %get-tuple-element.13.heads_ref, f32[1,2048]{1,0:T(1,128)S(1)} %get-tuple-element.14.head_sq_ref, bf16[16,768]{1,0:T(8,128)(2,1)S(1)} %get-tuple-element.15.refs_0_, ...), custom_call_target="tpu_custom_call" | custom-call | tf_op jit(solution)/shard_map/pallas_call | solution.py:41
  11.2 0.1 collective-permute-start.4
  11.3 0.0 collective-permute-done.5
  11.3 2.7 %collective-permute-start.6 = (s32[4,64]{1,0:T(4,128)S(1)}, s32[4,64]{1,0:T(4,128)S(1)}, u32[]{:S(2)}, u32[]{:S(2)}) collective-permute-start(s32[4,64]{1,0:T(4,128)S(1)} %pad_add_fusion.near_ref), channel_id=1, source_target_pairs={{0,4},{1,5},{2,6},{3,7},{4,0},{5,1},{6,2},{7,3},{8,12},{9,13},{10,... | collective-permute-start | bytes 3080 | tf_op jit(solution)/shard_map/ppermute | solution.py:21
  14.0 0.0 collective-permute-done.4
  14.0 1.5 %collective-permute-start.7 = (f32[8,128]{1,0:T(8,128)S(1)}, f32[8,128]{1,0:T(8,128)S(1)}, u32[]{:S(2)}, u32[]{:S(2)}) collective-permute-start(f32[8,128]{1,0:T(8,128)S(1)} %add.3.unused.mine_ref), channel_id=1, source_target_pairs={{0,16},{8,24},{16,0},{24,8},{1,17},{9,25},{17,1},{25,9},{2,18},{10... | collective-permute-start | bytes 12296 | tf_op jit(solution)/shard_map/ppermute | solution.py:21
  15.5 0.0 copy-done
  15.5 0.0 copy-done.1
  15.5 0.2 shard_map.70
  15.7 0.2 collective-permute-done.6.far_ref
  15.9 0.8 %shard_map.71.rows_ref = bf16[128,768]{1,0:T(8,128)(2,1)S(1)} custom-call(s32[4,64]{1,0:T(4,128)S(1)} %pad_add_fusion.near_ref, s32[4,64]{1,0:T(4,128)S(1)} %collective-permute-done.6.far_ref, bf16[2048,768]{1,0:T(8,128)(2,1)S(1)} %get-tuple-element.13.heads_ref, bf16[64,128]{1,0:T(8,128)(2,1)S(1)} %get-tuple-element.17.unused.back_ref), custom_call_target="tpu_custom_call" | custom-call | flops 402653184 | bytes 3145728 | tf_op jit(solution)/shard_map/pallas_call | solution.py:41
  16.7 0.9 %collective-permute-done.7.other_ref = f32[8,128]{1,0:T(8,128)S(1)} collective-permute-done((f32[8,128]{1,0:T(8,128)S(1)}, f32[8,128]{1,0:T(8,128)S(1)}, u32[]{:S(2)}, u32[]{:S(2)}) %collective-permute-start.7) | collective-permute-done | bytes 4128 | tf_op jit(solution)/shard_map/ppermute | solution.py:21
  17.6 9.6 %all_to_all.5.listed_ref = bf16[8,104,128]{2,1,0:T(8,128)(2,1)S(1)} all-to-all(bf16[8,104,128]{2,1,0:T(8,128)(2,1)S(1)} %shard_map.72), channel_id=1, replica_groups={{5,0,4,1,6,2,7,3},{13,8,12,9,14,10,15,11},{21,16,20,17,22,18,23,19},{29..., dimensions={0} | all-to-all | bytes 425984 | tf_op jit(solution)/shard_map/all_to_all | solution.py:312
  27.3 1.0 %shard_map.73 = (f32[1,16]{1,0:T(1,128)}, f32[1,16]{1,0:T(1,128)}, f32[1,64,128]{2,1,0:T(8,128)}) custom-call(bf16[64,128]{1,0:T(8,128)(2,1)S(1)} %get-tuple-element.17.unused.back_ref, f32[1,128]{1,0:T(1,128)S(1)} %get-tuple-element.18.vec_sq_ref, bf16[8,104,128]{2,1,0:T(8,128)(2,1)S(1)} %all_to_all.5.listed_ref, bf16[1,128,768]{2,1,0:T(8,128)(2,1)S(1)} %copy-done), custom_call_target="tpu_custom_call" | custom-call | flops 25165824 | bytes 393216 | tf_op jit(solution)/shard_map/pallas_call | solution.py:41
  (4 shorter events, 0.1 us)
Async XLA Ops:
  0.6 5.5 %collective-permute-start = (s32[1,64]{1,0:T(1,128)}, s32[1,64]{1,0:T(1,128)S(1)}, u32[]{:S(2)}, u32[]{:S(2)}) collective-permute-start(s32[1,64]{1,0:T(1,128)} %ids_ref.3), channel_id=1, source_target_pairs={{0,1},{1,0},{2,3},{3,2},{4,5},{5,4},{6,7},{7,6},{8,9},{9,8},{10,11... | collective-permute-start | bytes 776 | tf_op jit(solution)/shard_map/ppermute | solution.py:21
  3.6 6.3 %collective-permute-start.1 = (bf16[16,768]{1,0:T(8,128)(2,1)}, bf16[16,768]{1,0:T(8,128)(2,1)S(1)}, u32[]{:S(2)}, u32[]{:S(2)}) collective-permute-start(bf16[16,768]{1,0:T(8,128)(2,1)} %new_ref.1), channel_id=1, source_target_pairs={{0,8},{8,0},{16,24},{24,16},{1,9},{9,1},{17,25},{25,17},{2,10},{10... | collective-permute-start | bytes 73736 | tf_op jit(solution)/shard_map/ppermute | solution.py:21
  3.6 6.4 %collective-permute-start.2 = (bf16[16,768]{1,0:T(8,128)(2,1)}, bf16[16,768]{1,0:T(8,128)(2,1)S(1)}, u32[]{:S(2)}, u32[]{:S(2)}) collective-permute-start(bf16[16,768]{1,0:T(8,128)(2,1)} %new_ref.1), channel_id=1, source_target_pairs={{0,16},{8,24},{16,0},{24,8},{1,17},{9,25},{17,1},{25,9},{2,18},{10... | collective-permute-start | bytes 73736 | tf_op jit(solution)/shard_map/ppermute | solution.py:21
  5.2 4.8 %collective-permute-start.3 = (bf16[16,768]{1,0:T(8,128)(2,1)}, bf16[16,768]{1,0:T(8,128)(2,1)S(1)}, u32[]{:S(2)}, u32[]{:S(2)}) collective-permute-start(bf16[16,768]{1,0:T(8,128)(2,1)} %new_ref.1), channel_id=1, source_target_pairs={{0,24},{8,16},{16,8},{24,0},{1,25},{9,17},{17,9},{25,1},{2,26},{10... | collective-permute-start | bytes 73736 | tf_op jit(solution)/shard_map/ppermute | solution.py:21
  6.2 9.3 %copy-start = (bf16[1,128,768]{2,1,0:T(8,128)(2,1)S(1)}, bf16[1,128,768]{2,1,0:T(8,128)(2,1)}, u32[]{:S(2)}) copy-start(bf16[1,128,768]{2,1,0:T(8,128)(2,1)} %vectors_ref.3) | copy-start | bytes 589828
  6.2 9.3 %copy-start.1 = (s32[1,64]{1,0:T(1,128)S(1)}, s32[1,64]{1,0:T(1,128)}, u32[]{:S(2)}) copy-start(s32[1,64]{1,0:T(1,128)} %ids_ref.3) | copy-start | bytes 772
  6.2 5.1 %collective-permute-start.5 = (s32[2,64]{1,0:T(2,128)S(1)}, s32[2,64]{1,0:T(2,128)S(1)}, u32[]{:S(2)}, u32[]{:S(2)}) collective-permute-start(s32[2,64]{1,0:T(2,128)S(1)} %pad_add_fusion.1.unused.ids_ref), channel_id=1, source_target_pairs={{0,2},{1,3},{2,0},{3,1},{4,6},{5,7},{6,4},{7,5},{8,10},{9,11},{10,... | collective-permute-start | bytes 1544 | tf_op jit(solution)/shard_map/ppermute | solution.py:21
  11.2 2.8 %collective-permute-start.4 = (f32[8,128]{1,0:T(8,128)S(1)}, f32[8,128]{1,0:T(8,128)S(1)}, u32[]{:S(2)}, u32[]{:S(2)}) collective-permute-start(f32[8,128]{1,0:T(8,128)S(1)} %get-tuple-element.16), channel_id=1, source_target_pairs={{0,8},{8,0},{16,24},{24,16},{1,9},{9,1},{17,25},{25,17},{2,10},{10... | collective-permute-start | bytes 12296 | tf_op jit(solution)/shard_map/ppermute | solution.py:21
  11.3 4.5 %collective-permute-start.6 = (s32[4,64]{1,0:T(4,128)S(1)}, s32[4,64]{1,0:T(4,128)S(1)}, u32[]{:S(2)}, u32[]{:S(2)}) collective-permute-start(s32[4,64]{1,0:T(4,128)S(1)} %pad_add_fusion.near_ref), channel_id=1, source_target_pairs={{0,4},{1,5},{2,6},{3,7},{4,0},{5,1},{6,2},{7,3},{8,12},{9,13},{10,... | collective-permute-start | bytes 3080 | tf_op jit(solution)/shard_map/ppermute | solution.py:21
  14.0 3.6 %collective-permute-start.7 = (f32[8,128]{1,0:T(8,128)S(1)}, f32[8,128]{1,0:T(8,128)S(1)}, u32[]{:S(2)}, u32[]{:S(2)}) collective-permute-start(f32[8,128]{1,0:T(8,128)S(1)} %add.3.unused.mine_ref), channel_id=1, source_target_pairs={{0,16},{8,24},{16,0},{24,8},{1,17},{9,25},{17,1},{25,9},{2,18},{10... | collective-permute-start | bytes 12296 | tf_op jit(solution)/shard_map/ppermute | solution.py:21

commit v27 on v25

--- a/solution.py
+++ b/solution.py
@@ -23,12 +23,16 @@
 
 def by_turns(members):
     half = members // 2
-    return [place // 2 + (half if place % 2 == 0 else 0) for place in range(members)]
+    order = [half, 0]
+    for low in range(half - 1, 0, -1):
+        order += [half + low, low]
+    return order
 
 
 def turn_of(member, members):
     half = members // 2
-    return jnp.where(member < half, 2 * member + 1, 2 * (member - half))
+    low = member % half
+    return jnp.where(low == 0, 0, 2 * (half - low)) + jnp.where(member < half, 1, 0)
 
 
 def in_hbm(value):

time: 28.1 us -> 27.8 us (0.989)
  blocking collectives: 9.34 us -> 9.04 us
    all_to_all x1, blocking collectives: 9.34 us -> 9.04 us  [per_device(): lax.all_to_all(message, 'member', 0, 0, tiled=True, axis_index_groups=[by...]
where the time goes in v27:
time: 27.8 us; the launch traced here: 27.6 us
  starting transfers between devices  10.8 us (39%)
  blocking collectives  9.04 us (33%)
  Pallas kernels  5.98 us (22%)
  waiting for transfers between devices  1.09 us (4%)
  between operations  0.74 us (3%)
    ppermute x8, starting transfers between devices, from_partner(): lax.ppermute(value, axis, [(source, source ^ mask) for source in range(co...  10.8 us
    all_to_all x1, blocking collectives, per_device(): lax.all_to_all(message, 'member', 0, 0, tiled=True, axis_index_groups=[by...  9.04 us
    pallas_call x7, Pallas kernels, call(): pl.pallas_call(body, out_shape=shapes, in_specs=[pl.BlockSpec(memory_spac...  5.98 us
    ppermute x8, waiting for transfers between devices, from_partner(): lax.ppermute(value, axis, [(source, source ^ mask) for source in range(co...  1.09 us
  transfers between devices with their start and end apart: 8, of which 2 were waited for; matrix products, arithmetic and copies ran while one was open for 0% of the time, Pallas kernels for 18%

profile of v27, /device:TPU:0, one launch (start us, length us, event | category | flops | bytes accessed | tf_op | source)
XLA Modules:
  0.0 27.6 jit_solution(1775348255755707993)
XLA Ops:
  0.6 3.0 %collective-permute-start = (s32[1,64]{1,0:T(1,128)}, s32[1,64]{1,0:T(1,128)S(1)}, u32[]{:S(2)}, u32[]{:S(2)}) collective-permute-start(s32[1,64]{1,0:T(1,128)} %ids_ref.3), channel_id=1, source_target_pairs={{0,1},{1,0},{2,3},{3,2},{4,5},{5,4},{6,7},{7,6},{8,9},{9,8},{10,11... | collective-permute-start | bytes 776 | tf_op jit(solution)/shard_map/ppermute | solution.py:21
  3.6 0.0 collective-permute-start.1
  3.6 1.5 %collective-permute-start.2 = (bf16[16,768]{1,0:T(8,128)(2,1)}, bf16[16,768]{1,0:T(8,128)(2,1)S(1)}, u32[]{:S(2)}, u32[]{:S(2)}) collective-permute-start(bf16[16,768]{1,0:T(8,128)(2,1)} %new_ref.1), channel_id=1, source_target_pairs={{0,16},{8,24},{16,0},{24,8},{1,17},{9,25},{17,1},{25,9},{2,18},{10... | collective-permute-start | bytes 73736 | tf_op jit(solution)/shard_map/ppermute | solution.py:21
  5.2 0.3 %collective-permute-start.3 = (bf16[16,768]{1,0:T(8,128)(2,1)}, bf16[16,768]{1,0:T(8,128)(2,1)S(1)}, u32[]{:S(2)}, u32[]{:S(2)}) collective-permute-start(bf16[16,768]{1,0:T(8,128)(2,1)} %new_ref.1), channel_id=1, source_target_pairs={{0,24},{8,16},{16,8},{24,0},{1,25},{9,17},{17,9},{25,1},{2,26},{10... | collective-permute-start | bytes 73736 | tf_op jit(solution)/shard_map/ppermute | solution.py:21
  5.5 0.7 %shard_map.67 = s32[1,64]{1,0:T(1,128)S(1)} custom-call(s32[1,64]{1,0:T(1,128)} %ids_ref.3), custom_call_target="tpu_custom_call" | custom-call | tf_op jit(solution)/shard_map/pallas_call | solution.py:43
  6.2 0.0 collective-permute-done
  6.2 0.0 copy-start
  6.2 0.0 copy-start.1
  6.2 1.6 %collective-permute-start.5 = (s32[2,64]{1,0:T(2,128)S(1)}, s32[2,64]{1,0:T(2,128)S(1)}, u32[]{:S(2)}, u32[]{:S(2)}) collective-permute-start(s32[2,64]{1,0:T(2,128)S(1)} %pad_add_fusion.1.unused.ids_ref), channel_id=1, source_target_pairs={{0,2},{1,3},{2,0},{3,1},{4,6},{5,7},{6,4},{7,5},{8,10},{9,11},{10,... | collective-permute-start | bytes 1544 | tf_op jit(solution)/shard_map/ppermute | solution.py:21
  7.9 2.1 %shard_map.68 = (bf16[2048,768]{1,0:T(8,128)(2,1)S(1)}, f32[1,2048]{1,0:T(1,128)S(1)}, bf16[16,768]{1,0:T(8,128)(2,1)S(1)}) custom-call(bf16[2048,768]{1,0:T(8,128)(2,1)} %heads_ref.1, bf16[16,768]{1,0:T(8,128)(2,1)} %new_ref.1, s32[2,64]{1,0:T(2,128)S(1)} %pad_add_fusion.1.unused.ids_ref), custom_call_target="tpu_custom_call" | custom-call | tf_op jit(solution)/shard_map/pallas_call | solution.py:43
  10.0 0.0 collective-permute-done.1.refs_1_
  10.0 0.0 collective-permute-done.2.refs_2_
  10.0 0.0 collective-permute-done.3.refs_3_
  10.0 1.2 %shard_map.69 = (f32[8,128]{1,0:T(8,128)S(1)}, s32[2,64]{1,0:T(2,128)S(1)}) custom-call(s32[2,64]{1,0:T(2,128)S(1)} %pad_add_fusion.1.unused.ids_ref, bf16[2048,768]{1,0:T(8,128)(2,1)S(1)} %get-tuple-element.13.heads_ref, f32[1,2048]{1,0:T(1,128)S(1)} %get-tuple-element.14.head_sq_ref, bf16[16,768]{1,0:T(8,128)(2,1)S(1)} %get-tuple-element.15.refs_0_, ...), custom_call_target="tpu_custom_call" | custom-call | tf_op jit(solution)/shard_map/pallas_call | solution.py:43
  11.2 0.1 collective-permute-start.4
  11.3 0.0 collective-permute-done.5
  11.3 2.7 %collective-permute-start.6 = (s32[4,64]{1,0:T(4,128)S(1)}, s32[4,64]{1,0:T(4,128)S(1)}, u32[]{:S(2)}, u32[]{:S(2)}) collective-permute-start(s32[4,64]{1,0:T(4,128)S(1)} %pad_add_fusion.near_ref), channel_id=1, source_target_pairs={{0,4},{1,5},{2,6},{3,7},{4,0},{5,1},{6,2},{7,3},{8,12},{9,13},{10,... | collective-permute-start | bytes 3080 | tf_op jit(solution)/shard_map/ppermute | solution.py:21
  14.0 0.0 collective-permute-done.4
  14.0 1.5 %collective-permute-start.7 = (f32[8,128]{1,0:T(8,128)S(1)}, f32[8,128]{1,0:T(8,128)S(1)}, u32[]{:S(2)}, u32[]{:S(2)}) collective-permute-start(f32[8,128]{1,0:T(8,128)S(1)} %add.3.unused.mine_ref), channel_id=1, source_target_pairs={{0,16},{8,24},{16,0},{24,8},{1,17},{9,25},{17,1},{25,9},{2,18},{10... | collective-permute-start | bytes 12296 | tf_op jit(solution)/shard_map/ppermute | solution.py:21
  15.5 0.0 copy-done
  15.5 0.0 copy-done.1
  15.5 0.2 shard_map.70
  15.7 0.2 collective-permute-done.6.far_ref
  15.9 0.8 %shard_map.71.rows_ref = bf16[128,768]{1,0:T(8,128)(2,1)S(1)} custom-call(s32[4,64]{1,0:T(4,128)S(1)} %pad_add_fusion.near_ref, s32[4,64]{1,0:T(4,128)S(1)} %collective-permute-done.6.far_ref, bf16[2048,768]{1,0:T(8,128)(2,1)S(1)} %get-tuple-element.13.heads_ref, bf16[64,128]{1,0:T(8,128)(2,1)S(1)} %get-tuple-element.17.unused.back_ref), custom_call_target="tpu_custom_call" | custom-call | flops 402653184 | bytes 3145728 | tf_op jit(solution)/shard_map/pallas_call | solution.py:43
  16.7 0.9 %collective-permute-done.7.other_ref = f32[8,128]{1,0:T(8,128)S(1)} collective-permute-done((f32[8,128]{1,0:T(8,128)S(1)}, f32[8,128]{1,0:T(8,128)S(1)}, u32[]{:S(2)}, u32[]{:S(2)}) %collective-permute-start.7) | collective-permute-done | bytes 4128 | tf_op jit(solution)/shard_map/ppermute | solution.py:21
  17.6 9.0 %all_to_all.5.listed_ref = bf16[8,104,128]{2,1,0:T(8,128)(2,1)S(1)} all-to-all(bf16[8,104,128]{2,1,0:T(8,128)(2,1)S(1)} %shard_map.72), channel_id=1, replica_groups={{4,0,7,3,6,2,5,1},{12,8,15,11,14,10,13,9},{20,16,23,19,22,18,21,17},{28..., dimensions={0} | all-to-all | bytes 425984 | tf_op jit(solution)/shard_map/all_to_all | solution.py:314
  26.7 1.0 %shard_map.73 = (f32[1,16]{1,0:T(1,128)}, f32[1,16]{1,0:T(1,128)}, f32[1,64,128]{2,1,0:T(8,128)}) custom-call(bf16[64,128]{1,0:T(8,128)(2,1)S(1)} %get-tuple-element.17.unused.back_ref, f32[1,128]{1,0:T(1,128)S(1)} %get-tuple-element.18.vec_sq_ref, bf16[8,104,128]{2,1,0:T(8,128)(2,1)S(1)} %all_to_all.5.listed_ref, bf16[1,128,768]{2,1,0:T(8,128)(2,1)S(1)} %copy-done), custom_call_target="tpu_custom_call" | custom-call | flops 25165824 | bytes 393216 | tf_op jit(solution)/shard_map/pallas_call | solution.py:43
  (4 shorter events, 0.1 us)
Async XLA Ops:
  0.6 5.5 %collective-permute-start = (s32[1,64]{1,0:T(1,128)}, s32[1,64]{1,0:T(1,128)S(1)}, u32[]{:S(2)}, u32[]{:S(2)}) collective-permute-start(s32[1,64]{1,0:T(1,128)} %ids_ref.3), channel_id=1, source_target_pairs={{0,1},{1,0},{2,3},{3,2},{4,5},{5,4},{6,7},{7,6},{8,9},{9,8},{10,11... | collective-permute-start | bytes 776 | tf_op jit(solution)/shard_map/ppermute | solution.py:21
  3.6 6.3 %collective-permute-start.1 = (bf16[16,768]{1,0:T(8,128)(2,1)}, bf16[16,768]{1,0:T(8,128)(2,1)S(1)}, u32[]{:S(2)}, u32[]{:S(2)}) collective-permute-start(bf16[16,768]{1,0:T(8,128)(2,1)} %new_ref.1), channel_id=1, source_target_pairs={{0,8},{8,0},{16,24},{24,16},{1,9},{9,1},{17,25},{25,17},{2,10},{10... | collective-permute-start | bytes 73736 | tf_op jit(solution)/shard_map/ppermute | solution.py:21
  3.6 6.4 %collective-permute-start.2 = (bf16[16,768]{1,0:T(8,128)(2,1)}, bf16[16,768]{1,0:T(8,128)(2,1)S(1)}, u32[]{:S(2)}, u32[]{:S(2)}) collective-permute-start(bf16[16,768]{1,0:T(8,128)(2,1)} %new_ref.1), channel_id=1, source_target_pairs={{0,16},{8,24},{16,0},{24,8},{1,17},{9,25},{17,1},{25,9},{2,18},{10... | collective-permute-start | bytes 73736 | tf_op jit(solution)/shard_map/ppermute | solution.py:21
  5.2 4.8 %collective-permute-start.3 = (bf16[16,768]{1,0:T(8,128)(2,1)}, bf16[16,768]{1,0:T(8,128)(2,1)S(1)}, u32[]{:S(2)}, u32[]{:S(2)}) collective-permute-start(bf16[16,768]{1,0:T(8,128)(2,1)} %new_ref.1), channel_id=1, source_target_pairs={{0,24},{8,16},{16,8},{24,0},{1,25},{9,17},{17,9},{25,1},{2,26},{10... | collective-permute-start | bytes 73736 | tf_op jit(solution)/shard_map/ppermute | solution.py:21
  6.2 9.3 %copy-start = (bf16[1,128,768]{2,1,0:T(8,128)(2,1)S(1)}, bf16[1,128,768]{2,1,0:T(8,128)(2,1)}, u32[]{:S(2)}) copy-start(bf16[1,128,768]{2,1,0:T(8,128)(2,1)} %vectors_ref.3) | copy-start | bytes 589828
  6.2 9.3 %copy-start.1 = (s32[1,64]{1,0:T(1,128)S(1)}, s32[1,64]{1,0:T(1,128)}, u32[]{:S(2)}) copy-start(s32[1,64]{1,0:T(1,128)} %ids_ref.3) | copy-start | bytes 772
  6.2 5.1 %collective-permute-start.5 = (s32[2,64]{1,0:T(2,128)S(1)}, s32[2,64]{1,0:T(2,128)S(1)}, u32[]{:S(2)}, u32[]{:S(2)}) collective-permute-start(s32[2,64]{1,0:T(2,128)S(1)} %pad_add_fusion.1.unused.ids_ref), channel_id=1, source_target_pairs={{0,2},{1,3},{2,0},{3,1},{4,6},{5,7},{6,4},{7,5},{8,10},{9,11},{10,... | collective-permute-start | bytes 1544 | tf_op jit(solution)/shard_map/ppermute | solution.py:21
  11.2 2.8 %collective-permute-start.4 = (f32[8,128]{1,0:T(8,128)S(1)}, f32[8,128]{1,0:T(8,128)S(1)}, u32[]{:S(2)}, u32[]{:S(2)}) collective-permute-start(f32[8,128]{1,0:T(8,128)S(1)} %get-tuple-element.16), channel_id=1, source_target_pairs={{0,8},{8,0},{16,24},{24,16},{1,9},{9,1},{17,25},{25,17},{2,10},{10... | collective-permute-start | bytes 12296 | tf_op jit(solution)/shard_map/ppermute | solution.py:21
  11.3 4.5 %collective-permute-start.6 = (s32[4,64]{1,0:T(4,128)S(1)}, s32[4,64]{1,0:T(4,128)S(1)}, u32[]{:S(2)}, u32[]{:S(2)}) collective-permute-start(s32[4,64]{1,0:T(4,128)S(1)} %pad_add_fusion.near_ref), channel_id=1, source_target_pairs={{0,4},{1,5},{2,6},{3,7},{4,0},{5,1},{6,2},{7,3},{8,12},{9,13},{10,... | collective-permute-start | bytes 3080 | tf_op jit(solution)/shard_map/ppermute | solution.py:21
  14.0 3.6 %collective-permute-start.7 = (f32[8,128]{1,0:T(8,128)S(1)}, f32[8,128]{1,0:T(8,128)S(1)}, u32[]{:S(2)}, u32[]{:S(2)}) collective-permute-start(f32[8,128]{1,0:T(8,128)S(1)} %add.3.unused.mine_ref), channel_id=1, source_target_pairs={{0,16},{8,24},{16,0},{24,8},{1,17},{9,25},{17,1},{25,9},{2,18},{10... | collective-permute-start | bytes 12296 | tf_op jit(solution)/shard_map/ppermute | solution.py:21

commit v28 on v24

--- a/solution.py
+++ b/solution.py
@@ -21,13 +21,12 @@
     return lax.ppermute(value, axis, [(source, source ^ mask) for source in range(count)])
 
 
-def middle_first(members):
-    return [members // 2] + [member for member in range(members) if member != members // 2]
-
-
-def first_middle(member, members):
-    middle = members // 2
-    return jnp.where(member == middle, 0, jnp.where(member < middle, member + 1, member))
+def downward(members):
+    return [(members // 2 - place) % members for place in range(members)]
+
+
+def down_place(member, members):
+    return (members + members // 2 - member) % members
 
 
 def in_hbm(value):
@@ -145,7 +144,7 @@
     half = members // 2
     ids_ref[:half, :] = near_ref[...]
     ids_ref[half:, :] = far_ref[...]
-    ids = jnp.concatenate([ids_ref[pl.ds(me ^ member, 1), :] for member in middle_first(members)], axis=0)
+    ids = jnp.concatenate([ids_ref[pl.ds(me ^ member, 1), :] for member in downward(members)], axis=0)
     rows_ref[...] = listed_rows(ids, me, slots, heads_ref)
 
 
@@ -175,7 +174,7 @@
     owner = jnp.sum(jnp.where(eye, owner_row, 0), axis=1, keepdims=True)
     before = (owner_row == owner) & (iota(square, 1) < iota(square, 0))
     place = jnp.sum(before.astype(jnp.int32), axis=1, keepdims=True)
-    source = first_middle(owner, members) * slots + place
+    source = down_place(owner, members) * slots + place
     back_ref[...] = (source == iota(back_ref.shape, 1)).astype(jnp.bfloat16)
     vec_sq = jnp.sum(jnp.square(vectors_ref[0].astype(jnp.float32)), axis=1, keepdims=True)
     diagonal = iota((block, block), 0) == iota((block, block), 1)
@@ -307,7 +306,7 @@
         (0, members * slots * width * 4),
     )
     message = lax.all_to_all(
-        message, "member", 0, 0, tiled=True, axis_index_groups=[middle_first(members)]
+        message, "member", 0, 0, tiled=True, axis_index_groups=[downward(members)]
     )
 
     density, spread, reassign = call(

time: 28.8 us -> 28.5 us (0.990)
  blocking collectives: 10 us -> 9.69 us
    all_to_all x1, blocking collectives: 10 us -> 9.69 us  [per_device(): lax.all_to_all(message, 'member', 0, 0, tiled=True, axis_index_groups=[do...]
  transfers between devices with their start and end apart: 8 -> 8, of which waited for: 2 -> 2; matrix products, arithmetic and copies ran while one was open for 0% -> 0% of each run, Pallas kernels for 17% -> 18%
where the time goes in v28:
time: 28.5 us; the launch traced here: 28.3 us
  starting transfers between devices  10.8 us (38%)
  blocking collectives  9.69 us (34%)
  Pallas kernels  5.98 us (21%)
  waiting for transfers between devices  1.09 us (4%)
  between operations  0.74 us (3%)
    ppermute x8, starting transfers between devices, from_partner(): lax.ppermute(value, axis, [(source, source ^ mask) for source in range(co...  10.8 us
    all_to_all x1, blocking collectives, per_device(): lax.all_to_all(message, 'member', 0, 0, tiled=True, axis_index_groups=[do...  9.69 us
    pallas_call x7, Pallas kernels, call(): pl.pallas_call(body, out_shape=shapes, in_specs=[pl.BlockSpec(memory_spac...  5.98 us
    ppermute x8, waiting for transfers between devices, from_partner(): lax.ppermute(value, axis, [(source, source ^ mask) for source in range(co...  1.09 us
  transfers between devices with their start and end apart: 8, of which 2 were waited for; matrix products, arithmetic and copies ran while one was open for 0% of the time, Pallas kernels for 18%

profile of v28, /device:TPU:0, one launch (start us, length us, event | category | flops | bytes accessed | tf_op | source)
XLA Modules:
  0.0 28.3 jit_solution(15184330270115768541)
XLA Ops:
  0.6 3.0 %collective-permute-start = (s32[1,64]{1,0:T(1,128)}, s32[1,64]{1,0:T(1,128)S(1)}, u32[]{:S(2)}, u32[]{:S(2)}) collective-permute-start(s32[1,64]{1,0:T(1,128)} %ids_ref.3), channel_id=1, source_target_pairs={{0,1},{1,0},{2,3},{3,2},{4,5},{5,4},{6,7},{7,6},{8,9},{9,8},{10,11... | collective-permute-start | bytes 776 | tf_op jit(solution)/shard_map/ppermute | solution.py:21
  3.6 0.0 collective-permute-start.1
  3.6 1.5 %collective-permute-start.2 = (bf16[16,768]{1,0:T(8,128)(2,1)}, bf16[16,768]{1,0:T(8,128)(2,1)S(1)}, u32[]{:S(2)}, u32[]{:S(2)}) collective-permute-start(bf16[16,768]{1,0:T(8,128)(2,1)} %new_ref.1), channel_id=1, source_target_pairs={{0,16},{8,24},{16,0},{24,8},{1,17},{9,25},{17,1},{25,9},{2,18},{10... | collective-permute-start | bytes 73736 | tf_op jit(solution)/shard_map/ppermute | solution.py:21
  5.2 0.3 %collective-permute-start.3 = (bf16[16,768]{1,0:T(8,128)(2,1)}, bf16[16,768]{1,0:T(8,128)(2,1)S(1)}, u32[]{:S(2)}, u32[]{:S(2)}) collective-permute-start(bf16[16,768]{1,0:T(8,128)(2,1)} %new_ref.1), channel_id=1, source_target_pairs={{0,24},{8,16},{16,8},{24,0},{1,25},{9,17},{17,9},{25,1},{2,26},{10... | collective-permute-start | bytes 73736 | tf_op jit(solution)/shard_map/ppermute | solution.py:21
  5.5 0.7 %shard_map.67 = s32[1,64]{1,0:T(1,128)S(1)} custom-call(s32[1,64]{1,0:T(1,128)} %ids_ref.3), custom_call_target="tpu_custom_call" | custom-call | tf_op jit(solution)/shard_map/pallas_call | solution.py:37
  6.2 0.0 collective-permute-done
  6.2 0.0 copy-start
  6.2 0.0 copy-start.1
  6.2 1.6 %collective-permute-start.5 = (s32[2,64]{1,0:T(2,128)S(1)}, s32[2,64]{1,0:T(2,128)S(1)}, u32[]{:S(2)}, u32[]{:S(2)}) collective-permute-start(s32[2,64]{1,0:T(2,128)S(1)} %pad_add_fusion.1.unused.ids_ref), channel_id=1, source_target_pairs={{0,2},{1,3},{2,0},{3,1},{4,6},{5,7},{6,4},{7,5},{8,10},{9,11},{10,... | collective-permute-start | bytes 1544 | tf_op jit(solution)/shard_map/ppermute | solution.py:21
  7.9 2.1 %shard_map.68 = (bf16[2048,768]{1,0:T(8,128)(2,1)S(1)}, f32[1,2048]{1,0:T(1,128)S(1)}, bf16[16,768]{1,0:T(8,128)(2,1)S(1)}) custom-call(bf16[2048,768]{1,0:T(8,128)(2,1)} %heads_ref.1, bf16[16,768]{1,0:T(8,128)(2,1)} %new_ref.1, s32[2,64]{1,0:T(2,128)S(1)} %pad_add_fusion.1.unused.ids_ref), custom_call_target="tpu_custom_call" | custom-call | tf_op jit(solution)/shard_map/pallas_call | solution.py:37
  10.0 0.0 collective-permute-done.1.refs_1_
  10.0 0.0 collective-permute-done.2.refs_2_
  10.0 0.0 collective-permute-done.3.refs_3_
  10.0 1.2 %shard_map.69 = (f32[8,128]{1,0:T(8,128)S(1)}, s32[2,64]{1,0:T(2,128)S(1)}) custom-call(s32[2,64]{1,0:T(2,128)S(1)} %pad_add_fusion.1.unused.ids_ref, bf16[2048,768]{1,0:T(8,128)(2,1)S(1)} %get-tuple-element.13.heads_ref, f32[1,2048]{1,0:T(1,128)S(1)} %get-tuple-element.14.head_sq_ref, bf16[16,768]{1,0:T(8,128)(2,1)S(1)} %get-tuple-element.15.refs_0_, ...), custom_call_target="tpu_custom_call" | custom-call | tf_op jit(solution)/shard_map/pallas_call | solution.py:37
  11.2 0.1 collective-permute-start.4
  11.3 0.0 collective-permute-done.5
  11.3 2.7 %collective-permute-start.6 = (s32[4,64]{1,0:T(4,128)S(1)}, s32[4,64]{1,0:T(4,128)S(1)}, u32[]{:S(2)}, u32[]{:S(2)}) collective-permute-start(s32[4,64]{1,0:T(4,128)S(1)} %pad_add_fusion.near_ref), channel_id=1, source_target_pairs={{0,4},{1,5},{2,6},{3,7},{4,0},{5,1},{6,2},{7,3},{8,12},{9,13},{10,... | collective-permute-start | bytes 3080 | tf_op jit(solution)/shard_map/ppermute | solution.py:21
  14.0 0.0 collective-permute-done.4
  14.0 1.5 %collective-permute-start.7 = (f32[8,128]{1,0:T(8,128)S(1)}, f32[8,128]{1,0:T(8,128)S(1)}, u32[]{:S(2)}, u32[]{:S(2)}) collective-permute-start(f32[8,128]{1,0:T(8,128)S(1)} %add.3.unused.mine_ref), channel_id=1, source_target_pairs={{0,16},{8,24},{16,0},{24,8},{1,17},{9,25},{17,1},{25,9},{2,18},{10... | collective-permute-start | bytes 12296 | tf_op jit(solution)/shard_map/ppermute | solution.py:21
  15.5 0.0 copy-done
  15.5 0.0 copy-done.1
  15.5 0.2 shard_map.70
  15.7 0.2 collective-permute-done.6.far_ref
  15.9 0.8 %shard_map.71.rows_ref = bf16[128,768]{1,0:T(8,128)(2,1)S(1)} custom-call(s32[4,64]{1,0:T(4,128)S(1)} %pad_add_fusion.near_ref, s32[4,64]{1,0:T(4,128)S(1)} %collective-permute-done.6.far_ref, bf16[2048,768]{1,0:T(8,128)(2,1)S(1)} %get-tuple-element.13.heads_ref, bf16[64,128]{1,0:T(8,128)(2,1)S(1)} %get-tuple-element.17.unused.back_ref), custom_call_target="tpu_custom_call" | custom-call | flops 402653184 | bytes 3145728 | tf_op jit(solution)/shard_map/pallas_call | solution.py:37
  16.7 0.9 %collective-permute-done.7.other_ref = f32[8,128]{1,0:T(8,128)S(1)} collective-permute-done((f32[8,128]{1,0:T(8,128)S(1)}, f32[8,128]{1,0:T(8,128)S(1)}, u32[]{:S(2)}, u32[]{:S(2)}) %collective-permute-start.7) | collective-permute-done | bytes 4128 | tf_op jit(solution)/shard_map/ppermute | solution.py:21
  17.6 9.7 %all_to_all.5.listed_ref = bf16[8,104,128]{2,1,0:T(8,128)(2,1)S(1)} all-to-all(bf16[8,104,128]{2,1,0:T(8,128)(2,1)S(1)} %shard_map.72), channel_id=1, replica_groups={{4,3,2,1,0,7,6,5},{12,11,10,9,8,15,14,13},{20,19,18,17,16,23,22,21},{28..., dimensions={0} | all-to-all | bytes 425984 | tf_op jit(solution)/shard_map/all_to_all | solution.py:308
  27.3 1.0 %shard_map.73 = (f32[1,16]{1,0:T(1,128)}, f32[1,16]{1,0:T(1,128)}, f32[1,64,128]{2,1,0:T(8,128)}) custom-call(bf16[64,128]{1,0:T(8,128)(2,1)S(1)} %get-tuple-element.17.unused.back_ref, f32[1,128]{1,0:T(1,128)S(1)} %get-tuple-element.18.vec_sq_ref, bf16[8,104,128]{2,1,0:T(8,128)(2,1)S(1)} %all_to_all.5.listed_ref, bf16[1,128,768]{2,1,0:T(8,128)(2,1)S(1)} %copy-done), custom_call_target="tpu_custom_call" | custom-call | flops 25165824 | bytes 393216 | tf_op jit(solution)/shard_map/pallas_call | solution.py:37
  (4 shorter events, 0.1 us)
Async XLA Ops:
  0.6 5.5 %collective-permute-start = (s32[1,64]{1,0:T(1,128)}, s32[1,64]{1,0:T(1,128)S(1)}, u32[]{:S(2)}, u32[]{:S(2)}) collective-permute-start(s32[1,64]{1,0:T(1,128)} %ids_ref.3), channel_id=1, source_target_pairs={{0,1},{1,0},{2,3},{3,2},{4,5},{5,4},{6,7},{7,6},{8,9},{9,8},{10,11... | collective-permute-start | bytes 776 | tf_op jit(solution)/shard_map/ppermute | solution.py:21
  3.6 6.3 %collective-permute-start.1 = (bf16[16,768]{1,0:T(8,128)(2,1)}, bf16[16,768]{1,0:T(8,128)(2,1)S(1)}, u32[]{:S(2)}, u32[]{:S(2)}) collective-permute-start(bf16[16,768]{1,0:T(8,128)(2,1)} %new_ref.1), channel_id=1, source_target_pairs={{0,8},{8,0},{16,24},{24,16},{1,9},{9,1},{17,25},{25,17},{2,10},{10... | collective-permute-start | bytes 73736 | tf_op jit(solution)/shard_map/ppermute | solution.py:21
  3.6 6.4 %collective-permute-start.2 = (bf16[16,768]{1,0:T(8,128)(2,1)}, bf16[16,768]{1,0:T(8,128)(2,1)S(1)}, u32[]{:S(2)}, u32[]{:S(2)}) collective-permute-start(bf16[16,768]{1,0:T(8,128)(2,1)} %new_ref.1), channel_id=1, source_target_pairs={{0,16},{8,24},{16,0},{24,8},{1,17},{9,25},{17,1},{25,9},{2,18},{10... | collective-permute-start | bytes 73736 | tf_op jit(solution)/shard_map/ppermute | solution.py:21
  5.2 4.8 %collective-permute-start.3 = (bf16[16,768]{1,0:T(8,128)(2,1)}, bf16[16,768]{1,0:T(8,128)(2,1)S(1)}, u32[]{:S(2)}, u32[]{:S(2)}) collective-permute-start(bf16[16,768]{1,0:T(8,128)(2,1)} %new_ref.1), channel_id=1, source_target_pairs={{0,24},{8,16},{16,8},{24,0},{1,25},{9,17},{17,9},{25,1},{2,26},{10... | collective-permute-start | bytes 73736 | tf_op jit(solution)/shard_map/ppermute | solution.py:21
  6.2 9.3 %copy-start = (bf16[1,128,768]{2,1,0:T(8,128)(2,1)S(1)}, bf16[1,128,768]{2,1,0:T(8,128)(2,1)}, u32[]{:S(2)}) copy-start(bf16[1,128,768]{2,1,0:T(8,128)(2,1)} %vectors_ref.3) | copy-start | bytes 589828
  6.2 9.3 %copy-start.1 = (s32[1,64]{1,0:T(1,128)S(1)}, s32[1,64]{1,0:T(1,128)}, u32[]{:S(2)}) copy-start(s32[1,64]{1,0:T(1,128)} %ids_ref.3) | copy-start | bytes 772
  6.2 5.1 %collective-permute-start.5 = (s32[2,64]{1,0:T(2,128)S(1)}, s32[2,64]{1,0:T(2,128)S(1)}, u32[]{:S(2)}, u32[]{:S(2)}) collective-permute-start(s32[2,64]{1,0:T(2,128)S(1)} %pad_add_fusion.1.unused.ids_ref), channel_id=1, source_target_pairs={{0,2},{1,3},{2,0},{3,1},{4,6},{5,7},{6,4},{7,5},{8,10},{9,11},{10,... | collective-permute-start | bytes 1544 | tf_op jit(solution)/shard_map/ppermute | solution.py:21
  11.2 2.8 %collective-permute-start.4 = (f32[8,128]{1,0:T(8,128)S(1)}, f32[8,128]{1,0:T(8,128)S(1)}, u32[]{:S(2)}, u32[]{:S(2)}) collective-permute-start(f32[8,128]{1,0:T(8,128)S(1)} %get-tuple-element.16), channel_id=1, source_target_pairs={{0,8},{8,0},{16,24},{24,16},{1,9},{9,1},{17,25},{25,17},{2,10},{10... | collective-permute-start | bytes 12296 | tf_op jit(solution)/shard_map/ppermute | solution.py:21
  11.3 4.5 %collective-permute-start.6 = (s32[4,64]{1,0:T(4,128)S(1)}, s32[4,64]{1,0:T(4,128)S(1)}, u32[]{:S(2)}, u32[]{:S(2)}) collective-permute-start(s32[4,64]{1,0:T(4,128)S(1)} %pad_add_fusion.near_ref), channel_id=1, source_target_pairs={{0,4},{1,5},{2,6},{3,7},{4,0},{5,1},{6,2},{7,3},{8,12},{9,13},{10,... | collective-permute-start | bytes 3080 | tf_op jit(solution)/shard_map/ppermute | solution.py:21
  14.0 3.6 %collective-permute-start.7 = (f32[8,128]{1,0:T(8,128)S(1)}, f32[8,128]{1,0:T(8,128)S(1)}, u32[]{:S(2)}, u32[]{:S(2)}) collective-permute-start(f32[8,128]{1,0:T(8,128)S(1)} %add.3.unused.mine_ref), channel_id=1, source_target_pairs={{0,16},{8,24},{16,0},{24,8},{1,17},{9,25},{17,1},{25,9},{2,18},{10... | collective-permute-start | bytes 12296 | tf_op jit(solution)/shard_map/ppermute | solution.py:21

commit v29 on v27

--- a/solution.py
+++ b/solution.py
@@ -26,13 +26,13 @@
     order = [half, 0]
     for low in range(half - 1, 0, -1):
         order += [half + low, low]
-    return order
+    return order[-2:] + order[:-2]
 
 
 def turn_of(member, members):
     half = members // 2
     low = member % half
-    return jnp.where(low == 0, 0, 2 * (half - low)) + jnp.where(member < half, 1, 0)
+    return 2 * ((half + 1 - low) % half) + jnp.where(member < half, 1, 0)
 
 
 def in_hbm(value):

time: 27.8 us -> 28.7 us (1.032)
  blocking collectives: 9.04 us -> 9.92 us
    all_to_all x1, blocking collectives: 9.04 us -> 9.92 us  [per_device(): lax.all_to_all(message, 'member', 0, 0, tiled=True, axis_index_groups=[by...]
  transfers between devices with their start and end apart: 8 -> 8, of which waited for: 2 -> 2; matrix products, arithmetic and copies ran while one was open for 0% -> 0% of each run, Pallas kernels for 18% -> 17%
where the time goes in v29:
time: 28.7 us; the launch traced here: 28.5 us
  starting transfers between devices  10.8 us (38%)
  blocking collectives  9.92 us (35%)
  Pallas kernels  5.98 us (21%)
  waiting for transfers between devices  1.09 us (4%)
  between operations  0.74 us (3%)
    ppermute x8, starting transfers between devices, from_partner(): lax.ppermute(value, axis, [(source, source ^ mask) for source in range(co...  10.8 us
    all_to_all x1, blocking collectives, per_device(): lax.all_to_all(message, 'member', 0, 0, tiled=True, axis_index_groups=[by...  9.92 us
    pallas_call x7, Pallas kernels, call(): pl.pallas_call(body, out_shape=shapes, in_specs=[pl.BlockSpec(memory_spac...  5.98 us
    ppermute x8, waiting for transfers between devices, from_partner(): lax.ppermute(value, axis, [(source, source ^ mask) for source in range(co...  1.09 us
  transfers between devices with their start and end apart: 8, of which 2 were waited for; matrix products, arithmetic and copies ran while one was open for 0% of the time, Pallas kernels for 17%

profile of v29, /device:TPU:0, one launch (start us, length us, event | category | flops | bytes accessed | tf_op | source)
XLA Modules:
  0.0 28.5 jit_solution(636786869070205904)
XLA Ops:
  0.6 3.0 %collective-permute-start = (s32[1,64]{1,0:T(1,128)}, s32[1,64]{1,0:T(1,128)S(1)}, u32[]{:S(2)}, u32[]{:S(2)}) collective-permute-start(s32[1,64]{1,0:T(1,128)} %ids_ref.3), channel_id=1, source_target_pairs={{0,1},{1,0},{2,3},{3,2},{4,5},{5,4},{6,7},{7,6},{8,9},{9,8},{10,11... | collective-permute-start | bytes 776 | tf_op jit(solution)/shard_map/ppermute | solution.py:21
  3.6 0.0 collective-permute-start.1
  3.6 1.5 %collective-permute-start.2 = (bf16[16,768]{1,0:T(8,128)(2,1)}, bf16[16,768]{1,0:T(8,128)(2,1)S(1)}, u32[]{:S(2)}, u32[]{:S(2)}) collective-permute-start(bf16[16,768]{1,0:T(8,128)(2,1)} %new_ref.1), channel_id=1, source_target_pairs={{0,16},{8,24},{16,0},{24,8},{1,17},{9,25},{17,1},{25,9},{2,18},{10... | collective-permute-start | bytes 73736 | tf_op jit(solution)/shard_map/ppermute | solution.py:21
  5.2 0.3 %collective-permute-start.3 = (bf16[16,768]{1,0:T(8,128)(2,1)}, bf16[16,768]{1,0:T(8,128)(2,1)S(1)}, u32[]{:S(2)}, u32[]{:S(2)}) collective-permute-start(bf16[16,768]{1,0:T(8,128)(2,1)} %new_ref.1), channel_id=1, source_target_pairs={{0,24},{8,16},{16,8},{24,0},{1,25},{9,17},{17,9},{25,1},{2,26},{10... | collective-permute-start | bytes 73736 | tf_op jit(solution)/shard_map/ppermute | solution.py:21
  5.5 0.7 %shard_map.67 = s32[1,64]{1,0:T(1,128)S(1)} custom-call(s32[1,64]{1,0:T(1,128)} %ids_ref.3), custom_call_target="tpu_custom_call" | custom-call | tf_op jit(solution)/shard_map/pallas_call | solution.py:43
  6.2 0.0 collective-permute-done
  6.2 0.0 copy-start
  6.2 0.0 copy-start.1
  6.2 1.6 %collective-permute-start.5 = (s32[2,64]{1,0:T(2,128)S(1)}, s32[2,64]{1,0:T(2,128)S(1)}, u32[]{:S(2)}, u32[]{:S(2)}) collective-permute-start(s32[2,64]{1,0:T(2,128)S(1)} %pad_add_fusion.1.unused.ids_ref), channel_id=1, source_target_pairs={{0,2},{1,3},{2,0},{3,1},{4,6},{5,7},{6,4},{7,5},{8,10},{9,11},{10,... | collective-permute-start | bytes 1544 | tf_op jit(solution)/shard_map/ppermute | solution.py:21
  7.9 2.1 %shard_map.68 = (bf16[2048,768]{1,0:T(8,128)(2,1)S(1)}, f32[1,2048]{1,0:T(1,128)S(1)}, bf16[16,768]{1,0:T(8,128)(2,1)S(1)}) custom-call(bf16[2048,768]{1,0:T(8,128)(2,1)} %heads_ref.1, bf16[16,768]{1,0:T(8,128)(2,1)} %new_ref.1, s32[2,64]{1,0:T(2,128)S(1)} %pad_add_fusion.1.unused.ids_ref), custom_call_target="tpu_custom_call" | custom-call | tf_op jit(solution)/shard_map/pallas_call | solution.py:43
  10.0 0.0 collective-permute-done.1.refs_1_
  10.0 0.0 collective-permute-done.2.refs_2_
  10.0 0.0 collective-permute-done.3.refs_3_
  10.0 1.2 %shard_map.69 = (f32[8,128]{1,0:T(8,128)S(1)}, s32[2,64]{1,0:T(2,128)S(1)}) custom-call(s32[2,64]{1,0:T(2,128)S(1)} %pad_add_fusion.1.unused.ids_ref, bf16[2048,768]{1,0:T(8,128)(2,1)S(1)} %get-tuple-element.13.heads_ref, f32[1,2048]{1,0:T(1,128)S(1)} %get-tuple-element.14.head_sq_ref, bf16[16,768]{1,0:T(8,128)(2,1)S(1)} %get-tuple-element.15.refs_0_, ...), custom_call_target="tpu_custom_call" | custom-call | tf_op jit(solution)/shard_map/pallas_call | solution.py:43
  11.2 0.1 collective-permute-start.4
  11.3 0.0 collective-permute-done.5
  11.3 2.7 %collective-permute-start.6 = (s32[4,64]{1,0:T(4,128)S(1)}, s32[4,64]{1,0:T(4,128)S(1)}, u32[]{:S(2)}, u32[]{:S(2)}) collective-permute-start(s32[4,64]{1,0:T(4,128)S(1)} %pad_add_fusion.near_ref), channel_id=1, source_target_pairs={{0,4},{1,5},{2,6},{3,7},{4,0},{5,1},{6,2},{7,3},{8,12},{9,13},{10,... | collective-permute-start | bytes 3080 | tf_op jit(solution)/shard_map/ppermute | solution.py:21
  14.0 0.0 collective-permute-done.4
  14.0 1.5 %collective-permute-start.7 = (f32[8,128]{1,0:T(8,128)S(1)}, f32[8,128]{1,0:T(8,128)S(1)}, u32[]{:S(2)}, u32[]{:S(2)}) collective-permute-start(f32[8,128]{1,0:T(8,128)S(1)} %add.3.unused.mine_ref), channel_id=1, source_target_pairs={{0,16},{8,24},{16,0},{24,8},{1,17},{9,25},{17,1},{25,9},{2,18},{10... | collective-permute-start | bytes 12296 | tf_op jit(solution)/shard_map/ppermute | solution.py:21
  15.5 0.0 copy-done
  15.5 0.0 copy-done.1
  15.5 0.2 shard_map.70
  15.7 0.2 collective-permute-done.6.far_ref
  15.9 0.8 %shard_map.71.rows_ref = bf16[128,768]{1,0:T(8,128)(2,1)S(1)} custom-call(s32[4,64]{1,0:T(4,128)S(1)} %pad_add_fusion.near_ref, s32[4,64]{1,0:T(4,128)S(1)} %collective-permute-done.6.far_ref, bf16[2048,768]{1,0:T(8,128)(2,1)S(1)} %get-tuple-element.13.heads_ref, bf16[64,128]{1,0:T(8,128)(2,1)S(1)} %get-tuple-element.17.unused.back_ref), custom_call_target="tpu_custom_call" | custom-call | flops 402653184 | bytes 3145728 | tf_op jit(solution)/shard_map/pallas_call | solution.py:43
  16.7 0.9 %collective-permute-done.7.other_ref = f32[8,128]{1,0:T(8,128)S(1)} collective-permute-done((f32[8,128]{1,0:T(8,128)S(1)}, f32[8,128]{1,0:T(8,128)S(1)}, u32[]{:S(2)}, u32[]{:S(2)}) %collective-permute-start.7) | collective-permute-done | bytes 4128 | tf_op jit(solution)/shard_map/ppermute | solution.py:21
  17.6 9.9 %all_to_all.5.listed_ref = bf16[8,104,128]{2,1,0:T(8,128)(2,1)S(1)} all-to-all(bf16[8,104,128]{2,1,0:T(8,128)(2,1)S(1)} %shard_map.72), channel_id=1, replica_groups={{5,1,4,0,7,3,6,2},{13,9,12,8,15,11,14,10},{21,17,20,16,23,19,22,18},{29..., dimensions={0} | all-to-all | bytes 425984 | tf_op jit(solution)/shard_map/all_to_all | solution.py:314
  27.6 1.0 %shard_map.73 = (f32[1,16]{1,0:T(1,128)}, f32[1,16]{1,0:T(1,128)}, f32[1,64,128]{2,1,0:T(8,128)}) custom-call(bf16[64,128]{1,0:T(8,128)(2,1)S(1)} %get-tuple-element.17.unused.back_ref, f32[1,128]{1,0:T(1,128)S(1)} %get-tuple-element.18.vec_sq_ref, bf16[8,104,128]{2,1,0:T(8,128)(2,1)S(1)} %all_to_all.5.listed_ref, bf16[1,128,768]{2,1,0:T(8,128)(2,1)S(1)} %copy-done), custom_call_target="tpu_custom_call" | custom-call | flops 25165824 | bytes 393216 | tf_op jit(solution)/shard_map/pallas_call | solution.py:43
  (4 shorter events, 0.1 us)
Async XLA Ops:
  0.6 5.5 %collective-permute-start = (s32[1,64]{1,0:T(1,128)}, s32[1,64]{1,0:T(1,128)S(1)}, u32[]{:S(2)}, u32[]{:S(2)}) collective-permute-start(s32[1,64]{1,0:T(1,128)} %ids_ref.3), channel_id=1, source_target_pairs={{0,1},{1,0},{2,3},{3,2},{4,5},{5,4},{6,7},{7,6},{8,9},{9,8},{10,11... | collective-permute-start | bytes 776 | tf_op jit(solution)/shard_map/ppermute | solution.py:21
  3.6 6.3 %collective-permute-start.1 = (bf16[16,768]{1,0:T(8,128)(2,1)}, bf16[16,768]{1,0:T(8,128)(2,1)S(1)}, u32[]{:S(2)}, u32[]{:S(2)}) collective-permute-start(bf16[16,768]{1,0:T(8,128)(2,1)} %new_ref.1), channel_id=1, source_target_pairs={{0,8},{8,0},{16,24},{24,16},{1,9},{9,1},{17,25},{25,17},{2,10},{10... | collective-permute-start | bytes 73736 | tf_op jit(solution)/shard_map/ppermute | solution.py:21
  3.6 6.4 %collective-permute-start.2 = (bf16[16,768]{1,0:T(8,128)(2,1)}, bf16[16,768]{1,0:T(8,128)(2,1)S(1)}, u32[]{:S(2)}, u32[]{:S(2)}) collective-permute-start(bf16[16,768]{1,0:T(8,128)(2,1)} %new_ref.1), channel_id=1, source_target_pairs={{0,16},{8,24},{16,0},{24,8},{1,17},{9,25},{17,1},{25,9},{2,18},{10... | collective-permute-start | bytes 73736 | tf_op jit(solution)/shard_map/ppermute | solution.py:21
  5.2 4.8 %collective-permute-start.3 = (bf16[16,768]{1,0:T(8,128)(2,1)}, bf16[16,768]{1,0:T(8,128)(2,1)S(1)}, u32[]{:S(2)}, u32[]{:S(2)}) collective-permute-start(bf16[16,768]{1,0:T(8,128)(2,1)} %new_ref.1), channel_id=1, source_target_pairs={{0,24},{8,16},{16,8},{24,0},{1,25},{9,17},{17,9},{25,1},{2,26},{10... | collective-permute-start | bytes 73736 | tf_op jit(solution)/shard_map/ppermute | solution.py:21
  6.2 9.3 %copy-start = (bf16[1,128,768]{2,1,0:T(8,128)(2,1)S(1)}, bf16[1,128,768]{2,1,0:T(8,128)(2,1)}, u32[]{:S(2)}) copy-start(bf16[1,128,768]{2,1,0:T(8,128)(2,1)} %vectors_ref.3) | copy-start | bytes 589828
  6.2 9.3 %copy-start.1 = (s32[1,64]{1,0:T(1,128)S(1)}, s32[1,64]{1,0:T(1,128)}, u32[]{:S(2)}) copy-start(s32[1,64]{1,0:T(1,128)} %ids_ref.3) | copy-start | bytes 772
  6.2 5.1 %collective-permute-start.5 = (s32[2,64]{1,0:T(2,128)S(1)}, s32[2,64]{1,0:T(2,128)S(1)}, u32[]{:S(2)}, u32[]{:S(2)}) collective-permute-start(s32[2,64]{1,0:T(2,128)S(1)} %pad_add_fusion.1.unused.ids_ref), channel_id=1, source_target_pairs={{0,2},{1,3},{2,0},{3,1},{4,6},{5,7},{6,4},{7,5},{8,10},{9,11},{10,... | collective-permute-start | bytes 1544 | tf_op jit(solution)/shard_map/ppermute | solution.py:21
  11.2 2.8 %collective-permute-start.4 = (f32[8,128]{1,0:T(8,128)S(1)}, f32[8,128]{1,0:T(8,128)S(1)}, u32[]{:S(2)}, u32[]{:S(2)}) collective-permute-start(f32[8,128]{1,0:T(8,128)S(1)} %get-tuple-element.16), channel_id=1, source_target_pairs={{0,8},{8,0},{16,24},{24,16},{1,9},{9,1},{17,25},{25,17},{2,10},{10... | collective-permute-start | bytes 12296 | tf_op jit(solution)/shard_map/ppermute | solution.py:21
  11.3 4.5 %collective-permute-start.6 = (s32[4,64]{1,0:T(4,128)S(1)}, s32[4,64]{1,0:T(4,128)S(1)}, u32[]{:S(2)}, u32[]{:S(2)}) collective-permute-start(s32[4,64]{1,0:T(4,128)S(1)} %pad_add_fusion.near_ref), channel_id=1, source_target_pairs={{0,4},{1,5},{2,6},{3,7},{4,0},{5,1},{6,2},{7,3},{8,12},{9,13},{10,... | collective-permute-start | bytes 3080 | tf_op jit(solution)/shard_map/ppermute | solution.py:21
  14.0 3.6 %collective-permute-start.7 = (f32[8,128]{1,0:T(8,128)S(1)}, f32[8,128]{1,0:T(8,128)S(1)}, u32[]{:S(2)}, u32[]{:S(2)}) collective-permute-start(f32[8,128]{1,0:T(8,128)S(1)} %add.3.unused.mine_ref), channel_id=1, source_target_pairs={{0,16},{8,24},{16,0},{24,8},{1,17},{9,25},{17,1},{25,9},{2,18},{10... | collective-permute-start | bytes 12296 | tf_op jit(solution)/shard_map/ppermute | solution.py:21

commit v30 on v27

--- a/solution.py
+++ b/solution.py
@@ -39,12 +39,12 @@
     return pltpu.with_memory_space_constraint(value, HBM)
 
 
-def call(body, shapes, operands, cost, scratch=(), spaces=None):
+def call(body, shapes, operands, cost, scratch=(), spaces=None, outs=None):
     return pl.pallas_call(
         body,
         out_shape=shapes,
         in_specs=[pl.BlockSpec(memory_space=space) for space in spaces or [VMEM] * len(operands)],
-        out_specs=jax.tree.map(lambda unused: pl.BlockSpec(memory_space=VMEM), shapes),
+        out_specs=outs or jax.tree.map(lambda unused: pl.BlockSpec(memory_space=VMEM), shapes),
         scratch_shapes=scratch,
         compiler_params=pltpu.CompilerParams(vmem_limit_bytes=LIMIT),
         cost_estimate=pl.CostEstimate(flops=cost[0], bytes_accessed=cost[1], transcendentals=0),
@@ -205,10 +205,12 @@
 
 def tail_kernel(
     groups, slots, total_heads, back_ref, vec_sq_ref, listed_ref, vectors_ref,
-    density_ref, spread_ref, out_ref,
+    density_ref, spread_ref, out_ref, made_ref, sem,
 ):
     listed = listed_ref[...]
-    distances(slots, back_ref, vec_sq_ref, listed, vectors_ref, out_ref)
+    distances(slots, back_ref, vec_sq_ref, listed, vectors_ref, made_ref)
+    copy = pltpu.make_async_copy(made_ref, out_ref, sem)
+    copy.start()
     here = lax.axis_index("group")
     members = listed_ref.shape[0]
     new_count = density_ref.shape[1]
@@ -231,6 +233,7 @@
         found.append(jnp.sum(jnp.where(eye, column, 0.0), axis=0, keepdims=True))
     density_ref[...] = jnp.log(found[0] * (1.0 / total_heads))
     spread_ref[...] = found[1] / found[0]
+    copy.wait()
 
 
 def per_device(heads, new_heads, vectors, near_ids):
@@ -326,6 +329,10 @@
         ),
         (back, vec_sq, message, vectors),
         (4 * near * vectors.shape[1] * width, vectors.size * 4),
+        scratch=[
+            pltpu.VMEM((1, near, vectors.shape[1]), jnp.float32), pltpu.SemaphoreType.DMA
+        ],
+        outs=tuple(pl.BlockSpec(memory_space=space) for space in (VMEM, VMEM, HBM)),
     )
     return (density[0], spread[0], reassign)
 

time: 27.8 us -> 28.3 us (1.018)
  Pallas kernels: 5.98 us -> 6.5 us
    pallas_call x7, Pallas kernels: 5.98 us -> 6.5 us  [call(): pl.pallas_call(body, out_shape=shapes, in_specs=[pl.BlockSpec(memory_spac...]
where the time goes in v30:
time: 28.3 us; the launch traced here: 28.2 us
  starting transfers between devices  10.8 us (38%)
  blocking collectives  9.04 us (32%)
  Pallas kernels  6.5 us (23%)
  waiting for transfers between devices  1.09 us (4%)
  between operations  0.74 us (3%)
    ppermute x8, starting transfers between devices, from_partner(): lax.ppermute(value, axis, [(source, source ^ mask) for source in range(co...  10.8 us
    all_to_all x1, blocking collectives, per_device(): lax.all_to_all(message, 'member', 0, 0, tiled=True, axis_index_groups=[by...  9.04 us
    pallas_call x7, Pallas kernels, call(): pl.pallas_call(body, out_shape=shapes, in_specs=[pl.BlockSpec(memory_spac...  6.5 us
    ppermute x8, waiting for transfers between devices, from_partner(): lax.ppermute(value, axis, [(source, source ^ mask) for source in range(co...  1.09 us
  transfers between devices with their start and end apart: 8, of which 2 were waited for; matrix products, arithmetic and copies ran while one was open for 0% of the time, Pallas kernels for 18%

profile of v30, /device:TPU:0, one launch (start us, length us, event | category | flops | bytes accessed | tf_op | source)
XLA Modules:
  0.0 28.2 jit_solution(15914084060899809650)
XLA Ops:
  0.6 3.0 %collective-permute-start = (s32[1,64]{1,0:T(1,128)}, s32[1,64]{1,0:T(1,128)S(1)}, u32[]{:S(2)}, u32[]{:S(2)}) collective-permute-start(s32[1,64]{1,0:T(1,128)} %ids_ref.3), channel_id=1, source_target_pairs={{0,1},{1,0},{2,3},{3,2},{4,5},{5,4},{6,7},{7,6},{8,9},{9,8},{10,11... | collective-permute-start | bytes 776 | tf_op jit(solution)/shard_map/ppermute | solution.py:21
  3.6 0.0 collective-permute-start.1
  3.6 1.5 %collective-permute-start.2 = (bf16[16,768]{1,0:T(8,128)(2,1)}, bf16[16,768]{1,0:T(8,128)(2,1)S(1)}, u32[]{:S(2)}, u32[]{:S(2)}) collective-permute-start(bf16[16,768]{1,0:T(8,128)(2,1)} %new_ref.1), channel_id=1, source_target_pairs={{0,16},{8,24},{16,0},{24,8},{1,17},{9,25},{17,1},{25,9},{2,18},{10... | collective-permute-start | bytes 73736 | tf_op jit(solution)/shard_map/ppermute | solution.py:21
  5.2 0.3 %collective-permute-start.3 = (bf16[16,768]{1,0:T(8,128)(2,1)}, bf16[16,768]{1,0:T(8,128)(2,1)S(1)}, u32[]{:S(2)}, u32[]{:S(2)}) collective-permute-start(bf16[16,768]{1,0:T(8,128)(2,1)} %new_ref.1), channel_id=1, source_target_pairs={{0,24},{8,16},{16,8},{24,0},{1,25},{9,17},{17,9},{25,1},{2,26},{10... | collective-permute-start | bytes 73736 | tf_op jit(solution)/shard_map/ppermute | solution.py:21
  5.5 0.7 %shard_map.67 = s32[1,64]{1,0:T(1,128)S(1)} custom-call(s32[1,64]{1,0:T(1,128)} %ids_ref.3), custom_call_target="tpu_custom_call" | custom-call | tf_op jit(solution)/shard_map/pallas_call | solution.py:43
  6.2 0.0 collective-permute-done
  6.2 0.0 copy-start
  6.2 0.0 copy-start.1
  6.2 1.6 %collective-permute-start.5 = (s32[2,64]{1,0:T(2,128)S(1)}, s32[2,64]{1,0:T(2,128)S(1)}, u32[]{:S(2)}, u32[]{:S(2)}) collective-permute-start(s32[2,64]{1,0:T(2,128)S(1)} %pad_add_fusion.1.unused.ids_ref), channel_id=1, source_target_pairs={{0,2},{1,3},{2,0},{3,1},{4,6},{5,7},{6,4},{7,5},{8,10},{9,11},{10,... | collective-permute-start | bytes 1544 | tf_op jit(solution)/shard_map/ppermute | solution.py:21
  7.9 2.1 %shard_map.68 = (bf16[2048,768]{1,0:T(8,128)(2,1)S(1)}, f32[1,2048]{1,0:T(1,128)S(1)}, bf16[16,768]{1,0:T(8,128)(2,1)S(1)}) custom-call(bf16[2048,768]{1,0:T(8,128)(2,1)} %heads_ref.1, bf16[16,768]{1,0:T(8,128)(2,1)} %new_ref.1, s32[2,64]{1,0:T(2,128)S(1)} %pad_add_fusion.1.unused.ids_ref), custom_call_target="tpu_custom_call" | custom-call | tf_op jit(solution)/shard_map/pallas_call | solution.py:43
  10.0 0.0 collective-permute-done.1.refs_1_
  10.0 0.0 collective-permute-done.2.refs_2_
  10.0 0.0 collective-permute-done.3.refs_3_
  10.0 1.2 %shard_map.69 = (f32[8,128]{1,0:T(8,128)S(1)}, s32[2,64]{1,0:T(2,128)S(1)}) custom-call(s32[2,64]{1,0:T(2,128)S(1)} %pad_add_fusion.1.unused.ids_ref, bf16[2048,768]{1,0:T(8,128)(2,1)S(1)} %get-tuple-element.13.heads_ref, f32[1,2048]{1,0:T(1,128)S(1)} %get-tuple-element.14.head_sq_ref, bf16[16,768]{1,0:T(8,128)(2,1)S(1)} %get-tuple-element.15.refs_0_, ...), custom_call_target="tpu_custom_call" | custom-call | tf_op jit(solution)/shard_map/pallas_call | solution.py:43
  11.2 0.1 collective-permute-start.4
  11.3 0.0 collective-permute-done.5
  11.3 2.7 %collective-permute-start.6 = (s32[4,64]{1,0:T(4,128)S(1)}, s32[4,64]{1,0:T(4,128)S(1)}, u32[]{:S(2)}, u32[]{:S(2)}) collective-permute-start(s32[4,64]{1,0:T(4,128)S(1)} %pad_add_fusion.near_ref), channel_id=1, source_target_pairs={{0,4},{1,5},{2,6},{3,7},{4,0},{5,1},{6,2},{7,3},{8,12},{9,13},{10,... | collective-permute-start | bytes 3080 | tf_op jit(solution)/shard_map/ppermute | solution.py:21
  14.0 0.0 collective-permute-done.4
  14.0 1.5 %collective-permute-start.7 = (f32[8,128]{1,0:T(8,128)S(1)}, f32[8,128]{1,0:T(8,128)S(1)}, u32[]{:S(2)}, u32[]{:S(2)}) collective-permute-start(f32[8,128]{1,0:T(8,128)S(1)} %add.3.unused.mine_ref), channel_id=1, source_target_pairs={{0,16},{8,24},{16,0},{24,8},{1,17},{9,25},{17,1},{25,9},{2,18},{10... | collective-permute-start | bytes 12296 | tf_op jit(solution)/shard_map/ppermute | solution.py:21
  15.5 0.0 copy-done
  15.5 0.0 copy-done.1
  15.5 0.2 shard_map.70
  15.7 0.2 collective-permute-done.6.far_ref
  15.9 0.8 %shard_map.71.rows_ref = bf16[128,768]{1,0:T(8,128)(2,1)S(1)} custom-call(s32[4,64]{1,0:T(4,128)S(1)} %pad_add_fusion.near_ref, s32[4,64]{1,0:T(4,128)S(1)} %collective-permute-done.6.far_ref, bf16[2048,768]{1,0:T(8,128)(2,1)S(1)} %get-tuple-element.13.heads_ref, bf16[64,128]{1,0:T(8,128)(2,1)S(1)} %get-tuple-element.17.unused.back_ref), custom_call_target="tpu_custom_call" | custom-call | flops 402653184 | bytes 3145728 | tf_op jit(solution)/shard_map/pallas_call | solution.py:43
  16.7 0.9 %collective-permute-done.7.other_ref = f32[8,128]{1,0:T(8,128)S(1)} collective-permute-done((f32[8,128]{1,0:T(8,128)S(1)}, f32[8,128]{1,0:T(8,128)S(1)}, u32[]{:S(2)}, u32[]{:S(2)}) %collective-permute-start.7) | collective-permute-done | bytes 4128 | tf_op jit(solution)/shard_map/ppermute | solution.py:21
  17.6 9.0 %all_to_all.5.listed_ref = bf16[8,104,128]{2,1,0:T(8,128)(2,1)S(1)} all-to-all(bf16[8,104,128]{2,1,0:T(8,128)(2,1)S(1)} %shard_map.72), channel_id=1, replica_groups={{4,0,7,3,6,2,5,1},{12,8,15,11,14,10,13,9},{20,16,23,19,22,18,21,17},{28..., dimensions={0} | all-to-all | bytes 425984 | tf_op jit(solution)/shard_map/all_to_all | solution.py:317
  26.7 1.5 %shard_map.73 = (f32[1,16]{1,0:T(1,128)}, f32[1,16]{1,0:T(1,128)}, f32[1,64,128]{2,1,0:T(8,128)}) custom-call(bf16[64,128]{1,0:T(8,128)(2,1)S(1)} %get-tuple-element.17.unused.back_ref, f32[1,128]{1,0:T(1,128)S(1)} %get-tuple-element.18.vec_sq_ref, bf16[8,104,128]{2,1,0:T(8,128)(2,1)S(1)} %all_to_all.5.listed_ref, bf16[1,128,768]{2,1,0:T(8,128)(2,1)S(1)} %copy-done), custom_call_target="tpu_custom_call" | custom-call | flops 25165824 | bytes 393216 | tf_op jit(solution)/shard_map/pallas_call | solution.py:43
  (4 shorter events, 0.1 us)
Async XLA Ops:
  0.6 5.5 %collective-permute-start = (s32[1,64]{1,0:T(1,128)}, s32[1,64]{1,0:T(1,128)S(1)}, u32[]{:S(2)}, u32[]{:S(2)}) collective-permute-start(s32[1,64]{1,0:T(1,128)} %ids_ref.3), channel_id=1, source_target_pairs={{0,1},{1,0},{2,3},{3,2},{4,5},{5,4},{6,7},{7,6},{8,9},{9,8},{10,11... | collective-permute-start | bytes 776 | tf_op jit(solution)/shard_map/ppermute | solution.py:21
  3.6 6.3 %collective-permute-start.1 = (bf16[16,768]{1,0:T(8,128)(2,1)}, bf16[16,768]{1,0:T(8,128)(2,1)S(1)}, u32[]{:S(2)}, u32[]{:S(2)}) collective-permute-start(bf16[16,768]{1,0:T(8,128)(2,1)} %new_ref.1), channel_id=1, source_target_pairs={{0,8},{8,0},{16,24},{24,16},{1,9},{9,1},{17,25},{25,17},{2,10},{10... | collective-permute-start | bytes 73736 | tf_op jit(solution)/shard_map/ppermute | solution.py:21
  3.6 6.4 %collective-permute-start.2 = (bf16[16,768]{1,0:T(8,128)(2,1)}, bf16[16,768]{1,0:T(8,128)(2,1)S(1)}, u32[]{:S(2)}, u32[]{:S(2)}) collective-permute-start(bf16[16,768]{1,0:T(8,128)(2,1)} %new_ref.1), channel_id=1, source_target_pairs={{0,16},{8,24},{16,0},{24,8},{1,17},{9,25},{17,1},{25,9},{2,18},{10... | collective-permute-start | bytes 73736 | tf_op jit(solution)/shard_map/ppermute | solution.py:21
  5.2 4.8 %collective-permute-start.3 = (bf16[16,768]{1,0:T(8,128)(2,1)}, bf16[16,768]{1,0:T(8,128)(2,1)S(1)}, u32[]{:S(2)}, u32[]{:S(2)}) collective-permute-start(bf16[16,768]{1,0:T(8,128)(2,1)} %new_ref.1), channel_id=1, source_target_pairs={{0,24},{8,16},{16,8},{24,0},{1,25},{9,17},{17,9},{25,1},{2,26},{10... | collective-permute-start | bytes 73736 | tf_op jit(solution)/shard_map/ppermute | solution.py:21
  6.2 9.3 %copy-start = (bf16[1,128,768]{2,1,0:T(8,128)(2,1)S(1)}, bf16[1,128,768]{2,1,0:T(8,128)(2,1)}, u32[]{:S(2)}) copy-start(bf16[1,128,768]{2,1,0:T(8,128)(2,1)} %vectors_ref.3) | copy-start | bytes 589828
  6.2 9.3 %copy-start.1 = (s32[1,64]{1,0:T(1,128)S(1)}, s32[1,64]{1,0:T(1,128)}, u32[]{:S(2)}) copy-start(s32[1,64]{1,0:T(1,128)} %ids_ref.3) | copy-start | bytes 772
  6.2 5.1 %collective-permute-start.5 = (s32[2,64]{1,0:T(2,128)S(1)}, s32[2,64]{1,0:T(2,128)S(1)}, u32[]{:S(2)}, u32[]{:S(2)}) collective-permute-start(s32[2,64]{1,0:T(2,128)S(1)} %pad_add_fusion.1.unused.ids_ref), channel_id=1, source_target_pairs={{0,2},{1,3},{2,0},{3,1},{4,6},{5,7},{6,4},{7,5},{8,10},{9,11},{10,... | collective-permute-start | bytes 1544 | tf_op jit(solution)/shard_map/ppermute | solution.py:21
  11.2 2.8 %collective-permute-start.4 = (f32[8,128]{1,0:T(8,128)S(1)}, f32[8,128]{1,0:T(8,128)S(1)}, u32[]{:S(2)}, u32[]{:S(2)}) collective-permute-start(f32[8,128]{1,0:T(8,128)S(1)} %get-tuple-element.16), channel_id=1, source_target_pairs={{0,8},{8,0},{16,24},{24,16},{1,9},{9,1},{17,25},{25,17},{2,10},{10... | collective-permute-start | bytes 12296 | tf_op jit(solution)/shard_map/ppermute | solution.py:21
  11.3 4.5 %collective-permute-start.6 = (s32[4,64]{1,0:T(4,128)S(1)}, s32[4,64]{1,0:T(4,128)S(1)}, u32[]{:S(2)}, u32[]{:S(2)}) collective-permute-start(s32[4,64]{1,0:T(4,128)S(1)} %pad_add_fusion.near_ref), channel_id=1, source_target_pairs={{0,4},{1,5},{2,6},{3,7},{4,0},{5,1},{6,2},{7,3},{8,12},{9,13},{10,... | collective-permute-start | bytes 3080 | tf_op jit(solution)/shard_map/ppermute | solution.py:21
  14.0 3.6 %collective-permute-start.7 = (f32[8,128]{1,0:T(8,128)S(1)}, f32[8,128]{1,0:T(8,128)S(1)}, u32[]{:S(2)}, u32[]{:S(2)}) collective-permute-start(f32[8,128]{1,0:T(8,128)S(1)} %add.3.unused.mine_ref), channel_id=1, source_target_pairs={{0,16},{8,24},{16,0},{24,8},{1,17},{9,25},{17,1},{25,9},{2,18},{10... | collective-permute-start | bytes 12296 | tf_op jit(solution)/shard_map/ppermute | solution.py:21

commit v31 on v29

--- a/solution.py
+++ b/solution.py
@@ -26,13 +26,15 @@
     order = [half, 0]
     for low in range(half - 1, 0, -1):
         order += [half + low, low]
-    return order[-2:] + order[:-2]
+    return order[:2] + order[4:6] + order[2:4] + order[6:]
 
 
 def turn_of(member, members):
     half = members // 2
     low = member % half
-    return 2 * ((half + 1 - low) % half) + jnp.where(member < half, 1, 0)
+    pair = jnp.where(low == 0, 0, half - low)
+    pair = jnp.where(pair == 1, 2, jnp.where(pair == 2, 1, pair))
+    return 2 * pair + jnp.where(member < half, 1, 0)
 
 
 def in_hbm(value):

time: 28.7 us -> 28.6 us (level)
  transfers between devices with their start and end apart: 8 -> 8, of which waited for: 2 -> 2; matrix products, arithmetic and copies ran while one was open for 0% -> 0% of each run, Pallas kernels for 17% -> 18%
where the time goes in v31:
time: 28.6 us; the launch traced here: 28.4 us
  starting transfers between devices  10.8 us (38%)
  blocking collectives  9.8 us (34%)
  Pallas kernels  5.98 us (21%)
  waiting for transfers between devices  1.09 us (4%)
  between operations  0.74 us (3%)
    ppermute x8, starting transfers between devices, from_partner(): lax.ppermute(value, axis, [(source, source ^ mask) for source in range(co...  10.8 us
    all_to_all x1, blocking collectives, per_device(): lax.all_to_all(message, 'member', 0, 0, tiled=True, axis_index_groups=[by...  9.8 us
    pallas_call x7, Pallas kernels, call(): pl.pallas_call(body, out_shape=shapes, in_specs=[pl.BlockSpec(memory_spac...  5.98 us
    ppermute x8, waiting for transfers between devices, from_partner(): lax.ppermute(value, axis, [(source, source ^ mask) for source in range(co...  1.09 us
  transfers between devices with their start and end apart: 8, of which 2 were waited for; matrix products, arithmetic and copies ran while one was open for 0% of the time, Pallas kernels for 18%

profile of v31, /device:TPU:0, one launch (start us, length us, event | category | flops | bytes accessed | tf_op | source)
XLA Modules:
  0.0 28.4 jit_solution(1682967138960919446)
XLA Ops:
  0.6 3.0 %collective-permute-start = (s32[1,64]{1,0:T(1,128)}, s32[1,64]{1,0:T(1,128)S(1)}, u32[]{:S(2)}, u32[]{:S(2)}) collective-permute-start(s32[1,64]{1,0:T(1,128)} %ids_ref.3), channel_id=1, source_target_pairs={{0,1},{1,0},{2,3},{3,2},{4,5},{5,4},{6,7},{7,6},{8,9},{9,8},{10,11... | collective-permute-start | bytes 776 | tf_op jit(solution)/shard_map/ppermute | solution.py:21
  3.6 0.0 collective-permute-start.1
  3.6 1.5 %collective-permute-start.2 = (bf16[16,768]{1,0:T(8,128)(2,1)}, bf16[16,768]{1,0:T(8,128)(2,1)S(1)}, u32[]{:S(2)}, u32[]{:S(2)}) collective-permute-start(bf16[16,768]{1,0:T(8,128)(2,1)} %new_ref.1), channel_id=1, source_target_pairs={{0,16},{8,24},{16,0},{24,8},{1,17},{9,25},{17,1},{25,9},{2,18},{10... | collective-permute-start | bytes 73736 | tf_op jit(solution)/shard_map/ppermute | solution.py:21
  5.2 0.3 %collective-permute-start.3 = (bf16[16,768]{1,0:T(8,128)(2,1)}, bf16[16,768]{1,0:T(8,128)(2,1)S(1)}, u32[]{:S(2)}, u32[]{:S(2)}) collective-permute-start(bf16[16,768]{1,0:T(8,128)(2,1)} %new_ref.1), channel_id=1, source_target_pairs={{0,24},{8,16},{16,8},{24,0},{1,25},{9,17},{17,9},{25,1},{2,26},{10... | collective-permute-start | bytes 73736 | tf_op jit(solution)/shard_map/ppermute | solution.py:21
  5.5 0.7 %shard_map.67 = s32[1,64]{1,0:T(1,128)S(1)} custom-call(s32[1,64]{1,0:T(1,128)} %ids_ref.3), custom_call_target="tpu_custom_call" | custom-call | tf_op jit(solution)/shard_map/pallas_call | solution.py:45
  6.2 0.0 collective-permute-done
  6.2 0.0 copy-start
  6.2 0.0 copy-start.1
  6.2 1.6 %collective-permute-start.5 = (s32[2,64]{1,0:T(2,128)S(1)}, s32[2,64]{1,0:T(2,128)S(1)}, u32[]{:S(2)}, u32[]{:S(2)}) collective-permute-start(s32[2,64]{1,0:T(2,128)S(1)} %pad_add_fusion.1.unused.ids_ref), channel_id=1, source_target_pairs={{0,2},{1,3},{2,0},{3,1},{4,6},{5,7},{6,4},{7,5},{8,10},{9,11},{10,... | collective-permute-start | bytes 1544 | tf_op jit(solution)/shard_map/ppermute | solution.py:21
  7.9 2.1 %shard_map.68 = (bf16[2048,768]{1,0:T(8,128)(2,1)S(1)}, f32[1,2048]{1,0:T(1,128)S(1)}, bf16[16,768]{1,0:T(8,128)(2,1)S(1)}) custom-call(bf16[2048,768]{1,0:T(8,128)(2,1)} %heads_ref.1, bf16[16,768]{1,0:T(8,128)(2,1)} %new_ref.1, s32[2,64]{1,0:T(2,128)S(1)} %pad_add_fusion.1.unused.ids_ref), custom_call_target="tpu_custom_call" | custom-call | tf_op jit(solution)/shard_map/pallas_call | solution.py:45
  10.0 0.0 collective-permute-done.1.refs_1_
  10.0 0.0 collective-permute-done.2.refs_2_
  10.0 0.0 collective-permute-done.3.refs_3_
  10.0 1.2 %shard_map.69 = (f32[8,128]{1,0:T(8,128)S(1)}, s32[2,64]{1,0:T(2,128)S(1)}) custom-call(s32[2,64]{1,0:T(2,128)S(1)} %pad_add_fusion.1.unused.ids_ref, bf16[2048,768]{1,0:T(8,128)(2,1)S(1)} %get-tuple-element.13.heads_ref, f32[1,2048]{1,0:T(1,128)S(1)} %get-tuple-element.14.head_sq_ref, bf16[16,768]{1,0:T(8,128)(2,1)S(1)} %get-tuple-element.15.refs_0_, ...), custom_call_target="tpu_custom_call" | custom-call | tf_op jit(solution)/shard_map/pallas_call | solution.py:45
  11.2 0.1 collective-permute-start.4
  11.3 0.0 collective-permute-done.5
  11.3 2.7 %collective-permute-start.6 = (s32[4,64]{1,0:T(4,128)S(1)}, s32[4,64]{1,0:T(4,128)S(1)}, u32[]{:S(2)}, u32[]{:S(2)}) collective-permute-start(s32[4,64]{1,0:T(4,128)S(1)} %pad_add_fusion.near_ref), channel_id=1, source_target_pairs={{0,4},{1,5},{2,6},{3,7},{4,0},{5,1},{6,2},{7,3},{8,12},{9,13},{10,... | collective-permute-start | bytes 3080 | tf_op jit(solution)/shard_map/ppermute | solution.py:21
  14.0 0.0 collective-permute-done.4
  14.0 1.5 %collective-permute-start.7 = (f32[8,128]{1,0:T(8,128)S(1)}, f32[8,128]{1,0:T(8,128)S(1)}, u32[]{:S(2)}, u32[]{:S(2)}) collective-permute-start(f32[8,128]{1,0:T(8,128)S(1)} %add.3.unused.mine_ref), channel_id=1, source_target_pairs={{0,16},{8,24},{16,0},{24,8},{1,17},{9,25},{17,1},{25,9},{2,18},{10... | collective-permute-start | bytes 12296 | tf_op jit(solution)/shard_map/ppermute | solution.py:21
  15.5 0.0 copy-done
  15.5 0.0 copy-done.1
  15.5 0.2 shard_map.70
  15.7 0.2 collective-permute-done.6.far_ref
  15.9 0.8 %shard_map.71.rows_ref = bf16[128,768]{1,0:T(8,128)(2,1)S(1)} custom-call(s32[4,64]{1,0:T(4,128)S(1)} %pad_add_fusion.near_ref, s32[4,64]{1,0:T(4,128)S(1)} %collective-permute-done.6.far_ref, bf16[2048,768]{1,0:T(8,128)(2,1)S(1)} %get-tuple-element.13.heads_ref, bf16[64,128]{1,0:T(8,128)(2,1)S(1)} %get-tuple-element.17.unused.back_ref), custom_call_target="tpu_custom_call" | custom-call | flops 402653184 | bytes 3145728 | tf_op jit(solution)/shard_map/pallas_call | solution.py:45
  16.7 0.9 %collective-permute-done.7.other_ref = f32[8,128]{1,0:T(8,128)S(1)} collective-permute-done((f32[8,128]{1,0:T(8,128)S(1)}, f32[8,128]{1,0:T(8,128)S(1)}, u32[]{:S(2)}, u32[]{:S(2)}) %collective-permute-start.7) | collective-permute-done | bytes 4128 | tf_op jit(solution)/shard_map/ppermute | solution.py:21
  17.6 9.8 %all_to_all.5.listed_ref = bf16[8,104,128]{2,1,0:T(8,128)(2,1)S(1)} all-to-all(bf16[8,104,128]{2,1,0:T(8,128)(2,1)S(1)} %shard_map.72), channel_id=1, replica_groups={{4,0,6,2,7,3,5,1},{12,8,14,10,15,11,13,9},{20,16,22,18,23,19,21,17},{28..., dimensions={0} | all-to-all | bytes 425984 | tf_op jit(solution)/shard_map/all_to_all | solution.py:316
  27.4 1.0 %shard_map.73 = (f32[1,16]{1,0:T(1,128)}, f32[1,16]{1,0:T(1,128)}, f32[1,64,128]{2,1,0:T(8,128)}) custom-call(bf16[64,128]{1,0:T(8,128)(2,1)S(1)} %get-tuple-element.17.unused.back_ref, f32[1,128]{1,0:T(1,128)S(1)} %get-tuple-element.18.vec_sq_ref, bf16[8,104,128]{2,1,0:T(8,128)(2,1)S(1)} %all_to_all.5.listed_ref, bf16[1,128,768]{2,1,0:T(8,128)(2,1)S(1)} %copy-done), custom_call_target="tpu_custom_call" | custom-call | flops 25165824 | bytes 393216 | tf_op jit(solution)/shard_map/pallas_call | solution.py:45
  (4 shorter events, 0.1 us)
Async XLA Ops:
  0.6 5.5 %collective-permute-start = (s32[1,64]{1,0:T(1,128)}, s32[1,64]{1,0:T(1,128)S(1)}, u32[]{:S(2)}, u32[]{:S(2)}) collective-permute-start(s32[1,64]{1,0:T(1,128)} %ids_ref.3), channel_id=1, source_target_pairs={{0,1},{1,0},{2,3},{3,2},{4,5},{5,4},{6,7},{7,6},{8,9},{9,8},{10,11... | collective-permute-start | bytes 776 | tf_op jit(solution)/shard_map/ppermute | solution.py:21
  3.6 6.3 %collective-permute-start.1 = (bf16[16,768]{1,0:T(8,128)(2,1)}, bf16[16,768]{1,0:T(8,128)(2,1)S(1)}, u32[]{:S(2)}, u32[]{:S(2)}) collective-permute-start(bf16[16,768]{1,0:T(8,128)(2,1)} %new_ref.1), channel_id=1, source_target_pairs={{0,8},{8,0},{16,24},{24,16},{1,9},{9,1},{17,25},{25,17},{2,10},{10... | collective-permute-start | bytes 73736 | tf_op jit(solution)/shard_map/ppermute | solution.py:21
  3.6 6.4 %collective-permute-start.2 = (bf16[16,768]{1,0:T(8,128)(2,1)}, bf16[16,768]{1,0:T(8,128)(2,1)S(1)}, u32[]{:S(2)}, u32[]{:S(2)}) collective-permute-start(bf16[16,768]{1,0:T(8,128)(2,1)} %new_ref.1), channel_id=1, source_target_pairs={{0,16},{8,24},{16,0},{24,8},{1,17},{9,25},{17,1},{25,9},{2,18},{10... | collective-permute-start | bytes 73736 | tf_op jit(solution)/shard_map/ppermute | solution.py:21
  5.2 4.8 %collective-permute-start.3 = (bf16[16,768]{1,0:T(8,128)(2,1)}, bf16[16,768]{1,0:T(8,128)(2,1)S(1)}, u32[]{:S(2)}, u32[]{:S(2)}) collective-permute-start(bf16[16,768]{1,0:T(8,128)(2,1)} %new_ref.1), channel_id=1, source_target_pairs={{0,24},{8,16},{16,8},{24,0},{1,25},{9,17},{17,9},{25,1},{2,26},{10... | collective-permute-start | bytes 73736 | tf_op jit(solution)/shard_map/ppermute | solution.py:21
  6.2 9.3 %copy-start = (bf16[1,128,768]{2,1,0:T(8,128)(2,1)S(1)}, bf16[1,128,768]{2,1,0:T(8,128)(2,1)}, u32[]{:S(2)}) copy-start(bf16[1,128,768]{2,1,0:T(8,128)(2,1)} %vectors_ref.3) | copy-start | bytes 589828
  6.2 9.3 %copy-start.1 = (s32[1,64]{1,0:T(1,128)S(1)}, s32[1,64]{1,0:T(1,128)}, u32[]{:S(2)}) copy-start(s32[1,64]{1,0:T(1,128)} %ids_ref.3) | copy-start | bytes 772
  6.2 5.1 %collective-permute-start.5 = (s32[2,64]{1,0:T(2,128)S(1)}, s32[2,64]{1,0:T(2,128)S(1)}, u32[]{:S(2)}, u32[]{:S(2)}) collective-permute-start(s32[2,64]{1,0:T(2,128)S(1)} %pad_add_fusion.1.unused.ids_ref), channel_id=1, source_target_pairs={{0,2},{1,3},{2,0},{3,1},{4,6},{5,7},{6,4},{7,5},{8,10},{9,11},{10,... | collective-permute-start | bytes 1544 | tf_op jit(solution)/shard_map/ppermute | solution.py:21
  11.2 2.8 %collective-permute-start.4 = (f32[8,128]{1,0:T(8,128)S(1)}, f32[8,128]{1,0:T(8,128)S(1)}, u32[]{:S(2)}, u32[]{:S(2)}) collective-permute-start(f32[8,128]{1,0:T(8,128)S(1)} %get-tuple-element.16), channel_id=1, source_target_pairs={{0,8},{8,0},{16,24},{24,16},{1,9},{9,1},{17,25},{25,17},{2,10},{10... | collective-permute-start | bytes 12296 | tf_op jit(solution)/shard_map/ppermute | solution.py:21
  11.3 4.5 %collective-permute-start.6 = (s32[4,64]{1,0:T(4,128)S(1)}, s32[4,64]{1,0:T(4,128)S(1)}, u32[]{:S(2)}, u32[]{:S(2)}) collective-permute-start(s32[4,64]{1,0:T(4,128)S(1)} %pad_add_fusion.near_ref), channel_id=1, source_target_pairs={{0,4},{1,5},{2,6},{3,7},{4,0},{5,1},{6,2},{7,3},{8,12},{9,13},{10,... | collective-permute-start | bytes 3080 | tf_op jit(solution)/shard_map/ppermute | solution.py:21
  14.0 3.6 %collective-permute-start.7 = (f32[8,128]{1,0:T(8,128)S(1)}, f32[8,128]{1,0:T(8,128)S(1)}, u32[]{:S(2)}, u32[]{:S(2)}) collective-permute-start(f32[8,128]{1,0:T(8,128)S(1)} %add.3.unused.mine_ref), channel_id=1, source_target_pairs={{0,16},{8,24},{16,0},{24,8},{1,17},{9,25},{17,1},{25,9},{2,18},{10... | collective-permute-start | bytes 12296 | tf_op jit(solution)/shard_map/ppermute | solution.py:21

commit v32 on v27

--- a/solution.py
+++ b/solution.py
@@ -63,7 +63,7 @@
 
 def early_kernel(heads_ref, new_ref, unused, kept_ref, head_sq_ref, kept_new_ref, sems):
     head_dev, width = heads_ref.shape
-    tiles = 4
+    tiles = 2
     tile = head_dev // tiles
     parts = [pl.ds(i * tile, tile) for i in range(tiles)]
     copies = [
@@ -262,7 +262,7 @@
         ),
         (in_hbm(heads), in_hbm(new_heads), ids),
         (0, 0),
-        scratch=[pltpu.SemaphoreType.DMA((5,))],
+        scratch=[pltpu.SemaphoreType.DMA((3,))],
         spaces=[HBM, HBM, pl.ANY],
     )
     lines = 2 * groups * new_count // LANES

time: 27.8 us -> 28 us (level)
  transfers between devices with their start and end apart: 8 -> 8, of which waited for: 2 -> 2; matrix products, arithmetic and copies ran while one was open for 0% -> 0% of each run, Pallas kernels for 18% -> 19%
where the time goes in v32:
time: 28 us; the launch traced here: 27.8 us
  starting transfers between devices  10.7 us (38%)
  blocking collectives  9.04 us (32%)
  Pallas kernels  6.16 us (22%)
  waiting for transfers between devices  1.1 us (4%)
  between operations  0.74 us (3%)
    ppermute x8, starting transfers between devices, from_partner(): lax.ppermute(value, axis, [(source, source ^ mask) for source in range(co...  10.7 us
    all_to_all x1, blocking collectives, per_device(): lax.all_to_all(message, 'member', 0, 0, tiled=True, axis_index_groups=[by...  9.04 us
    pallas_call x7, Pallas kernels, call(): pl.pallas_call(body, out_shape=shapes, in_specs=[pl.BlockSpec(memory_spac...  6.16 us
    ppermute x8, waiting for transfers between devices, from_partner(): lax.ppermute(value, axis, [(source, source ^ mask) for source in range(co...  1.1 us
  transfers between devices with their start and end apart: 8, of which 2 were waited for; matrix products, arithmetic and copies ran while one was open for 0% of the time, Pallas kernels for 19%

profile of v32, /device:TPU:0, one launch (start us, length us, event | category | flops | bytes accessed | tf_op | source)
XLA Modules:
  0.0 27.8 jit_solution(647703001910419610)
XLA Ops:
  0.6 3.0 %collective-permute-start = (s32[1,64]{1,0:T(1,128)}, s32[1,64]{1,0:T(1,128)S(1)}, u32[]{:S(2)}, u32[]{:S(2)}) collective-permute-start(s32[1,64]{1,0:T(1,128)} %ids_ref.3), channel_id=1, source_target_pairs={{0,1},{1,0},{2,3},{3,2},{4,5},{5,4},{6,7},{7,6},{8,9},{9,8},{10,11... | collective-permute-start | bytes 776 | tf_op jit(solution)/shard_map/ppermute | solution.py:21
  3.6 0.0 collective-permute-start.1
  3.6 1.5 %collective-permute-start.2 = (bf16[16,768]{1,0:T(8,128)(2,1)}, bf16[16,768]{1,0:T(8,128)(2,1)S(1)}, u32[]{:S(2)}, u32[]{:S(2)}) collective-permute-start(bf16[16,768]{1,0:T(8,128)(2,1)} %new_ref.1), channel_id=1, source_target_pairs={{0,16},{8,24},{16,0},{24,8},{1,17},{9,25},{17,1},{25,9},{2,18},{10... | collective-permute-start | bytes 73736 | tf_op jit(solution)/shard_map/ppermute | solution.py:21
  5.2 0.3 %collective-permute-start.3 = (bf16[16,768]{1,0:T(8,128)(2,1)}, bf16[16,768]{1,0:T(8,128)(2,1)S(1)}, u32[]{:S(2)}, u32[]{:S(2)}) collective-permute-start(bf16[16,768]{1,0:T(8,128)(2,1)} %new_ref.1), channel_id=1, source_target_pairs={{0,24},{8,16},{16,8},{24,0},{1,25},{9,17},{17,9},{25,1},{2,26},{10... | collective-permute-start | bytes 73736 | tf_op jit(solution)/shard_map/ppermute | solution.py:21
  5.5 0.7 %shard_map.67 = s32[1,64]{1,0:T(1,128)S(1)} custom-call(s32[1,64]{1,0:T(1,128)} %ids_ref.3), custom_call_target="tpu_custom_call" | custom-call | tf_op jit(solution)/shard_map/pallas_call | solution.py:43
  6.2 0.0 collective-permute-done
  6.2 0.0 copy-start
  6.2 0.0 copy-start.1
  6.2 1.6 %collective-permute-start.5 = (s32[2,64]{1,0:T(2,128)S(1)}, s32[2,64]{1,0:T(2,128)S(1)}, u32[]{:S(2)}, u32[]{:S(2)}) collective-permute-start(s32[2,64]{1,0:T(2,128)S(1)} %pad_add_fusion.1.unused.ids_ref), channel_id=1, source_target_pairs={{0,2},{1,3},{2,0},{3,1},{4,6},{5,7},{6,4},{7,5},{8,10},{9,11},{10,... | collective-permute-start | bytes 1544 | tf_op jit(solution)/shard_map/ppermute | solution.py:21
  7.9 2.3 %shard_map.68 = (bf16[2048,768]{1,0:T(8,128)(2,1)S(1)}, f32[1,2048]{1,0:T(1,128)S(1)}, bf16[16,768]{1,0:T(8,128)(2,1)S(1)}) custom-call(bf16[2048,768]{1,0:T(8,128)(2,1)} %heads_ref.1, bf16[16,768]{1,0:T(8,128)(2,1)} %new_ref.1, s32[2,64]{1,0:T(2,128)S(1)} %pad_add_fusion.1.unused.ids_ref), custom_call_target="tpu_custom_call" | custom-call | tf_op jit(solution)/shard_map/pallas_call | solution.py:43
  10.1 0.0 collective-permute-done.1.refs_1_
  10.2 0.0 collective-permute-done.2.refs_2_
  10.2 0.0 collective-permute-done.3.refs_3_
  10.2 1.2 %shard_map.69 = (f32[8,128]{1,0:T(8,128)S(1)}, s32[2,64]{1,0:T(2,128)S(1)}) custom-call(s32[2,64]{1,0:T(2,128)S(1)} %pad_add_fusion.1.unused.ids_ref, bf16[2048,768]{1,0:T(8,128)(2,1)S(1)} %get-tuple-element.13.heads_ref, f32[1,2048]{1,0:T(1,128)S(1)} %get-tuple-element.14.head_sq_ref, bf16[16,768]{1,0:T(8,128)(2,1)S(1)} %get-tuple-element.15.refs_0_, ...), custom_call_target="tpu_custom_call" | custom-call | tf_op jit(solution)/shard_map/pallas_call | solution.py:43
  11.4 0.1 collective-permute-start.4
  11.5 0.0 collective-permute-done.5
  11.5 2.7 %collective-permute-start.6 = (s32[4,64]{1,0:T(4,128)S(1)}, s32[4,64]{1,0:T(4,128)S(1)}, u32[]{:S(2)}, u32[]{:S(2)}) collective-permute-start(s32[4,64]{1,0:T(4,128)S(1)} %pad_add_fusion.near_ref), channel_id=1, source_target_pairs={{0,4},{1,5},{2,6},{3,7},{4,0},{5,1},{6,2},{7,3},{8,12},{9,13},{10,... | collective-permute-start | bytes 3080 | tf_op jit(solution)/shard_map/ppermute | solution.py:21
  14.2 0.0 collective-permute-done.4
  14.2 1.5 %collective-permute-start.7 = (f32[8,128]{1,0:T(8,128)S(1)}, f32[8,128]{1,0:T(8,128)S(1)}, u32[]{:S(2)}, u32[]{:S(2)}) collective-permute-start(f32[8,128]{1,0:T(8,128)S(1)} %add.3.unused.mine_ref), channel_id=1, source_target_pairs={{0,16},{8,24},{16,0},{24,8},{1,17},{9,25},{17,1},{25,9},{2,18},{10... | collective-permute-start | bytes 12296 | tf_op jit(solution)/shard_map/ppermute | solution.py:21
  15.7 0.0 copy-done
  15.7 0.0 copy-done.1
  15.7 0.2 shard_map.70
  15.9 0.2 collective-permute-done.6.far_ref
  16.0 0.8 %shard_map.71.rows_ref = bf16[128,768]{1,0:T(8,128)(2,1)S(1)} custom-call(s32[4,64]{1,0:T(4,128)S(1)} %pad_add_fusion.near_ref, s32[4,64]{1,0:T(4,128)S(1)} %collective-permute-done.6.far_ref, bf16[2048,768]{1,0:T(8,128)(2,1)S(1)} %get-tuple-element.13.heads_ref, bf16[64,128]{1,0:T(8,128)(2,1)S(1)} %get-tuple-element.17.unused.back_ref), custom_call_target="tpu_custom_call" | custom-call | flops 402653184 | bytes 3145728 | tf_op jit(solution)/shard_map/pallas_call | solution.py:43
  16.9 0.9 %collective-permute-done.7.other_ref = f32[8,128]{1,0:T(8,128)S(1)} collective-permute-done((f32[8,128]{1,0:T(8,128)S(1)}, f32[8,128]{1,0:T(8,128)S(1)}, u32[]{:S(2)}, u32[]{:S(2)}) %collective-permute-start.7) | collective-permute-done | bytes 4128 | tf_op jit(solution)/shard_map/ppermute | solution.py:21
  17.8 9.0 %all_to_all.5.listed_ref = bf16[8,104,128]{2,1,0:T(8,128)(2,1)S(1)} all-to-all(bf16[8,104,128]{2,1,0:T(8,128)(2,1)S(1)} %shard_map.72), channel_id=1, replica_groups={{4,0,7,3,6,2,5,1},{12,8,15,11,14,10,13,9},{20,16,23,19,22,18,21,17},{28..., dimensions={0} | all-to-all | bytes 425984 | tf_op jit(solution)/shard_map/all_to_all | solution.py:314
  26.9 1.0 %shard_map.73 = (f32[1,16]{1,0:T(1,128)}, f32[1,16]{1,0:T(1,128)}, f32[1,64,128]{2,1,0:T(8,128)}) custom-call(bf16[64,128]{1,0:T(8,128)(2,1)S(1)} %get-tuple-element.17.unused.back_ref, f32[1,128]{1,0:T(1,128)S(1)} %get-tuple-element.18.vec_sq_ref, bf16[8,104,128]{2,1,0:T(8,128)(2,1)S(1)} %all_to_all.5.listed_ref, bf16[1,128,768]{2,1,0:T(8,128)(2,1)S(1)} %copy-done), custom_call_target="tpu_custom_call" | custom-call | flops 25165824 | bytes 393216 | tf_op jit(solution)/shard_map/pallas_call | solution.py:43
  (4 shorter events, 0.1 us)
Async XLA Ops:
  0.6 5.5 %collective-permute-start = (s32[1,64]{1,0:T(1,128)}, s32[1,64]{1,0:T(1,128)S(1)}, u32[]{:S(2)}, u32[]{:S(2)}) collective-permute-start(s32[1,64]{1,0:T(1,128)} %ids_ref.3), channel_id=1, source_target_pairs={{0,1},{1,0},{2,3},{3,2},{4,5},{5,4},{6,7},{7,6},{8,9},{9,8},{10,11... | collective-permute-start | bytes 776 | tf_op jit(solution)/shard_map/ppermute | solution.py:21
  3.6 6.5 %collective-permute-start.1 = (bf16[16,768]{1,0:T(8,128)(2,1)}, bf16[16,768]{1,0:T(8,128)(2,1)S(1)}, u32[]{:S(2)}, u32[]{:S(2)}) collective-permute-start(bf16[16,768]{1,0:T(8,128)(2,1)} %new_ref.1), channel_id=1, source_target_pairs={{0,8},{8,0},{16,24},{24,16},{1,9},{9,1},{17,25},{25,17},{2,10},{10... | collective-permute-start | bytes 73736 | tf_op jit(solution)/shard_map/ppermute | solution.py:21
  3.6 6.5 %collective-permute-start.2 = (bf16[16,768]{1,0:T(8,128)(2,1)}, bf16[16,768]{1,0:T(8,128)(2,1)S(1)}, u32[]{:S(2)}, u32[]{:S(2)}) collective-permute-start(bf16[16,768]{1,0:T(8,128)(2,1)} %new_ref.1), channel_id=1, source_target_pairs={{0,16},{8,24},{16,0},{24,8},{1,17},{9,25},{17,1},{25,9},{2,18},{10... | collective-permute-start | bytes 73736 | tf_op jit(solution)/shard_map/ppermute | solution.py:21
  5.2 5.0 %collective-permute-start.3 = (bf16[16,768]{1,0:T(8,128)(2,1)}, bf16[16,768]{1,0:T(8,128)(2,1)S(1)}, u32[]{:S(2)}, u32[]{:S(2)}) collective-permute-start(bf16[16,768]{1,0:T(8,128)(2,1)} %new_ref.1), channel_id=1, source_target_pairs={{0,24},{8,16},{16,8},{24,0},{1,25},{9,17},{17,9},{25,1},{2,26},{10... | collective-permute-start | bytes 73736 | tf_op jit(solution)/shard_map/ppermute | solution.py:21
  6.2 9.5 %copy-start = (bf16[1,128,768]{2,1,0:T(8,128)(2,1)S(1)}, bf16[1,128,768]{2,1,0:T(8,128)(2,1)}, u32[]{:S(2)}) copy-start(bf16[1,128,768]{2,1,0:T(8,128)(2,1)} %vectors_ref.3) | copy-start | bytes 589828
  6.2 9.5 %copy-start.1 = (s32[1,64]{1,0:T(1,128)S(1)}, s32[1,64]{1,0:T(1,128)}, u32[]{:S(2)}) copy-start(s32[1,64]{1,0:T(1,128)} %ids_ref.3) | copy-start | bytes 772
  6.2 5.3 %collective-permute-start.5 = (s32[2,64]{1,0:T(2,128)S(1)}, s32[2,64]{1,0:T(2,128)S(1)}, u32[]{:S(2)}, u32[]{:S(2)}) collective-permute-start(s32[2,64]{1,0:T(2,128)S(1)} %pad_add_fusion.1.unused.ids_ref), channel_id=1, source_target_pairs={{0,2},{1,3},{2,0},{3,1},{4,6},{5,7},{6,4},{7,5},{8,10},{9,11},{10,... | collective-permute-start | bytes 1544 | tf_op jit(solution)/shard_map/ppermute | solution.py:21
  11.4 2.8 %collective-permute-start.4 = (f32[8,128]{1,0:T(8,128)S(1)}, f32[8,128]{1,0:T(8,128)S(1)}, u32[]{:S(2)}, u32[]{:S(2)}) collective-permute-start(f32[8,128]{1,0:T(8,128)S(1)} %get-tuple-element.16), channel_id=1, source_target_pairs={{0,8},{8,0},{16,24},{24,16},{1,9},{9,1},{17,25},{25,17},{2,10},{10... | collective-permute-start | bytes 12296 | tf_op jit(solution)/shard_map/ppermute | solution.py:21
  11.5 4.5 %collective-permute-start.6 = (s32[4,64]{1,0:T(4,128)S(1)}, s32[4,64]{1,0:T(4,128)S(1)}, u32[]{:S(2)}, u32[]{:S(2)}) collective-permute-start(s32[4,64]{1,0:T(4,128)S(1)} %pad_add_fusion.near_ref), channel_id=1, source_target_pairs={{0,4},{1,5},{2,6},{3,7},{4,0},{5,1},{6,2},{7,3},{8,12},{9,13},{10,... | collective-permute-start | bytes 3080 | tf_op jit(solution)/shard_map/ppermute | solution.py:21
  14.2 3.6 %collective-permute-start.7 = (f32[8,128]{1,0:T(8,128)S(1)}, f32[8,128]{1,0:T(8,128)S(1)}, u32[]{:S(2)}, u32[]{:S(2)}) collective-permute-start(f32[8,128]{1,0:T(8,128)S(1)} %add.3.unused.mine_ref), channel_id=1, source_target_pairs={{0,16},{8,24},{16,0},{24,8},{1,17},{9,25},{17,1},{25,9},{2,18},{10... | collective-permute-start | bytes 12296 | tf_op jit(solution)/shard_map/ppermute | solution.py:21
